TPU v7x, 32 devices: a whole 2x2x4 slice. The times are simulated.
32 devices in a mesh: dp: 8 (over y, x, core), tensor: 4 (over z).
Axes of the slice: x: 2, y: 2, z: 4, core: 2. Of those that a mesh axis runs over, the one named last changes fastest.
Arguments:
- inputs: bfloat16 [2, 8, 1024, 1024], P(None, 'dp', 'tensor'), may hold values from -6 to 6
- cotangent: bfloat16 [2, 8, 1024, 1024], P(None, 'dp', 'tensor'), may hold values from -6 to 6
- lengths: int32 [2, 8], P(None, 'dp'), may hold values from 256 to 1024, as said below
- qkv_weight: bfloat16 [1024, 3, 1024], P('dp', None, 'tensor'), may hold values from -0.1875 to 0.1875
- attn_out_weight: bfloat16 [1024, 1024], P('dp', 'tensor'), may hold values from -1.5 to 1.5
- ffn_in_weight: bfloat16 [1024, 2, 2624], P('dp', None, 'tensor'), may hold values from -0.1875 to 0.1875
- ffn_out_weight: bfloat16 [1024, 2624], P('dp', 'tensor'), may hold values from -0.125 to 0.125
- norm_gains: float32 [2, 1024], replicated, may hold values from 0.5 to 1.5
- qkv_moment: float32 [1024, 3, 1024], P('dp', None, 'tensor'), may hold values from -384 to 384
- attn_out_moment: float32 [1024, 1024], P('dp', 'tensor'), may hold values from -64 to 64
- ffn_in_moment: float32 [1024, 2, 2624], P('dp', None, 'tensor'), may hold values from -320 to 320
- ffn_out_moment: float32 [1024, 2624], P('dp', 'tensor'), may hold values from -512 to 512
- gain_first: float32 [2, 1024], replicated, may hold values from -80 to 80
- gain_second: float32 [2, 1024], replicated, may hold values from 655.36 to 2621.44
Outputs:
- outputs: bfloat16 [2, 8, 1024, 1024], P(None, 'dp', 'tensor')
- input_grad: float32 [2, 8, 1024, 1024], P(None, 'dp', 'tensor')
- qkv_moment_new: float32 [1024, 3, 1024], P('dp', None, 'tensor')
- qkv_weight_new: float32 [1024, 3, 1024], P('dp', None, 'tensor')
- attn_out_moment_new: float32 [1024, 1024], P('dp', 'tensor')
- attn_out_weight_new: float32 [1024, 1024], P('dp', 'tensor')
- ffn_in_moment_new: float32 [1024, 2, 2624], P('dp', None, 'tensor')
- ffn_in_weight_new: float32 [1024, 2, 2624], P('dp', None, 'tensor')
- ffn_out_moment_new: float32 [1024, 2624], P('dp', 'tensor')
- ffn_out_weight_new: float32 [1024, 2624], P('dp', 'tensor')
- gain_first_new: float32 [2, 1024], replicated
- gain_second_new: float32 [2, 1024], replicated
- norm_gains_new: float32 [2, 1024], replicated
Inputs may be any that keep to these rules, and one draw needn't show every extreme that they name: lengths[m, s] counts the real tokens of sequence s of micro-batch m, which stand first in its slot; in every column s some micro-batch's sequence fills its whole slot of 1024.
All inputs are finite; a program needn't handle non-finite values.
Results may differ from a plain program's by a relative error of at most 0.013.
Values may be sent and summed in bfloat16 or wider, within the bound.
A program may use at most 192 MiB of HBM per device.

v0:
```python
import math

import jax
import jax.numpy as jnp
from jax import lax
from jax.sharding import PartitionSpec as P

HEAD_DIM = 64
NS_ITERS = 5
STEP = 10


ROPE_BASE = 160000.0
NORM_EPS = 1e-05
MASK_VALUE = -1e30
MOMENTUM = 0.95
MUON_RATE = 0.1
DECAY_RATE = 0.01
QUINTIC_ONE = 3.4445
QUINTIC_THREE = -4.775
QUINTIC_FIVE = 2.0315
NORM_FLOOR = 1e-07
BETA_ONE = 0.9
BETA_TWO = 0.95
ADAM_RATE = 0.2
ADAM_EPS = 1e-08


def rotary(length):
    half_size = HEAD_DIM // 2
    exponents = jnp.arange(half_size).astype(jnp.float32) / half_size
    frequency = jnp.power(ROPE_BASE, -exponents)
    angles = jnp.arange(length).astype(jnp.float32)[:, None] * frequency[None, :]
    return (jnp.cos(angles), jnp.sin(angles))


def rotate(vectors, cosine_table, sine_table):
    half_size = vectors.shape[-1] // 2
    first_half = vectors[..., :half_size]
    second_half = vectors[..., half_size:]
    cos_part = cosine_table[:, None, :]
    sin_part = sine_table[:, None, :]
    return jnp.concatenate(
        [
            first_half * cos_part - second_half * sin_part,
            second_half * cos_part + first_half * sin_part,
        ],
        axis=-1,
    )


def layer_norm_parts(vectors, gain):
    centre = vectors - jnp.mean(vectors, axis=-1, keepdims=True)
    inverse = lax.rsqrt(jnp.mean(centre * centre, axis=-1, keepdims=True) + NORM_EPS)
    normed = centre * inverse
    return (normed, inverse, normed * gain)


def layer_norm_back(grad_out, normed, inverse, gain):
    grad_normed = grad_out * gain
    mean_grad = jnp.mean(grad_normed, axis=-1, keepdims=True)
    mean_cross = jnp.mean(grad_normed * normed, axis=-1, keepdims=True)
    return (
        inverse * (grad_normed - mean_grad - normed * mean_cross),
        jnp.sum(grad_out * normed, axis=0),
    )


def contract_rows(left, right):
    return lax.dot_general(
        left, right, (((0,), (0,)), ((), ())), preferred_element_type=jnp.float32
    )


def contract_cols(left, right):
    return lax.dot_general(
        left, right, (((1,), (1,)), ((), ())), preferred_element_type=jnp.float32
    )


def highest_dot(left, right):
    return jnp.dot(left, right, precision=lax.Precision.HIGHEST)


def quintic(column_block, gram_sum):
    product = highest_dot(gram_sum, column_block)
    return (
        QUINTIC_ONE * column_block
        + QUINTIC_THREE * product
        + QUINTIC_FIVE * highest_dot(gram_sum, product)
    )


def attention_forward(queries, key_rows, values, length):
    seq_len, head_count, head_size = queries.shape
    block_rows = min(512, seq_len)
    key_valid = (jnp.arange(seq_len) < length)[None, None, :]
    score_scale = 1.0 / math.sqrt(head_size)

    def one_block(first_row):
        query_block = lax.dynamic_slice_in_dim(queries, first_row, block_rows, 0)
        scores = (
            jnp.einsum("qhd,khd->hqk", query_block, key_rows, preferred_element_type=jnp.float32)
            * score_scale
        )
        scores = jnp.where(key_valid, scores, MASK_VALUE)
        highest = jnp.max(scores, axis=-1, keepdims=True)
        exponent = jnp.exp(scores - highest)
        row_total = jnp.sum(exponent, axis=-1, keepdims=True)
        soft_weights = (exponent / row_total).astype(jnp.bfloat16)
        context = jnp.einsum(
            "hqk,khd->qhd", soft_weights, values, preferred_element_type=jnp.float32
        )
        return (context, highest[..., 0] + jnp.log(row_total[..., 0]))

    starts = jnp.arange(seq_len // block_rows) * block_rows
    context, log_total = lax.map(one_block, starts)
    return (context.reshape(seq_len, head_count, head_size), log_total)


def attention_backward(queries, key_rows, values, log_total, grad_context, length):
    seq_len, head_count, head_size = queries.shape
    block_rows = min(512, seq_len)
    key_valid = (jnp.arange(seq_len) < length)[None, None, :]
    score_scale = 1.0 / math.sqrt(head_size)

    def one_block(carry, entry):
        grad_keys, grad_values = carry
        first_row, block_total = entry
        query_block = lax.dynamic_slice_in_dim(queries, first_row, block_rows, 0)
        grad_block = lax.dynamic_slice_in_dim(grad_context, first_row, block_rows, 0)
        scores = (
            jnp.einsum("qhd,khd->hqk", query_block, key_rows, preferred_element_type=jnp.float32)
            * score_scale
        )
        scores = jnp.where(key_valid, scores, MASK_VALUE)
        soft_weights = jnp.exp(scores - block_total[..., None])
        grad_probs = jnp.einsum(
            "qhd,khd->hqk", grad_block, values, preferred_element_type=jnp.float32
        )
        inner_sum = jnp.sum(soft_weights * grad_probs, axis=-1, keepdims=True)
        grad_scores = (soft_weights * (grad_probs - inner_sum)).astype(jnp.bfloat16)
        grad_query = (
            jnp.einsum("hqk,khd->qhd", grad_scores, key_rows, preferred_element_type=jnp.float32)
            * score_scale
        )
        grad_keys = (
            grad_keys
            + jnp.einsum(
                "hqk,qhd->khd", grad_scores, query_block, preferred_element_type=jnp.float32
            )
            * score_scale
        )
        grad_values = grad_values + jnp.einsum(
            "hqk,qhd->khd",
            soft_weights.astype(jnp.bfloat16),
            grad_block,
            preferred_element_type=jnp.float32,
        )
        return ((grad_keys, grad_values), grad_query)

    starts = jnp.arange(seq_len // block_rows) * block_rows
    empty = jnp.zeros((seq_len, head_count, head_size), jnp.float32)
    (grad_keys, grad_values), grad_query = lax.scan(one_block, (empty, empty), (starts, log_total))
    return (grad_query.reshape(seq_len, head_count, head_size), grad_keys, grad_values)


def gather_weights(qkv_weight, attn_out_weight, ffn_in_weight, ffn_out_weight):
    return (
        lax.all_gather(qkv_weight, "dp", axis=0, tiled=True),
        lax.all_gather(attn_out_weight, "dp", axis=0, tiled=True),
        lax.all_gather(ffn_in_weight, "dp", axis=0, tiled=True),
        lax.all_gather(ffn_out_weight, "dp", axis=0, tiled=True),
    )


def reduce_grads(weight_grads):
    return (
        lax.psum_scatter(weight_grads[0], "dp", scatter_dimension=0, tiled=True),
        lax.psum_scatter(weight_grads[1], "dp", scatter_dimension=0, tiled=True),
        lax.psum_scatter(weight_grads[2], "dp", scatter_dimension=0, tiled=True),
        lax.psum_scatter(weight_grads[3], "dp", scatter_dimension=0, tiled=True),
    )


def micro_batch(rows_in, grad_rows, length, gathered, norm_gains, cosine_table, sine_table):
    qkv_all, attn_all, ffn_in_all, ffn_out_all = gathered
    model_width = rows_in.shape[1]
    qkv_matrix = qkv_all.reshape(model_width, -1)
    ffn_matrix = ffn_in_all.reshape(model_width, -1)
    hidden_local = ffn_out_all.shape[1]
    head_count = attn_all.shape[1] // HEAD_DIM
    normed_one, inverse_one, scaled_one = layer_norm_parts(rows_in, norm_gains[0])
    full_one = lax.all_gather(scaled_one.astype(jnp.bfloat16), "tensor", axis=0, tiled=True)
    seq_len = full_one.shape[0]
    projected = jnp.dot(full_one, qkv_matrix, preferred_element_type=jnp.float32).reshape(
        seq_len, 3, head_count, HEAD_DIM
    )
    queries = rotate(projected[:, 0], cosine_table, sine_table).astype(jnp.bfloat16)
    key_rows = rotate(projected[:, 1], cosine_table, sine_table).astype(jnp.bfloat16)
    values = projected[:, 2].astype(jnp.bfloat16)
    context, log_total = attention_forward(queries, key_rows, values, length)
    context_low = context.astype(jnp.bfloat16).reshape(seq_len, head_count * HEAD_DIM)
    branch = lax.psum_scatter(
        contract_cols(context_low, attn_all), "tensor", scatter_dimension=0, tiled=True
    )
    middle = rows_in + branch
    normed_two, inverse_two, scaled_two = layer_norm_parts(middle, norm_gains[1])
    full_two = lax.all_gather(scaled_two.astype(jnp.bfloat16), "tensor", axis=0, tiled=True)
    gate_up = jnp.dot(full_two, ffn_matrix, preferred_element_type=jnp.float32)

    def activate(gate_part, up_part):
        return jax.nn.gelu(gate_part, approximate=False) * up_part

    hidden, activate_back = jax.vjp(activate, gate_up[:, :hidden_local], gate_up[:, hidden_local:])
    hidden_low = hidden.astype(jnp.bfloat16)
    ffn_branch = lax.psum_scatter(
        contract_cols(hidden_low, ffn_out_all), "tensor", scatter_dimension=0, tiled=True
    )
    result_rows = (middle + ffn_branch).astype(jnp.bfloat16)
    full_grad = lax.all_gather(grad_rows, "tensor", axis=0, tiled=True)
    grad_hidden = jnp.dot(full_grad, ffn_out_all, preferred_element_type=jnp.float32)
    grad_ffn_out = contract_rows(full_grad, hidden_low)
    grad_gate, grad_up = activate_back(grad_hidden)
    grad_gate_up = jnp.concatenate([grad_gate, grad_up], axis=1).astype(jnp.bfloat16)
    grad_ffn_in = contract_rows(full_two, grad_gate_up).reshape(ffn_in_all.shape)
    grad_scaled_two = lax.psum_scatter(
        contract_cols(grad_gate_up, ffn_matrix), "tensor", scatter_dimension=0, tiled=True
    )
    grad_from_two, gain_two = layer_norm_back(
        grad_scaled_two, normed_two, inverse_two, norm_gains[1]
    )
    grad_middle = grad_rows.astype(jnp.float32) + grad_from_two
    full_middle = lax.all_gather(grad_middle.astype(jnp.bfloat16), "tensor", axis=0, tiled=True)
    grad_context = jnp.dot(full_middle, attn_all, preferred_element_type=jnp.float32)
    grad_attn_out = contract_rows(full_middle, context_low)
    grad_context_low = grad_context.astype(jnp.bfloat16).reshape(seq_len, head_count, HEAD_DIM)
    grad_query, grad_keys, grad_values = attention_backward(
        queries, key_rows, values, log_total, grad_context_low, length
    )
    grad_projected = jnp.stack(
        [
            rotate(grad_query, cosine_table, -sine_table),
            rotate(grad_keys, cosine_table, -sine_table),
            grad_values,
        ],
        axis=1,
    )
    grad_projected = grad_projected.astype(jnp.bfloat16).reshape(seq_len, -1)
    grad_qkv = contract_rows(full_one, grad_projected).reshape(qkv_all.shape)
    grad_scaled_one = lax.psum_scatter(
        contract_cols(grad_projected, qkv_matrix), "tensor", scatter_dimension=0, tiled=True
    )
    grad_from_one, gain_one = layer_norm_back(
        grad_scaled_one, normed_one, inverse_one, norm_gains[0]
    )
    grad_input = grad_middle + grad_from_one
    return (
        result_rows,
        grad_input,
        (grad_qkv, grad_attn_out, grad_ffn_in, grad_ffn_out),
        jnp.stack([gain_one, gain_two]),
    )


def on_device(
    inputs,
    cotangent,
    lengths,
    qkv_weight,
    attn_out_weight,
    ffn_in_weight,
    ffn_out_weight,
    norm_gains,
    qkv_moment,
    attn_out_moment,
    ffn_in_moment,
    ffn_out_moment,
    gain_first,
    gain_second,
):
    tensor_count = lax.axis_size("tensor")
    seq_len = inputs.shape[2] * tensor_count
    cosine_table, sine_table = rotary(seq_len)
    reduced = None
    gain_total = jnp.zeros((2, inputs.shape[3]), jnp.float32)
    result_list = []
    input_list = []
    for micro_index in range(inputs.shape[0]):
        current = gather_weights(qkv_weight, attn_out_weight, ffn_in_weight, ffn_out_weight)
        result_rows, grad_input, weight_grads, gain_part = micro_batch(
            inputs[micro_index, 0].astype(jnp.float32),
            cotangent[micro_index, 0],
            lengths[micro_index, 0],
            current,
            norm_gains,
            cosine_table,
            sine_table,
        )
        result_list.append(result_rows)
        input_list.append(grad_input)
        gain_total = gain_total + gain_part
        weight_grads = reduce_grads(weight_grads)
        if reduced is None:
            reduced = weight_grads
        else:
            reduced = tuple(
                (left_sum + right_sum for left_sum, right_sum in zip(reduced, weight_grads))
            )
    reduced = tuple(reduced)
    outputs = jnp.stack(result_list)[:, None]
    input_grad = jnp.stack(input_list)[:, None]
    weights = (qkv_weight, attn_out_weight, ffn_in_weight, ffn_out_weight)
    moments = (qkv_moment, attn_out_moment, ffn_in_moment, ffn_out_moment)
    new_moments = [MOMENTUM * moment + gradient for moment, gradient in zip(moments, reduced)]
    flattened = [moment.reshape(moment.shape[0], -1) for moment in new_moments]
    local_widths = [matrix.shape[1] for matrix in flattened]
    gain_grad = lax.psum(gain_total, ("dp", "tensor"))
    widest = max(local_widths)
    row_count = flattened[0].shape[0]
    stacked = jnp.stack(
        [jnp.pad(matrix, ((0, 0), (0, widest - matrix.shape[1]))) for matrix in flattened], axis=1
    )
    owned = lax.all_to_all(stacked, "tensor", split_axis=1, concat_axis=1, tiled=True)
    owned_matrix = owned.reshape(row_count, tensor_count * widest)
    column_block = lax.all_to_all(owned_matrix, "dp", split_axis=1, concat_axis=0, tiled=True)
    for sweep_index in range(NS_ITERS):
        gram_sum = lax.psum(highest_dot(column_block, column_block.T), "dp")
        if sweep_index == 0:
            factor = 1.0 / (jnp.sqrt(jnp.trace(gram_sum)) + NORM_FLOOR)
            column_block = column_block * factor
            gram_sum = gram_sum * (factor * factor)
        column_block = quintic(column_block, gram_sum)
    back_rows = lax.all_to_all(column_block, "dp", split_axis=0, concat_axis=1, tiled=True)
    back_rows = back_rows[:, : tensor_count * widest].reshape(row_count, tensor_count, widest)
    returned = lax.all_to_all(back_rows, "tensor", split_axis=1, concat_axis=1, tiled=True)
    ortho_list = [returned[:, index, : local_widths[index]] for index in range(4)]
    new_weights = []
    for weight, moment, ortho_block, local_width in zip(
        weights, new_moments, ortho_list, local_widths
    ):
        ortho_step = ortho_block.reshape(moment.shape)
        full_width = local_width * tensor_count
        new_weights.append(
            weight.astype(jnp.float32) * (1.0 - MUON_RATE * DECAY_RATE)
            - MUON_RATE * 0.2 * math.sqrt(full_width) * ortho_step
        )
    gain_first_new = BETA_ONE * gain_first + (1.0 - BETA_ONE) * gain_grad
    gain_second_new = BETA_TWO * gain_second + (1.0 - BETA_TWO) * gain_grad * gain_grad
    first_hat = gain_first_new / (1.0 - BETA_ONE**STEP)
    second_hat = gain_second_new / (1.0 - BETA_TWO**STEP)
    norm_gains_new = norm_gains - ADAM_RATE * (
        first_hat / (jnp.sqrt(second_hat) + ADAM_EPS) + DECAY_RATE * norm_gains
    )
    return (
        outputs,
        input_grad,
        new_moments[0],
        new_weights[0],
        new_moments[1],
        new_weights[1],
        new_moments[2],
        new_weights[2],
        new_moments[3],
        new_weights[3],
        gain_first_new,
        gain_second_new,
        norm_gains_new,
    )


def solution(mesh):
    in_specs = (
        P(None, "dp", "tensor", None),
        P(None, "dp", "tensor", None),
        P(None, "dp"),
        P("dp", None, "tensor"),
        P("dp", "tensor"),
        P("dp", None, "tensor"),
        P("dp", "tensor"),
        P(),
        P("dp", None, "tensor"),
        P("dp", "tensor"),
        P("dp", None, "tensor"),
        P("dp", "tensor"),
        P(),
        P(),
    )
    out_specs = (
        P(None, "dp", "tensor", None),
        P(None, "dp", "tensor", None),
        P("dp", None, "tensor"),
        P("dp", None, "tensor"),
        P("dp", "tensor"),
        P("dp", "tensor"),
        P("dp", None, "tensor"),
        P("dp", None, "tensor"),
        P("dp", "tensor"),
        P("dp", "tensor"),
        P(),
        P(),
        P(),
    )
    return jax.shard_map(
        on_device, mesh=mesh, in_specs=in_specs, out_specs=out_specs, check_vma=False
    )
```

profile of v0, /device:TPU:9, one launch (start us, length us, event | category | flops | bytes accessed | tf_op | source)
XLA Modules:
  0.0 2136.5 jit_solution(3103086694799970826)
XLA Ops:
  15.7 11.1 all_gather.42
  28.0 11.1 all-gather.16.cloned.1.call-done
  39.1 45.8 %all-gather.24.cloned.1.call-done = bf16[1024,1024]{1,0:T(8,128)(2,1)} async-done(((bf16[256,1024]{1,0:T(8,128)(2,1)}), bf16[1024,1024]{1,0:T(8,128)(2,1)}) %all-gather.24.cloned.1.call-update) | async-done | bytes 2097168 | tf_op jit(solution)/shard_map/all_gather | solution.py:194
  89.9 41.9 %all-gather.14.cloned.1.call-done = bf16[1024,1024]{1,0:T(8,128)(2,1)} async-done(((bf16[256,1024]{1,0:T(8,128)(2,1)}), bf16[1024,1024]{1,0:T(8,128)(2,1)}) %all-gather.14.cloned.1.call-update) | async-done | bytes 2097168 | tf_op jit(solution)/shard_map/all_gather | solution.py:194
  139.8 22.5 %while.57 = (s32[]{:T(128)}, bf16[2,512,4,64]{1,3,2,0:T(8,128)(2,1)S(1)}, f32[2,4,512]{2,1,0:T(4,128)S(1)}, s32[2]{0:T(128)S(1)}, bf16[1024,4,64]{0,2,1:T(8,128)...) while((s32[]{:T(128)}, ...), condition=%wide.region_15.16_spmd.clone, body=%wide.region_12.15_spmd.clone.sunk | while | flops 562035712 | bytes 27070644 | solution.py:117
  170.6 22.7 %while.56 = (s32[]{:T(128)}, bf16[2,512,4,64]{1,3,2,0:T(8,128)(2,1)S(1)}, f32[2,4,512]{2,1,0:T(4,128)S(1)}, s32[2]{0:T(128)S(1)}, bf16[1024,4,64]{0,2,1:T(8,128)...) while((s32[]{:T(128)}, ...), condition=%wide.region_5.6_spmd.clone, body=%wide.region_2.5_spmd.clone.sunk | while | flops 562035712 | bytes 27070644 | solution.py:117
  198.0 46.1 %reduce-scatter.17.cloned.1.call-done = f32[256,1024]{1,0:T(8,128)} async-done(((f32[1024,1024]{1,0:T(8,128)}), f32[256,1024]{1,0:T(8,128)}) %reduce-scatter.17.cloned.1.call-update) | async-done | bytes 1048592 | tf_op jit(solution)/shard_map/reduce_scatter | solution.py:204
  244.1 79.5 %reduce-scatter.13.cloned.1.call-done = f32[256,1024]{1,0:T(8,128)} async-done(((f32[1024,1024]{1,0:T(8,128)}), f32[256,1024]{1,0:T(8,128)}) %reduce-scatter.13.cloned.1.call-update) | async-done | bytes 1048592 | tf_op jit(solution)/shard_map/reduce_scatter | solution.py:204
  329.6 27.5 %all-gather.20.cloned.1.call-done = bf16[1024,2,656]{0,2,1:T(8,128)(2,1)} async-done(((bf16[128,2,656]{0,2,1:T(8,128)(2,1)}), bf16[1024,2,656]{0,2,1:T(8,128)(2,1)}) %all-gather.20.cloned.1.call-update) | async-done | bytes 2686992 | tf_op jit(solution)/shard_map/all_gather | solution.py:172
  357.1 45.8 %all-gather.18.cloned.1.call-done = bf16[1024,1024]{1,0:T(8,128)(2,1)} async-done(((bf16[256,1024]{1,0:T(8,128)(2,1)}), bf16[1024,1024]{1,0:T(8,128)(2,1)}) %all-gather.18.cloned.1.call-update) | async-done | bytes 2097168 | tf_op jit(solution)/shard_map/all_gather | solution.py:209
  402.9 7.8 fusion.188
  410.7 20.0 all-gather.22.cloned.1.call-done
  430.7 45.3 %all-gather.32.cloned.1.call-done = bf16[1,1,1024,1024]{3,2,1,0:T(8,128)(2,1)} async-done(((bf16[1,1,256,1024]{3,2,1,0:T(8,128)(2,1)}), bf16[1,1,1024,1024]{3,2,1,0:T(8,128)(2,1)}) %all-gather.32.cloned.1.call-update) | async-done | bytes 2097168 | tf_op jit(solution)/shard_map/all_gather | solution.py:221
  475.9 10.9 add_convert_fusion.1
  497.0 76.1 %reduce-scatter.21.cloned.1.call-done = f32[256,1024]{1,0:T(8,128)} async-done(((f32[1024,1024]{1,0:T(8,128)}), f32[256,1024]{1,0:T(8,128)}) %reduce-scatter.21.cloned.1.call-update) | async-done | bytes 1048592 | tf_op jit(solution)/shard_map/reduce_scatter | solution.py:227
  577.0 43.9 %all-gather.26.cloned.1.call-done = bf16[1024,1024]{1,0:T(8,128)(2,1)} async-done(((bf16[256,1024]{1,0:T(8,128)(2,1)}), bf16[1024,1024]{1,0:T(8,128)(2,1)}) %all-gather.26.cloned.1.call-update) | async-done | bytes 2097168 | tf_op jit(solution)/shard_map/all_gather | solution.py:209
  620.9 7.8 fusion.191
  628.7 38.4 %all-gather.34.cloned.1.call-done = bf16[1,1,1024,1024]{3,2,1,0:T(8,128)(2,1)} async-done(((bf16[1,1,256,1024]{3,2,1,0:T(8,128)(2,1)}), bf16[1,1,1024,1024]{3,2,1,0:T(8,128)(2,1)}) %all-gather.34.cloned.1.call-update) | async-done | bytes 2097168 | tf_op jit(solution)/shard_map/all_gather | solution.py:221
  667.1 10.9 add_convert_fusion
  681.7 5.0 fusion.120
  686.8 5.6 fusion.189
  692.7 5.9 fusion.192
  698.7 65.6 %reduce-scatter.25.cloned.1.call-done = f32[256,1024]{1,0:T(8,128)} async-done(((f32[1024,1024]{1,0:T(8,128)}), f32[256,1024]{1,0:T(8,128)}) %reduce-scatter.25.cloned.1.call-update) | async-done | bytes 1048592 | tf_op jit(solution)/shard_map/reduce_scatter | solution.py:227
  766.6 77.1 %reduce-scatter.15.cloned.1.call-done = f32[256,1024]{1,0:T(8,128)} async-done(((f32[1024,1024]{1,0:T(8,128)}), f32[256,1024]{1,0:T(8,128)}) %reduce-scatter.15.cloned.1.call-update) | async-done | bytes 1048592 | tf_op jit(solution)/shard_map/reduce_scatter | solution.py:217
  843.8 79.6 %reduce-scatter.19.cloned.1.call-done = f32[256,1024]{1,0:T(8,128)} async-done(((f32[1024,1024]{1,0:T(8,128)}), f32[256,1024]{1,0:T(8,128)}) %reduce-scatter.19.cloned.1.call-update) | async-done | bytes 1048592 | tf_op jit(solution)/shard_map/reduce_scatter | solution.py:217
  935.2 5.8 fusion.121
  941.0 5.9 convolution_add_fusion
  947.4 24.9 %all-gather.30.cloned.1.call-done = bf16[1024,1024]{1,0:T(8,128)(2,1)} async-done(((bf16[256,1024]{1,0:T(8,128)(2,1)}), bf16[1024,1024]{1,0:T(8,128)(2,1)}) %all-gather.30.cloned.1.call-update) | async-done | bytes 2097168 | tf_op jit(solution)/shard_map/all_gather | solution.py:234
  976.7 58.0 %while.59 = (s32[]{:T(128)}, f32[1024,4,64]{0,2,1:T(8,128)S(1)}, f32[1024,4,64]{0,2,1:T(8,128)}, f32[2,512,4,64]{1,0,3,2:T(2,128)}, s32[2]{0:T(128)S(1)}, /*inde...) while((s32[]{:T(128)}, f32[1024,4,64]{0,2,1:T(8,128)S(1)}, ...), condition=%wide.region_34.35_spmd.clone, body=%wide.region_32.34_spmd.clone.sunk | while | flops 1375075328 | bytes 82899256 | solution.py:164
  995.3 10.4 dynamic_update_slice.41
  1024.2 10.4 dynamic_update_slice.41
  1042.4 59.5 %while.58 = (s32[]{:T(128)}, f32[1024,4,64]{0,2,1:T(8,128)S(1)}, f32[1024,4,64]{0,2,1:T(8,128)}, f32[2,512,4,64]{1,0,3,2:T(2,128)}, s32[2]{0:T(128)S(1)}, /*inde...) while((s32[]{:T(128)}, f32[1024,4,64]{0,2,1:T(8,128)S(1)}, ...), condition=%wide.region_25.26_spmd.clone, body=%wide.region_23.25_spmd.clone.sunk | while | flops 1375075328 | bytes 80802072 | solution.py:164
  1061.8 10.4 dynamic_update_slice.40
  1091.5 10.4 dynamic_update_slice.40
  1129.0 37.8 %reduce-scatter.31.cloned.1.call-done = f32[128,256]{0,1:T(8,128)} async-done(((f32[1024,256]{0,1:T(8,128)}), f32[128,256]{0,1:T(8,128)}) %reduce-scatter.31.cloned.1.call-update) | async-done | bytes 131088 | tf_op jit(solution)/shard_map/reduce_scatter | solution.py:180
  1168.4 48.1 %reduce-scatter.29.cloned.1.call-done = f32[128,3,256]{2,0,1:T(8,128)} async-done(((f32[1024,3,256]{2,0,1:T(8,128)}), f32[128,3,256]{2,0,1:T(8,128)}) %reduce-scatter.29.cloned.1.call-update) | async-done | bytes 393232 | tf_op jit(solution)/shard_map/reduce_scatter | solution.py:179
  1218.3 62.9 %all_to_all.45 = f32[128,4,1312]{0,2,1:T(8,128)S(1)} all-to-all(f32[128,4,1312]{0,2,1:T(8,128)S(1)} %pad_maximum_fusion.2), channel_id=1, replica_groups=mesh['dp'=8,'tensor'=4] {'tensor'}, dimensions={1} | all-to-all | bytes 5373952 | tf_op jit(solution)/shard_map/all_to_all | solution.py:324
  1281.2 36.6 %all_to_all.46 = f32[128,8,656]{0,2,1:T(8,128)S(1)} all-to-all(f32[128,8,656]{0,2,1:T(8,128)S(1)} %bitcast.421), channel_id=1, replica_groups=mesh['dp'=8,'tensor'=4] {'dp'}, dimensions={1} | all-to-all | bytes 5373952 | tf_op jit(solution)/shard_map/all_to_all | solution.py:326
  1317.8 11.7 fusion.84
  1330.0 79.2 %all-reduce.9.cloned.1.call-done = f32[1024,1024]{1,0:T(8,128)} async-done(((f32[1024,1024]{1,0:T(8,128)}), f32[1024,1024]{1,0:T(8,128)}) %all-reduce.9.cloned.1.call-update) | async-done | bytes 4194320 | tf_op jit(solution)/shard_map/psum | solution.py:328
  1412.8 11.2 fusion.80
  1424.1 9.2 multiply_add_fusion.3
  1434.8 12.0 fusion.195
  1446.8 81.2 %all-reduce.11.cloned.1.call-done = f32[1024,1024]{1,0:T(8,128)} async-done(((f32[1024,1024]{1,0:T(8,128)}), f32[1024,1024]{1,0:T(8,128)}) %all-reduce.11.cloned.1.call-update) | async-done | bytes 4194320 | tf_op jit(solution)/shard_map/psum | solution.py:328
  1528.0 11.3 fusion.196
  1539.4 9.2 multiply_add_fusion.2
  1550.1 12.2 fusion.197
  1562.4 81.2 %all-reduce.13.cloned.1.call-done = f32[1024,1024]{1,0:T(8,128)} async-done(((f32[1024,1024]{1,0:T(8,128)}), f32[1024,1024]{1,0:T(8,128)}) %all-reduce.13.cloned.1.call-update) | async-done | bytes 4194320 | tf_op jit(solution)/shard_map/psum | solution.py:328
  1643.6 11.3 fusion.198
  1654.9 9.2 multiply_add_fusion.1
  1665.6 12.0 fusion.199
  1677.7 81.2 %all-reduce.15.cloned.1.call-done = f32[1024,1024]{1,0:T(8,128)} async-done(((f32[1024,1024]{1,0:T(8,128)}), f32[1024,1024]{1,0:T(8,128)}) %all-reduce.15.cloned.1.call-update) | async-done | bytes 4194320 | tf_op jit(solution)/shard_map/psum | solution.py:328
  1759.0 11.5 fusion.200
  1770.4 9.1 multiply_add_fusion
  1779.5 11.9 fusion.201
  1791.5 5.7 fusion.194
  1797.3 6.2 fusion.193
  1803.5 69.2 %all-reduce.17.cloned.1.call-done = f32[1024,1024]{1,0:T(8,128)} async-done(((f32[1024,1024]{1,0:T(8,128)}), f32[1024,1024]{1,0:T(8,128)}) %all-reduce.17.cloned.1.call-update) | async-done | bytes 4194320 | tf_op jit(solution)/shard_map/psum | solution.py:328
  1872.7 11.3 fusion.202
  1884.0 9.2 add_bitcast_fusion.1
  1893.4 36.1 %all_to_all.47 = f32[8,128,656]{1,2,0:T(8,128)} all-to-all(f32[8,128,656]{1,2,0:T(8,128)S(1)} %bitcast.422), channel_id=1, replica_groups=mesh['dp'=8,'tensor'=4] {'dp'}, dimensions={0} | all-to-all | bytes 5373952 | tf_op jit(solution)/shard_map/all_to_all | solution.py:334
  1937.9 34.9 %reduce-scatter.27.cloned.1.call-done = f32[256,1024]{1,0:T(8,128)} async-done(((f32[1024,1024]{1,0:T(8,128)}), f32[256,1024]{1,0:T(8,128)}) %reduce-scatter.27.cloned.1.call-update) | async-done | bytes 1048592 | tf_op jit(solution)/shard_map/reduce_scatter | solution.py:251
  1972.8 104.3 %reduce-scatter.23.cloned.1.call-done = f32[256,1024]{1,0:T(8,128)} async-done(((f32[1024,1024]{1,0:T(8,128)}), f32[256,1024]{1,0:T(8,128)}) %reduce-scatter.23.cloned.1.call-update) | async-done | bytes 1048592 | tf_op jit(solution)/shard_map/reduce_scatter | solution.py:251
  2079.6 37.5 %psum.47 = f32[2,1024]{1,0:T(2,128)S(1)} all-reduce(f32[2,1024]{1,0:T(2,128)S(1)} %maximum_add_fusion), channel_id=1, replica_groups=mesh['dp'=8,'tensor'=4] {'dp','tensor'}, use_global_device_ids=true, to_apply=%region_56.57 | all-reduce | flops 2048 | bytes 16384 | tf_op jit(solution)/shard_map/psum | solution.py:318
  (445 shorter events, 252.0 us)
Async XLA Ops:
  7.2 31.9 %all-gather.16.cloned.1.call-start = ((), (), s32[]{:S(2)}) async-start(), calls=%async_computation.17 | async-start | bytes 1769472 | tf_op jit(solution)/shard_map/all_gather | solution.py:170
  9.1 6.0 copy-start.91
  9.1 6.6 copy-start.67
  9.1 75.8 %all-gather.24.cloned.1.call-start = ((), (), s32[]{:S(2)}) async-start(), calls=%async_computation.23 | async-start | bytes 2621440 | tf_op jit(solution)/shard_map/all_gather | solution.py:194
  14.3 117.5 %all-gather.14.cloned.1.call-start = ((), (), s32[]{:S(2)}) async-start(), calls=%async_computation.16 | async-start | bytes 2621440 | tf_op jit(solution)/shard_map/all_gather | solution.py:194
  15.0 229.1 %reduce-scatter.17.cloned.1.call-start = ((), (), s32[]{:S(2)}) async-start(), calls=%async_computation.24 | async-start | bytes 5242880 | tf_op jit(solution)/shard_map/reduce_scatter | solution.py:204
  26.8 945.5 %copy-start.24 = (bf16[1024,256]{1,0:T(8,128)(2,1)}, bf16[1024,256]{1,0:T(8,128)(2,1)S(1)}, u32[]{:S(2)}) copy-start(bf16[1024,256]{1,0:T(8,128)(2,1)S(1)} %all_gather.42) | copy-start | bytes 1572868
  28.0 109.5 %copy-start.45 = (f32[1024,32]{0,1:T(8,128)}, f32[1024,32]{0,1:T(8,128)S(1)}, u32[]{:S(2)}) copy-start(f32[1024,32]{0,1:T(8,128)S(1)} %get-tuple-element.564) | copy-start | bytes 393220
  166.5 157.1 %reduce-scatter.13.cloned.1.call-start = ((), (), s32[]{:S(2)}) async-start(), calls=%async_computation.18 | async-start | bytes 5242880 | tf_op jit(solution)/shard_map/reduce_scatter | solution.py:204
  197.3 126.3 %copy-start.6 = (bf16[2,1,256,1024]{3,2,1,0:T(8,128)(2,1)S(1)}, bf16[2,1,256,1024]{3,2,1,0:T(8,128)(2,1)}, u32[]{:S(2)}) copy-start(bf16[2,1,256,1024]{3,2,1,0:T(8,128)(2,1)} %param.22) | copy-start | bytes 3145732
  197.3 159.7 %all-gather.20.cloned.1.call-start = ((), (), s32[]{:S(2)}) async-start(), calls=%async_computation.20 | async-start | bytes 3022848 | tf_op jit(solution)/shard_map/all_gather | solution.py:172
  197.9 128.7 %copy-start.74 = (f32[1,1024]{1,0:T(1,128)S(1)}, f32[1,1024]{1,0:T(1,128)}, u32[]{:S(2)}) copy-start(f32[1,1024]{1,0:T(1,128)} %get-tuple-element.560) | copy-start | bytes 12292
  197.9 205.0 %all-gather.18.cloned.1.call-start = ((), (), s32[]{:S(2)}) async-start(), calls=%async_computation.19 | async-start | bytes 2621440 | tf_op jit(solution)/shard_map/all_gather | solution.py:209
  327.7 103.0 %all-gather.22.cloned.1.call-start = ((), (), s32[]{:S(2)}) async-start(), calls=%async_computation.21 | async-start | bytes 1511424 | tf_op jit(solution)/shard_map/all_gather | solution.py:173
  328.4 147.5 %all-gather.32.cloned.1.call-start = ((), (), s32[]{:S(2)}) async-start(), calls=%async_computation.38 | async-start | bytes 2621440 | tf_op jit(solution)/shard_map/all_gather | solution.py:221
  329.5 243.6 %reduce-scatter.21.cloned.1.call-start = ((), (), s32[]{:S(2)}) async-start(), calls=%async_computation.27 | async-start | bytes 5242880 | tf_op jit(solution)/shard_map/reduce_scatter | solution.py:227
  475.9 11.0 copy-start.20
  495.6 125.4 %all-gather.26.cloned.1.call-start = ((), (), s32[]{:S(2)}) async-start(), calls=%async_computation.25 | async-start | bytes 2621440 | tf_op jit(solution)/shard_map/all_gather | solution.py:209
  576.2 90.9 %all-gather.34.cloned.1.call-start = ((), (), s32[]{:S(2)}) async-start(), calls=%async_computation.39 | async-start | bytes 2621440 | tf_op jit(solution)/shard_map/all_gather | solution.py:221
  576.8 187.5 %reduce-scatter.25.cloned.1.call-start = ((), (), s32[]{:S(2)}) async-start(), calls=%async_computation.30 | async-start | bytes 5242880 | tf_op jit(solution)/shard_map/reduce_scatter | solution.py:227
  667.1 11.0 copy-start.21
  686.8 157.0 %reduce-scatter.15.cloned.1.call-start = ((), (), s32[]{:S(2)}) async-start(), calls=%async_computation.22 | async-start | bytes 5242880 | tf_op jit(solution)/shard_map/reduce_scatter | solution.py:217
  692.4 230.9 %reduce-scatter.19.cloned.1.call-start = ((), (), s32[]{:S(2)}) async-start(), calls=%async_computation.26 | async-start | bytes 5242880 | tf_op jit(solution)/shard_map/reduce_scatter | solution.py:217
  698.7 273.6 %all-gather.30.cloned.1.call-start = ((), (), s32[]{:S(2)}) async-start(), calls=%async_computation.31 | async-start | bytes 2621440 | tf_op jit(solution)/shard_map/all_gather | solution.py:234
  927.6 110.3 %all-gather.28.cloned.1.call-start = ((), (), s32[]{:S(2)}) async-start(), calls=%async_computation.28 | async-start | bytes 2621440 | tf_op jit(solution)/shard_map/all_gather | solution.py:234
  928.2 194.4 %reduce-scatter.35.cloned.1.call-start = ((), (), s32[]{:S(2)}) async-start(), calls=%async_computation.43 | async-start | bytes 3022848 | tf_op jit(solution)/shard_map/reduce_scatter | solution.py:182
  935.1 192.8 %reduce-scatter.33.cloned.1.call-start = ((), (), s32[]{:S(2)}) async-start(), calls=%async_computation.42 | async-start | bytes 6045696 | tf_op jit(solution)/shard_map/reduce_scatter | solution.py:181
  935.2 5.8 copy-start.42
  946.9 29.8 %copy-start.3 = (bf16[1024,4,64]{0,2,1:T(8,128)(2,1)S(1)}, bf16[1024,4,64]{0,2,1:T(8,128)(2,1)}, u32[]{:S(2)}) copy-start(bf16[1024,4,64]{0,2,1:T(8,128)(2,1)} %copy-done.2) | copy-start | bytes 1572868
  946.9 29.7 %copy-start.70 = (f32[2,4,512]{2,1,0:T(4,128)S(1)}, f32[2,4,512]{2,1,0:T(4,128)}, u32[]{:S(2)}) copy-start(f32[2,4,512]{2,1,0:T(4,128)} %copy-done.69) | copy-start | bytes 49156
  946.9 219.8 %reduce-scatter.31.cloned.1.call-start = ((), (), s32[]{:S(2)}) async-start(), calls=%async_computation.41 | async-start | bytes 1179648 | tf_op jit(solution)/shard_map/reduce_scatter | solution.py:180
  1042.4 62.8 %copy-start.46 = (f32[1024,32]{0,1:T(8,128)S(1)}, f32[1024,32]{0,1:T(8,128)}, u32[]{:S(2)}) copy-start(f32[1024,32]{0,1:T(8,128)} %copy-done.45) | copy-start | bytes 393220
  1111.8 104.7 %reduce-scatter.29.cloned.1.call-start = ((), (), s32[]{:S(2)}) async-start(), calls=%async_computation.40 | async-start | bytes 3538944 | tf_op jit(solution)/shard_map/reduce_scatter | solution.py:179
  1121.6 6.2 copy-start.64
  1121.6 94.9 %copy-start.65 = (f32[128,3,256]{2,0,1:T(8,128)S(1)}, f32[128,3,256]{2,0,1:T(8,128)}, u32[]{:S(2)}) copy-start(f32[128,3,256]{2,0,1:T(8,128)} %param.30) | copy-start | bytes 1179652
  1121.6 287.6 %all-reduce.9.cloned.1.call-start = ((), (), s32[]{:S(2)}) async-start(), calls=%async_computation.33 | async-start | bytes 8388608 | tf_op jit(solution)/shard_map/psum | solution.py:328
  1129.0 89.0 %copy-start.32 = (f32[128,2,656]{0,2,1:T(8,128)}, f32[128,2,656]{0,2,1:T(8,128)S(1)}, u32[]{:S(2)}) copy-start(f32[128,2,656]{0,2,1:T(8,128)S(1)} %multiply_add_fusion.4) | copy-start | bytes 2015236
  1329.5 198.5 %all-reduce.11.cloned.1.call-start = ((), (), s32[]{:S(2)}) async-start(), calls=%async_computation.34 | async-start | bytes 8388608 | tf_op jit(solution)/shard_map/psum | solution.py:328
  1412.8 11.2 copy-start.4
  1446.8 81.3 %copy-start.10 = (f32[1024,656]{0,1:T(8,128)S(1)}, f32[1024,656]{0,1:T(8,128)}, u32[]{:S(2)}) copy-start(f32[1024,656]{0,1:T(8,128)} %copy-done.9) | copy-start | bytes 8060932
  1446.8 196.8 %all-reduce.13.cloned.1.call-start = ((), (), s32[]{:S(2)}) async-start(), calls=%async_computation.35 | async-start | bytes 8388608 | tf_op jit(solution)/shard_map/psum | solution.py:328
  1528.0 11.3 copy-start.17
  1562.3 81.3 %copy-start.12 = (f32[1024,656]{0,1:T(8,128)S(1)}, f32[1024,656]{0,1:T(8,128)}, u32[]{:S(2)}) copy-start(f32[1024,656]{0,1:T(8,128)} %copy-done.11) | copy-start | bytes 8060932
  1562.4 196.6 %all-reduce.15.cloned.1.call-start = ((), (), s32[]{:S(2)}) async-start(), calls=%async_computation.36 | async-start | bytes 8388608 | tf_op jit(solution)/shard_map/psum | solution.py:328
  1643.6 11.3 copy-start.18
  1677.7 81.3 %copy-start.14 = (f32[1024,656]{0,1:T(8,128)S(1)}, f32[1024,656]{0,1:T(8,128)}, u32[]{:S(2)}) copy-start(f32[1024,656]{0,1:T(8,128)} %copy-done.13) | copy-start | bytes 8060932
  1677.7 195.0 %all-reduce.17.cloned.1.call-start = ((), (), s32[]{:S(2)}) async-start(), calls=%async_computation.37 | async-start | bytes 8388608 | tf_op jit(solution)/shard_map/psum | solution.py:328
  1758.9 11.5 copy-start.15
  1759.0 11.5 copy-start.19
  1791.5 181.3 %reduce-scatter.27.cloned.1.call-start = ((), (), s32[]{:S(2)}) async-start(), calls=%async_computation.32 | async-start | bytes 5242880 | tf_op jit(solution)/shard_map/reduce_scatter | solution.py:251
  1797.2 279.8 %reduce-scatter.23.cloned.1.call-start = ((), (), s32[]{:S(2)}) async-start(), calls=%async_computation.29 | async-start | bytes 5242880 | tf_op jit(solution)/shard_map/reduce_scatter | solution.py:251
  1872.7 11.3 copy-start.16
  1929.5 7.6 copy-start.48
  1929.6 147.5 %copy-start.7 = (bf16[2,1,256,1024]{3,2,1,0:T(8,128)(2,1)S(1)}, bf16[2,1,256,1024]{3,2,1,0:T(8,128)(2,1)}, u32[]{:S(2)}) copy-start(bf16[2,1,256,1024]{3,2,1,0:T(8,128)(2,1)} %param.22) | copy-start | bytes 3145732
  1929.6 147.5 %copy-start.76 = (f32[1,1024]{1,0:T(1,128)S(1)}, f32[1,1024]{1,0:T(1,128)}, u32[]{:S(2)}) copy-start(f32[1,1024]{1,0:T(1,128)} %copy-done.75) | copy-start | bytes 12292
  1929.6 147.5 %copy-start.80 = (f32[256]{0:T(256)S(1)}, f32[256]{0:T(256)}, u32[]{:S(2)}) copy-start(f32[256]{0:T(256)} %copy-done.79) | copy-start | bytes 3076
  1929.6 147.5 %copy-start.82 = (f32[256]{0:T(256)S(1)}, f32[256]{0:T(256)}, u32[]{:S(2)}) copy-start(f32[256]{0:T(256)} %copy-done.81) | copy-start | bytes 3076
  1929.6 147.5 %copy-start.86 = (f32[256]{0:T(256)S(1)}, f32[256]{0:T(256)}, u32[]{:S(2)}) copy-start(f32[256]{0:T(256)} %copy-done.85) | copy-start | bytes 3076
  1929.6 147.5 %copy-start.88 = (f32[256]{0:T(256)S(1)}, f32[256]{0:T(256)}, u32[]{:S(2)}) copy-start(f32[256]{0:T(256)} %copy-done.87) | copy-start | bytes 3076
  1929.6 192.1 %all-to-all-start.3 = ((f32[128,4,1312]{0,2,1:T(8,128)}), f32[128,4,1312]{0,2,1:T(8,128)}, u32[]{:S(2)}, u32[]{:S(2)}) async-start(f32[128,4,1312]{0,2,1:T(8,128)} %bitcast.420), calls=%async_computation.11 | async-start | bytes 5373952 | tf_op jit(solution)/shard_map/all_to_all | solution.py:336
  1934.6 144.9 %copy-start.83 = (f32[1024]{0:T(1024)S(1)}, f32[1024]{0:T(1024)}, u32[]{:S(2)}) copy-start(f32[1024]{0:T(1024)} %get-tuple-element.397) | copy-start | bytes 12292
  1934.7 144.9 %copy-start.84 = (f32[1024]{0:T(1024)S(1)}, f32[1024]{0:T(1024)}, u32[]{:S(2)}) copy-start(f32[1024]{0:T(1024)} %get-tuple-element.401) | copy-start | bytes 12292
  1934.7 182.5 %copy-start.29 = (f32[256,1024]{1,0:T(8,128)S(1)}, f32[256,1024]{1,0:T(8,128)}, u32[]{:S(2)}) copy-start(f32[256,1024]{1,0:T(8,128)} %get-tuple-element.493) | copy-start | bytes 3145732
  1934.7 182.5 %copy-start.30 = (f32[256,1024]{1,0:T(8,128)S(1)}, f32[256,1024]{1,0:T(8,128)}, u32[]{:S(2)}) copy-start(f32[256,1024]{1,0:T(8,128)} %get-tuple-element.539) | copy-start | bytes 3145732
  (71 other events, 193.5 us)
Sparse Core Ops, SparseCore 0:
  10.5 28.5 all-gather.15
  41.2 43.6 all-gather.23
  87.1 44.6 all-gather.13
  166.7 77.3 reduce-scatter.16
  246.4 77.2 reduce-scatter.12
  325.4 31.6 all-gather.19
  359.2 43.6 all-gather.17
  404.8 25.8 all-gather.21
  432.3 43.6 all-gather.31
  495.7 77.3 reduce-scatter.20
  576.4 44.5 all-gather.25
  622.4 44.6 all-gather.33
  686.9 77.3 reduce-scatter.24
  766.5 77.2 reduce-scatter.14
  846.0 77.2 reduce-scatter.18
  927.7 44.5 all-gather.29
  973.7 44.6 all-gather.27
  1021.7 45.4 reduce-scatter.34
  1070.5 57.2 reduce-scatter.32
  1130.8 35.8 reduce-scatter.30
  1170.2 46.3 reduce-scatter.28
  1329.7 79.4 all-reduce.8
  1446.9 81.0 all-reduce.10
  1562.5 81.0 all-reduce.12
  1677.8 81.0 all-reduce.14
  1791.6 81.0 all-reduce.16
  1874.8 97.8 reduce-scatter.26
  1975.2 101.8 reduce-scatter.22
where the time goes:
time: 2150 us; the launch traced here: 2140 us
  waiting for transfers between devices  1390 us (65%)
  matrix products  355 us (17%)
  blocking collectives  184 us (9%)
  local copies, waits for them, and re-layouts  87.2 us (4%)
  other arithmetic  76.6 us (4%)
    psum x5, waiting for transfers between devices, on_device(): gram_sum = lax.psum(highest_dot(column_block, column_block.T), 'dp')  392 us
    dot_general x15, matrix products, highest_dot(): return jnp.dot(left, right, precision=lax.Precision.HIGHEST)  162 us
    reduce_scatter x2, waiting for transfers between devices, micro_batch(): lax.psum_scatter(contract_cols(hidden_low, ffn_out_all), 'tensor', scatte...  157 us
    reduce_scatter x2, waiting for transfers between devices, micro_batch(): lax.psum_scatter(contract_cols(grad_gate_up, ffn_matrix), 'tensor', scatt...  142 us
    reduce_scatter x2, waiting for transfers between devices, micro_batch(): lax.psum_scatter(contract_cols(grad_projected, qkv_matrix), 'tensor', sca...  139 us
    reduce_scatter x2, waiting for transfers between devices, micro_batch(): lax.psum_scatter(contract_cols(context_low, attn_all), 'tensor', scatter_...  126 us
    all_gather x2, waiting for transfers between devices, micro_batch(): lax.all_gather(scaled_two.astype(jnp.bfloat16), 'tensor', axis=0, tiled=T...  89.7 us
    all_gather x2, waiting for transfers between devices, micro_batch(): lax.all_gather(scaled_one.astype(jnp.bfloat16), 'tensor', axis=0, tiled=T...  87.7 us
  transfers between devices with their start and end apart: 29, of which 26 were waited for; matrix products, arithmetic and copies ran while one was open for 13% of the time, Pallas kernels for 0%

commit v1 on v0

v1 whole, which is shorter than its diff:
```python
import functools
import math

import jax
import jax.numpy as jnp
from jax import lax
from jax.experimental import pallas as pl
from jax.experimental.pallas import tpu as pltpu
from jax.sharding import PartitionSpec as P

HEAD_DIM = 64
NS_ITERS = 5
STEP = 10


ROPE_BASE = 160000.0
NORM_EPS = 1e-05
MASK_VALUE = -1e30
MOMENTUM = 0.95
MUON_RATE = 0.1
DECAY_RATE = 0.01
QUINTIC_ONE = 3.4445
QUINTIC_THREE = -4.775
QUINTIC_FIVE = 2.0315
NORM_FLOOR = 1e-07
BETA_ONE = 0.9
BETA_TWO = 0.95
ADAM_RATE = 0.2
ADAM_EPS = 1e-08
BOTH = ("dp", "tensor")
MESH = pl.DeviceIdType.MESH


def rotary(first, length):
    half_size = HEAD_DIM // 2
    exponents = jnp.arange(half_size).astype(jnp.float32) / half_size
    frequency = jnp.power(ROPE_BASE, -exponents)
    positions = (first + jnp.arange(length)).astype(jnp.float32)
    angles = positions[:, None] * frequency[None, :]
    return (jnp.cos(angles), jnp.sin(angles))


def rotate(vectors, cosine_table, sine_table):
    half_size = vectors.shape[-1] // 2
    first_half = vectors[..., :half_size]
    second_half = vectors[..., half_size:]
    cos_part = cosine_table[:, None, :]
    sin_part = sine_table[:, None, :]
    return jnp.concatenate(
        [
            first_half * cos_part - second_half * sin_part,
            second_half * cos_part + first_half * sin_part,
        ],
        axis=-1,
    )


def layer_norm_parts(vectors, gain):
    centre = vectors - jnp.mean(vectors, axis=-1, keepdims=True)
    inverse = lax.rsqrt(jnp.mean(centre * centre, axis=-1, keepdims=True) + NORM_EPS)
    normed = centre * inverse
    return (normed, inverse, normed * gain)


def layer_norm_back(grad_out, normed, inverse, gain):
    grad_normed = grad_out * gain
    mean_grad = jnp.mean(grad_normed, axis=-1, keepdims=True)
    mean_cross = jnp.mean(grad_normed * normed, axis=-1, keepdims=True)
    return (
        inverse * (grad_normed - mean_grad - normed * mean_cross),
        jnp.sum(grad_out * normed, axis=0),
    )


def einsum(spec, *operands):
    return jnp.einsum(spec, *operands, preferred_element_type=jnp.float32)


def low(values):
    return values.astype(jnp.bfloat16)


def attention_forward(queries, key_rows, values, key_valid):
    score_scale = 1.0 / math.sqrt(queries.shape[-1])
    scores = einsum("qhd,khd->hqk", queries, key_rows) * score_scale
    scores = jnp.where(key_valid, scores, MASK_VALUE)
    highest = jnp.max(scores, axis=-1, keepdims=True)
    exponent = jnp.exp(scores - highest)
    row_total = jnp.sum(exponent, axis=-1, keepdims=True)
    context = einsum("hqk,khd->qhd", low(exponent / row_total), values)
    return (context, highest[..., 0] + jnp.log(row_total[..., 0]))


def attention_backward(queries, key_rows, values, log_total, grad_context, key_valid):
    score_scale = 1.0 / math.sqrt(queries.shape[-1])
    scores = einsum("qhd,khd->hqk", queries, key_rows) * score_scale
    scores = jnp.where(key_valid, scores, MASK_VALUE)
    soft_weights = jnp.exp(scores - log_total[..., None])
    grad_probs = einsum("qhd,khd->hqk", grad_context, values)
    inner_sum = jnp.sum(soft_weights * grad_probs, axis=-1, keepdims=True)
    grad_scores = low(soft_weights * (grad_probs - inner_sum))
    grad_query = einsum("hqk,khd->qhd", grad_scores, key_rows) * score_scale
    grad_keys = einsum("hqk,qhd->khd", grad_scores, queries) * score_scale
    grad_values = einsum("hqk,qhd->khd", low(soft_weights), grad_context)
    return (grad_query, grad_keys, grad_values)


def exchange_lists(chip_count, tensor_count):
    first_list, second_list = [], []
    for chip in range(chip_count):
        for core in range(2):
            for slot in range(tensor_count):
                for micro in range(2):
                    source = (2 * chip + core) * tensor_count + slot
                    target = (2 * chip + slot // 2) * tensor_count + 2 * micro + core
                    pair = (source, target)
                    (first_list if slot % 2 == micro else second_list).append(pair)
    return (first_list, second_list)


def to_sequences(blocks, lists, odd, upper):
    first = lax.ppermute(jnp.where(odd, blocks[1], blocks[0]), BOTH, lists[0])
    second = lax.ppermute(jnp.where(odd, blocks[0], blocks[1]), BOTH, lists[1])
    return jnp.where(
        upper, jnp.concatenate([second, first]), jnp.concatenate([first, second])
    )


def from_sequences(rows, lists, odd, upper):
    half = rows.shape[0] // 2
    top, bottom = rows[:half], rows[half:]
    back = [[(target, source) for source, target in pairs] for pairs in lists]
    first = lax.ppermute(jnp.where(upper, bottom, top), BOTH, back[0])
    second = lax.ppermute(jnp.where(upper, top, bottom), BOTH, back[1])
    return jnp.where(odd, jnp.stack([second, first]), jnp.stack([first, second]))


def swap_partner(values):
    count = lax.axis_size("dp")
    return lax.ppermute(values, "dp", [(index, index ^ 1) for index in range(count)])


def mean_split(matrix):
    mean = jnp.trace(matrix) / matrix.shape[0]
    return (mean, matrix - mean * jnp.eye(matrix.shape[0], dtype=jnp.float32))


def split_product(left, right):
    left_mean, left_rest = left
    right_mean, right_rest = right
    product = einsum("ij,jk->ik", low(left_rest), low(right_rest))
    product = product + left_mean * right_rest + right_mean * left_rest
    mean, rest = mean_split(product)
    return (mean + left_mean * right_mean, rest)


def newton_schulz(gram):
    factor = 1.0 / (jnp.sqrt(jnp.trace(gram)) + NORM_FLOOR)
    iterate = mean_split(gram * (factor * factor))
    whole = None
    for sweep_index in range(NS_ITERS):
        square = split_product(iterate, iterate)
        poly = (
            QUINTIC_ONE + QUINTIC_THREE * iterate[0] + QUINTIC_FIVE * square[0],
            QUINTIC_THREE * iterate[1] + QUINTIC_FIVE * square[1],
        )
        whole = poly if whole is None else split_product(poly, whole)
        if sweep_index < NS_ITERS - 1:
            iterate = split_product(poly, split_product(poly, iterate))
    return (whole[0] * factor, whole[1] * factor)


def step_of(rows):
    return next(step for step in (128, 64, 32, 16) if rows % step == 0)


def lanes(block):
    return pl.ds(pl.multiple_of(block * 128, 128), 128)

def neighbours():
    me = lax.axis_index("dp")
    core, across, down = lax.rem(me, 2), lax.rem(lax.div(me, 2), 2), lax.div(me, 4)
    return (me, me + 1 - 2 * core, me + 2 - 4 * across, me + 4 - 8 * down)

def greet(plane, others, planes):
    barrier = pltpu.get_barrier_semaphore()
    me = lax.axis_index("dp")
    for other in others:
        pl.semaphore_signal(barrier, inc=1, device_id=(other, plane), device_id_type=MESH)
    for other in planes:
        pl.semaphore_signal(barrier, inc=1, device_id=(me, other), device_id_type=MESH)
    pl.semaphore_wait(barrier, len(others) + len(planes))

def gather_kernel(count, *refs):
    shards, wholes = refs[:count], refs[count : 2 * count]
    (own_sem, send_z, recv_z, send_x, recv_x, send_y, recv_y, send_d, recv_d, send_c, recv_c) = refs[2 * count :]
    me, partner, across, down = neighbours()
    plane = lax.axis_index("tensor")
    diagonal = across + down - me
    planes = [lax.rem(plane + offset, 4) for offset in (1, 2, 3)]
    greet(plane, (partner, across, down), planes)
    started = []

    def remote(source, target, send, recv, device):
        copy = pltpu.make_async_remote_copy(source, target, send, recv, device_id=device, device_id_type=MESH)
        copy.start()
        started.append(copy)

    def spread(part, source, slot, block):
        view = wholes[part].at[slot, :, lanes(block)]
        remote(source, view, send_x.at[part, slot], recv_x.at[part, slot], (across, plane))
        remote(source, view, send_y.at[part, slot], recv_y.at[part, slot], (down, plane))
        remote(source, view, send_c.at[part, slot, 0], recv_c.at[part, slot, 0], (partner, plane))

    def landed(part, slot, block, sem):
        view = wholes[part].at[slot, :, lanes(block)]
        pltpu.make_async_copy(view, view, sem).wait()
        return view

    locals_ = []
    def stage_first(part):
        view = wholes[part].at[plane, :, lanes(me)]
        copy = pltpu.make_async_copy(shards[part], view, own_sem.at[part])
        copy.start()
        locals_.append(copy)
        for index, other in enumerate(planes):
            remote(shards[part], view, send_z.at[part, index], recv_z.at[part, index], (me, other))
        spread(part, shards[part], plane, me)

    def stage_z(part):
        for index, offset in enumerate((1, 2, 3)):
            slot = lax.rem(plane + 4 - offset, 4)
            view = landed(part, slot, me, recv_z.at[part, index])
            spread(part, view, slot, me)

    def stage_xy(part):
        for slot in range(4):
            view = landed(part, slot, across, recv_x.at[part, slot])
            remote(view, view, send_c.at[part, slot, 1], recv_c.at[part, slot, 1], (partner, plane))
            if slot < 2:
                remote(view, view, send_d.at[part, slot], recv_d.at[part, slot], (down, plane))
            view = landed(part, slot, down, recv_y.at[part, slot])
            remote(view, view, send_c.at[part, slot, 2], recv_c.at[part, slot, 2], (partner, plane))
            if slot >= 2:
                remote(view, view, send_d.at[part, slot], recv_d.at[part, slot], (across, plane))

    def stage_diagonal(part):
        for slot in range(4):
            view = landed(part, slot, diagonal, recv_d.at[part, slot])
            remote(view, view, send_c.at[part, slot, 3], recv_c.at[part, slot, 3], (partner, plane))

    stages = (stage_first, stage_z, stage_xy, stage_diagonal)
    for part in range(count):
        stage_first(part)
    for step in range(count + 2):
        for stage in (3, 2, 1):
            part = step - (stage - 1)
            if 0 <= part < count:
                stages[stage](part)
    flip = lambda block: block + 1 - 2 * lax.rem(block, 2)
    for part in range(count):
        for slot in range(4):
            for index, block in enumerate((me, across, down, diagonal)):
                landed(part, slot, flip(block), recv_c.at[part, slot, index])
    for copy in locals_:
        copy.wait()
    for copy in started:
        copy.wait_send()

def gather_blocks(shards, collective_id):
    count = len(shards)
    sem = pltpu.SemaphoreType.DMA
    return pl.pallas_call(
        functools.partial(gather_kernel, count),
        out_shape=[jax.ShapeDtypeStruct((4, s.shape[0], 1024), s.dtype) for s in shards],
        in_specs=[pl.BlockSpec(memory_space=pl.ANY)] * count,
        out_specs=[pl.BlockSpec(memory_space=pl.ANY)] * count,
        scratch_shapes=[sem((count,)), sem((count, 3)), sem((count, 3))] + [sem((count, 4))] * 6 + [sem((count, 4, 4))] * 2,
        compiler_params=pltpu.CompilerParams(collective_id=collective_id, has_side_effects=True),
        name="gather_blocks",
    )(*shards)


def add_into(target, source, rows, step):
    @pl.loop(0, rows // step)
    def _(index):
        window = pl.ds(pl.multiple_of(index * step, step), step)
        total = target[:, window].astype(jnp.float32) + source[:, window].astype(jnp.float32)
        target[:, window] = total.astype(jnp.bfloat16)


def scatter_kernel(count, *refs):
    grads, sums = refs[:count], refs[count : 2 * count]
    own, from_core, from_x, from_y, from_yx, from_xy, from_z = (
        refs[(2 + index) * count : (3 + index) * count] for index in range(7)
    )
    (load_sem, send_c, recv_c, send_x, recv_x, send_y, recv_y, send_yx, recv_yx, send_xy, recv_xy, send_z, recv_z) = refs[9 * count :]
    me, partner, across, down = neighbours()
    plane = lax.axis_index("tensor")
    planes = [lax.rem(plane + offset, 4) for offset in (1, 2, 3)]
    greet(plane, (partner, across, down), planes)
    flip = lambda block: block + 1 - 2 * lax.rem(block, 2)
    blocks = (me, across, down, across + down - me)
    started = []

    def remote(source, target, send, recv, device):
        copy = pltpu.make_async_remote_copy(source, target, send, recv, device_id=device, device_id_type=MESH)
        copy.start()
        started.append(copy)

    def wait(view, sem):
        pltpu.make_async_copy(view, view, sem).wait()

    order = (3, 1, 2, 0)
    def stage_core(part):
        for index in order:
            remote(grads[part].at[:, :, lanes(flip(blocks[index]))], from_core[part].at[index],
                   send_c.at[part, index], recv_c.at[part, index], (partner, plane))
            pltpu.make_async_copy(grads[part].at[:, :, lanes(blocks[index])], own[part].at[index], load_sem.at[part, index]).start()

    def stage_first(part):
        rows = sums[part].shape[0]
        for index in order:
            wait(own[part].at[index], load_sem.at[part, index])
            wait(from_core[part].at[index], recv_c.at[part, index])
            add_into(own[part].at[index], from_core[part].at[index], rows, step_of(rows))
            if index % 2 == 1:
                remote(own[part].at[index, 0:2], from_x[part].at[index // 2], send_x.at[part, index // 2], recv_x.at[part, index // 2], (across, plane))
            if index // 2 == 1:
                remote(own[part].at[index, 2:4], from_y[part].at[index % 2], send_y.at[part, index % 2], recv_y.at[part, index % 2], (down, plane))

    def stage_second(part):
        rows = sums[part].shape[0]
        for side in (1, 0):
            wait(from_x[part].at[side], recv_x.at[part, side])
            add_into(own[part].at[2 * side, 0:2], from_x[part].at[side], rows, step_of(rows))
            wait(from_y[part].at[side], recv_y.at[part, side])
            add_into(own[part].at[side, 2:4], from_y[part].at[side], rows, step_of(rows))
            if side == 1:
                remote(own[part].at[2, 0:2], from_yx[part], send_yx.at[part], recv_yx.at[part], (down, plane))
                remote(own[part].at[1, 2:4], from_xy[part], send_xy.at[part], recv_xy.at[part], (across, plane))

    def stage_third(part):
        rows = sums[part].shape[0]
        wait(from_yx[part], recv_yx.at[part])
        add_into(own[part].at[0, 0:2], from_yx[part], rows, step_of(rows))
        wait(from_xy[part], recv_xy.at[part])
        add_into(own[part].at[0, 2:4], from_xy[part], rows, step_of(rows))
        for index, other in enumerate(planes):
            remote(own[part].at[0, other], from_z[part].at[index], send_z.at[part, index], recv_z.at[part, index], (me, other))

    def stage_last(part):
        rows = sums[part].shape[0]
        step = step_of(rows)
        for index in range(3):
            wait(from_z[part].at[index], recv_z.at[part, index])
        @pl.loop(0, rows // step)
        def _(index):
            window = pl.ds(pl.multiple_of(index * step, step), step)
            total = own[part][0, plane, window].astype(jnp.float32)
            for other in range(3):
                total = total + from_z[part][other, window].astype(jnp.float32)
            sums[part][window] = total

    stages = (stage_core, stage_first, stage_second, stage_third, stage_last)
    for part in range(count):
        stage_core(part)
    for step in range(count + 3):
        for stage in (4, 3, 2, 1):
            part = step - (stage - 1)
            if 0 <= part < count:
                stages[stage](part)
    for copy in started:
        copy.wait_send()

def scatter_grads(grads, collective_id):
    count = len(grads)
    rows = [g.shape[1] for g in grads]
    sem = pltpu.SemaphoreType.DMA
    vm = lambda *lead: [pltpu.VMEM(lead + (r, 128), jnp.bfloat16) for r in rows]
    scratch = vm(4, 4) + vm(4, 4) + vm(2, 2) + vm(2, 2) + vm(2) + vm(2) + vm(3)
    sems = [sem((count, 4))] * 3 + [sem((count, 2))] * 4 + [sem((count,))] * 4 + [sem((count, 3))] * 2
    return pl.pallas_call(
        functools.partial(scatter_kernel, count),
        out_shape=[jax.ShapeDtypeStruct((r, 128), jnp.float32) for r in rows],
        in_specs=[pl.BlockSpec(memory_space=pl.ANY)] * count,
        out_specs=[pl.BlockSpec(memory_space=pltpu.VMEM)] * count,
        scratch_shapes=scratch + sems,
        compiler_params=pltpu.CompilerParams(collective_id=collective_id, has_side_effects=True, vmem_limit_bytes=58 * 1024 * 1024),
        name="scatter_grads",
    )(*grads)


def gather_weights(weights):
    tensor_count, dp_count = lax.axis_size("tensor"), lax.axis_size("dp")
    shards = [
        weight.transpose(1, 2, 0) if weight.ndim == 3 else weight.T for weight in weights
    ]
    shards = [shard.reshape(-1, shard.shape[-1]) for shard in shards]
    if (tensor_count, dp_count, shards[0].shape[1]) == (4, 8, 128):
        return gather_blocks(shards, 1)
    wholes = [lax.all_gather(shard, ("tensor", "dp")) for shard in shards]
    wholes = [
        whole.reshape(tensor_count, dp_count, *whole.shape[1:]).transpose(0, 2, 1, 3)
        for whole in wholes
    ]
    return [whole.reshape(*whole.shape[:2], -1) for whole in wholes]


def reduce_grads(grads):
    tensor_count, dp_count = lax.axis_size("tensor"), lax.axis_size("dp")
    if (tensor_count, dp_count, grads[0].shape[2]) == (4, 8, 1024):
        return scatter_grads(grads, 2)
    sums = []
    for grad in grads:
        blocks = grad.reshape(*grad.shape[:2], dp_count, -1).transpose(0, 2, 1, 3)
        blocks = blocks.reshape(-1, *blocks.shape[2:])
        part = lax.psum_scatter(blocks, ("tensor", "dp"), scatter_dimension=0, tiled=True)
        sums.append(part[0].astype(jnp.float32))
    return sums


def on_device(
    inputs,
    cotangent,
    lengths,
    qkv_weight,
    attn_out_weight,
    ffn_in_weight,
    ffn_out_weight,
    norm_gains,
    qkv_moment,
    attn_out_moment,
    ffn_in_moment,
    ffn_out_moment,
    gain_first,
    gain_second,
):
    tensor_count = lax.axis_size("tensor")
    dp_count = lax.axis_size("dp")
    dp_index = lax.axis_index("dp")
    tensor_index = lax.axis_index("tensor")
    core = dp_index % 2
    odd = tensor_index % 2 == 1
    upper = tensor_index >= tensor_count // 2
    lists = exchange_lists(dp_count // 2, tensor_count)
    weights = (qkv_weight, attn_out_weight, ffn_in_weight, ffn_out_weight)
    row_count = qkv_weight.shape[0]

    rows_low = to_sequences(inputs[:, 0], lists, odd, upper)
    qkv_all, attn_all, ffn_in_all, ffn_out_all = gather_weights(weights)
    cotangent_low = to_sequences(cotangent[:, 0], lists, odd, upper)
    rows_in = rows_low.astype(jnp.float32)
    grad_rows = cotangent_low.astype(jnp.float32)
    local_rows = rows_in.shape[0]
    own_lengths = swap_partner(lengths)
    both_lengths = jnp.where(
        core == 0,
        jnp.concatenate([lengths, own_lengths], 1),
        jnp.concatenate([own_lengths, lengths], 1),
    )
    length = lax.dynamic_index_in_dim(both_lengths.reshape(-1), tensor_index, 0, keepdims=False)
    first_row = core * local_rows
    cosine_table, sine_table = rotary(first_row, local_rows)
    own_positions = first_row + jnp.arange(local_rows)
    other_positions = (1 - core) * local_rows + jnp.arange(local_rows)
    key_valid = (jnp.concatenate([own_positions, other_positions]) < length)[None, None, :]

    normed_one, inverse_one, scaled_one = layer_norm_parts(rows_in, norm_gains[0])
    low_one = low(scaled_one)
    width = rows_in.shape[1]
    heads = width // HEAD_DIM
    qkv_rows = qkv_all.reshape(-1, width)
    attn_rows = attn_all.reshape(-1, width)
    ffn_in_rows = ffn_in_all.reshape(-1, width)
    ffn_out_rows = ffn_out_all.reshape(-1, width)
    projected = einsum("sk,nk->sn", low_one, qkv_rows)
    projected = projected.reshape(local_rows, tensor_count, 3, -1, HEAD_DIM)
    projected = projected.transpose(2, 0, 1, 3, 4).reshape(3, local_rows, heads, HEAD_DIM)
    queries = low(rotate(projected[0], cosine_table, sine_table))
    own_keys = low(rotate(projected[1], cosine_table, sine_table))
    own_values = low(projected[2])
    own_pair = jnp.stack([own_keys, own_values])
    pair = jnp.concatenate([own_pair, swap_partner(own_pair)], axis=1)
    context, log_total = attention_forward(queries, pair[0], pair[1], key_valid)
    context_low = low(context).reshape(local_rows, width)
    middle = rows_in + einsum("sk,kn->sn", context_low, attn_rows)
    normed_two, inverse_two, scaled_two = layer_norm_parts(middle, norm_gains[1])
    low_two = low(scaled_two)
    gate_up = einsum("kn,sn->ks", ffn_in_rows, low_two)
    gate_up = gate_up.reshape(tensor_count, 2, -1, local_rows)

    def activate(gate_part, up_part):
        return jax.nn.gelu(gate_part, approximate=False) * up_part

    hidden, activate_back = jax.vjp(activate, gate_up[:, 0], gate_up[:, 1])
    hidden_low = low(hidden).reshape(-1, local_rows)
    result = low(middle + einsum("ks,kn->sn", hidden_low, ffn_out_rows))
    outputs = from_sequences(result, lists, odd, upper)[:, None]

    grad_hidden = einsum("kn,sn->ks", ffn_out_rows, cotangent_low)
    grad_ffn_out = low(einsum("ks,sn->kn", hidden_low, cotangent_low))
    grad_gate, grad_up = activate_back(grad_hidden.reshape(hidden.shape))
    grad_gate_up = low(jnp.stack([grad_gate, grad_up], axis=1)).reshape(-1, local_rows)
    grad_ffn_in = low(einsum("ks,sn->kn", grad_gate_up, low_two))
    grad_scaled_two = einsum("ks,kn->sn", grad_gate_up, ffn_in_rows)
    grad_from_two, gain_two = layer_norm_back(
        grad_scaled_two, normed_two, inverse_two, norm_gains[1]
    )
    grad_middle = grad_rows + grad_from_two
    grad_branch = low(grad_middle)
    grad_context = low(einsum("sn,kn->sk", grad_branch, attn_rows))
    grad_attn_out = low(einsum("sk,sn->kn", context_low, grad_branch))
    grad_query, grad_keys, grad_values = attention_backward(
        queries,
        pair[0],
        pair[1],
        log_total,
        grad_context.reshape(local_rows, heads, HEAD_DIM),
        key_valid,
    )
    grad_pair = jnp.stack([grad_keys, grad_values])
    grad_pair = grad_pair[:, :local_rows] + swap_partner(low(grad_pair[:, local_rows:])).astype(
        jnp.float32
    )
    grad_projected = jnp.stack(
        [
            rotate(grad_query, cosine_table, -sine_table),
            rotate(grad_pair[0], cosine_table, -sine_table),
            grad_pair[1],
        ]
    )
    grad_projected = low(grad_projected).reshape(3, local_rows, tensor_count, -1)
    grad_projected = grad_projected.transpose(1, 2, 0, 3).reshape(local_rows, -1)
    grad_qkv = low(einsum("sk,sn->kn", grad_projected, low_one))
    grads = (grad_qkv, grad_attn_out, grad_ffn_in, grad_ffn_out)
    grads = [grad.reshape(tensor_count, -1, width) for grad in grads]
    sums = reduce_grads(grads[::-1])[::-1]
    grad_scaled_one = einsum("sk,kn->sn", grad_projected, qkv_rows)
    grad_from_one, gain_one = layer_norm_back(
        grad_scaled_one, normed_one, inverse_one, norm_gains[0]
    )
    grad_input = grad_middle + grad_from_one
    input_grad = from_sequences(low(grad_input), lists, odd, upper)[:, None].astype(jnp.float32)

    moments = (qkv_moment, attn_out_moment, ffn_in_moment, ffn_out_moment)
    sums = [
        part.reshape(*moment.shape[1:], row_count).transpose(
            (2, 0, 1) if moment.ndim == 3 else (1, 0)
        )
        for part, moment in zip(sums, moments)
    ]
    new_moments = [MOMENTUM * moment + part for moment, part in zip(moments, sums)]
    gain_grad = lax.psum(jnp.stack([gain_one, gain_two]), BOTH)
    flattened = [low(moment).reshape(row_count, -1) for moment in new_moments]
    local_widths = [matrix.shape[1] for matrix in flattened]
    widest = max(local_widths)
    stacked = jnp.stack(
        [jnp.pad(matrix, ((0, 0), (0, widest - matrix.shape[1]))) for matrix in flattened]
    )
    owned = lax.all_to_all(stacked, "tensor", split_axis=0, concat_axis=0, tiled=True)
    whole = lax.all_gather(owned, "dp", axis=1, tiled=True)
    gram = einsum("tik,tjk->ij", whole, whole)
    mean, rest = newton_schulz(gram)
    own_rows = lax.dynamic_slice_in_dim(rest, dp_index * row_count, row_count, 0)
    own_whole = lax.dynamic_slice_in_dim(whole, dp_index * row_count, row_count, 1)
    step_rows = low(einsum("ij,tjk->tik", low(own_rows), whole) + mean * own_whole)
    returned = lax.all_to_all(step_rows, "tensor", split_axis=0, concat_axis=0, tiled=True)
    new_weights = []
    for index, (weight, width) in enumerate(zip(weights, local_widths)):
        ortho_step = returned[index, :, :width].reshape(weight.shape).astype(jnp.float32)
        new_weights.append(
            weight.astype(jnp.float32) * (1.0 - MUON_RATE * DECAY_RATE)
            - MUON_RATE * 0.2 * math.sqrt(width * tensor_count) * ortho_step
        )
    gain_first_new = BETA_ONE * gain_first + (1.0 - BETA_ONE) * gain_grad
    gain_second_new = BETA_TWO * gain_second + (1.0 - BETA_TWO) * gain_grad * gain_grad
    first_hat = gain_first_new / (1.0 - BETA_ONE**STEP)
    second_hat = gain_second_new / (1.0 - BETA_TWO**STEP)
    norm_gains_new = norm_gains - ADAM_RATE * (
        first_hat / (jnp.sqrt(second_hat) + ADAM_EPS) + DECAY_RATE * norm_gains
    )
    return (
        outputs,
        input_grad,
        new_moments[0],
        new_weights[0],
        new_moments[1],
        new_weights[1],
        new_moments[2],
        new_weights[2],
        new_moments[3],
        new_weights[3],
        gain_first_new,
        gain_second_new,
        norm_gains_new,
    )


def solution(mesh):
    in_specs = (
        P(None, "dp", "tensor", None),
        P(None, "dp", "tensor", None),
        P(None, "dp"),
        P("dp", None, "tensor"),
        P("dp", "tensor"),
        P("dp", None, "tensor"),
        P("dp", "tensor"),
        P(),
        P("dp", None, "tensor"),
        P("dp", "tensor"),
        P("dp", None, "tensor"),
        P("dp", "tensor"),
        P(),
        P(),
    )
    out_specs = (
        P(None, "dp", "tensor", None),
        P(None, "dp", "tensor", None),
        P("dp", None, "tensor"),
        P("dp", None, "tensor"),
        P("dp", "tensor"),
        P("dp", "tensor"),
        P("dp", None, "tensor"),
        P("dp", None, "tensor"),
        P("dp", "tensor"),
        P("dp", "tensor"),
        P(),
        P(),
        P(),
    )
    return jax.shard_map(
        on_device, mesh=mesh, in_specs=in_specs, out_specs=out_specs, check_vma=False
    )
```

time: 2150 us -> 1070 us (0.50)
  waiting for transfers between devices: 1390 us -> 63.7 us
  Pallas kernels: 0 us -> 273 us
  blocking collectives: 184 us -> 89.7 us
  matrix products: 355 us -> 432 us
  local copies, waits for them, and re-layouts: 87.2 us -> 17.8 us
  other arithmetic: 76.6 us -> 125 us
    reduce_scatter x12 -> x0, waiting for transfers between devices: 653 us -> none  [the longest x2 157 us: micro_batch(): lax.psum_scatter(contract_cols(hidden_low, ffn_out_all), 'tensor', scatte...]
    psum x5 -> x0, waiting for transfers between devices: 392 us -> none  [on_device(): gram_sum = lax.psum(highest_dot(column_block, column_block.T), 'dp')]
    all_gather x11 -> x1, waiting for transfers between devices: 345 us -> 46.7 us  [on_device(): whole = lax.all_gather(owned, 'dp', axis=1, tiled=True)]
    pallas_call x0 -> x2, Pallas kernels: none -> 273 us  [the longest x1 140 us: gather_blocks(): pl.pallas_call(functools.partial(gather_kernel, count), out_shape=[jax.Sh...]
    all_to_all x3 -> x1, blocking collectives: 136 us -> 34.5 us  [on_device(): lax.all_to_all(stacked, 'tensor', split_axis=0, concat_axis=0, tiled=True)]
    dot_general x67 -> x37, matrix products: 355 us -> 432 us  [einsum(): return jnp.einsum(spec, *operands, preferred_element_type=jnp.float32)]
    dynamic_update_slice x8 -> x0, local copies, waits for them, and re-layouts: 43.8 us -> none  [attention_forward(): context, log_total = lax.map(one_block, starts)]
    convert_element_type x10, other arithmetic: 15.8 us -> 54.8 us  [the longest x8 51.7 us: low(): return values.astype(jnp.bfloat16)]
  transfers between devices with their start and end apart: 29 -> 13, of which waited for: 26 -> 3; matrix products, arithmetic and copies ran while one was open for 13% -> 32% of each run, Pallas kernels for 0% -> 13%
where the time goes in v1:
time: 1070 us; the launch traced here: 1060 us
  matrix products  432 us (40%)
  Pallas kernels  273 us (26%)
  other arithmetic  125 us (12%)
  blocking collectives  89.7 us (8%)
  waiting for transfers between devices  63.7 us (6%)
  between operations  30.1 us (3%)
  starting transfers between devices  27 us (3%)
  local copies, waits for them, and re-layouts  17.8 us (2%)
    dot_general x37, matrix products, einsum(): return jnp.einsum(spec, *operands, preferred_element_type=jnp.float32)  432 us
    pallas_call x1, Pallas kernels, gather_blocks(): pl.pallas_call(functools.partial(gather_kernel, count), out_shape=[jax.Sh...  140 us
    pallas_call x1, Pallas kernels, scatter_grads(): pl.pallas_call(functools.partial(scatter_kernel, count), out_shape=[jax.S...  133 us
    psum x1, blocking collectives, on_device(): gain_grad = lax.psum(jnp.stack([gain_one, gain_two]), BOTH)  55.3 us
    convert_element_type x8, other arithmetic, low(): return values.astype(jnp.bfloat16)  51.7 us
    all_gather x1, waiting for transfers between devices, on_device(): whole = lax.all_gather(owned, 'dp', axis=1, tiled=True)  46.7 us
    all_to_all x1, blocking collectives, on_device(): lax.all_to_all(stacked, 'tensor', split_axis=0, concat_axis=0, tiled=True)  34.5 us
    another operation x2, other arithmetic, on_device(): jnp.stack([grad_gate, grad_up], axis=1)  22.4 us
  transfers between devices with their start and end apart: 13, of which 3 were waited for; matrix products, arithmetic and copies ran while one was open for 32% of the time, Pallas kernels for 13%

profile of v1, /device:TPU:9, one launch (start us, length us, event | category | flops | bytes accessed | tf_op | source)
XLA Modules:
  0.0 1057.8 jit_solution(3997989677207321184)
XLA Ops:
  9.2 4.1 collective-permute-start.1
  16.7 139.6 %gather_blocks.1 = (bf16[4,768,1024]{2,1,0:T(8,128)(2,1)}, bf16[4,256,1024]{2,1,0:T(8,128)(2,1)}, bf16[4,1312,1024]{2,1,0:T(8,128)(2,1)}, bf16[4,656,1024]{2,1,0:T(8,128)(2,1)}) custom-call(bf16[768,128]{1,0:T(8,128)(2,1)} %bitcast.406, bf16[256,128]{1,0:T(8,128)(2,1)} %bitcast.410, bf16[1312,128]{1,0:T(8,128)(2,1)} %bitcast.403, bf16[656,128]{1,0:T(8,128)(2,1)} %bitcast.409), custom_call_target="tpu_custom_call" | custom-call | tf_op jit(solution)/shard_map/gather_blocks/pallas_call | solution.py:273
  159.0 6.3 convolution_bitcast_fusion.1
  169.5 2.5 collective-permute-start.7
  172.1 4.3 collective-permute-start.3
  178.6 16.9 %collective-permute-done.7 = bf16[256,1024]{1,0:T(8,128)(2,1)} collective-permute-done((bf16[256,1024]{1,0:T(8,128)(2,1)}, bf16[256,1024]{1,0:T(8,128)(2,1)}, u32[]{:S(2)}, u32[]{:S(2)}) %collective-permute-start.7) | collective-permute-done | bytes 524320 | tf_op jit(solution)/shard_map/ppermute | solution.py:122
  195.6 8.4 fusion.150
  204.0 2.1 pad_maximum_fusion.1
  206.1 13.2 %fusion.6 = (f32[16,512]{1,0:T(8,128)S(1)}, f32[16,512,1024]{2,1,0:T(8,128)}) fusion(pred[1024]{0:T(1024)(128)(4,1)S(1)} %add_compare_fusion, bf16[2,1024,16,64]{1,3,2,0:T(8,128)(2,1)S(1)} %pad_maximum_fusion.1, bf16[512,16,32]{0,2,1:T(8,128)(2,1)S(1)} %get-tuple-element.83, bf16[512,16,32]{0,2,1:T(8,128)(2,1)S(1)} %get-tuple-element.82), kind=kOutput, calls=%fused_computation.11 | convolution fusion | flops 1100996608 | bytes 36733952 | tf_op jit(solution)/shard_map/qhd,khd->hqk/dot_general | solution.py:76
  219.3 14.6 %fusion = f32[16,512]{1,0:T(8,128)S(1)} fusion(f32[16,512]{1,0:T(8,128)S(1)} %get-tuple-element.103, f32[16,512,1024]{2,1,0:T(8,128)} %get-tuple-element.104, pred[1024]{0:T(1024)(128)(4,1)S(1)} %add_compare_fusion), kind=kLoop, calls=%fused_computation.6 | loop fusion | flops 33546240 | bytes 33620992 | tf_op jit(solution)/shard_map/reduce_sum | solution.py:89
  233.9 13.9 %fusion.141 = bf16[16,64,512]{2,1,0:T(8,128)(2,1)S(1)} fusion(f32[16,512]{1,0:T(8,128)S(1)} %fusion, f32[16,512]{1,0:T(8,128)S(1)} %get-tuple-element.103, f32[16,512,1024]{2,1,0:T(8,128)} %get-tuple-element.104, pred[1024]{0:T(1024)(128)(4,1)S(1)} %add_compare_fusion, bf16[2,1024,16,64]{1,3,2,0:T(8,128)(2,1)S(1)} %pad_maximum_fusion.1), kind=kOutput, calls=%fused_computation.224 | convolution fusion | flops 1116209152 | bytes 36766720 | tf_op jit(solution)/shard_map/hqk,khd->qhd/dot_general | solution.py:76
  249.7 8.9 fusion.147
  258.6 14.7 %fusion.20 = (bf16[4,1,656,512]{3,2,0,1:T(8,128)(2,1)}, f32[4,656,512]{2,1,0:T(8,128)}) fusion(f32[4,656,512]{2,1,0:T(8,128)S(1)} %bitcast.381, f32[4,2,656,512]{3,2,1,0:T(8,128)S(1)} %fusion.147), kind=kLoop, calls=%fused_computation.51 | loop fusion | flops 98074624 | bytes 24182784 | tf_op jit(solution)/shard_map/stack | solution.py:504
  273.3 7.7 multiply_bitcast_fusion
  281.1 3.1 maximum_convert_fusion
  284.6 11.7 %multiply_reduce_fusion.1 = (f32[1024]{0:T(1024)}, f32[512]{0:T(512)S(1)}, f32[512]{0:T(512)S(1)}, f32[512,1024]{1,0:T(8,128)S(1)}) fusion(f32[512,1024]{1,0:T(8,128)S(1)} %get-tuple-element.106, f32[512]{0:T(512)S(1)} %add_rsqrt_fusion, f32[512]{0:T(512)S(1)} %broadcast_multiply_fusion.4, f32[1024]{0:T(1024)S(1)} %bitcast.413, ...), kind=kOutput, calls=%fused_computation.185 | convolution fusion | flops 5507119104 | bytes 20332544 | tf_op jit(solution)/shard_map/ks,kn->sn/dot_general | solution.py:76
  296.3 2.6 multiply_add_fusion.18
  300.2 2.3 convolution_convert_fusion.4
  304.0 25.0 %multiply_reduce_fusion = (f32[16,512]{1,0:T(8,128)S(1)}, f32[16,512,1024]{2,1,0:T(8,128)}) fusion(f32[16,512]{1,0:T(8,128)S(1)} %log_add_fusion, f32[16,512,1024]{2,1,0:T(8,128)} %get-tuple-element.104, pred[1024]{0:T(1024)(128)(4,1)S(1)} %add_compare_fusion, bf16[512,16,64]{0,2,1:T(8,128)(2,1)S(1)} %bitcast.387, bf16[2,1024,16,64]{1,3,2,0:T(8,128)(2,1)} %copy-done.1), kind=kOutput, calls=%fused_computation.1 | convolution fusion | flops 1115676672 | bytes 70321152 | tf_op jit(solution)/shard_map/qhd,khd->hqk/dot_general | solution.py:76
  329.0 15.8 %fusion.69 = f32[1,1024,16,64]{1,3,2,0:T(8,128)} fusion(bf16[512,16,64]{0,2,1:T(8,128)(2,1)S(1)} %bitcast.388, f32[16,512]{1,0:T(8,128)S(1)} %log_add_fusion, f32[16,512,1024]{2,1,0:T(8,128)} %get-tuple-element.104, pred[1024]{0:T(1024)(128)(4,1)S(1)} %add_compare_fusion), kind=kOutput, calls=%fused_computation.160 | convolution fusion | flops 1107296256 | bytes 38831104 | tf_op jit(solution)/shard_map/hqk,qhd->khd/dot_general | solution.py:76
  344.8 28.2 %multiply_convert_fusion = bf16[16,512,1024]{2,1,0:T(8,128)(2,1)} fusion(f32[16,512,1024]{2,1,0:T(8,128)} %get-tuple-element.109, f32[16,512]{1,0:T(8,128)S(1)} %get-tuple-element.108, f32[16,512]{1,0:T(8,128)S(1)} %log_add_fusion, f32[16,512,1024]{2,1,0:T(8,128)} %get-tuple-element.104, pred[1024]{0:T(1024)(128)(4,1)S(1)} %add_compare_fusion), kind=kLoop, calls=%fused_computation | loop fusion | flops 50331648 | bytes 83952640 | tf_op jit(solution)/shard_map/convert_element_type | solution.py:80
  373.0 10.7 %multiply_bitcast_fusion.1 = f32[1,1024,16,64]{1,3,2,0:T(8,128)} fusion(bf16[16,512,1024]{2,1,0:T(8,128)(2,1)} %multiply_convert_fusion, bf16[512,16,32]{0,2,1:T(8,128)(2,1)S(1)} %copy-done.12, bf16[512,16,32]{0,2,1:T(8,128)(2,1)S(1)} %copy-done.10), kind=kOutput, calls=%fused_computation.136 | convolution fusion | flops 1076887552 | bytes 22020096 | tf_op jit(solution)/shard_map/hqk,qhd->khd/dot_general | solution.py:76
  383.7 13.0 %multiply_bitcast_fusion.2 = f32[512,16,64]{0,2,1:T(8,128)} fusion(bf16[16,512,1024]{2,1,0:T(8,128)(2,1)} %multiply_convert_fusion, bf16[2,1024,16,64]{1,3,2,0:T(8,128)(2,1)} %copy-done.1), kind=kOutput, calls=%fused_computation.208 | convolution fusion | flops 1074266112 | bytes 20971520 | tf_op jit(solution)/shard_map/hqk,khd->qhd/dot_general | solution.py:76
  396.7 4.0 fusion.46
  405.0 11.4 %fusion.11 = bf16[2624,512]{1,0:T(8,128)(2,1)S(1)} fusion(f32[4,1,656,512]{3,2,1,0:T(8,128)S(1)} %slice-done, f32[4,1,656,512]{3,2,0,1:T(8,128)S(1)} %get-tuple-element.75, f32[4,1,656,512]{3,2,0,1:T(8,128)S(1)} %get-tuple-element.74), kind=kLoop, calls=%fused_computation.29 | loop fusion | flops 84639744 | bytes 18808832 | tf_op jit(solution)/shard_map/convert_element_type | solution.py:80
  416.4 2.6 convolution_convert_fusion.3
  419.0 6.7 convolution_convert_fusion.2
  425.7 8.8 convolution_convert_fusion
  434.6 2.5 fusion.48
  440.7 5.7 convolution_convert_fusion.1
  446.4 133.1 %scatter_grads.1 = (f32[656,128]{1,0:T(8,128)}, f32[1312,128]{1,0:T(8,128)}, f32[256,128]{1,0:T(8,128)}, f32[768,128]{1,0:T(8,128)}) custom-call(bf16[4,656,1024]{2,1,0:T(8,128)(2,1)} %bitcast.394, bf16[4,1312,1024]{2,1,0:T(8,128)(2,1)} %bitcast.382, bf16[4,256,1024]{2,1,0:T(8,128)(2,1)} %bitcast.401, bf16[4,768,1024]{2,1,0:T(8,128)(2,1)} %bitcast.389), custom_call_target="tpu_custom_call" | custom-call | tf_op jit(solution)/shard_map/scatter_grads/pallas_call | solution.py:383
  584.1 1.8 fusion.218
  586.1 2.2 fusion.220
  588.5 34.5 %all_to_all.10 = bf16[4,128,1312]{1,2,0:T(8,128)(2,1)} all-to-all(bf16[4,128,1312]{1,2,0:T(8,128)(2,1)S(1)} %pad_maximum_fusion.4), channel_id=1, replica_groups=mesh['dp'=8,'tensor'=4] {'tensor'}, dimensions={0} | all-to-all | bytes 2686976 | tf_op jit(solution)/shard_map/all_to_all | solution.py:561
  624.3 11.4 %fusion.110 = bf16[512,1024]{1,0:T(8,128)(2,1)S(1)} fusion(f32[512,1024]{1,0:T(8,128)S(1)} %get-tuple-element.106, bf16[4,656,1024]{2,1,0:T(8,128)(2,1)} %get-tuple-element.24, f32[4,656,512]{2,1,0:T(8,128)} %get-tuple-element.73, f32[4,2,656,512]{3,2,1,0:T(8,128)} %copy-done), kind=kOutput, calls=%fused_computation.184 | convolution fusion | flops 2757885952 | bytes 24641536 | tf_op jit(solution)/shard_map/ks,kn->sn/dot_general | solution.py:76
  636.7 2.1 collective-permute-start.5
  638.8 4.8 collective-permute-start.4
  643.6 46.7 %all-gather.2.cloned.1.call-done = bf16[4,1024,1312]{1,2,0:T(8,128)(2,1)} async-done(((bf16[4,128,1312]{1,2,0:T(8,128)(2,1)}), bf16[4,1024,1312]{1,2,0:T(8,128)(2,1)}) %all-gather.2.cloned.1.call-update) | async-done | bytes 10747920 | tf_op jit(solution)/shard_map/all_gather | solution.py:562
  690.3 18.2 %fusion.50 = (f32[]{:T(128)}, f32[1024,1024,1]{1,0,2:T(8,128)}) fusion(bf16[4,1024,1312]{1,2,0:T(8,128)(2,1)} %all-gather.2.cloned.1.call-done), kind=kOutput, calls=%fused_computation.87 | convolution fusion | flops 11008999424 | bytes 14942212 | tf_op jit(solution)/shard_map/tik,tjk->ij/dot_general | solution.py:76
  709.2 2.9 select_reduce_fusion.17
  714.1 9.9 select_reduce_fusion.16
  725.3 14.4 %select_reduce_fusion.15 = (f32[]{:T(128)}, f32[1024,1024]{1,0:T(8,128)}) fusion(f32[]{:T(128)S(6)} %div.124, f32[1024,1024]{1,0:T(8,128)} %get-tuple-element.114, f32[]{:T(128)S(6)} %div.123, f32[]{:T(128)S(6)} %mul.926, f32[1024,1024,1]{1,0,2:T(8,128)} %get-tuple-element.112, f32[]{:T(128)S(6)} %add.355), kind=kOutput, calls=%fused_computation.129 | convolution fusion | flops 2185232384 | bytes 12582932 | tf_op jit(solution)/shard_map/ij,jk->ik/dot_general | solution.py:76
  740.4 16.4 %select_reduce_fusion.14 = (f32[]{:T(128)}, f32[1024,1024]{1,0:T(8,128)}) fusion(f32[]{:T(128)S(6)} %div.124, f32[1024,1024]{1,0:T(8,128)} %get-tuple-element.114, f32[]{:T(128)S(6)} %div.123, f32[]{:T(128)S(6)} %mul.926, f32[1024,1024,1]{1,0,2:T(8,128)} %get-tuple-element.112, f32[]{:T(128)S(6)} %add.359, f32[1024,1024]{1,0:T(8,128)} %get-tuple-element.116, ...), kind=kOutput, calls=%fused_computation.126 | convolution fusion | flops 2186280960 | bytes 16777244 | tf_op jit(solution)/shard_map/ij,jk->ik/dot_general | solution.py:76
  757.4 9.6 select_reduce_fusion.13
  767.6 12.9 %select_reduce_fusion.12 = (f32[]{:T(128)}, f32[1024,1024]{1,0:T(8,128)}) fusion(f32[]{:T(128)S(6)} %div.127, f32[1024,1024]{1,0:T(8,128)} %get-tuple-element.120, f32[]{:T(128)S(6)} %add.361, f32[1024,1024]{1,0:T(8,128)} %get-tuple-element.118, f32[]{:T(128)S(6)} %div.126, f32[]{:T(128)S(6)} %add.367), kind=kOutput, calls=%fused_computation.121 | convolution fusion | flops 2182086656 | bytes 12582932 | tf_op jit(solution)/shard_map/ij,jk->ik/dot_general | solution.py:76
  781.2 15.5 %select_reduce_fusion.11 = (f32[]{:T(128)}, f32[1024,1024]{1,0:T(8,128)}) fusion(f32[]{:T(128)S(6)} %div.127, f32[1024,1024]{1,0:T(8,128)} %get-tuple-element.120, f32[]{:T(128)S(6)} %add.361, f32[1024,1024]{1,0:T(8,128)} %get-tuple-element.118, f32[]{:T(128)S(6)} %div.126, f32[]{:T(128)S(6)} %add.371, f32[1024,1024]{1,0:T(8,128)} %get-tuple-element.124, ...), kind=kOutput, calls=%fused_computation.118 | convolution fusion | flops 2184183808 | bytes 16777244 | tf_op jit(solution)/shard_map/ij,jk->ik/dot_general | solution.py:76
  797.4 9.9 select_reduce_fusion.10
  807.9 13.1 %select_reduce_fusion.9 = (f32[]{:T(128)}, f32[1024,1024]{1,0:T(8,128)}) fusion(f32[]{:T(128)S(6)} %div.130, f32[1024,1024]{1,0:T(8,128)} %get-tuple-element.128, f32[]{:T(128)S(6)} %add.373, f32[1024,1024]{1,0:T(8,128)} %get-tuple-element.126, f32[]{:T(128)S(6)} %div.129, f32[]{:T(128)S(6)} %add.379), kind=kOutput, calls=%fused_computation.113 | convolution fusion | flops 2182086656 | bytes 12582932 | tf_op jit(solution)/shard_map/ij,jk->ik/dot_general | solution.py:76
  821.7 15.7 %select_reduce_fusion.8 = (f32[]{:T(128)}, f32[1024,1024]{1,0:T(8,128)}) fusion(f32[]{:T(128)S(6)} %div.130, f32[1024,1024]{1,0:T(8,128)} %get-tuple-element.128, f32[]{:T(128)S(6)} %add.373, f32[1024,1024]{1,0:T(8,128)} %get-tuple-element.126, f32[]{:T(128)S(6)} %div.129, f32[]{:T(128)S(6)} %add.383, f32[1024,1024]{1,0:T(8,128)} %get-tuple-element.132, ...), kind=kOutput, calls=%fused_computation.110 | convolution fusion | flops 2184183808 | bytes 16777244 | tf_op jit(solution)/shard_map/ij,jk->ik/dot_general | solution.py:76
  838.0 19.3 %select_reduce_fusion.3 = (f32[]{:T(128)}, f32[1024,1024]{1,0:T(8,128)}) fusion(f32[]{:T(128)S(6)} %div.127, f32[1024,1024]{1,0:T(8,128)} %get-tuple-element.120, f32[]{:T(128)S(6)} %add.361, f32[1024,1024]{1,0:T(8,128)} %get-tuple-element.118, f32[]{:T(128)S(6)} %div.126, f32[]{:T(128)S(6)} %add.355, f32[]{:T(128)S(6)} %div.124, ...), kind=kOutput, calls=%fused_computation.97 | convolution fusion | flops 2203058176 | bytes 20971556 | tf_op jit(solution)/shard_map/ij,jk->ik/dot_general | solution.py:76
  857.3 9.6 select_reduce_fusion.7
  867.6 13.0 %select_reduce_fusion.6 = (f32[]{:T(128)}, f32[1024,1024]{1,0:T(8,128)}) fusion(f32[]{:T(128)S(6)} %div.133, f32[1024,1024]{1,0:T(8,128)} %get-tuple-element.136, f32[]{:T(128)S(6)} %add.385, f32[1024,1024]{1,0:T(8,128)} %get-tuple-element.134, f32[]{:T(128)S(6)} %div.132, f32[]{:T(128)S(6)} %add.391), kind=kOutput, calls=%fused_computation.105 | convolution fusion | flops 2182086656 | bytes 12582932 | tf_op jit(solution)/shard_map/ij,jk->ik/dot_general | solution.py:76
  881.3 15.9 %select_reduce_fusion.5 = (f32[]{:T(128)}, f32[1024,1024]{1,0:T(8,128)}) fusion(f32[]{:T(128)S(6)} %div.133, f32[1024,1024]{1,0:T(8,128)} %get-tuple-element.136, f32[]{:T(128)S(6)} %add.385, f32[1024,1024]{1,0:T(8,128)} %get-tuple-element.134, f32[]{:T(128)S(6)} %div.132, f32[]{:T(128)S(6)} %add.395, f32[1024,1024]{1,0:T(8,128)} %get-tuple-element.140, ...), kind=kOutput, calls=%fused_computation.102 | convolution fusion | flops 2184183808 | bytes 16777244 | tf_op jit(solution)/shard_map/ij,jk->ik/dot_general | solution.py:76
  897.9 9.7 select_reduce_fusion.4
  908.9 15.7 %select_reduce_fusion.2 = (f32[]{:T(128)}, f32[1024,1024]{1,0:T(8,128)}) fusion(f32[]{:T(128)S(6)} %div.130, f32[1024,1024]{1,0:T(8,128)} %get-tuple-element.128, f32[]{:T(128)S(6)} %add.373, f32[1024,1024]{1,0:T(8,128)} %get-tuple-element.126, f32[]{:T(128)S(6)} %div.129, f32[]{:T(128)S(6)} %add.404, f32[1024,1024]{1,0:T(8,128)} %get-tuple-element.122, ...), kind=kOutput, calls=%fused_computation.94 | convolution fusion | flops 2184183808 | bytes 16777244 | tf_op jit(solution)/shard_map/ij,jk->ik/dot_general | solution.py:76
  925.2 15.9 %select_reduce_fusion.1 = (f32[]{:T(128)}, f32[1024,1024]{1,0:T(8,128)}) fusion(f32[]{:T(128)S(6)} %div.133, f32[1024,1024]{1,0:T(8,128)} %get-tuple-element.136, f32[]{:T(128)S(6)} %add.385, f32[1024,1024]{1,0:T(8,128)} %get-tuple-element.134, f32[]{:T(128)S(6)} %div.132, f32[]{:T(128)S(6)} %add.407, f32[1024,1024]{1,0:T(8,128)} %get-tuple-element.130, ...), kind=kOutput, calls=%fused_computation.91 | convolution fusion | flops 2184183808 | bytes 16777244 | tf_op jit(solution)/shard_map/ij,jk->ik/dot_general | solution.py:76
  941.8 15.7 %select_reduce_fusion = (f32[]{:T(128)}, f32[1024,1024]{1,0:T(8,128)}) fusion(f32[]{:T(128)S(6)} %div.136, f32[1024,1024]{1,0:T(8,128)} %get-tuple-element.144, f32[]{:T(128)S(6)} %add.397, f32[1024,1024]{1,0:T(8,128)} %get-tuple-element.142, f32[]{:T(128)S(6)} %div.135, f32[]{:T(128)S(6)} %add.413, f32[1024,1024]{1,0:T(8,128)} %get-tuple-element.138, ...), kind=kOutput, calls=%fused_computation.88 | convolution fusion | flops 2184183808 | bytes 16777244 | tf_op jit(solution)/shard_map/ij,jk->ik/dot_general | solution.py:76
  958.3 8.8 fusion.59
  967.0 4.6 all-to-all-start.1
  971.6 7.2 fusion.78
  980.8 3.2 collective-permute-start.10
  984.5 2.7 maximum_select_fusion.1
  987.9 55.3 %psum.7 = f32[2,1024]{1,0:T(2,128)S(1)} all-reduce(f32[2,1024]{1,0:T(2,128)S(1)} %pad_maximum_fusion.10), channel_id=1, replica_groups=mesh['dp'=8,'tensor'=4] {'dp','tensor'}, use_global_device_ids=true, to_apply=%region_32.33 | all-reduce | flops 2048 | bytes 16384 | tf_op jit(solution)/shard_map/psum | solution.py:554
  1043.9 3.1 fusion.146
  (198 shorter events, 41.9 us)
Async XLA Ops:
  7.2 683.1 %all-gather.2.cloned.1.call-start = ((), (), s32[]{:S(2)}) async-start(), calls=%async_computation.2 | async-start | bytes 12091392 | tf_op jit(solution)/shard_map/all_gather | solution.py:562
  8.5 149.5 %collective-permute-start = (bf16[256,1024]{1,0:T(8,128)(2,1)S(1)}, bf16[256,1024]{1,0:T(8,128)(2,1)S(1)}, u32[]{:S(2)}, u32[]{:S(2)}) collective-permute-start(bf16[256,1024]{1,0:T(8,128)(2,1)S(1)} %get-tuple-element.93), channel_id=1, source_target_pairs={{0,2},{1,0},{2,6},{3,4},{4,3},{5,1},{6,7},{7,5},{8,10},{9,8},{10,1... | collective-permute-start | bytes 1572872 | tf_op jit(solution)/shard_map/ppermute | solution.py:123
  9.2 148.8 %collective-permute-start.1 = (bf16[256,1024]{1,0:T(8,128)(2,1)S(1)}, bf16[256,1024]{1,0:T(8,128)(2,1)S(1)}, u32[]{:S(2)}, u32[]{:S(2)}) collective-permute-start(bf16[256,1024]{1,0:T(8,128)(2,1)S(1)} %get-tuple-element.92), channel_id=1, source_target_pairs={{0,0},{1,2},{2,4},{3,6},{4,1},{5,3},{6,5},{7,7},{8,8},{9,10},{10,1... | collective-permute-start | bytes 1572872 | tf_op jit(solution)/shard_map/ppermute | solution.py:122
  157.1 8.2 copy-start.38
  158.0 8.2 copy-start.26
  158.4 6.9 copy-start.35
  158.9 6.4 copy-start.41
  166.2 2.3 copy-start.23
  166.9 39.2 %copy-start.9 = (bf16[512,16,32]{0,2,1:T(8,128)(2,1)}, bf16[512,16,32]{0,2,1:T(8,128)(2,1)S(1)}, u32[]{:S(2)}) copy-start(bf16[512,16,32]{0,2,1:T(8,128)(2,1)S(1)} %get-tuple-element.82) | copy-start | bytes 1572868
  166.9 39.2 %copy-start.11 = (bf16[512,16,32]{0,2,1:T(8,128)(2,1)}, bf16[512,16,32]{0,2,1:T(8,128)(2,1)S(1)}, u32[]{:S(2)}) copy-start(bf16[512,16,32]{0,2,1:T(8,128)(2,1)S(1)} %get-tuple-element.83) | copy-start | bytes 1572868
  166.9 5.2 copy-start.47
  166.9 9.4 copy-start.33
  168.4 35.5 %collective-permute-start.2 = (bf16[2,512,16,64]{1,3,2,0:T(8,128)(2,1)}, bf16[2,512,16,64]{1,3,2,0:T(8,128)(2,1)}, u32[]{:S(2)}, u32[]{:S(2)}) collective-permute-start(bf16[2,512,16,64]{1,3,2,0:T(8,128)(2,1)} %pad_maximum_fusion.3), channel_id=1, source_target_pairs={{0,4},{4,0},{8,12},{12,8},{16,20},{20,16},{24,28},{28,24},{1,5},{5... | collective-permute-start | bytes 6291464 | tf_op jit(solution)/shard_map/ppermute | solution.py:140
  169.5 26.0 %collective-permute-start.7 = (bf16[256,1024]{1,0:T(8,128)(2,1)}, bf16[256,1024]{1,0:T(8,128)(2,1)}, u32[]{:S(2)}, u32[]{:S(2)}) collective-permute-start(bf16[256,1024]{1,0:T(8,128)(2,1)} %get-tuple-element.91), channel_id=1, source_target_pairs={{0,0},{1,2},{2,4},{3,6},{4,1},{5,3},{6,5},{7,7},{8,8},{9,10},{10,1... | collective-permute-start | bytes 1572872 | tf_op jit(solution)/shard_map/ppermute | solution.py:122
  172.1 23.5 %collective-permute-start.6 = (bf16[256,1024]{1,0:T(8,128)(2,1)}, bf16[256,1024]{1,0:T(8,128)(2,1)}, u32[]{:S(2)}, u32[]{:S(2)}) collective-permute-start(bf16[256,1024]{1,0:T(8,128)(2,1)} %get-tuple-element.90), channel_id=1, source_target_pairs={{0,2},{1,0},{2,6},{3,4},{4,3},{5,1},{6,7},{7,5},{8,10},{9,8},{10,1... | collective-permute-start | bytes 1572872 | tf_op jit(solution)/shard_map/ppermute | solution.py:123
  172.1 5.1 collective-permute-start.3
  206.1 27.8 %copy-start.1 = (bf16[2,1024,16,64]{1,3,2,0:T(8,128)(2,1)}, bf16[2,1024,16,64]{1,3,2,0:T(8,128)(2,1)S(1)}, u32[]{:S(2)}) copy-start(bf16[2,1024,16,64]{1,3,2,0:T(8,128)(2,1)S(1)} %pad_maximum_fusion.1) | copy-start | bytes 12582916
  233.9 13.9 %copy-start.14 = (bf16[256,1024]{1,0:T(8,128)(2,1)S(1)}, bf16[256,1024]{1,0:T(8,128)(2,1)}, u32[]{:S(2)}) copy-start(bf16[256,1024]{1,0:T(8,128)(2,1)} %copy-done.13) | copy-start | bytes 1572868
  233.9 13.9 %copy-start.18 = (bf16[256,1024]{1,0:T(8,128)(2,1)S(1)}, bf16[256,1024]{1,0:T(8,128)(2,1)}, u32[]{:S(2)}) copy-start(bf16[256,1024]{1,0:T(8,128)(2,1)} %copy-done.17) | copy-start | bytes 1572868
  233.9 13.9 %copy-start.48 = (bf16[4,256,1024]{2,1,0:T(8,128)(2,1)S(1)}, bf16[4,256,1024]{2,1,0:T(8,128)(2,1)}, u32[]{:S(2)}) copy-start(bf16[4,256,1024]{2,1,0:T(8,128)(2,1)} %get-tuple-element.22) | copy-start | bytes 6291460
  247.8 1.5 copy-start.50
  247.9 10.7 %slice-start.1 = ((s8[5373952]{0:T(1024)(128)(4,1)}), s8[4194304]{0:T(1024)(128)(4,1)S(1)}, s32[]{:S(2)}) async-start(s8[5373952]{0:T(1024)(128)(4,1)} %bitcast.380), calls=%async_computation.4 | async-start | bytes 8388608
  249.6 9.0 slice-start.2
  258.6 14.7 %copy-start = (f32[4,2,656,512]{3,2,1,0:T(8,128)}, f32[4,2,656,512]{3,2,1,0:T(8,128)S(1)}, u32[]{:S(2)}) copy-start(f32[4,2,656,512]{3,2,1,0:T(8,128)S(1)} %fusion.147) | copy-start | bytes 32243716
  284.6 11.7 %copy-start.8 = (bf16[4,2,656,512]{3,2,1,0:T(8,128)(2,1)}, bf16[4,2,656,512]{3,2,1,0:T(8,128)(2,1)S(1)}, u32[]{:S(2)}) copy-start(bf16[4,2,656,512]{3,2,1,0:T(8,128)(2,1)S(1)} %copy.44) | copy-start | bytes 16121860
  296.3 3.9 copy-start.49
  298.9 1.3 copy-start.5
  344.8 28.2 %copy-start.10 = (bf16[512,16,32]{0,2,1:T(8,128)(2,1)S(1)}, bf16[512,16,32]{0,2,1:T(8,128)(2,1)}, u32[]{:S(2)}) copy-start(bf16[512,16,32]{0,2,1:T(8,128)(2,1)} %copy-done.9) | copy-start | bytes 1572868
  344.8 28.2 %copy-start.12 = (bf16[512,16,32]{0,2,1:T(8,128)(2,1)S(1)}, bf16[512,16,32]{0,2,1:T(8,128)(2,1)}, u32[]{:S(2)}) copy-start(bf16[512,16,32]{0,2,1:T(8,128)(2,1)} %copy-done.11) | copy-start | bytes 1572868
  396.7 4.1 copy-start.2
  396.7 5.1 copy-start.3
  401.7 3.3 slice-start
  403.4 31.2 %collective-permute-start.8 = (bf16[2,512,16,64]{1,3,2,0:T(8,128)(2,1)}, bf16[2,512,16,64]{1,3,2,0:T(8,128)(2,1)}, u32[]{:S(2)}, u32[]{:S(2)}) collective-permute-start(bf16[2,512,16,64]{1,3,2,0:T(8,128)(2,1)} %fusion.49), channel_id=1, source_target_pairs={{0,4},{4,0},{8,12},{12,8},{16,20},{20,16},{24,28},{28,24},{1,5},{5... | collective-permute-start | bytes 6291464 | tf_op jit(solution)/shard_map/ppermute | solution.py:140
  405.0 11.4 %copy-start.6 = (f32[512,1024]{1,0:T(8,128)S(1)}, f32[512,1024]{1,0:T(8,128)}, u32[]{:S(2)}) copy-start(f32[512,1024]{1,0:T(8,128)} %copy-done.5) | copy-start | bytes 6291460
  405.0 11.4 %copy-start.51 = (bf16[16,64,512]{2,1,0:T(8,128)(2,1)S(1)}, bf16[16,64,512]{2,1,0:T(8,128)(2,1)}, u32[]{:S(2)}) copy-start(bf16[16,64,512]{2,1,0:T(8,128)(2,1)} %copy-done.50) | copy-start | bytes 3145732
  416.4 9.3 slice-start.3
  419.0 6.7 slice-start.4
  437.1 1.6 copy-start.4
  437.1 1.6 copy-start.27
  437.1 1.6 copy-start.32
  439.5 1.2 copy-start.19
  440.0 6.4 copy-start.21
  446.4 134.3 %copy-start.31 = (f32[128,656]{0,1:T(8,128)S(1)}, f32[128,656]{0,1:T(8,128)}, u32[]{:S(2)}) copy-start(f32[128,656]{0,1:T(8,128)} %param.25) | copy-start | bytes 1007620
  446.4 136.1 %copy-start.30 = (f32[128,256]{0,1:T(8,128)S(1)}, f32[128,256]{0,1:T(8,128)}, u32[]{:S(2)}) copy-start(f32[128,256]{0,1:T(8,128)} %copy.51) | copy-start | bytes 393220
  636.7 347.7 %collective-permute-start.5 = (bf16[256,1024]{1,0:T(8,128)(2,1)}, bf16[256,1024]{1,0:T(8,128)(2,1)}, u32[]{:S(2)}, u32[]{:S(2)}) collective-permute-start(bf16[256,1024]{1,0:T(8,128)(2,1)} %get-tuple-element.89), channel_id=1, source_target_pairs={{0,0},{2,1},{4,2},{6,3},{1,4},{3,5},{5,6},{7,7},{8,8},{10,9},{12,1... | collective-permute-start | bytes 1572872 | tf_op jit(solution)/shard_map/ppermute | solution.py:133
  638.8 345.6 %collective-permute-start.4 = (bf16[256,1024]{1,0:T(8,128)(2,1)}, bf16[256,1024]{1,0:T(8,128)(2,1)}, u32[]{:S(2)}, u32[]{:S(2)}) collective-permute-start(bf16[256,1024]{1,0:T(8,128)(2,1)} %get-tuple-element.88), channel_id=1, source_target_pairs={{2,0},{0,1},{6,2},{4,3},{3,4},{1,5},{7,6},{5,7},{10,8},{8,9},{14,1... | collective-permute-start | bytes 1572872 | tf_op jit(solution)/shard_map/ppermute | solution.py:134
  958.2 13.4 %copy-start.16 = (bf16[256,1024]{1,0:T(8,128)(2,1)S(1)}, bf16[256,1024]{1,0:T(8,128)(2,1)}, u32[]{:S(2)}) copy-start(bf16[256,1024]{1,0:T(8,128)(2,1)} %copy-done.13) | copy-start | bytes 1572868
  958.2 13.4 %copy-start.20 = (bf16[256,1024]{1,0:T(8,128)(2,1)S(1)}, bf16[256,1024]{1,0:T(8,128)(2,1)}, u32[]{:S(2)}) copy-start(bf16[256,1024]{1,0:T(8,128)(2,1)} %copy-done.17) | copy-start | bytes 1572868
  958.2 13.4 %copy-start.37 = (f32[512]{0:T(512)S(1)}, f32[512]{0:T(512)}, u32[]{:S(2)}) copy-start(f32[512]{0:T(512)} %copy-done.35) | copy-start | bytes 6148
  958.2 13.4 %copy-start.40 = (f32[1,1024]{1,0:T(1,128)S(1)}, f32[1,1024]{1,0:T(1,128)}, u32[]{:S(2)}) copy-start(f32[1,1024]{1,0:T(1,128)} %copy-done.38) | copy-start | bytes 12292
  958.3 13.4 %copy-start.43 = (f32[512]{0:T(512)S(1)}, f32[512]{0:T(512)}, u32[]{:S(2)}) copy-start(f32[512]{0:T(512)} %copy-done.41) | copy-start | bytes 6148
  967.0 79.9 %all-to-all-start.1 = ((bf16[4,128,1312]{1,2,0:T(8,128)(2,1)}), bf16[4,128,1312]{1,2,0:T(8,128)(2,1)S(1)}, u32[]{:S(2)}, u32[]{:S(2)}) async-start(bf16[4,128,1312]{1,2,0:T(8,128)(2,1)} %fusion.59), calls=%async_computation.1 | async-start | bytes 2686976 | tf_op jit(solution)/shard_map/all_to_all | solution.py:568
  971.6 7.3 copy-start.7
  978.9 8.2 copy-start.29
  978.9 8.9 copy-start.46
  978.9 64.2 %copy-start.34 = (f32[2,1024]{1,0:T(2,128)S(1)}, f32[2,1024]{1,0:T(2,128)}, u32[]{:S(2)}) copy-start(f32[2,1024]{1,0:T(2,128)} %param.21) | copy-start | bytes 24580
  979.0 64.2 %copy-start.44 = (f32[2,1024]{1,0:T(2,128)S(1)}, f32[2,1024]{1,0:T(2,128)}, u32[]{:S(2)}) copy-start(f32[2,1024]{1,0:T(2,128)} %param.27) | copy-start | bytes 24580
  979.0 64.2 %copy-start.45 = (f32[2,1024]{1,0:T(2,128)S(1)}, f32[2,1024]{1,0:T(2,128)}, u32[]{:S(2)}) copy-start(f32[2,1024]{1,0:T(2,128)} %param.26) | copy-start | bytes 24580
  980.7 66.5 %copy-start.24 = (bf16[128,3,256]{2,0,1:T(8,128)(2,1)S(1)}, bf16[128,3,256]{2,0,1:T(8,128)(2,1)}, u32[]{:S(2)}) copy-start(bf16[128,3,256]{2,0,1:T(8,128)(2,1)} %param.17) | copy-start | bytes 589828
  980.8 67.2 %copy-start.28 = (bf16[128,256]{0,1:T(8,128)(2,1)S(1)}, bf16[128,256]{0,1:T(8,128)(2,1)}, u32[]{:S(2)}) copy-start(bf16[128,256]{0,1:T(8,128)(2,1)} %copy.41) | copy-start | bytes 196612
  980.8 63.1 %collective-permute-start.10 = (bf16[256,1024]{1,0:T(8,128)(2,1)S(1)}, bf16[256,1024]{1,0:T(8,128)(2,1)}, u32[]{:S(2)}, u32[]{:S(2)}) collective-permute-start(bf16[256,1024]{1,0:T(8,128)(2,1)S(1)} %get-tuple-element.87), channel_id=1, source_target_pairs={{0,0},{2,1},{4,2},{6,3},{1,4},{3,5},{5,6},{7,7},{8,8},{10,9},{12,1... | collective-permute-start | bytes 1572872 | tf_op jit(solution)/shard_map/ppermute | solution.py:133
  984.0 59.9 %collective-permute-start.9 = (bf16[256,1024]{1,0:T(8,128)(2,1)S(1)}, bf16[256,1024]{1,0:T(8,128)(2,1)}, u32[]{:S(2)}, u32[]{:S(2)}) collective-permute-start(bf16[256,1024]{1,0:T(8,128)(2,1)S(1)} %get-tuple-element.86), channel_id=1, source_target_pairs={{2,0},{0,1},{6,2},{4,3},{3,4},{1,5},{7,6},{5,7},{10,8},{8,9},{14,1... | collective-permute-start | bytes 1572872 | tf_op jit(solution)/shard_map/ppermute | solution.py:134
  987.1 61.7 %copy-start.22 = (bf16[128,2,656]{0,2,1:T(8,128)(2,1)S(1)}, bf16[128,2,656]{0,2,1:T(8,128)(2,1)}, u32[]{:S(2)}) copy-start(bf16[128,2,656]{0,2,1:T(8,128)(2,1)} %param.19) | copy-start | bytes 1007620
  1043.9 5.9 copy-start.25
  (6 other events, 6.4 us)
Sparse Core Ops, SparseCore 0:
  623.1 67.1 all-gather.1

commit v2 on v1

--- a/solution.py
+++ b/solution.py
@@ -391,12 +391,286 @@
     )(*grads)
 
 
+def owner_kernel(rows, *refs):
+    count = len(rows)
+    shards, gain, whole, gain_out = refs[:count], refs[count], refs[count + 1], refs[count + 2]
+    (gain_parts, own_sem, send_z, recv_z, send_x, recv_x, send_y, recv_y, send_d, recv_d, send_c, recv_c, send_g, recv_g) = refs[count + 3 :]
+    me, partner, across, down = neighbours()
+    plane = lax.axis_index("tensor")
+    diagonal = across + down - me
+    planes = [lax.rem(plane + offset, 4) for offset in (1, 2, 3)]
+    greet(plane, (partner, across, down), planes)
+    flip = lambda block: block + 1 - 2 * lax.rem(block, 2)
+
+    def remote(source, target, send, recv, device):
+        copy = pltpu.make_async_remote_copy(source, target, send, recv, device_id=device, device_id_type=MESH)
+        copy.start()
+        return copy
+
+    def wait(view, sem):
+        pltpu.make_async_copy(view, view, sem).wait()
+
+    def place(part, slot, block):
+        height = rows[part]
+        first = pl.multiple_of(slot * height, 16)
+        return whole.at[pl.ds(first, height), lanes(block)]
+
+    for part in range(count):
+        @pl.when(plane != part)
+        def _():
+            offset = lax.rem(plane + 3 - part, 4)
+            remote(shards[part], place(part, plane, me), send_z.at[part], recv_z.at[offset], (me, part))
+    gain_copies = [
+        remote(gain, gain_parts.at[index], send_g.at[index], recv_g.at[index], (me, other))
+        for index, other in enumerate(planes)
+    ]
+
+    def spread(part, source, slot):
+        view = place(part, slot, me)
+        remote(source, view, send_x.at[slot], recv_x.at[slot], (across, plane))
+        remote(source, view, send_y.at[slot], recv_y.at[slot], (down, plane))
+        remote(source, view, send_c.at[slot, 0], recv_c.at[slot, 0], (partner, plane))
+
+    for part in range(count):
+        @pl.when(plane == part)
+        def _():
+            pltpu.make_async_copy(shards[part], place(part, part, me), own_sem).start()
+            spread(part, shards[part], part)
+            for distance in (1, 3, 2):
+                slot = (part + distance) % 4
+                view = place(part, slot, me)
+                wait(view, recv_z.at[(slot + 3 - part) % 4])
+                spread(part, view, slot)
+            for slot in range(4):
+                view = place(part, slot, across)
+                wait(view, recv_x.at[slot])
+                remote(view, view, send_c.at[slot, 1], recv_c.at[slot, 1], (partner, plane))
+                if slot < 2:
+                    remote(view, view, send_d.at[slot], recv_d.at[slot], (down, plane))
+                view = place(part, slot, down)
+                wait(view, recv_y.at[slot])
+                remote(view, view, send_c.at[slot, 2], recv_c.at[slot, 2], (partner, plane))
+                if slot >= 2:
+                    remote(view, view, send_d.at[slot], recv_d.at[slot], (across, plane))
+
+    total = gain[...]
+    for index in range(3):
+        gain_copies[index].wait()
+        total = total + gain_parts[index]
+    gain_out[...] = total
+    for index, other in ((3, across), (4, down), (5, partner)):
+        copy = remote(gain_out, gain_parts.at[index], send_g.at[index], recv_g.at[index], (other, plane))
+        copy.wait()
+        gain_out[...] = gain_out[...] + gain_parts[index]
+
+    for part in range(count):
+        @pl.when(plane == part)
+        def _():
+            for slot in range(4):
+                view = place(part, slot, diagonal)
+                wait(view, recv_d.at[slot])
+                remote(view, view, send_c.at[slot, 3], recv_c.at[slot, 3], (partner, plane))
+            for slot in range(4):
+                for index, block in enumerate((me, across, down, diagonal)):
+                    wait(place(part, slot, flip(block)), recv_c.at[slot, index])
+            wait(place(part, part, me), own_sem)
+            for slot in range(4):
+                view = place(part, slot, me)
+                for sem in (send_x.at[slot], send_y.at[slot], send_d.at[slot]):
+                    wait(view, sem)
+                for index in range(4):
+                    wait(view, send_c.at[slot, index])
+        @pl.when(plane != part)
+        def _():
+            wait(shards[part], send_z.at[part])
+
+def own_matrix(shards, gain, collective_id):
+    rows = [s.shape[0] for s in shards]
+    count = len(shards)
+    sem = pltpu.SemaphoreType.DMA
+    anyspec = pl.BlockSpec(memory_space=pl.ANY)
+    vm = pl.BlockSpec(memory_space=pltpu.VMEM)
+    return pl.pallas_call(
+        functools.partial(owner_kernel, rows),
+        out_shape=[jax.ShapeDtypeStruct((4 * max(rows), 1024), shards[0].dtype), jax.ShapeDtypeStruct(gain.shape, gain.dtype)],
+        in_specs=[anyspec] * count + [vm],
+        out_specs=[anyspec, vm],
+        scratch_shapes=[pltpu.VMEM((6,) + gain.shape, gain.dtype), sem, sem((count,)), sem((3,))] + [sem((4,))] * 6 + [sem((4, 4))] * 2 + [sem((6,))] * 2,
+        compiler_params=pltpu.CompilerParams(collective_id=collective_id, has_side_effects=True),
+        name="own_matrix",
+    )(*shards, gain)
+
+def return_kernel(rows, *refs):
+    count = len(rows)
+    steps, outs = refs[0], refs[1 : 1 + count]
+    own_sem, send_z, recv_z = refs[1 + count :]
+    me = lax.axis_index("dp")
+    plane = lax.axis_index("tensor")
+    planes = [lax.rem(plane + offset, 4) for offset in (1, 2, 3)]
+    greet(plane, (), planes)
+    wait = lambda view, sem: pltpu.make_async_copy(view, view, sem).wait()
+    for part in range(count):
+        @pl.when(plane == part)
+        def _():
+            for slot in range(4):
+                view = steps.at[pl.ds(slot * rows[part], rows[part]), :]
+                if slot == part:
+                    pltpu.make_async_copy(view, outs[part], own_sem).start()
+                else:
+                    pltpu.make_async_remote_copy(view, outs[part], send_z.at[slot], recv_z.at[part], device_id=(me, slot), device_id_type=MESH).start()
+    for part in range(count):
+        @pl.when(plane == part)
+        def _():
+            wait(outs[part], own_sem)
+            for slot in range(4):
+                if slot != part:
+                    wait(outs[part], send_z.at[slot])
+        @pl.when(plane != part)
+        def _():
+            wait(outs[part], recv_z.at[part])
+
+def return_steps(steps, rows, collective_id):
+    sem = pltpu.SemaphoreType.DMA
+    anyspec = pl.BlockSpec(memory_space=pl.ANY)
+    return pl.pallas_call(
+        functools.partial(return_kernel, rows),
+        out_shape=[jax.ShapeDtypeStruct((r, 128), steps.dtype) for r in rows],
+        in_specs=[anyspec],
+        out_specs=[anyspec] * len(rows),
+        scratch_shapes=[sem, sem((4,)), sem((4,))],
+        compiler_params=pltpu.CompilerParams(collective_id=collective_id, has_side_effects=True),
+        name="return_steps",
+    )(steps)
+
+def product_of(left, right, dims):
+    return lax.dot_general(left, right, (dims, ((), ())), preferred_element_type=jnp.float32)
+
+def iterate_kernel(rows, whole, steps, iterate, poly, product, total, iterate_low, poly_low, other_low, total_low):
+    size, tile = iterate.shape[0], 256
+    plane = lax.axis_index("tensor")
+    me = lax.axis_index("dp")
+    f32, bf16 = jnp.float32, jnp.bfloat16
+    windows = [pl.ds(first, tile) for first in range(0, size, tile)]
+    zero = jnp.zeros((1, 1), f32)
+    corner = lax.broadcasted_iota(jnp.int32, (tile, tile), 0) == lax.broadcasted_iota(jnp.int32, (tile, tile), 1)
+
+    def store(window, result, shift, full, low_copy):
+        fixed = [
+            result[:, columns.start : columns.start + tile]
+            - (jnp.where(corner, shift, 0.0) if columns.start == window.start else 0.0)
+            for columns in windows
+        ]
+        result = jnp.concatenate(fixed, axis=1)
+        full[window] = result
+        low_copy[window] = result.astype(bf16)
+        return result
+
+    def fold(values):
+        return jnp.sum(values, axis=0, keepdims=True)
+
+    def finish(row):
+        return jnp.sum(row, axis=1, keepdims=True) / size
+
+    for part, height in enumerate(rows):
+        @pl.when(plane == part)
+        def _():
+            @pl.loop(0, size // tile)
+            def _(index):
+                window = pl.ds(pl.multiple_of(index * tile, tile), tile)
+                block = whole[0 : 4 * height, window]
+                iterate[window] = product_of(block, whole[0 : 4 * height, :], ((0,), (0,)))
+    trace = zero
+    for window in windows:
+        block = jnp.where(corner, iterate[window, window], 0.0)
+        trace = trace + jnp.sum(fold(block), axis=1, keepdims=True)
+    factor = 1.0 / (jnp.sqrt(trace) + NORM_FLOOR)
+    squared = factor * factor
+    mean = trace * squared / size
+    row = jnp.zeros((1, size), f32)
+    for window in windows:
+        rest = store(window, iterate[window] * squared, mean, iterate, iterate_low)
+        row = row + fold(rest * rest)
+    square = finish(row)
+    total_mean = None
+    for sweep in range(NS_ITERS):
+        first_sweep = sweep == 0
+        linear = QUINTIC_THREE + 2.0 * QUINTIC_FIVE * mean
+        shift = QUINTIC_FIVE * square
+        poly_mean = QUINTIC_ONE + QUINTIC_THREE * mean + QUINTIC_FIVE * (mean * mean) + shift
+        row = jnp.zeros((1, size), f32)
+        total_row = row
+        for window in windows:
+            mine = iterate[window]
+            rest = linear * mine + QUINTIC_FIVE * product_of(iterate_low[window], iterate_low[...], ((1,), (0,)))
+            rest = store(window, rest, shift, poly, poly_low)
+            row = row + fold(rest * mine)
+            if not first_sweep:
+                total_row = total_row + fold(rest * total[window])
+        cross, cross_total = finish(row), finish(total_row)
+        if first_sweep:
+            total_mean = poly_mean
+            source, source_low = poly, poly_low
+            for window in windows:
+                total[window] = poly[window]
+                total_low[window] = poly_low[window]
+        else:
+            results = []
+            for window in windows:
+                result = poly_mean * total[window] + total_mean * poly[window]
+                result = result + product_of(poly_low[window], total_low[...], ((1,), (0,)))
+                store(window, result, cross_total, total, other_low)
+            for window in windows:
+                total_low[window] = other_low[window]
+            total_mean = poly_mean * total_mean + cross_total
+        if sweep == NS_ITERS - 1:
+            break
+        row = jnp.zeros((1, size), f32)
+        for window in windows:
+            rest = poly[window]
+            result = poly_mean * iterate[window] + mean * rest
+            result = result + product_of(poly_low[window], iterate_low[...], ((1,), (0,)))
+            result = store(window, result, cross, product, other_low)
+            row = row + fold(result * rest)
+        product_mean = poly_mean * mean + cross
+        cross = finish(row)
+        row = jnp.zeros((1, size), f32)
+        for window in windows:
+            result = poly_mean * product[window] + product_mean * poly[window]
+            result = result + product_of(poly_low[window], other_low[...], ((1,), (0,)))
+            result = store(window, result, cross, iterate, iterate_low)
+            row = row + fold(result * result)
+        square = finish(row)
+        mean = poly_mean * product_mean + cross
+
+    mine = pl.ds(pl.multiple_of(me * 128, 128), 128)
+    columns = total_low[:, mine]
+    for part, height in enumerate(rows):
+        @pl.when(plane == part)
+        def _():
+            @pl.loop(0, 4)
+            def _(slot):
+                window = pl.ds(pl.multiple_of(slot * height, 16), height)
+                result = product_of(whole[window, :], columns, ((1,), (0,)))
+                result = result + total_mean * whole[window, mine].astype(f32)
+                steps[window, :] = (factor * result).astype(bf16)
+
+def iterate_owned(whole, rows):
+    size = whole.shape[1]
+    f32, bf16 = jnp.float32, jnp.bfloat16
+    return pl.pallas_call(
+        functools.partial(iterate_kernel, rows),
+        out_shape=jax.ShapeDtypeStruct((whole.shape[0], 128), bf16),
+        in_specs=[pl.BlockSpec(memory_space=pltpu.VMEM)],
+        out_specs=pl.BlockSpec(memory_space=pltpu.VMEM),
+        scratch_shapes=[pltpu.VMEM((size, size), f32)] * 4 + [pltpu.VMEM((size, size), bf16)] * 4,
+        compiler_params=pltpu.CompilerParams(vmem_limit_bytes=58 * 1024 * 1024),
+        name="iterate_owned",
+    )(whole)
+
+
 def gather_weights(weights):
     tensor_count, dp_count = lax.axis_size("tensor"), lax.axis_size("dp")
-    shards = [
-        weight.transpose(1, 2, 0) if weight.ndim == 3 else weight.T for weight in weights
-    ]
-    shards = [shard.reshape(-1, shard.shape[-1]) for shard in shards]
+    shards = [turn(weight) for weight in weights]
     if (tensor_count, dp_count, shards[0].shape[1]) == (4, 8, 128):
         return gather_blocks(shards, 1)
     wholes = [lax.all_gather(shard, ("tensor", "dp")) for shard in shards]
@@ -418,6 +692,39 @@
         part = lax.psum_scatter(blocks, ("tensor", "dp"), scatter_dimension=0, tiled=True)
         sums.append(part[0].astype(jnp.float32))
     return sums
+
+
+def turn(block):
+    return block.transpose(*range(1, block.ndim), 0).reshape(-1, block.shape[0])
+
+
+def turn_back(rows, like):
+    rows = rows.reshape(*like.shape[1:], like.shape[0])
+    return rows.transpose(rows.ndim - 1, *range(rows.ndim - 1))
+
+
+def orthogonal_steps(blocks, gain_part):
+    tensor_count, dp_count = lax.axis_size("tensor"), lax.axis_size("dp")
+    heights = [block.shape[0] for block in blocks]
+    if (tensor_count, dp_count, blocks[0].shape[1]) == (4, 8, 128):
+        whole, gain_grad = own_matrix(blocks, gain_part, 3)
+        steps = iterate_owned(whole, heights)
+        return (return_steps(steps, heights, 4), gain_grad)
+    row_count = blocks[0].shape[1]
+    first_row = lax.axis_index("dp") * row_count
+    gain_grad = lax.psum(gain_part, BOTH)
+    widest = max(heights)
+    stacked = jnp.stack(
+        [jnp.pad(block.T, ((0, 0), (0, widest - block.shape[0]))) for block in blocks]
+    )
+    owned = lax.all_to_all(stacked, "tensor", split_axis=0, concat_axis=0, tiled=True)
+    whole = lax.all_gather(owned, "dp", axis=1, tiled=True)
+    mean, rest = newton_schulz(einsum("tik,tjk->ij", whole, whole))
+    own_rows = lax.dynamic_slice_in_dim(rest, first_row, row_count, 0)
+    own_whole = lax.dynamic_slice_in_dim(whole, first_row, row_count, 1)
+    step_rows = low(einsum("ij,tjk->tik", low(own_rows), whole) + mean * own_whole)
+    returned = lax.all_to_all(step_rows, "tensor", split_axis=0, concat_axis=0, tiled=True)
+    return ([returned[index, :, :height].T for index, height in enumerate(heights)], gain_grad)
 
 
 def on_device(
@@ -544,35 +851,19 @@
     input_grad = from_sequences(low(grad_input), lists, odd, upper)[:, None].astype(jnp.float32)
 
     moments = (qkv_moment, attn_out_moment, ffn_in_moment, ffn_out_moment)
-    sums = [
-        part.reshape(*moment.shape[1:], row_count).transpose(
-            (2, 0, 1) if moment.ndim == 3 else (1, 0)
-        )
-        for part, moment in zip(sums, moments)
+    gain_part = jnp.stack([gain_one, gain_two])
+    turned = [turn(moment) for moment in moments]
+    turned = [MOMENTUM * moment + part for moment, part in zip(turned, sums)]
+    new_moments = [turn_back(part, moment) for part, moment in zip(turned, moments)]
+    steps, gain_grad = orthogonal_steps([low(part) for part in turned], gain_part)
+    new_weights = [
+        weight.astype(jnp.float32) * (1.0 - MUON_RATE * DECAY_RATE)
+        - MUON_RATE
+        * 0.2
+        * math.sqrt(step.shape[0] * tensor_count)
+        * turn_back(step, weight).astype(jnp.float32)
+        for weight, step in zip(weights, steps)
     ]
-    new_moments = [MOMENTUM * moment + part for moment, part in zip(moments, sums)]
-    gain_grad = lax.psum(jnp.stack([gain_one, gain_two]), BOTH)
-    flattened = [low(moment).reshape(row_count, -1) for moment in new_moments]
-    local_widths = [matrix.shape[1] for matrix in flattened]
-    widest = max(local_widths)
-    stacked = jnp.stack(
-        [jnp.pad(matrix, ((0, 0), (0, widest - matrix.shape[1]))) for matrix in flattened]
-    )
-    owned = lax.all_to_all(stacked, "tensor", split_axis=0, concat_axis=0, tiled=True)
-    whole = lax.all_gather(owned, "dp", axis=1, tiled=True)
-    gram = einsum("tik,tjk->ij", whole, whole)
-    mean, rest = newton_schulz(gram)
-    own_rows = lax.dynamic_slice_in_dim(rest, dp_index * row_count, row_count, 0)
-    own_whole = lax.dynamic_slice_in_dim(whole, dp_index * row_count, row_count, 1)
-    step_rows = low(einsum("ij,tjk->tik", low(own_rows), whole) + mean * own_whole)
-    returned = lax.all_to_all(step_rows, "tensor", split_axis=0, concat_axis=0, tiled=True)
-    new_weights = []
-    for index, (weight, width) in enumerate(zip(weights, local_widths)):
-        ortho_step = returned[index, :, :width].reshape(weight.shape).astype(jnp.float32)
-        new_weights.append(
-            weight.astype(jnp.float32) * (1.0 - MUON_RATE * DECAY_RATE)
-            - MUON_RATE * 0.2 * math.sqrt(width * tensor_count) * ortho_step
-        )
     gain_first_new = BETA_ONE * gain_first + (1.0 - BETA_ONE) * gain_grad
     gain_second_new = BETA_TWO * gain_second + (1.0 - BETA_TWO) * gain_grad * gain_grad
     first_hat = gain_first_new / (1.0 - BETA_ONE**STEP)

time: 1070 us -> 794 us (0.74)
  matrix products: 432 us -> 169 us
  Pallas kernels: 273 us -> 430 us
  blocking collectives: 89.7 us -> 0 us
  waiting for transfers between devices: 63.7 us -> 20.8 us
  between operations: 30.1 us -> 1.78 us
  starting transfers between devices: 27 us -> 14 us
    dot_general x37 -> x18, matrix products: 432 us -> 169 us  [einsum(): return jnp.einsum(spec, *operands, preferred_element_type=jnp.float32)]
    pallas_call x0 -> x3, Pallas kernels: none -> 157 us  [the longest x1 64 us: return_steps(): pl.pallas_call(functools.partial(return_kernel, rows), out_shape=[jax.Sha...]
    psum x1 -> x0, blocking collectives: 55.3 us -> none  [on_device(): gain_grad = lax.psum(jnp.stack([gain_one, gain_two]), BOTH)]
    all_gather x1 -> x0, waiting for transfers between devices: 46.7 us -> none  [on_device(): whole = lax.all_gather(owned, 'dp', axis=1, tiled=True)]
    all_to_all x1 -> x0, blocking collectives: 34.5 us -> none  [on_device(): lax.all_to_all(stacked, 'tensor', split_axis=0, concat_axis=0, tiled=True)]
    convert_element_type x8 -> x6, other arithmetic: 51.7 us -> 48.8 us  [low(): return values.astype(jnp.bfloat16)]
  transfers between devices with their start and end apart: 13 -> 11, of which waited for: 3 -> 2; matrix products, arithmetic and copies ran while one was open for 32% -> 10% of each run, Pallas kernels for 13% -> 55%
where the time goes in v2:
time: 794 us; the launch traced here: 785 us
  Pallas kernels  430 us (54%)
  matrix products  169 us (21%)
  other arithmetic  126 us (16%)
  local copies, waits for them, and re-layouts  23.6 us (3%)
  waiting for transfers between devices  20.8 us (3%)
  starting transfers between devices  14 us (2%)
    dot_general x18, matrix products, einsum(): return jnp.einsum(spec, *operands, preferred_element_type=jnp.float32)  169 us
    pallas_call x1, Pallas kernels, gather_blocks(): pl.pallas_call(functools.partial(gather_kernel, count), out_shape=[jax.Sh...  140 us
    pallas_call x1, Pallas kernels, scatter_grads(): pl.pallas_call(functools.partial(scatter_kernel, count), out_shape=[jax.S...  134 us
    pallas_call x1, Pallas kernels, return_steps(): pl.pallas_call(functools.partial(return_kernel, rows), out_shape=[jax.Sha...  64 us
    pallas_call x1, Pallas kernels, iterate_owned(): pl.pallas_call(functools.partial(iterate_kernel, rows), out_shape=jax.Sha...  56.5 us
    convert_element_type x6, other arithmetic, low(): return values.astype(jnp.bfloat16)  48.8 us
    pallas_call x1, Pallas kernels, own_matrix(): pl.pallas_call(functools.partial(owner_kernel, rows), out_shape=[jax.Shap...  36.1 us
    another operation x2, other arithmetic, on_device(): jnp.stack([grad_gate, grad_up], axis=1)  22.1 us
  transfers between devices with their start and end apart: 11, of which 2 were waited for; matrix products, arithmetic and copies ran while one was open for 10% of the time, Pallas kernels for 55%

profile of v2, /device:TPU:9, one launch (start us, length us, event | category | flops | bytes accessed | tf_op | source)
XLA Modules:
  0.0 785.0 jit_solution(11820651645720805729)
XLA Ops:
  0.7 1.3 select_bitcast_fusion.2
  2.7 4.1 collective-permute-start.1
  6.8 1.7 copy.40
  8.5 1.6 copy.41
  10.1 139.5 %gather_blocks.1 = (bf16[4,768,1024]{2,1,0:T(8,128)(2,1)}, bf16[4,256,1024]{2,1,0:T(8,128)(2,1)}, bf16[4,1312,1024]{2,1,0:T(8,128)(2,1)}, bf16[4,656,1024]{2,1,0:T(8,128)(2,1)}) custom-call(bf16[768,128]{1,0:T(8,128)(2,1)} %bitcast.358, bf16[256,128]{1,0:T(8,128)(2,1)} %bitcast.362, bf16[1312,128]{1,0:T(8,128)(2,1)} %bitcast.357, bf16[656,128]{1,0:T(8,128)(2,1)} %bitcast.361), custom_call_target="tpu_custom_call" | custom-call | tf_op jit(solution)/shard_map/gather_blocks/pallas_call | solution.py:273
  152.4 6.3 convolution_bitcast_fusion
  160.4 1.6 pad_maximum_fusion.3
  162.5 1.0 select_bitcast_fusion.1
  163.6 2.1 collective-permute-start.7
  165.7 1.0 multiply_bitcast_fusion.3
  167.7 1.7 copy.51
  169.4 2.0 broadcast_multiply_fusion
  173.5 16.1 %collective-permute-done.7 = bf16[256,1024]{1,0:T(8,128)(2,1)} collective-permute-done((bf16[256,1024]{1,0:T(8,128)(2,1)}, bf16[256,1024]{1,0:T(8,128)(2,1)}, u32[]{:S(2)}, u32[]{:S(2)}) %collective-permute-start.7) | collective-permute-done | bytes 524320 | tf_op jit(solution)/shard_map/ppermute | solution.py:122
  189.6 8.5 %fusion.80 = f32[4,656,512]{2,1,0:T(8,128)} fusion(bf16[4,656,1024]{2,1,0:T(8,128)(2,1)} %get-tuple-element.30, bf16[256,1024]{1,0:T(8,128)(2,1)} %collective-permute-done.7, bf16[256,1024]{1,0:T(8,128)(2,1)} %collective-permute-done.6, pred[]{:T(512)S(6)} %ge.3), kind=kOutput, calls=%fused_computation.136 | convolution fusion | flops 2756182016 | bytes 11796481 | tf_op jit(solution)/shard_map/kn,sn->ks/dot_general | solution.py:76
  198.1 2.0 pad_maximum_fusion.1
  200.2 13.2 %fusion.6 = (f32[16,512]{1,0:T(8,128)S(1)}, f32[16,512,1024]{2,1,0:T(8,128)}) fusion(pred[1024]{0:T(1024)(128)(4,1)S(1)} %add_compare_fusion, bf16[2,1024,16,64]{1,3,2,0:T(8,128)(2,1)S(1)} %pad_maximum_fusion.1, bf16[512,16,32]{0,2,1:T(8,128)(2,1)S(1)} %get-tuple-element.91, bf16[512,16,32]{0,2,1:T(8,128)(2,1)S(1)} %get-tuple-element.90), kind=kOutput, calls=%fused_computation.11 | convolution fusion | flops 1100996608 | bytes 36733952 | tf_op jit(solution)/shard_map/qhd,khd->hqk/dot_general | solution.py:76
  213.4 14.6 %fusion = f32[16,512]{1,0:T(8,128)S(1)} fusion(f32[16,512]{1,0:T(8,128)S(1)} %get-tuple-element.115, f32[16,512,1024]{2,1,0:T(8,128)} %get-tuple-element.116, pred[1024]{0:T(1024)(128)(4,1)S(1)} %add_compare_fusion), kind=kLoop, calls=%fused_computation.6 | loop fusion | flops 33546240 | bytes 33620992 | tf_op jit(solution)/shard_map/reduce_sum | solution.py:89
  228.1 13.9 %fusion.75 = bf16[16,64,512]{2,1,0:T(8,128)(2,1)S(1)} fusion(f32[16,512]{1,0:T(8,128)S(1)} %fusion, f32[16,512]{1,0:T(8,128)S(1)} %get-tuple-element.115, f32[16,512,1024]{2,1,0:T(8,128)} %get-tuple-element.116, pred[1024]{0:T(1024)(128)(4,1)S(1)} %add_compare_fusion, bf16[2,1024,16,64]{1,3,2,0:T(8,128)(2,1)S(1)} %pad_maximum_fusion.1), kind=kOutput, calls=%fused_computation.124 | convolution fusion | flops 1116209152 | bytes 36766720 | tf_op jit(solution)/shard_map/hqk,khd->qhd/dot_general | solution.py:76
  242.0 1.4 fusion.109
  243.8 8.9 %fusion.77 = f32[4,2,656,512]{3,2,1,0:T(8,128)S(1)} fusion(bf16[4,2,656,1024]{3,2,1,0:T(8,128)(2,1)} %bitcast.376, f32[512,1024]{1,0:T(8,128)S(1)} %get-tuple-element.118, f32[1024]{0:T(1024)S(1)} %bitcast.366, f32[512]{0:T(512)S(1)} %add_rsqrt_fusion, f32[512]{0:T(512)S(1)} %broadcast_multiply_fusion.5), kind=kOutput, calls=%fused_computation.133 | convolution fusion | flops 5505024000 | bytes 23601152 | tf_op jit(solution)/shard_map/kn,sn->ks/dot_general | solution.py:76
  252.8 14.4 %fusion.20 = (bf16[4,1,656,512]{3,2,0,1:T(8,128)(2,1)}, f32[4,656,512]{2,1,0:T(8,128)S(1)}) fusion(f32[4,656,512]{2,1,0:T(8,128)S(1)} %bitcast.336, f32[4,2,656,512]{3,2,1,0:T(8,128)S(1)} %fusion.77), kind=kLoop, calls=%fused_computation.46 | loop fusion | flops 98074624 | bytes 24182784 | tf_op jit(solution)/shard_map/stack | solution.py:811
  267.2 2.3 copy-done.1
  269.5 7.6 fusion.69
  277.1 7.7 multiply_bitcast_fusion
  284.8 3.1 maximum_convert_fusion
  288.4 11.7 %multiply_reduce_fusion.1 = (f32[1024]{0:T(1024)}, f32[512]{0:T(512)S(1)}, f32[512]{0:T(512)S(1)}, f32[512,1024]{1,0:T(8,128)S(1)}) fusion(f32[512,1024]{1,0:T(8,128)S(1)} %get-tuple-element.118, f32[512]{0:T(512)S(1)} %add_rsqrt_fusion, f32[512]{0:T(512)S(1)} %broadcast_multiply_fusion.5, f32[1024]{0:T(1024)S(1)} %bitcast.367, ...), kind=kOutput, calls=%fused_computation.110 | convolution fusion | flops 5507119104 | bytes 20332544 | tf_op jit(solution)/shard_map/ks,kn->sn/dot_general | solution.py:76
  300.1 2.6 multiply_add_fusion
  302.7 1.3 copy-done.6
  304.0 2.3 convolution_convert_fusion.4
  306.3 1.5 copy.45
  307.8 25.2 %multiply_reduce_fusion = (f32[16,512]{1,0:T(8,128)S(1)}, f32[16,512,1024]{2,1,0:T(8,128)}) fusion(f32[16,512]{1,0:T(8,128)S(1)} %log_add_fusion, f32[16,512,1024]{2,1,0:T(8,128)} %get-tuple-element.116, pred[1024]{0:T(1024)(128)(4,1)S(1)} %add_compare_fusion, bf16[512,16,64]{0,2,1:T(8,128)(2,1)S(1)} %bitcast.342, bf16[2,1024,16,64]{1,3,2,0:T(8,128)(2,1)} %copy-done.2), kind=kOutput, calls=%fused_computation.1 | convolution fusion | flops 1115676672 | bytes 70321152 | tf_op jit(solution)/shard_map/qhd,khd->hqk/dot_general | solution.py:76
  333.0 15.9 %fusion.58 = f32[1,1024,16,64]{1,3,2,0:T(8,128)} fusion(bf16[512,16,64]{0,2,1:T(8,128)(2,1)S(1)} %bitcast.343, f32[16,512]{1,0:T(8,128)S(1)} %log_add_fusion, f32[16,512,1024]{2,1,0:T(8,128)} %get-tuple-element.116, pred[1024]{0:T(1024)(128)(4,1)S(1)} %add_compare_fusion), kind=kOutput, calls=%fused_computation.93 | convolution fusion | flops 1107296256 | bytes 38831104 | tf_op jit(solution)/shard_map/hqk,qhd->khd/dot_general | solution.py:76
  348.8 28.0 %multiply_convert_fusion = bf16[16,512,1024]{2,1,0:T(8,128)(2,1)} fusion(f32[16,512,1024]{2,1,0:T(8,128)} %get-tuple-element.121, f32[16,512]{1,0:T(8,128)S(1)} %get-tuple-element.120, f32[16,512]{1,0:T(8,128)S(1)} %log_add_fusion, f32[16,512,1024]{2,1,0:T(8,128)} %get-tuple-element.116, pred[1024]{0:T(1024)(128)(4,1)S(1)} %add_compare_fusion), kind=kLoop, calls=%fused_computation | loop fusion | flops 50331648 | bytes 83952640 | tf_op jit(solution)/shard_map/convert_element_type | solution.py:80
  376.8 10.8 %multiply_bitcast_fusion.1 = f32[1,1024,16,64]{1,3,2,0:T(8,128)} fusion(bf16[16,512,1024]{2,1,0:T(8,128)(2,1)} %multiply_convert_fusion, bf16[512,16,32]{0,2,1:T(8,128)(2,1)S(1)} %copy-done.12, bf16[512,16,32]{0,2,1:T(8,128)(2,1)S(1)} %copy-done.10), kind=kOutput, calls=%fused_computation.80 | convolution fusion | flops 1076887552 | bytes 22020096 | tf_op jit(solution)/shard_map/hqk,qhd->khd/dot_general | solution.py:76
  387.6 12.9 %multiply_bitcast_fusion.2 = f32[512,16,64]{0,2,1:T(8,128)} fusion(bf16[16,512,1024]{2,1,0:T(8,128)(2,1)} %multiply_convert_fusion, bf16[2,1024,16,64]{1,3,2,0:T(8,128)(2,1)} %copy-done.2), kind=kOutput, calls=%fused_computation.111 | convolution fusion | flops 1074266112 | bytes 20971520 | tf_op jit(solution)/shard_map/hqk,khd->qhd/dot_general | solution.py:76
  400.6 4.1 fusion.46
  404.7 2.6 convolution_convert_fusion.3
  407.4 1.6 copy-done.4
  408.9 1.7 fusion.49
  410.6 1.6 slice-done
  412.2 12.1 %fusion.11 = bf16[2624,512]{1,0:T(8,128)(2,1)} fusion(f32[4,1,656,512]{3,2,1,0:T(8,128)S(1)} %slice-done, f32[4,1,656,512]{3,2,0,1:T(8,128)S(1)} %get-tuple-element.83, f32[4,1,656,512]{3,2,0,1:T(8,128)S(1)} %get-tuple-element.82), kind=kLoop, calls=%fused_computation.24 | loop fusion | flops 84639744 | bytes 18808832 | tf_op jit(solution)/shard_map/convert_element_type | solution.py:80
  424.5 2.2 collective-permute-start.5
  426.7 11.9 %convolution_convert_fusion = bf16[5248,1024]{1,0:T(8,128)(2,1)} fusion(bf16[5248,512]{1,0:T(8,128)(2,1)} %bitcast.347, f32[512,1024]{1,0:T(8,128)S(1)} %get-tuple-element.118, f32[1024]{0:T(1024)S(1)} %bitcast.369, f32[512]{0:T(512)S(1)} %add_rsqrt_fusion, f32[512]{0:T(512)S(1)} %broadcast_multiply_fusion.5), kind=kOutput, calls=%fused_computation.12 | convolution fusion | flops 5510397952 | bytes 18227200 | tf_op jit(solution)/shard_map/ks,sn->kn/dot_general | solution.py:76
  438.6 6.3 convolution_convert_fusion.2
  445.0 4.6 collective-permute-done.4
  449.6 1.1 maximum_select_fusion.1
  450.7 2.3 fusion.48
  453.4 1.2 copy-done.5
  458.1 4.0 fusion.67
  462.1 1.7 fusion.66
  463.9 1.9 collective-permute-start.10
  465.8 2.3 collective-permute-start.9
  468.2 5.9 convolution_convert_fusion.1
  474.0 133.5 %scatter_grads.1 = (f32[656,128]{1,0:T(8,128)}, f32[1312,128]{1,0:T(8,128)}, f32[256,128]{1,0:T(8,128)}, f32[768,128]{1,0:T(8,128)}) custom-call(bf16[4,656,1024]{2,1,0:T(8,128)(2,1)} %bitcast.345, bf16[4,1312,1024]{2,1,0:T(8,128)(2,1)} %bitcast.337, bf16[4,256,1024]{2,1,0:T(8,128)(2,1)} %bitcast.354, bf16[4,768,1024]{2,1,0:T(8,128)(2,1)} %bitcast.344), custom_call_target="tpu_custom_call" | custom-call | tf_op jit(solution)/shard_map/scatter_grads/pallas_call | solution.py:383
  607.6 1.7 fusion.105
  609.3 1.6 fusion.88
  610.9 2.1 fusion.104
  613.0 1.8 fusion.86
  615.4 36.1 %own_matrix.1 = (bf16[5248,1024]{1,0:T(8,128)(2,1)}, f32[2,1024]{1,0:T(2,128)}) custom-call(bf16[768,128]{1,0:T(8,128)(2,1)} %get-tuple-element.78.refs_0_, bf16[256,128]{1,0:T(8,128)(2,1)} %get-tuple-element.105.refs_1_, bf16[1312,128]{1,0:T(8,128)(2,1)} %get-tuple-element.76.refs_2_, bf16[656,128]{1,0:T(8,128)(2,1)} %get-tuple-element.103.refs_3_, ...), custom_call_target="tpu_custom_call" | custom-call | tf_op jit(solution)/shard_map/own_matrix/pallas_call | solution.py:493
  651.6 56.5 %iterate_owned.1.refs_0_ = bf16[5248,128]{1,0:T(8,128)(2,1)} custom-call(bf16[5248,1024]{1,0:T(8,128)(2,1)} %get-tuple-element.35.whole), custom_call_target="tpu_custom_call" | custom-call | tf_op jit(solution)/shard_map/iterate_owned/pallas_call | solution.py:660
  708.1 64.0 %return_steps.1 = (bf16[768,128]{1,0:T(8,128)(2,1)}, bf16[256,128]{1,0:T(8,128)(2,1)}, bf16[1312,128]{1,0:T(8,128)(2,1)}, bf16[656,128]{1,0:T(8,128)(2,1)}) custom-call(bf16[5248,128]{1,0:T(8,128)(2,1)} %iterate_owned.1.refs_0_), custom_call_target="tpu_custom_call" | custom-call | tf_op jit(solution)/shard_map/return_steps/pallas_call | solution.py:535
  774.0 1.0 convert_multiply_fusion
  775.0 1.7 bitcast_subtract_fusion.1
  781.7 3.0 fusion.76
  (165 shorter events, 20.9 us)
Async XLA Ops:
  1.9 149.5 %collective-permute-start = (bf16[256,1024]{1,0:T(8,128)(2,1)S(1)}, bf16[256,1024]{1,0:T(8,128)(2,1)S(1)}, u32[]{:S(2)}, u32[]{:S(2)}) collective-permute-start(bf16[256,1024]{1,0:T(8,128)(2,1)S(1)} %get-tuple-element.101), channel_id=1, source_target_pairs={{0,2},{1,0},{2,6},{3,4},{4,3},{5,1},{6,7},{7,5},{8,10},{9,8},{10,1... | collective-permute-start | bytes 1572872 | tf_op jit(solution)/shard_map/ppermute | solution.py:123
  2.7 148.8 %collective-permute-start.1 = (bf16[256,1024]{1,0:T(8,128)(2,1)S(1)}, bf16[256,1024]{1,0:T(8,128)(2,1)S(1)}, u32[]{:S(2)}, u32[]{:S(2)}) collective-permute-start(bf16[256,1024]{1,0:T(8,128)(2,1)S(1)} %get-tuple-element.100), channel_id=1, source_target_pairs={{0,0},{1,2},{2,4},{3,6},{4,1},{5,3},{6,5},{7,7},{8,8},{9,10},{10,1... | collective-permute-start | bytes 1572872 | tf_op jit(solution)/shard_map/ppermute | solution.py:122
  150.5 8.2 %copy-start.36 = (f32[1,1024]{1,0:T(1,128)}, f32[1,1024]{1,0:T(1,128)S(1)}, u32[]{:S(2)}) copy-start(f32[1,1024]{1,0:T(1,128)S(1)} %get-tuple-element.111) | copy-start | bytes 12292
  151.4 8.2 %copy-start.27 = (f32[512,32]{0,1:T(8,128)}, f32[512,32]{0,1:T(8,128)S(1)}, u32[]{:S(2)}) copy-start(f32[512,32]{0,1:T(8,128)S(1)} %get-tuple-element.114) | copy-start | bytes 196612
  151.4 1.0 copy-start.16
  151.8 6.9 copy-start.34
  152.3 6.4 copy-start.38
  159.6 2.4 copy-start.44
  159.6 2.9 copy-start.24
  160.4 39.8 %copy-start.9 = (bf16[512,16,32]{0,2,1:T(8,128)(2,1)}, bf16[512,16,32]{0,2,1:T(8,128)(2,1)S(1)}, u32[]{:S(2)}) copy-start(bf16[512,16,32]{0,2,1:T(8,128)(2,1)S(1)} %get-tuple-element.90) | copy-start | bytes 1572868
  160.4 39.8 %copy-start.11 = (bf16[512,16,32]{0,2,1:T(8,128)(2,1)}, bf16[512,16,32]{0,2,1:T(8,128)(2,1)S(1)}, u32[]{:S(2)}) copy-start(bf16[512,16,32]{0,2,1:T(8,128)(2,1)S(1)} %get-tuple-element.91) | copy-start | bytes 1572868
  162.0 36.1 %collective-permute-start.2 = (bf16[2,512,16,64]{1,3,2,0:T(8,128)(2,1)}, bf16[2,512,16,64]{1,3,2,0:T(8,128)(2,1)}, u32[]{:S(2)}, u32[]{:S(2)}) collective-permute-start(bf16[2,512,16,64]{1,3,2,0:T(8,128)(2,1)} %pad_maximum_fusion.3), channel_id=1, source_target_pairs={{0,4},{4,0},{8,12},{12,8},{16,20},{20,16},{24,28},{28,24},{1,5},{5... | collective-permute-start | bytes 6291464 | tf_op jit(solution)/shard_map/ppermute | solution.py:140
  162.0 9.3 %collective-permute-start.3 = (s32[2,1]{0,1:T(1,128)S(1)}, s32[2,1]{0,1:T(1,128)}, u32[]{:S(2)}, u32[]{:S(2)}) collective-permute-start(s32[2,1]{0,1:T(1,128)S(1)} %copy-done.44), channel_id=1, source_target_pairs={{0,4},{4,0},{8,12},{12,8},{16,20},{20,16},{24,28},{28,24},{1,5},{5... | collective-permute-start | bytes 32 | tf_op jit(solution)/shard_map/ppermute | solution.py:140
  163.6 26.0 %collective-permute-start.7 = (bf16[256,1024]{1,0:T(8,128)(2,1)}, bf16[256,1024]{1,0:T(8,128)(2,1)}, u32[]{:S(2)}, u32[]{:S(2)}) collective-permute-start(bf16[256,1024]{1,0:T(8,128)(2,1)} %get-tuple-element.99), channel_id=1, source_target_pairs={{0,0},{1,2},{2,4},{3,6},{4,1},{5,3},{6,5},{7,7},{8,8},{9,10},{10,1... | collective-permute-start | bytes 1572872 | tf_op jit(solution)/shard_map/ppermute | solution.py:122
  165.6 24.0 %collective-permute-start.6 = (bf16[256,1024]{1,0:T(8,128)(2,1)}, bf16[256,1024]{1,0:T(8,128)(2,1)}, u32[]{:S(2)}, u32[]{:S(2)}) collective-permute-start(bf16[256,1024]{1,0:T(8,128)(2,1)} %get-tuple-element.98), channel_id=1, source_target_pairs={{0,2},{1,0},{2,6},{3,4},{4,3},{5,1},{6,7},{7,5},{8,10},{9,8},{10,1... | collective-permute-start | bytes 1572872 | tf_op jit(solution)/shard_map/ppermute | solution.py:123
  200.2 27.9 %copy-start.2 = (bf16[2,1024,16,64]{1,3,2,0:T(8,128)(2,1)}, bf16[2,1024,16,64]{1,3,2,0:T(8,128)(2,1)S(1)}, u32[]{:S(2)}) copy-start(bf16[2,1024,16,64]{1,3,2,0:T(8,128)(2,1)S(1)} %pad_maximum_fusion.1) | copy-start | bytes 12582916
  228.0 13.9 %copy-start.14 = (bf16[256,1024]{1,0:T(8,128)(2,1)S(1)}, bf16[256,1024]{1,0:T(8,128)(2,1)}, u32[]{:S(2)}) copy-start(bf16[256,1024]{1,0:T(8,128)(2,1)} %copy-done.13) | copy-start | bytes 1572868
  228.0 13.9 %copy-start.17 = (bf16[256,1024]{1,0:T(8,128)(2,1)S(1)}, bf16[256,1024]{1,0:T(8,128)(2,1)}, u32[]{:S(2)}) copy-start(bf16[256,1024]{1,0:T(8,128)(2,1)} %copy-done.16) | copy-start | bytes 1572868
  228.0 13.9 %copy-start.45 = (bf16[4,256,1024]{2,1,0:T(8,128)(2,1)S(1)}, bf16[4,256,1024]{2,1,0:T(8,128)(2,1)}, u32[]{:S(2)}) copy-start(bf16[4,256,1024]{2,1,0:T(8,128)(2,1)} %get-tuple-element.28) | copy-start | bytes 6291460
  241.9 1.8 copy-start.47
  242.0 10.8 %slice-start.1 = ((s8[5373952]{0:T(1024)(128)(4,1)}), s8[4194304]{0:T(1024)(128)(4,1)S(1)}, s32[]{:S(2)}) async-start(s8[5373952]{0:T(1024)(128)(4,1)} %bitcast.335), calls=%async_computation.1 | async-start | bytes 8388608
  243.8 9.0 %slice-start.2 = ((s8[5373952]{0:T(1024)(128)(4,1)}), s8[1179648]{0:T(1024)(128)(4,1)S(1)}, s32[]{:S(2)}) async-start(s8[5373952]{0:T(1024)(128)(4,1)} %bitcast.335), calls=%async_computation.2 | async-start | bytes 2359296
  252.7 24.3 %copy-start = (f32[4,2,656,512]{3,2,1,0:T(8,128)}, f32[4,2,656,512]{3,2,1,0:T(8,128)S(1)}, u32[]{:S(2)}) copy-start(f32[4,2,656,512]{3,2,1,0:T(8,128)S(1)} %fusion.77) | copy-start | bytes 32243716
  267.2 2.3 copy-start.1
  288.4 11.7 %copy-start.8 = (bf16[4,2,656,512]{3,2,1,0:T(8,128)(2,1)}, bf16[4,2,656,512]{3,2,1,0:T(8,128)(2,1)S(1)}, u32[]{:S(2)}) copy-start(bf16[4,2,656,512]{3,2,1,0:T(8,128)(2,1)S(1)} %copy.44) | copy-start | bytes 16121860
  300.1 3.9 copy-start.46
  302.7 1.3 copy-start.6
  348.8 28.0 %copy-start.10 = (bf16[512,16,32]{0,2,1:T(8,128)(2,1)S(1)}, bf16[512,16,32]{0,2,1:T(8,128)(2,1)}, u32[]{:S(2)}) copy-start(bf16[512,16,32]{0,2,1:T(8,128)(2,1)} %copy-done.9) | copy-start | bytes 1572868
  348.8 28.0 %copy-start.12 = (bf16[512,16,32]{0,2,1:T(8,128)(2,1)S(1)}, bf16[512,16,32]{0,2,1:T(8,128)(2,1)}, u32[]{:S(2)}) copy-start(bf16[512,16,32]{0,2,1:T(8,128)(2,1)} %copy-done.11) | copy-start | bytes 1572868
  400.6 4.1 copy-start.7
  400.6 4.1 copy-start.48
  404.7 2.7 copy-start.3
  404.7 4.2 copy-start.4
  408.9 3.3 slice-start
  410.6 40.1 %collective-permute-start.8 = (bf16[2,512,16,64]{1,3,2,0:T(8,128)(2,1)}, bf16[2,512,16,64]{1,3,2,0:T(8,128)(2,1)}, u32[]{:S(2)}, u32[]{:S(2)}) collective-permute-start(bf16[2,512,16,64]{1,3,2,0:T(8,128)(2,1)} %fusion.49), channel_id=1, source_target_pairs={{0,4},{4,0},{8,12},{12,8},{16,20},{20,16},{24,28},{28,24},{1,5},{5... | collective-permute-start | bytes 6291464 | tf_op jit(solution)/shard_map/ppermute | solution.py:140
  412.2 12.2 %copy-start.19 = (bf16[512,1024]{1,0:T(8,128)(2,1)S(1)}, bf16[512,1024]{1,0:T(8,128)(2,1)}, u32[]{:S(2)}) copy-start(bf16[512,1024]{1,0:T(8,128)(2,1)} %fusion.69) | copy-start | bytes 3145732
  424.5 20.5 %collective-permute-start.5 = (bf16[256,1024]{1,0:T(8,128)(2,1)S(1)}, bf16[256,1024]{1,0:T(8,128)(2,1)S(1)}, u32[]{:S(2)}, u32[]{:S(2)}) collective-permute-start(bf16[256,1024]{1,0:T(8,128)(2,1)S(1)} %get-tuple-element.97), channel_id=1, source_target_pairs={{0,0},{2,1},{4,2},{6,3},{1,4},{3,5},{5,6},{7,7},{8,8},{10,9},{12,1... | collective-permute-start | bytes 1572872 | tf_op jit(solution)/shard_map/ppermute | solution.py:133
  426.7 12.0 %copy-start.20 = (bf16[2624,512]{1,0:T(8,128)(2,1)S(1)}, bf16[2624,512]{1,0:T(8,128)(2,1)}, u32[]{:S(2)}) copy-start(bf16[2624,512]{1,0:T(8,128)(2,1)} %fusion.11) | copy-start | bytes 8060932
  426.7 22.9 %collective-permute-start.4 = (bf16[256,1024]{1,0:T(8,128)(2,1)S(1)}, bf16[256,1024]{1,0:T(8,128)(2,1)S(1)}, u32[]{:S(2)}, u32[]{:S(2)}) collective-permute-start(bf16[256,1024]{1,0:T(8,128)(2,1)S(1)} %get-tuple-element.96), channel_id=1, source_target_pairs={{2,0},{0,1},{6,2},{4,3},{3,4},{1,5},{7,6},{5,7},{10,8},{8,9},{14,1... | collective-permute-start | bytes 1572872 | tf_op jit(solution)/shard_map/ppermute | solution.py:134
  453.1 1.6 copy-start.5
  453.1 1.6 copy-start.28
  453.1 1.6 copy-start.32
  454.7 2.2 slice-start.3
  455.4 1.8 copy-start.15
  455.4 1.9 copy-start.18
  455.4 1.9 copy-start.35
  455.4 1.9 copy-start.37
  455.4 1.9 copy-start.39
  455.5 2.6 slice-start.4
  463.9 317.8 %collective-permute-start.10 = (bf16[256,1024]{1,0:T(8,128)(2,1)S(1)}, bf16[256,1024]{1,0:T(8,128)(2,1)}, u32[]{:S(2)}, u32[]{:S(2)}) collective-permute-start(bf16[256,1024]{1,0:T(8,128)(2,1)S(1)} %get-tuple-element.95), channel_id=1, source_target_pairs={{0,0},{2,1},{4,2},{6,3},{1,4},{3,5},{5,6},{7,7},{8,8},{10,9},{12,1... | collective-permute-start | bytes 1572872 | tf_op jit(solution)/shard_map/ppermute | solution.py:133
  465.8 315.9 %collective-permute-start.9 = (bf16[256,1024]{1,0:T(8,128)(2,1)S(1)}, bf16[256,1024]{1,0:T(8,128)(2,1)}, u32[]{:S(2)}, u32[]{:S(2)}) collective-permute-start(bf16[256,1024]{1,0:T(8,128)(2,1)S(1)} %get-tuple-element.94), channel_id=1, source_target_pairs={{2,0},{0,1},{6,2},{4,3},{3,4},{1,5},{7,6},{5,7},{10,8},{8,9},{14,1... | collective-permute-start | bytes 1572872 | tf_op jit(solution)/shard_map/ppermute | solution.py:134
  474.0 133.5 %copy-start.22 = (f32[3,256,128]{2,1,0:T(8,128)S(1)}, f32[3,256,128]{2,1,0:T(8,128)}, u32[]{:S(2)}) copy-start(f32[3,256,128]{2,1,0:T(8,128)} %copy.49) | copy-start | bytes 1179652
  474.0 135.3 %copy-start.30 = (f32[128,256]{0,1:T(8,128)S(1)}, f32[128,256]{0,1:T(8,128)}, u32[]{:S(2)}) copy-start(f32[128,256]{0,1:T(8,128)} %copy.51) | copy-start | bytes 393220
  474.0 136.8 %copy-start.21 = (f32[128,2,656]{0,2,1:T(8,128)S(1)}, f32[128,2,656]{0,2,1:T(8,128)}, u32[]{:S(2)}) copy-start(f32[128,2,656]{0,2,1:T(8,128)} %broadcast_multiply_fusion) | copy-start | bytes 2015236
  474.0 139.0 %copy-start.31 = (f32[128,656]{0,1:T(8,128)S(1)}, f32[128,656]{0,1:T(8,128)}, u32[]{:S(2)}) copy-start(f32[128,656]{0,1:T(8,128)} %param.25) | copy-start | bytes 1007620
  607.6 7.2 copy-start.43
  651.5 121.6 %copy-start.29 = (bf16[128,256]{0,1:T(8,128)(2,1)S(1)}, bf16[128,256]{0,1:T(8,128)(2,1)}, u32[]{:S(2)}) copy-start(bf16[128,256]{0,1:T(8,128)(2,1)} %copy.41) | copy-start | bytes 196612
  651.5 123.5 %copy-start.26 = (bf16[128,656]{0,1:T(8,128)(2,1)S(1)}, bf16[128,656]{0,1:T(8,128)(2,1)}, u32[]{:S(2)}) copy-start(bf16[128,656]{0,1:T(8,128)(2,1)} %param.20) | copy-start | bytes 503812
  651.5 125.2 %copy-start.33 = (f32[2,1024]{1,0:T(2,128)S(1)}, f32[2,1024]{1,0:T(2,128)}, u32[]{:S(2)}) copy-start(f32[2,1024]{1,0:T(2,128)} %param.21) | copy-start | bytes 24580
  651.5 125.2 %copy-start.40 = (f32[2,1024]{1,0:T(2,128)S(1)}, f32[2,1024]{1,0:T(2,128)}, u32[]{:S(2)}) copy-start(f32[2,1024]{1,0:T(2,128)} %param.27) | copy-start | bytes 24580
  651.6 125.2 %copy-start.41 = (f32[2,1024]{1,0:T(2,128)S(1)}, f32[2,1024]{1,0:T(2,128)}, u32[]{:S(2)}) copy-start(f32[2,1024]{1,0:T(2,128)} %param.26) | copy-start | bytes 24580
  651.6 125.2 %copy-start.42 = (f32[2,1024]{1,0:T(2,128)S(1)}, f32[2,1024]{1,0:T(2,128)}, u32[]{:S(2)}) copy-start(f32[2,1024]{1,0:T(2,128)} %get-tuple-element.40) | copy-start | bytes 24580
  708.1 71.9 %copy-start.25 = (bf16[128,3,256]{2,0,1:T(8,128)(2,1)S(1)}, bf16[128,3,256]{2,0,1:T(8,128)(2,1)}, u32[]{:S(2)}) copy-start(bf16[128,3,256]{2,0,1:T(8,128)(2,1)} %param.17) | copy-start | bytes 589828
  708.1 72.7 %copy-start.23 = (bf16[128,2,656]{0,2,1:T(8,128)(2,1)S(1)}, bf16[128,2,656]{0,2,1:T(8,128)(2,1)}, u32[]{:S(2)}) copy-start(bf16[128,2,656]{0,2,1:T(8,128)(2,1)} %param.19) | copy-start | bytes 1007620
  (1 other events, 0.9 us)

commit v3 on v2

--- a/solution.py
+++ b/solution.py
@@ -11,6 +11,7 @@
 HEAD_DIM = 64
 NS_ITERS = 5
 STEP = 10
+SCORE_SCALE = 1.0 / math.sqrt(HEAD_DIM)
 
 
 ROPE_BASE = 160000.0
@@ -31,27 +32,15 @@
 MESH = pl.DeviceIdType.MESH
 
 
-def rotary(first, length):
+def rotary(positions):
     half_size = HEAD_DIM // 2
     exponents = jnp.arange(half_size).astype(jnp.float32) / half_size
     frequency = jnp.power(ROPE_BASE, -exponents)
-    positions = (first + jnp.arange(length)).astype(jnp.float32)
-    angles = positions[:, None] * frequency[None, :]
-    return (jnp.cos(angles), jnp.sin(angles))
-
-
-def rotate(vectors, cosine_table, sine_table):
-    half_size = vectors.shape[-1] // 2
-    first_half = vectors[..., :half_size]
-    second_half = vectors[..., half_size:]
-    cos_part = cosine_table[:, None, :]
-    sin_part = sine_table[:, None, :]
-    return jnp.concatenate(
-        [
-            first_half * cos_part - second_half * sin_part,
-            second_half * cos_part + first_half * sin_part,
-        ],
-        axis=-1,
+    angles = positions.astype(jnp.float32)[:, None] * frequency[None, :]
+    cosine, sine = jnp.cos(angles), jnp.sin(angles)
+    return (
+        jnp.concatenate([cosine] * 4, axis=1),
+        jnp.concatenate([-sine, sine, -sine, sine], axis=1),
     )
 
 
@@ -78,31 +67,6 @@
 
 def low(values):
     return values.astype(jnp.bfloat16)
-
-
-def attention_forward(queries, key_rows, values, key_valid):
-    score_scale = 1.0 / math.sqrt(queries.shape[-1])
-    scores = einsum("qhd,khd->hqk", queries, key_rows) * score_scale
-    scores = jnp.where(key_valid, scores, MASK_VALUE)
-    highest = jnp.max(scores, axis=-1, keepdims=True)
-    exponent = jnp.exp(scores - highest)
-    row_total = jnp.sum(exponent, axis=-1, keepdims=True)
-    context = einsum("hqk,khd->qhd", low(exponent / row_total), values)
-    return (context, highest[..., 0] + jnp.log(row_total[..., 0]))
-
-
-def attention_backward(queries, key_rows, values, log_total, grad_context, key_valid):
-    score_scale = 1.0 / math.sqrt(queries.shape[-1])
-    scores = einsum("qhd,khd->hqk", queries, key_rows) * score_scale
-    scores = jnp.where(key_valid, scores, MASK_VALUE)
-    soft_weights = jnp.exp(scores - log_total[..., None])
-    grad_probs = einsum("qhd,khd->hqk", grad_context, values)
-    inner_sum = jnp.sum(soft_weights * grad_probs, axis=-1, keepdims=True)
-    grad_scores = low(soft_weights * (grad_probs - inner_sum))
-    grad_query = einsum("hqk,khd->qhd", grad_scores, key_rows) * score_scale
-    grad_keys = einsum("hqk,qhd->khd", grad_scores, queries) * score_scale
-    grad_values = einsum("hqk,qhd->khd", low(soft_weights), grad_context)
-    return (grad_query, grad_keys, grad_values)
 
 
 def exchange_lists(chip_count, tensor_count):
@@ -185,11 +149,13 @@
 def greet(plane, others, planes):
     barrier = pltpu.get_barrier_semaphore()
     me = lax.axis_index("dp")
+    crossed = list(others[:1])
     for other in others:
         pl.semaphore_signal(barrier, inc=1, device_id=(other, plane), device_id_type=MESH)
     for other in planes:
-        pl.semaphore_signal(barrier, inc=1, device_id=(me, other), device_id_type=MESH)
-    pl.semaphore_wait(barrier, len(others) + len(planes))
+        for same_place in [me] + crossed:
+            pl.semaphore_signal(barrier, inc=1, device_id=(same_place, other), device_id_type=MESH)
+    pl.semaphore_wait(barrier, len(others) + len(planes) * (1 + len(crossed)))
 
 def gather_kernel(count, *refs):
     shards, wholes = refs[:count], refs[count : 2 * count]
@@ -289,106 +255,325 @@
         target[:, window] = total.astype(jnp.bfloat16)
 
 
-def scatter_kernel(count, *refs):
-    grads, sums = refs[:count], refs[count : 2 * count]
-    own, from_core, from_x, from_y, from_yx, from_xy, from_z = (
-        refs[(2 + index) * count : (3 + index) * count] for index in range(7)
-    )
-    (load_sem, send_c, recv_c, send_x, recv_x, send_y, recv_y, send_yx, recv_yx, send_xy, recv_xy, send_z, recv_z) = refs[9 * count :]
+def send_to(source, target, send, recv, device):
+    pltpu.make_async_remote_copy(
+        source, target, send, recv, device_id=device, device_id_type=MESH
+    ).start()
+
+
+def wait_for(view, sem):
+    pltpu.make_async_copy(view, view, sem).wait()
+
+
+def move_plan(outward, source, target, send, recv, own):
+    me, partner, _, _ = neighbours()
+    plane = lax.axis_index("tensor")
+    core = lax.rem(me, 2)
+    column = me - core
+    high, parity = lax.div(plane, 2), lax.rem(plane, 2)
+    height = target.shape[1] if outward else source.shape[1]
+
+    def owner_of(slot):
+        return (column + parity, 2 * core + slot)
+
+    def keeper_of(micro):
+        return (column + high, 2 * micro + core)
+
+    def same(device):
+        return jnp.logical_and(device[0] == me, device[1] == plane)
+
+    def half(rows, index):
+        return rows.at[pl.ds(pl.multiple_of(index * height, height), height), :]
+
+    def start():
+        for index in range(2):
+            if outward:
+                device = owner_of(index)
+                piece, goal, arrival = half(source, index), target.at[high], high
+            else:
+                device = keeper_of(index)
+                piece, goal, arrival = source.at[index], half(target, parity), parity
+
+            @pl.when(same(device))
+            def _():
+                pltpu.make_async_copy(piece, goal, own).start()
+
+            @pl.when(jnp.logical_not(same(device)))
+            def _():
+                send_to(piece, goal, send.at[index], recv.at[arrival], device)
+
+    def finish():
+        for index in range(2):
+            if outward:
+                sent_to, came_from = owner_of(index), keeper_of(index)
+                piece, goal = half(source, index), target.at[index]
+            else:
+                sent_to, came_from = keeper_of(index), owner_of(index)
+                piece, goal = source.at[index], half(target, index)
+
+            @pl.when(same(sent_to))
+            def _():
+                wait_for(piece, own)
+
+            @pl.when(jnp.logical_not(same(sent_to)))
+            def _():
+                wait_for(piece, send.at[index])
+
+            @pl.when(jnp.logical_not(same(came_from)))
+            def _():
+                wait_for(goal, recv.at[index])
+
+    return (start, finish)
+
+
+def scatter_plan(grads, sums, buffers, sems):
+    held, from_x, from_y, from_yx, from_xy, from_z = buffers[:6]
+    staging = buffers[6][0]
+    (load_sem, send_c, recv_c, send_x, recv_x, send_y, recv_y, send_yx, recv_yx, send_xy, recv_xy, send_z, recv_z) = sems
     me, partner, across, down = neighbours()
     plane = lax.axis_index("tensor")
     planes = [lax.rem(plane + offset, 4) for offset in (1, 2, 3)]
-    greet(plane, (partner, across, down), planes)
     flip = lambda block: block + 1 - 2 * lax.rem(block, 2)
     blocks = (me, across, down, across + down - me)
-    started = []
-
-    def remote(source, target, send, recv, device):
-        copy = pltpu.make_async_remote_copy(source, target, send, recv, device_id=device, device_id_type=MESH)
-        copy.start()
-        started.append(copy)
-
-    def wait(view, sem):
-        pltpu.make_async_copy(view, view, sem).wait()
-
     order = (3, 1, 2, 0)
+
+    def view(part, block):
+        ref, first, rows = grads[part]
+        return ref.at[:, pl.ds(first, rows), lanes(block)]
+
+    def slot(part, index):
+        return staging.at[index, :, pl.ds(0, grads[part][2])]
+
     def stage_core(part):
         for index in order:
-            remote(grads[part].at[:, :, lanes(flip(blocks[index]))], from_core[part].at[index],
-                   send_c.at[part, index], recv_c.at[part, index], (partner, plane))
-            pltpu.make_async_copy(grads[part].at[:, :, lanes(blocks[index])], own[part].at[index], load_sem.at[part, index]).start()
+            send_to(view(part, flip(blocks[index])), held[part].at[index], send_c.at[part, index], recv_c.at[part, index], (partner, plane))
+
+    def load(part):
+        for index in order:
+            pltpu.make_async_copy(view(part, blocks[index]), slot(part, index), load_sem.at[part, index]).start()
 
     def stage_first(part):
-        rows = sums[part].shape[0]
+        rows = grads[part][2]
+        load(part)
         for index in order:
-            wait(own[part].at[index], load_sem.at[part, index])
-            wait(from_core[part].at[index], recv_c.at[part, index])
-            add_into(own[part].at[index], from_core[part].at[index], rows, step_of(rows))
+            wait_for(slot(part, index), load_sem.at[part, index])
+            wait_for(held[part].at[index], recv_c.at[part, index])
+            add_into(held[part].at[index], slot(part, index), rows, step_of(rows))
             if index % 2 == 1:
-                remote(own[part].at[index, 0:2], from_x[part].at[index // 2], send_x.at[part, index // 2], recv_x.at[part, index // 2], (across, plane))
+                send_to(held[part].at[index, 0:2], from_x[part].at[index // 2], send_x.at[part, index // 2], recv_x.at[part, index // 2], (across, plane))
             if index // 2 == 1:
-                remote(own[part].at[index, 2:4], from_y[part].at[index % 2], send_y.at[part, index % 2], recv_y.at[part, index % 2], (down, plane))
+                send_to(held[part].at[index, 2:4], from_y[part].at[index % 2], send_y.at[part, index % 2], recv_y.at[part, index % 2], (down, plane))
 
     def stage_second(part):
-        rows = sums[part].shape[0]
+        rows = grads[part][2]
         for side in (1, 0):
-            wait(from_x[part].at[side], recv_x.at[part, side])
-            add_into(own[part].at[2 * side, 0:2], from_x[part].at[side], rows, step_of(rows))
-            wait(from_y[part].at[side], recv_y.at[part, side])
-            add_into(own[part].at[side, 2:4], from_y[part].at[side], rows, step_of(rows))
+            wait_for(from_x[part].at[side], recv_x.at[part, side])
+            add_into(held[part].at[2 * side, 0:2], from_x[part].at[side], rows, step_of(rows))
             if side == 1:
-                remote(own[part].at[2, 0:2], from_yx[part], send_yx.at[part], recv_yx.at[part], (down, plane))
-                remote(own[part].at[1, 2:4], from_xy[part], send_xy.at[part], recv_xy.at[part], (across, plane))
+                send_to(held[part].at[2, 0:2], from_yx[part], send_yx.at[part], recv_yx.at[part], (down, plane))
+            wait_for(from_y[part].at[side], recv_y.at[part, side])
+            add_into(held[part].at[side, 2:4], from_y[part].at[side], rows, step_of(rows))
+            if side == 1:
+                send_to(held[part].at[1, 2:4], from_xy[part], send_xy.at[part], recv_xy.at[part], (across, plane))
 
     def stage_third(part):
-        rows = sums[part].shape[0]
-        wait(from_yx[part], recv_yx.at[part])
-        add_into(own[part].at[0, 0:2], from_yx[part], rows, step_of(rows))
-        wait(from_xy[part], recv_xy.at[part])
-        add_into(own[part].at[0, 2:4], from_xy[part], rows, step_of(rows))
+        rows = grads[part][2]
+        wait_for(from_yx[part], recv_yx.at[part])
+        add_into(held[part].at[0, 0:2], from_yx[part], rows, step_of(rows))
+        wait_for(from_xy[part], recv_xy.at[part])
+        add_into(held[part].at[0, 2:4], from_xy[part], rows, step_of(rows))
         for index, other in enumerate(planes):
-            remote(own[part].at[0, other], from_z[part].at[index], send_z.at[part, index], recv_z.at[part, index], (me, other))
+            send_to(held[part].at[0, other], from_z[part].at[index], send_z.at[part, index], recv_z.at[part, index], (me, other))
 
     def stage_last(part):
-        rows = sums[part].shape[0]
+        rows = grads[part][2]
         step = step_of(rows)
+        target, first = sums[part]
         for index in range(3):
-            wait(from_z[part].at[index], recv_z.at[part, index])
+            wait_for(from_z[part].at[index], recv_z.at[part, index])
+
         @pl.loop(0, rows // step)
         def _(index):
-            window = pl.ds(pl.multiple_of(index * step, step), step)
-            total = own[part][0, plane, window].astype(jnp.float32)
+            offset = pl.multiple_of(index * step, step)
+            window = pl.ds(offset, step)
+            total = held[part][0, plane, window].astype(jnp.float32)
             for other in range(3):
                 total = total + from_z[part][other, window].astype(jnp.float32)
-            sums[part][window] = total
-
-    stages = (stage_core, stage_first, stage_second, stage_third, stage_last)
-    for part in range(count):
-        stage_core(part)
-    for step in range(count + 3):
-        for stage in (4, 3, 2, 1):
-            part = step - (stage - 1)
-            if 0 <= part < count:
-                stages[stage](part)
-    for copy in started:
-        copy.wait_send()
-
-def scatter_grads(grads, collective_id):
-    count = len(grads)
-    rows = [g.shape[1] for g in grads]
+            target[pl.ds(pl.multiple_of(first + offset, 16), step)] = total
+
+    def finish(part):
+        for index in range(4):
+            wait_for(held[part].at[index], send_c.at[part, index])
+        for side in range(2):
+            wait_for(from_x[part].at[side], send_x.at[part, side])
+            wait_for(from_y[part].at[side], send_y.at[part, side])
+        wait_for(from_yx[part], send_yx.at[part])
+        wait_for(from_xy[part], send_xy.at[part])
+        for index in range(3):
+            wait_for(from_z[part].at[index], send_z.at[part, index])
+
+    return ((stage_core, stage_first, stage_second, stage_third, stage_last), finish)
+
+
+def scatter_scratch(heights):
     sem = pltpu.SemaphoreType.DMA
-    vm = lambda *lead: [pltpu.VMEM(lead + (r, 128), jnp.bfloat16) for r in rows]
-    scratch = vm(4, 4) + vm(4, 4) + vm(2, 2) + vm(2, 2) + vm(2) + vm(2) + vm(3)
+    count = len(heights)
+    leads = ((4, 4), (2, 2), (2, 2), (2,), (2,), (3,))
+    buffers = [pltpu.VMEM(lead + (rows, 128), jnp.bfloat16) for lead in leads for rows in heights]
+    buffers.append(pltpu.VMEM((4, 4, max(heights), 128), jnp.bfloat16))
     sems = [sem((count, 4))] * 3 + [sem((count, 2))] * 4 + [sem((count,))] * 4 + [sem((count, 3))] * 2
-    return pl.pallas_call(
-        functools.partial(scatter_kernel, count),
-        out_shape=[jax.ShapeDtypeStruct((r, 128), jnp.float32) for r in rows],
-        in_specs=[pl.BlockSpec(memory_space=pl.ANY)] * count,
-        out_specs=[pl.BlockSpec(memory_space=pltpu.VMEM)] * count,
-        scratch_shapes=scratch + sems,
-        compiler_params=pltpu.CompilerParams(collective_id=collective_id, has_side_effects=True, vmem_limit_bytes=58 * 1024 * 1024),
-        name="scatter_grads",
-    )(*grads)
+    return (buffers, sems)
+
+
+def take(refs, count):
+    taken, refs[:] = refs[:count], refs[count:]
+    return taken
+
+
+def backward_kernel(*refs):
+    refs = list(refs)
+    grad_out, grad_in, grad_attn, rows_in = take(refs, 4)
+    low_rows, queries, own, other, bias, grad, context, log_total, cosine, sine = take(refs, 10)
+    sums, (grad_query, grad_pair), (rows_out,) = take(refs, 4), take(refs, 2), take(refs, 1)
+    weight_grads = take(refs, 3)
+    grad_other, arrived, staged = take(refs, 3)
+    buffers = [take(refs, 7) for _ in range(6)] + [take(refs, 1)]
+    sems = take(refs, 13)
+    pair_send, pair_recv, stage_sem, move_send, move_recv, move_own = refs
+    me, partner, across, down = neighbours()
+    plane = lax.axis_index("tensor")
+    height, third = grad_out.shape[1], grad_attn.shape[1]
+    parts = [(grad_out, 0, height), (grad_in, 0, height), (grad_in, height, height)]
+    parts += [(grad_attn, 0, third)] + [(ref, 0, third) for ref in weight_grads]
+    sum_qkv, sum_attn, sum_in, sum_out = sums
+    targets = [(sum_out, 0), (sum_in, 0), (sum_in, height), (sum_attn, 0)]
+    targets += [(sum_qkv, third * index) for index in range(3)]
+    stages, finish = scatter_plan(parts, targets, buffers, sems)
+    start_move, finish_move = move_plan(True, rows_in, rows_out, move_send, move_recv, move_own)
+    greet(plane, (partner, across, down), [lax.rem(plane + offset, 4) for offset in (1, 2, 3)])
+    stages[0](0)
+    schedule = {0: ((0, 1),), 1: ((1, 0), (0, 2)), 3: ((1, 1), (0, 3)), 6: ((2, 0),), 7: ((1, 2),)}
+
+    @pl.loop(0, queries.shape[1] // 128)
+    def _(index):
+        for position, calls in schedule.items():
+            @pl.when(index == position)
+            def _():
+                for stage, part in calls:
+                    stages[stage](part)
+
+        attend_back_pair(lanes(index), queries, own, other, bias, grad, context, log_total.at[index], cosine, sine, grad_query, grad_pair, grad_other)
+
+    send_to(grad_other, arrived, pair_send, pair_recv, (partner, plane))
+    start_move()
+
+    def weight_grad(which, values):
+        target = weight_grads[which]
+        for group in range(4):
+            slot = staged.at[group % 2]
+            if group >= 2:
+                wait_for(slot, stage_sem.at[group % 2])
+            block = values[:, third * group : third * group + third]
+            slot[...] = low(product_of(block, low_rows[...], ((0,), (0,))))
+            pltpu.make_async_copy(slot, target.at[group], stage_sem.at[group % 2]).start()
+        for group in range(2):
+            wait_for(staged.at[group], stage_sem.at[group])
+
+    weight_grad(0, grad_query)
+    stages[0](4)
+    stages[2](1)
+    wait_for(arrived, pair_recv)
+    step = 128
+
+    @pl.loop(0, grad_pair.shape[1] // step)
+    def _(index):
+        window = pl.ds(pl.multiple_of(index * step, step), step)
+        total = grad_pair[:, window].astype(jnp.float32) + arrived[:, window].astype(jnp.float32)
+        grad_pair[:, window] = low(total)
+
+    weight_grad(1, grad_pair.at[0])
+    stages[0](5)
+    stages[1](3)
+    weight_grad(2, grad_pair.at[1])
+    stages[0](6)
+    calls = [(stage, step - (stage - 1)) for step in range(10) for stage in (4, 3, 2, 1)]
+    done = {(1, 0), (1, 1), (1, 2), (1, 3), (2, 0), (2, 1)}
+    for stage, part in calls:
+        if 0 <= part < 7 and (stage, part) not in done:
+            stages[stage](part)
+    for part in range(7):
+        finish(part)
+    wait_for(grad_other, pair_send)
+    finish_move()
+
+
+def backward(grad_out, grad_in, grad_attn, rows_in, low_rows, queries, own, other, bias, grad, context, log_total, cosine, sine, collective_id):
+    height, third = grad_out.shape[1], grad_attn.shape[1]
+    count, width = queries.shape
+    buffers, sems = scatter_scratch([height] * 3 + [third] * 4)
+    sem = pltpu.SemaphoreType.DMA
+    anywhere = pl.BlockSpec(memory_space=pl.ANY)
+    local = pl.BlockSpec(memory_space=pltpu.VMEM)
+    bf16 = jnp.bfloat16
+    outs = pl.pallas_call(
+        backward_kernel,
+        out_shape=[
+            jax.ShapeDtypeStruct((rows, 128), jnp.float32)
+            for rows in (3 * third, third, 2 * height, height)
+        ]
+        + [
+            jax.ShapeDtypeStruct((count, width), bf16),
+            jax.ShapeDtypeStruct((2, count, width), bf16),
+            jax.ShapeDtypeStruct((2, count // 2, width), rows_in.dtype),
+        ]
+        + [jax.ShapeDtypeStruct(grad_attn.shape, bf16)] * 3,
+        in_specs=[anywhere] * 4 + [local] * 10,
+        out_specs=[local] * 6 + [anywhere] * 4,
+        scratch_shapes=[
+            pltpu.VMEM((2, count, width), bf16),
+            pltpu.VMEM((2, count, width), bf16),
+            pltpu.VMEM((2, third, width), bf16),
+        ]
+        + buffers
+        + sems
+        + [sem, sem, sem((2,)), sem((2,)), sem((2,)), sem],
+        compiler_params=pltpu.CompilerParams(
+            collective_id=collective_id, has_side_effects=True, vmem_limit_bytes=60 * 1024 * 1024
+        ),
+        name="backward",
+    )(grad_out, grad_in, grad_attn, rows_in, low_rows, queries, own, other, bias, grad, context, log_total, cosine, sine)
+    return outs[:7]
+
+
+def attend_back_pair(columns, queries, own, other, bias, grad, context, log_total, cosine, sine, grad_query, grad_own, grad_other):
+    count = queries.shape[0]
+    query_rows, grad_rows = queries[:, columns], grad[:, columns]
+    query_turned, grad_turned = query_rows.T, grad_rows.T
+    inner = (grad_rows.astype(jnp.float32) * context[:, columns].astype(jnp.float32)).T
+    query_parts = [None, None]
+    for half, (pair, result) in enumerate(((own, grad_own), (other, grad_other))):
+        keys, values = pair[0, :, columns], pair[1, :, columns]
+        key_turned = keys.T
+        grad_keys, grad_values = None, None
+        window = pl.ds(half * count, count)
+        for head in range(2):
+            lanes_of_head = slice(64 * head, 64 * head + 64)
+            scores = scores_of(keys, head_rows(query_turned, head), bias[window])
+            weights = jnp.exp(scores - log_total[head : head + 1])
+            grad_weights = product_of(values, head_rows(grad_turned, head), ((1,), (0,)))
+            inner_row = jnp.sum(inner[lanes_of_head], axis=0, keepdims=True)
+            grad_scores = low(weights * (grad_weights - inner_row))
+            value_part = product_of(low(weights), head_lanes(grad_rows, head), ((1,), (0,)))
+            key_part = product_of(grad_scores, head_lanes(query_rows, head), ((1,), (0,)))
+            query_part = product_of(key_turned[lanes_of_head], grad_scores, ((1,), (0,)))
+            grad_values = value_part if head == 0 else grad_values + value_part
+            grad_keys = key_part if head == 0 else grad_keys + key_part
+            query_parts[head] = query_part if half == 0 else query_parts[head] + query_part
+        result[0, :, columns] = turned(grad_keys, cosine[window], -sine[window]).astype(result.dtype)
+        result[1, :, columns] = grad_values.astype(result.dtype)
+    query_rows = jnp.concatenate(query_parts, axis=0).T * SCORE_SCALE
+    own_rows = pl.ds(0, count)
+    grad_query[:, columns] = low(turned(query_rows, cosine[own_rows], -sine[own_rows]))
 
 
 def owner_kernel(rows, *refs):
@@ -591,40 +776,34 @@
         rest = store(window, iterate[window] * squared, mean, iterate, iterate_low)
         row = row + fold(rest * rest)
     square = finish(row)
-    total_mean = None
-    for sweep in range(NS_ITERS):
-        first_sweep = sweep == 0
+    blank = jnp.zeros((1, size), f32)
+
+    def polynomial(mean, square, with_total):
         linear = QUINTIC_THREE + 2.0 * QUINTIC_FIVE * mean
         shift = QUINTIC_FIVE * square
         poly_mean = QUINTIC_ONE + QUINTIC_THREE * mean + QUINTIC_FIVE * (mean * mean) + shift
-        row = jnp.zeros((1, size), f32)
-        total_row = row
+        row, total_row = blank, blank
         for window in windows:
             mine = iterate[window]
-            rest = linear * mine + QUINTIC_FIVE * product_of(iterate_low[window], iterate_low[...], ((1,), (0,)))
+            rest = product_of(iterate_low[window], iterate_low[...], ((1,), (0,)))
+            rest = linear * mine + QUINTIC_FIVE * rest
             rest = store(window, rest, shift, poly, poly_low)
             row = row + fold(rest * mine)
-            if not first_sweep:
+            if with_total:
                 total_row = total_row + fold(rest * total[window])
-        cross, cross_total = finish(row), finish(total_row)
-        if first_sweep:
-            total_mean = poly_mean
-            source, source_low = poly, poly_low
-            for window in windows:
-                total[window] = poly[window]
-                total_low[window] = poly_low[window]
-        else:
-            results = []
-            for window in windows:
-                result = poly_mean * total[window] + total_mean * poly[window]
-                result = result + product_of(poly_low[window], total_low[...], ((1,), (0,)))
-                store(window, result, cross_total, total, other_low)
-            for window in windows:
-                total_low[window] = other_low[window]
-            total_mean = poly_mean * total_mean + cross_total
-        if sweep == NS_ITERS - 1:
-            break
-        row = jnp.zeros((1, size), f32)
+        return (poly_mean, finish(row), finish(total_row))
+
+    def grow_total(poly_mean, total_mean, cross):
+        for window in windows:
+            result = poly_mean * total[window] + total_mean * poly[window]
+            result = result + product_of(poly_low[window], total_low[...], ((1,), (0,)))
+            store(window, result, cross, total, other_low)
+        for window in windows:
+            total_low[window] = other_low[window]
+        return poly_mean * total_mean + cross
+
+    def advance(poly_mean, mean, cross):
+        row = blank
         for window in windows:
             rest = poly[window]
             result = poly_mean * iterate[window] + mean * rest
@@ -633,14 +812,29 @@
             row = row + fold(result * rest)
         product_mean = poly_mean * mean + cross
         cross = finish(row)
-        row = jnp.zeros((1, size), f32)
+        row = blank
         for window in windows:
             result = poly_mean * product[window] + product_mean * poly[window]
             result = result + product_of(poly_low[window], other_low[...], ((1,), (0,)))
             result = store(window, result, cross, iterate, iterate_low)
             row = row + fold(result * result)
-        square = finish(row)
-        mean = poly_mean * product_mean + cross
+        return (poly_mean * product_mean + cross, finish(row))
+
+    total_mean, cross, _ = polynomial(mean, square, False)
+    for window in windows:
+        total[window] = poly[window]
+        total_low[window] = poly_low[window]
+    mean, square = advance(total_mean, mean, cross)
+
+    def sweep(_, carry):
+        mean, square, total_mean = carry
+        poly_mean, cross, cross_total = polynomial(mean, square, True)
+        total_mean = grow_total(poly_mean, total_mean, cross_total)
+        return advance(poly_mean, mean, cross) + (total_mean,)
+
+    mean, square, total_mean = lax.fori_loop(0, NS_ITERS - 2, sweep, (mean, square, total_mean))
+    poly_mean, _, cross_total = polynomial(mean, square, True)
+    total_mean = grow_total(poly_mean, total_mean, cross_total)
 
     mine = pl.ds(pl.multiple_of(me * 128, 128), 128)
     columns = total_low[:, mine]
@@ -671,6 +865,8 @@
 def gather_weights(weights):
     tensor_count, dp_count = lax.axis_size("tensor"), lax.axis_size("dp")
     shards = [turn(weight) for weight in weights]
+    third = shards[0].shape[0] // 3
+    shards = [shards[0][third * part : third * part + third] for part in range(3)] + shards[1:]
     if (tensor_count, dp_count, shards[0].shape[1]) == (4, 8, 128):
         return gather_blocks(shards, 1)
     wholes = [lax.all_gather(shard, ("tensor", "dp")) for shard in shards]
@@ -683,8 +879,6 @@
 
 def reduce_grads(grads):
     tensor_count, dp_count = lax.axis_size("tensor"), lax.axis_size("dp")
-    if (tensor_count, dp_count, grads[0].shape[2]) == (4, 8, 1024):
-        return scatter_grads(grads, 2)
     sums = []
     for grad in grads:
         blocks = grad.reshape(*grad.shape[:2], dp_count, -1).transpose(0, 2, 1, 3)
@@ -692,6 +886,175 @@
         part = lax.psum_scatter(blocks, ("tensor", "dp"), scatter_dimension=0, tiled=True)
         sums.append(part[0].astype(jnp.float32))
     return sums
+
+
+def lane_of(shape):
+    return lax.broadcasted_iota(jnp.int32, shape, 1)
+
+def turned(vectors, cosine, sine):
+    lane = lax.rem(lane_of(vectors.shape), 64)
+    swapped = jnp.where(lane < 32, pltpu.roll(vectors, 96, 1), pltpu.roll(vectors, 32, 1))
+    return vectors * cosine + swapped * sine
+
+def project_kernel(rows, query_weight, key_weight, value_weight, cosine, sine, queries, pair):
+    rows = rows[...]
+    for weight, target in ((query_weight, 0), (key_weight, 1)):
+        result = product_of(rows, weight[0], ((1,), (1,)))
+        for first in range(0, result.shape[1], 128):
+            part = turned(result[:, first : first + 128], cosine[...], sine[...])
+            if target == 0:
+                queries[:, first : first + 128] = low(part * SCORE_SCALE)
+            else:
+                pair[0, :, first : first + 128] = low(part)
+    pair[1] = low(product_of(rows, value_weight[0], ((1,), (1,))))
+
+def project(rows, query_weight, key_weight, value_weight, cosine, sine):
+    count, width = rows.shape
+    groups, height, _ = query_weight.shape
+    whole = lambda *shape: pl.BlockSpec(shape, lambda i: (0,) * len(shape))
+    weight = pl.BlockSpec((1, height, width), lambda i: (i, 0, 0))
+    return pl.pallas_call(
+        project_kernel,
+        grid=(groups,),
+        out_shape=[jax.ShapeDtypeStruct((count, width), jnp.bfloat16), jax.ShapeDtypeStruct((2, count, width), jnp.bfloat16)],
+        in_specs=[whole(count, width), weight, weight, weight, whole(count, 128), whole(count, 128)],
+        out_specs=[pl.BlockSpec((count, height), lambda i: (0, i)), pl.BlockSpec((2, count, height), lambda i: (0, 0, i))],
+        compiler_params=pltpu.CompilerParams(vmem_limit_bytes=40 * 1024 * 1024),
+        name="project",
+    )(rows, query_weight, key_weight, value_weight, cosine, sine)
+
+def head_rows(transposed, head):
+    rows = lax.broadcasted_iota(jnp.int32, transposed.shape, 0)
+    return jnp.where(lax.div(rows, 64) == head, transposed, jnp.zeros_like(transposed))
+
+def head_lanes(values, head):
+    return jnp.where(lax.div(lane_of(values.shape), 64) == head, values, jnp.zeros_like(values))
+
+def scores_of(keys, queries_turned, bias):
+    scores = product_of(keys, queries_turned, ((1,), (0,)))
+    return scores + jnp.concatenate([bias] * (scores.shape[1] // 128), axis=1)
+
+def attend_kernel(queries, own, other, bias, context, log_total):
+    query_turned = queries[...].T
+    keys = jnp.concatenate([own[0], other[0]], axis=0)
+    value_turned = jnp.concatenate([own[1].T, other[1].T], axis=1)
+    parts, logs = [], []
+    for head in range(2):
+        scores = scores_of(keys, head_rows(query_turned, head), bias[...])
+        highest = jnp.max(scores, axis=0, keepdims=True)
+        weights = jnp.exp(scores - highest)
+        total = jnp.sum(weights, axis=0, keepdims=True)
+        part = product_of(value_turned[64 * head : 64 * head + 64], low(weights), ((1,), (0,)))
+        parts.append(part / total)
+        logs.append(highest + jnp.log(total))
+    context[...] = low(jnp.concatenate(parts, axis=0)).T
+    log_total[0] = jnp.concatenate(logs + logs * 3, axis=0)
+
+def attend(queries, own, other, bias):
+    count, width = queries.shape
+    pairs = width // 128
+    column = pl.BlockSpec((count, 128), lambda i: (0, i))
+    double = pl.BlockSpec((2, count, 128), lambda i: (0, 0, i))
+    return pl.pallas_call(
+        attend_kernel,
+        grid=(pairs,),
+        out_shape=[jax.ShapeDtypeStruct((count, width), jnp.bfloat16), jax.ShapeDtypeStruct((pairs, 8, count), jnp.float32)],
+        in_specs=[column, double, double, pl.BlockSpec((2 * count, 128), lambda i: (0, 0))],
+        out_specs=[column, pl.BlockSpec((1, 8, count), lambda i: (i, 0, 0))],
+        compiler_params=pltpu.CompilerParams(vmem_limit_bytes=40 * 1024 * 1024),
+        name="attend",
+    )(queries, own, other, bias)
+
+def attend_back_kernel(queries, own, other, bias, grad, context, log_total, cosine, sine, grad_query, grad_own, grad_other):
+    count = queries.shape[0]
+    query_turned, grad_turned = queries[...].T, grad[...].T
+    inner = (grad[...].astype(jnp.float32) * context[...].astype(jnp.float32)).T
+    query_parts = [None, None]
+    for half, (pair, result) in enumerate(((own, grad_own), (other, grad_other))):
+        keys, values = pair[0], pair[1]
+        key_turned = keys.T
+        grad_keys, grad_values = None, None
+        window = pl.ds(half * count, count)
+        for head in range(2):
+            lanes_of_head = slice(64 * head, 64 * head + 64)
+            scores = scores_of(keys, head_rows(query_turned, head), bias[window])
+            weights = jnp.exp(scores - log_total[0, head : head + 1])
+            grad_weights = product_of(values, head_rows(grad_turned, head), ((1,), (0,)))
+            inner_row = jnp.sum(inner[lanes_of_head], axis=0, keepdims=True)
+            grad_scores = low(weights * (grad_weights - inner_row))
+            value_part = product_of(low(weights), head_lanes(grad[...], head), ((1,), (0,)))
+            key_part = product_of(grad_scores, head_lanes(queries[...], head), ((1,), (0,)))
+            query_part = product_of(key_turned[lanes_of_head], grad_scores, ((1,), (0,)))
+            grad_values = value_part if head == 0 else grad_values + value_part
+            grad_keys = key_part if head == 0 else grad_keys + key_part
+            query_parts[head] = query_part if half == 0 else query_parts[head] + query_part
+        result[0] = turned(grad_keys, cosine[window], -sine[window]).astype(result.dtype)
+        result[1] = grad_values.astype(result.dtype)
+    grad_rows = jnp.concatenate(query_parts, axis=0).T * SCORE_SCALE
+    own_rows = pl.ds(0, count)
+    grad_query[...] = low(turned(grad_rows, cosine[own_rows], -sine[own_rows]))
+
+def attend_back(queries, own, other, bias, grad, context, log_total, cosine, sine):
+    count, width = queries.shape
+    pairs = width // 128
+    column = pl.BlockSpec((count, 128), lambda i: (0, i))
+    double = pl.BlockSpec((2, count, 128), lambda i: (0, 0, i))
+    table = pl.BlockSpec((2 * count, 128), lambda i: (0, 0))
+    return pl.pallas_call(
+        attend_back_kernel,
+        grid=(pairs,),
+        out_shape=[
+            jax.ShapeDtypeStruct((count, width), jnp.bfloat16),
+            jax.ShapeDtypeStruct((2, count, width), jnp.float32),
+            jax.ShapeDtypeStruct((2, count, width), jnp.bfloat16),
+        ],
+        in_specs=[column, double, double, table, column, column, pl.BlockSpec((1, 8, count), lambda i: (i, 0, 0)), table, table],
+        out_specs=[column, double, double],
+        compiler_params=pltpu.CompilerParams(vmem_limit_bytes=48 * 1024 * 1024),
+        name="attend_back",
+    )(queries, own, other, bias, grad, context, log_total, cosine, sine)
+
+def feed_kernel(rows, cotangent, in_weight, out_weight, result, grad_rows, grad_in, grad_out):
+    height = out_weight.shape[1]
+    @pl.when(pl.program_id(0) == 0)
+    def _():
+        result[...] = jnp.zeros_like(result)
+        grad_rows[...] = jnp.zeros_like(grad_rows)
+    gate = product_of(in_weight[0, 0:height], rows[...], ((1,), (1,)))
+    up = product_of(in_weight[0, height:], rows[...], ((1,), (1,)))
+    grad_hidden = product_of(out_weight[0], cotangent[...], ((1,), (1,)))
+    below = 0.5 + 0.5 * lax.erf(gate * math.sqrt(0.5))
+    active = gate * below
+    hidden = low(active * up)
+    slope = below + gate * jnp.exp(-0.5 * gate * gate) * (1.0 / math.sqrt(2.0 * math.pi))
+    grad_gate = low(grad_hidden * up * slope)
+    grad_up = low(grad_hidden * active)
+    grad_out[0] = low(product_of(hidden, cotangent[...], ((1,), (0,))))
+    grad_in[0, 0:height] = low(product_of(grad_gate, rows[...], ((1,), (0,))))
+    grad_in[0, height:] = low(product_of(grad_up, rows[...], ((1,), (0,))))
+    result[...] += product_of(hidden, out_weight[0], ((0,), (0,)))
+    grad_rows[...] += product_of(grad_gate, in_weight[0, 0:height], ((0,), (0,)))
+    grad_rows[...] += product_of(grad_up, in_weight[0, height:], ((0,), (0,)))
+
+def feed(rows, cotangent, in_weight, out_weight):
+    count, width = rows.shape
+    groups, height, _ = out_weight.shape
+    whole = pl.BlockSpec((count, width), lambda i: (0, 0))
+    block = lambda size: pl.BlockSpec((1, size, width), lambda i: (i, 0, 0))
+    return pl.pallas_call(
+        feed_kernel,
+        grid=(groups,),
+        out_shape=[
+            jax.ShapeDtypeStruct((count, width), jnp.float32),
+            jax.ShapeDtypeStruct((count, width), jnp.float32),
+            jax.ShapeDtypeStruct(in_weight.shape, jnp.bfloat16),
+            jax.ShapeDtypeStruct(out_weight.shape, jnp.bfloat16),
+        ],
+        in_specs=[whole, whole, block(2 * height), block(height)],
+        out_specs=[whole, whole, block(2 * height), block(height)],
+        compiler_params=pltpu.CompilerParams(vmem_limit_bytes=60 * 1024 * 1024),
+        name="feed",
+    )(rows, cotangent, in_weight, out_weight)
 
 
 def turn(block):
@@ -755,7 +1118,7 @@
     row_count = qkv_weight.shape[0]
 
     rows_low = to_sequences(inputs[:, 0], lists, odd, upper)
-    qkv_all, attn_all, ffn_in_all, ffn_out_all = gather_weights(weights)
+    query_all, key_all, value_all, attn_all, ffn_in_all, ffn_out_all = gather_weights(weights)
     cotangent_low = to_sequences(cotangent[:, 0], lists, odd, upper)
     rows_in = rows_low.astype(jnp.float32)
     grad_rows = cotangent_low.astype(jnp.float32)
@@ -767,88 +1130,61 @@
         jnp.concatenate([own_lengths, lengths], 1),
     )
     length = lax.dynamic_index_in_dim(both_lengths.reshape(-1), tensor_index, 0, keepdims=False)
-    first_row = core * local_rows
-    cosine_table, sine_table = rotary(first_row, local_rows)
-    own_positions = first_row + jnp.arange(local_rows)
-    other_positions = (1 - core) * local_rows + jnp.arange(local_rows)
-    key_valid = (jnp.concatenate([own_positions, other_positions]) < length)[None, None, :]
+    positions = jnp.concatenate(
+        [core * local_rows + jnp.arange(local_rows), (1 - core) * local_rows + jnp.arange(local_rows)]
+    )
+    cosine, sine = rotary(positions)
+    bias = jnp.where(positions < length, 0.0, MASK_VALUE).astype(jnp.float32)
+    bias = jnp.broadcast_to(bias[:, None], (positions.shape[0], 128))
 
     normed_one, inverse_one, scaled_one = layer_norm_parts(rows_in, norm_gains[0])
     low_one = low(scaled_one)
     width = rows_in.shape[1]
-    heads = width // HEAD_DIM
-    qkv_rows = qkv_all.reshape(-1, width)
     attn_rows = attn_all.reshape(-1, width)
-    ffn_in_rows = ffn_in_all.reshape(-1, width)
-    ffn_out_rows = ffn_out_all.reshape(-1, width)
-    projected = einsum("sk,nk->sn", low_one, qkv_rows)
-    projected = projected.reshape(local_rows, tensor_count, 3, -1, HEAD_DIM)
-    projected = projected.transpose(2, 0, 1, 3, 4).reshape(3, local_rows, heads, HEAD_DIM)
-    queries = low(rotate(projected[0], cosine_table, sine_table))
-    own_keys = low(rotate(projected[1], cosine_table, sine_table))
-    own_values = low(projected[2])
-    own_pair = jnp.stack([own_keys, own_values])
-    pair = jnp.concatenate([own_pair, swap_partner(own_pair)], axis=1)
-    context, log_total = attention_forward(queries, pair[0], pair[1], key_valid)
-    context_low = low(context).reshape(local_rows, width)
-    middle = rows_in + einsum("sk,kn->sn", context_low, attn_rows)
+    queries, own = project(
+        low_one, query_all, key_all, value_all, cosine[:local_rows], sine[:local_rows]
+    )
+    other = swap_partner(own)
+    context, log_total = attend(queries, own, other, bias)
+    middle = rows_in + einsum("sk,kn->sn", context, attn_rows)
     normed_two, inverse_two, scaled_two = layer_norm_parts(middle, norm_gains[1])
     low_two = low(scaled_two)
-    gate_up = einsum("kn,sn->ks", ffn_in_rows, low_two)
-    gate_up = gate_up.reshape(tensor_count, 2, -1, local_rows)
-
-    def activate(gate_part, up_part):
-        return jax.nn.gelu(gate_part, approximate=False) * up_part
-
-    hidden, activate_back = jax.vjp(activate, gate_up[:, 0], gate_up[:, 1])
-    hidden_low = low(hidden).reshape(-1, local_rows)
-    result = low(middle + einsum("ks,kn->sn", hidden_low, ffn_out_rows))
-    outputs = from_sequences(result, lists, odd, upper)[:, None]
-
-    grad_hidden = einsum("kn,sn->ks", ffn_out_rows, cotangent_low)
-    grad_ffn_out = low(einsum("ks,sn->kn", hidden_low, cotangent_low))
-    grad_gate, grad_up = activate_back(grad_hidden.reshape(hidden.shape))
-    grad_gate_up = low(jnp.stack([grad_gate, grad_up], axis=1)).reshape(-1, local_rows)
-    grad_ffn_in = low(einsum("ks,sn->kn", grad_gate_up, low_two))
-    grad_scaled_two = einsum("ks,kn->sn", grad_gate_up, ffn_in_rows)
+    ffn_branch, grad_scaled_two, grad_ffn_in, grad_ffn_out = feed(
+        low_two, cotangent_low, ffn_in_all, ffn_out_all
+    )
+    result = low(middle + ffn_branch)
     grad_from_two, gain_two = layer_norm_back(
         grad_scaled_two, normed_two, inverse_two, norm_gains[1]
     )
     grad_middle = grad_rows + grad_from_two
     grad_branch = low(grad_middle)
     grad_context = low(einsum("sn,kn->sk", grad_branch, attn_rows))
-    grad_attn_out = low(einsum("sk,sn->kn", context_low, grad_branch))
-    grad_query, grad_keys, grad_values = attention_backward(
-        queries,
-        pair[0],
-        pair[1],
-        log_total,
-        grad_context.reshape(local_rows, heads, HEAD_DIM),
-        key_valid,
-    )
-    grad_pair = jnp.stack([grad_keys, grad_values])
-    grad_pair = grad_pair[:, :local_rows] + swap_partner(low(grad_pair[:, local_rows:])).astype(
-        jnp.float32
-    )
-    grad_projected = jnp.stack(
-        [
-            rotate(grad_query, cosine_table, -sine_table),
-            rotate(grad_pair[0], cosine_table, -sine_table),
-            grad_pair[1],
-        ]
-    )
-    grad_projected = low(grad_projected).reshape(3, local_rows, tensor_count, -1)
-    grad_projected = grad_projected.transpose(1, 2, 0, 3).reshape(local_rows, -1)
-    grad_qkv = low(einsum("sk,sn->kn", grad_projected, low_one))
-    grads = (grad_qkv, grad_attn_out, grad_ffn_in, grad_ffn_out)
-    grads = [grad.reshape(tensor_count, -1, width) for grad in grads]
-    sums = reduce_grads(grads[::-1])[::-1]
-    grad_scaled_one = einsum("sk,kn->sn", grad_projected, qkv_rows)
+    grad_attn_out = low(einsum("sk,sn->kn", context, grad_branch)).reshape(attn_all.shape)
+    fits = (tensor_count, dp_count, row_count, width) == (4, 8, 128, 1024)
+    attention = (queries, own, other, bias, grad_context, context, log_total, cosine, sine)
+    if fits:
+        outs = backward(grad_ffn_out, grad_ffn_in, grad_attn_out, result, low_one, *attention, 2)
+        sums, (grad_query, grad_pair, outputs) = outs[:4], outs[4:]
+    else:
+        grad_query, grad_own, grad_other = attend_back(*attention)
+        grad_pair = low(grad_own + swap_partner(grad_other).astype(jnp.float32))
+    grad_parts = (grad_query, grad_pair[0], grad_pair[1])
+    grad_scaled_one = sum(
+        einsum("sk,kn->sn", part, weight.reshape(-1, width))
+        for part, weight in zip(grad_parts, (query_all, key_all, value_all))
+    )
     grad_from_one, gain_one = layer_norm_back(
         grad_scaled_one, normed_one, inverse_one, norm_gains[0]
     )
-    grad_input = grad_middle + grad_from_one
-    input_grad = from_sequences(low(grad_input), lists, odd, upper)[:, None].astype(jnp.float32)
+    input_low = low(grad_middle + grad_from_one)
+    if not fits:
+        grads = [low(einsum("sk,sn->kn", part, low_one)) for part in grad_parts]
+        grads = [grad.reshape(query_all.shape) for grad in grads]
+        sums = reduce_grads(grads + [grad_attn_out, grad_ffn_in, grad_ffn_out])
+        outputs = from_sequences(result, lists, odd, upper)
+        sums = [jnp.concatenate(sums[:3])] + list(sums[3:])
+    input_grad = from_sequences(input_low, lists, odd, upper)
+    outputs, input_grad = outputs[:, None], input_grad[:, None].astype(jnp.float32)
 
     moments = (qkv_moment, attn_out_moment, ffn_in_moment, ffn_out_moment)
     gain_part = jnp.stack([gain_one, gain_two])

time: 794 us -> 613 us (0.77)
  matrix products: 169 us -> 14.5 us
  other arithmetic: 126 us -> 40.4 us
  Pallas kernels: 430 us -> 494 us
    dot_general x18 -> x6, matrix products: 169 us -> 14.5 us  [einsum(): return jnp.einsum(spec, *operands, preferred_element_type=jnp.float32)]
    pallas_call x1 -> x4, Pallas kernels: 134 us -> 200 us  [the longest x1 144 us: backward(): pl.pallas_call(backward_kernel, out_shape=[jax.ShapeDtypeStruct((rows, 12...]
    convert_element_type x6, other arithmetic: 48.8 us -> 10 us  [low(): return values.astype(jnp.bfloat16)]
    another operation x7 -> x0, other arithmetic: 27.2 us -> none  [the longest x2 22.1 us: on_device(): jnp.stack([grad_gate, grad_up], axis=1)]
    reduce_sum x1, other arithmetic: 14.6 us -> 2.55 us  [layer_norm_back(): jnp.sum(grad_out * normed, axis=0)]
  transfers between devices with their start and end apart: 11 -> 8, of which waited for: 2 -> 4; matrix products, arithmetic and copies ran while one was open for 10% -> 4% of each run, Pallas kernels for 55% -> 22%
where the time goes in v3:
time: 613 us; the launch traced here: 603 us
  Pallas kernels  494 us (81%)
  other arithmetic  40.4 us (7%)
  waiting for transfers between devices  21.4 us (3%)
  local copies, waits for them, and re-layouts  20.2 us (3%)
  matrix products  14.5 us (2%)
  starting transfers between devices  10.9 us (2%)
    pallas_call x1, Pallas kernels, backward(): pl.pallas_call(backward_kernel, out_shape=[jax.ShapeDtypeStruct((rows, 12...  144 us
    pallas_call x1, Pallas kernels, gather_blocks(): pl.pallas_call(functools.partial(gather_kernel, count), out_shape=[jax.Sh...  135 us
    pallas_call x1, Pallas kernels, return_steps(): pl.pallas_call(functools.partial(return_kernel, rows), out_shape=[jax.Sha...  65.5 us
    pallas_call x1, Pallas kernels, iterate_owned(): pl.pallas_call(functools.partial(iterate_kernel, rows), out_shape=jax.Sha...  55.6 us
    pallas_call x1, Pallas kernels, own_matrix(): pl.pallas_call(functools.partial(owner_kernel, rows), out_shape=[jax.Shap...  37.7 us
    pallas_call x1, Pallas kernels, feed(): pl.pallas_call(feed_kernel, grid=(groups,), out_shape=[jax.ShapeDtypeStru...  32.6 us
    pallas_call x1, Pallas kernels, attend(): pl.pallas_call(attend_kernel, grid=(pairs,), out_shape=[jax.ShapeDtypeStr...  18.5 us
    dot_general x6, matrix products, einsum(): return jnp.einsum(spec, *operands, preferred_element_type=jnp.float32)  14.5 us
  transfers between devices with their start and end apart: 8, of which 4 were waited for; matrix products, arithmetic and copies ran while one was open for 4% of the time, Pallas kernels for 22%

profile of v3, /device:TPU:9, one launch (start us, length us, event | category | flops | bytes accessed | tf_op | source)
XLA Modules:
  0.0 603.4 jit_solution(14465777568282013554)
XLA Ops:
  0.7 2.1 select_bitcast_fusion.2
  2.7 0.7 collective-permute-start
  3.4 4.1 collective-permute-start.1
  7.6 1.9 fusion.25
  10.6 0.8 slice.85.cosine
  11.5 0.7 copy.39
  12.2 0.7 slice_bitcast_fusion
  12.9 135.2 %gather_blocks.1 = (bf16[4,256,1024]{2,1,0:T(8,128)(2,1)}, bf16[4,256,1024]{2,1,0:T(8,128)(2,1)}, bf16[4,256,1024]{2,1,0:T(8,128)(2,1)}, bf16[4,256,1024]{2,1,0:...) custom-call(bf16[256,128]{1,0:T(8,128)(2,1)} %get-tuple-element.120.refs_0_, ...), custom_call_target="tpu_custom_call" | custom-call | tf_op jit(solution)/shard_map/gather_blocks/pallas_call | solution.py:239
  149.5 0.5 copy-done.5
  150.1 1.0 copy-done.7
  151.1 1.6 copy-done.9
  152.7 0.9 copy-done.13
  153.6 5.3 project.1
  159.0 1.0 copy-done.3
  159.9 0.5 collective-permute-start.3
  160.4 1.1 select_bitcast_fusion.1
  161.6 3.5 collective-permute-start.5
  165.3 1.7 copy.44
  167.0 2.0 broadcast_multiply_fusion
  169.0 1.3 add_select_fusion
  170.3 1.3 copy.41
  171.7 1.3 select_n.115
  172.9 1.2 dynamic_slice.4
  174.2 1.4 compare_select_fusion
  175.5 0.9 collective-permute-done.4
  176.4 10.5 %collective-permute-done.5 = bf16[256,1024]{1,0:T(8,128)(2,1)} collective-permute-done((bf16[256,1024]{1,0:T(8,128)(2,1)}, bf16[256,1024]{1,0:T(8,128)(2,1)}, u32[]{:S(2)}, u32[]{:S(2)}) %collective-permute-start.5) | collective-permute-done | bytes 524320 | tf_op jit(solution)/shard_map/ppermute | solution.py:86
  186.9 2.9 maximum_select_fusion.1.cotangent
  190.1 18.5 %attend.1 = (bf16[512,1024]{1,0:T(8,128)(2,1)S(1)}, f32[8,8,512]{2,1,0:T(8,128)S(1)}) custom-call(bf16[512,1024]{1,0:T(8,128)(2,1)S(1)} %copy-done.4, bf16[2,512,1024]{2,1,0:T(8,128)(2,1)S(1)} %get-tuple-element.44.own.refs_6_, bf16[2,512,1024]{2,1,0:T(8,128)(2,1)} %collective-permute-done.2.other.refs_7_, f32[1024,128]{1,0:T(8,128)S(1)} %broadcast_in_dim.14.bias.refs_8_), custom_call_target="tpu_custom_call" | custom-call | tf_op jit(solution)/shard_map/attend/pallas_call | solution.py:958
  208.7 1.4 fusion.36
  210.4 1.3 multiply_convert_fusion.rows
  211.7 32.6 %feed.1 = (f32[512,1024]{1,0:T(8,128)}, f32[512,1024]{1,0:T(8,128)}, bf16[4,1312,1024]{2,1,0:T(8,128)(2,1)}, bf16[4,656,1024]{2,1,0:T(8,128)(2,1)}) custom-call(bf16[512,1024]{1,0:T(8,128)(2,1)} %multiply_convert_fusion.rows, bf16[512,1024]{1,0:T(8,128)(2,1)} %maximum_select_fusion.1.cotangent, bf16[4,1312,1024]{2,1,0:T(8,128)(2,1)} %get-tuple-element.47.in_weight, ...), custom_call_target="tpu_custom_call" | custom-call | tf_op jit(solution)/shard_map/feed/pallas_call | solution.py:1044
  244.4 2.6 multiply_reduce_fusion
  247.0 3.5 add_convert_fusion
  250.5 2.3 convolution_convert_fusion.1.refs_9_
  252.8 2.6 convolution_convert_fusion
  255.5 143.6 %backward.1 = (f32[768,128]{1,0:T(8,128)}, f32[256,128]{1,0:T(8,128)}, f32[1312,128]{1,0:T(8,128)}, f32[656,128]{1,0:T(8,128)}, bf16[512,1024]{1,0:T(8,128)(2,1)...) custom-call(bf16[4,656,1024]{2,1,0:T(8,128)(2,1)} %get-tuple-element, ...), custom_call_target="tpu_custom_call" | custom-call | tf_op jit(solution)/shard_map/backward/pallas_call | solution.py:518
  399.1 2.6 fusion.19
  401.8 1.3 fusion.37
  403.6 0.7 copy-done.56
  404.3 4.4 fusion.12
  408.7 0.6 pad_maximum_fusion.2.refs_4_
  409.3 1.0 fusion.33
  410.3 0.9 fusion.34
  411.2 0.8 fusion.26
  412.0 0.7 fusion.28
  412.7 37.7 %own_matrix.1 = (bf16[5248,1024]{1,0:T(8,128)(2,1)}, f32[2,1024]{1,0:T(2,128)}) custom-call(bf16[768,128]{1,0:T(8,128)(2,1)} %get-tuple-element.104.refs_0_, bf16[256,128]{1,0:T(8,128)(2,1)} %get-tuple-element.117.refs_1_, bf16[1312,128]{1,0:T(8,128)(2,1)} %get-tuple-element.102.refs_2_, bf16[656,128]{1,0:T(8,128)(2,1)} %get-tuple-element.115.refs_3_, ...), custom_call_target="tpu_custom_call" | custom-call | tf_op jit(solution)/shard_map/own_matrix/pallas_call | solution.py:678
  450.4 55.6 %iterate_owned.1.refs_0_ = bf16[5248,128]{1,0:T(8,128)(2,1)} custom-call(bf16[5248,1024]{1,0:T(8,128)(2,1)} %get-tuple-element.61.whole), custom_call_target="tpu_custom_call" | custom-call | tf_op jit(solution)/shard_map/iterate_owned/pallas_call | solution.py:854
  506.1 65.5 %return_steps.1 = (bf16[768,128]{1,0:T(8,128)(2,1)}, bf16[256,128]{1,0:T(8,128)(2,1)}, bf16[1312,128]{1,0:T(8,128)(2,1)}, bf16[656,128]{1,0:T(8,128)(2,1)}) custom-call(bf16[5248,128]{1,0:T(8,128)(2,1)} %iterate_owned.1.refs_0_), custom_call_target="tpu_custom_call" | custom-call | tf_op jit(solution)/shard_map/return_steps/pallas_call | solution.py:720
  571.6 1.9 convert_multiply_fusion
  573.5 1.0 convert_multiply_fusion.1
  574.5 1.8 bitcast_subtract_fusion.1
  576.3 0.7 bitcast_subtract_fusion.2
  577.0 2.8 fusion.11
  580.1 2.1 collective-permute-start.7
  582.2 0.6 multiply_subtract_fusion.1
  583.0 1.7 copy.49
  584.6 0.9 copy.43
  585.5 1.7 copy.48
  587.2 0.8 bitcast_subtract_fusion
  588.0 0.9 multiply_subtract_fusion
  588.9 3.0 collective-permute-done.6
  591.9 7.1 %collective-permute-done.7 = bf16[256,1024]{1,0:T(8,128)(2,1)} collective-permute-done((bf16[256,1024]{1,0:T(8,128)(2,1)S(1)}, bf16[256,1024]{1,0:T(8,128)(2,1)}, u32[]{:S(2)}, u32[]{:S(2)}) %collective-permute-start.7) | collective-permute-done | bytes 524320 | tf_op jit(solution)/shard_map/ppermute | solution.py:97
  599.0 3.1 fusion.14
  602.0 1.0 copy.51
  (142 shorter events, 4.3 us)
Async XLA Ops:
  2.7 145.4 %collective-permute-start = (bf16[256,1024]{1,0:T(8,128)(2,1)}, bf16[256,1024]{1,0:T(8,128)(2,1)S(1)}, u32[]{:S(2)}, u32[]{:S(2)}) collective-permute-start(bf16[256,1024]{1,0:T(8,128)(2,1)} %get-tuple-element.113), channel_id=1, source_target_pairs={{0,2},{1,0},{2,6},{3,4},{4,3},{5,1},{6,7},{7,5},{8,10},{9,8},{10,1... | collective-permute-start | bytes 1572872 | tf_op jit(solution)/shard_map/ppermute | solution.py:87
  3.4 144.8 %collective-permute-start.1 = (bf16[256,1024]{1,0:T(8,128)(2,1)S(1)}, bf16[256,1024]{1,0:T(8,128)(2,1)S(1)}, u32[]{:S(2)}, u32[]{:S(2)}) collective-permute-start(bf16[256,1024]{1,0:T(8,128)(2,1)S(1)} %get-tuple-element.112), channel_id=1, source_target_pairs={{0,0},{1,2},{2,4},{3,6},{4,1},{5,3},{6,5},{7,7},{8,8},{9,10},{10,1... | collective-permute-start | bytes 1572872 | tf_op jit(solution)/shard_map/ppermute | solution.py:86
  7.5 2.0 copy-start.47
  7.6 2.0 copy-start.48
  9.5 1.8 copy-start.33
  9.5 2.0 copy-start.43
  10.0 138.5 %copy-start.25 = (f32[1024,128]{1,0:T(8,128)}, f32[1024,128]{1,0:T(8,128)S(1)}, u32[]{:S(2)}) copy-start(f32[1024,128]{1,0:T(8,128)S(1)} %pad_maximum_fusion.1.refs_13_) | copy-start | bytes 1572868
  10.0 138.1 %copy-start.45 = (f32[2,1024]{1,0:T(2,128)S(1)}, f32[2,1024]{1,0:T(2,128)}, u32[]{:S(2)}) copy-start(f32[2,1024]{1,0:T(2,128)} %param.21) | copy-start | bytes 24580
  10.5 138.5 %copy-start.26 = (f32[1024,128]{1,0:T(8,128)}, f32[1024,128]{1,0:T(8,128)S(1)}, u32[]{:S(2)}) copy-start(f32[1024,128]{1,0:T(8,128)S(1)} %pad_maximum_fusion.refs_12_) | copy-start | bytes 1572868
  148.1 2.0 copy-start.5
  148.1 3.0 copy-start.7
  148.1 1.4 copy-start.16
  148.2 1.4 copy-start.19
  149.5 9.4 %copy-start = (bf16[512,1024]{1,0:T(8,128)(2,1)}, bf16[512,1024]{1,0:T(8,128)(2,1)S(1)}, u32[]{:S(2)}) copy-start(bf16[512,1024]{1,0:T(8,128)(2,1)S(1)} %fusion.6.rows.refs_4_) | copy-start | bytes 3145732
  151.1 1.6 copy-start.9
  153.6 6.8 %copy-start.31 = (bf16[2,1,256,1024]{3,2,1,0:T(8,128)(2,1)S(1)}, bf16[2,1,256,1024]{3,2,1,0:T(8,128)(2,1)}, u32[]{:S(2)}) copy-start(bf16[2,1,256,1024]{3,2,1,0:T(8,128)(2,1)} %param.15) | copy-start | bytes 3145732
  159.9 30.1 %copy-start.1 = (bf16[2,512,1024]{2,1,0:T(8,128)(2,1)}, bf16[2,512,1024]{2,1,0:T(8,128)(2,1)S(1)}, u32[]{:S(2)}) copy-start(bf16[2,512,1024]{2,1,0:T(8,128)(2,1)S(1)} %get-tuple-element.44.own.refs_6_) | copy-start | bytes 6291460
  159.9 5.1 copy-start.38
  159.9 29.9 %collective-permute-start.2 = (bf16[2,512,1024]{2,1,0:T(8,128)(2,1)S(1)}, bf16[2,512,1024]{2,1,0:T(8,128)(2,1)}, u32[]{:S(2)}, u32[]{:S(2)}) collective-permute-start(bf16[2,512,1024]{2,1,0:T(8,128)(2,1)S(1)} %get-tuple-element.44.own.refs_6_), channel_id=1, source_target_pairs={{0,4},{4,0},{8,12},{12,8},{16,20},{20,16},{24,28},{28,24},{1,5},{5... | collective-permute-start | bytes 6291464 | tf_op jit(solution)/shard_map/ppermute | solution.py:104
  159.9 9.1 %collective-permute-start.3 = (s32[2,1]{0,1:T(1,128)}, s32[2,1]{0,1:T(1,128)}, u32[]{:S(2)}, u32[]{:S(2)}) collective-permute-start(s32[2,1]{0,1:T(1,128)} %param.16), channel_id=1, source_target_pairs={{0,4},{4,0},{8,12},{12,8},{16,20},{20,16},{24,28},{28,24},{1,5},{5... | collective-permute-start | bytes 32 | tf_op jit(solution)/shard_map/ppermute | solution.py:104
  161.6 14.9 %collective-permute-start.4 = (bf16[256,1024]{1,0:T(8,128)(2,1)}, bf16[256,1024]{1,0:T(8,128)(2,1)}, u32[]{:S(2)}, u32[]{:S(2)}) collective-permute-start(bf16[256,1024]{1,0:T(8,128)(2,1)} %get-tuple-element.110), channel_id=1, source_target_pairs={{0,2},{1,0},{2,6},{3,4},{4,3},{5,1},{6,7},{7,5},{8,10},{9,8},{10,1... | collective-permute-start | bytes 1572872 | tf_op jit(solution)/shard_map/ppermute | solution.py:87
  161.6 25.4 %collective-permute-start.5 = (bf16[256,1024]{1,0:T(8,128)(2,1)}, bf16[256,1024]{1,0:T(8,128)(2,1)}, u32[]{:S(2)}, u32[]{:S(2)}) collective-permute-start(bf16[256,1024]{1,0:T(8,128)(2,1)} %get-tuple-element.111), channel_id=1, source_target_pairs={{0,0},{1,2},{2,4},{3,6},{4,1},{5,3},{6,5},{7,7},{8,8},{9,10},{10,1... | collective-permute-start | bytes 1572872 | tf_op jit(solution)/shard_map/ppermute | solution.py:86
  165.3 24.8 %copy-start.4 = (bf16[512,1024]{1,0:T(8,128)(2,1)S(1)}, bf16[512,1024]{1,0:T(8,128)(2,1)}, u32[]{:S(2)}) copy-start(bf16[512,1024]{1,0:T(8,128)(2,1)} %copy-done.3) | copy-start | bytes 3145732
  190.1 18.6 %copy-start.2 = (f32[1024,128]{1,0:T(8,128)}, f32[1024,128]{1,0:T(8,128)S(1)}, u32[]{:S(2)}) copy-start(f32[1024,128]{1,0:T(8,128)S(1)} %broadcast_in_dim.14.bias.refs_8_) | copy-start | bytes 1572868
  190.1 18.6 %copy-start.17 = (bf16[256,1024]{1,0:T(8,128)(2,1)S(1)}, bf16[256,1024]{1,0:T(8,128)(2,1)}, u32[]{:S(2)}) copy-start(bf16[256,1024]{1,0:T(8,128)(2,1)} %copy-done.16) | copy-start | bytes 1572868
  190.1 18.6 %copy-start.20 = (bf16[256,1024]{1,0:T(8,128)(2,1)S(1)}, bf16[256,1024]{1,0:T(8,128)(2,1)}, u32[]{:S(2)}) copy-start(bf16[256,1024]{1,0:T(8,128)(2,1)} %copy-done.19) | copy-start | bytes 1572868
  190.1 18.6 %copy-start.54 = (bf16[4,256,1024]{2,1,0:T(8,128)(2,1)S(1)}, bf16[4,256,1024]{2,1,0:T(8,128)(2,1)}, u32[]{:S(2)}) copy-start(bf16[4,256,1024]{2,1,0:T(8,128)(2,1)} %get-tuple-element.46) | copy-start | bytes 6291460
  208.6 1.4 copy-start.11
  208.7 1.4 copy-start.14
  244.4 2.6 copy-start.15
  244.4 2.6 copy-start.24
  247.0 3.5 copy-start.55
  250.5 2.3 copy-start.22
  250.5 2.3 copy-start.12
  255.5 143.6 %copy-start.10 = (bf16[4,256,1024]{2,1,0:T(8,128)(2,1)S(1)}, bf16[4,256,1024]{2,1,0:T(8,128)(2,1)}, u32[]{:S(2)}) copy-start(bf16[4,256,1024]{2,1,0:T(8,128)(2,1)} %get-tuple-element.41.key_weight) | copy-start | bytes 6291460
  399.1 2.7 copy-start.8
  399.1 2.7 copy-start.57
  401.8 1.6 copy-start.6
  401.8 1.7 copy-start.18
  401.8 1.8 copy-start.21
  401.8 2.5 copy-start.56
  404.3 5.0 copy-start.28
  404.3 5.0 copy-start.35
  408.7 1.7 copy-start.39
  408.7 2.5 copy-start.40
  408.7 2.5 copy-start.41
  409.3 2.8 copy-start.37
  409.3 2.8 copy-start.42
  506.1 70.9 %copy-start.23 = (f32[512,1024]{1,0:T(8,128)S(1)}, f32[512,1024]{1,0:T(8,128)}, u32[]{:S(2)}) copy-start(f32[512,1024]{1,0:T(8,128)} %copy-done.22) | copy-start | bytes 6291460
  571.5 4.7 copy-start.36
  571.6 4.7 copy-start.44
  571.6 5.4 copy-start.53
  571.6 5.4 copy-start.52
  579.8 2.3 copy-start.46
  579.8 2.3 copy-start.49
  579.8 2.3 copy-start.50
  579.8 2.3 copy-start.51
  579.9 4.8 copy-start.29
  579.9 7.3 %copy-start.34 = (bf16[128,3,256]{2,0,1:T(8,128)(2,1)S(1)}, bf16[128,3,256]{2,0,1:T(8,128)(2,1)}, u32[]{:S(2)}) copy-start(bf16[128,3,256]{2,0,1:T(8,128)(2,1)} %param.17) | copy-start | bytes 589828
  580.0 8.0 %copy-start.27 = (f32[1312,128]{1,0:T(8,128)S(1)}, f32[1312,128]{1,0:T(8,128)}, u32[]{:S(2)}) copy-start(f32[1312,128]{1,0:T(8,128)} %convert_multiply_fusion) | copy-start | bytes 2015236
  580.0 8.0 %copy-start.30 = (bf16[128,2,656]{0,2,1:T(8,128)(2,1)S(1)}, bf16[128,2,656]{0,2,1:T(8,128)(2,1)}, u32[]{:S(2)}) copy-start(bf16[128,2,656]{0,2,1:T(8,128)(2,1)} %param.19) | copy-start | bytes 1007620
  580.0 11.9 %collective-permute-start.6 = (bf16[256,1024]{1,0:T(8,128)(2,1)S(1)}, bf16[256,1024]{1,0:T(8,128)(2,1)}, u32[]{:S(2)}, u32[]{:S(2)}) collective-permute-start(bf16[256,1024]{1,0:T(8,128)(2,1)S(1)} %get-tuple-element.108), channel_id=1, source_target_pairs={{2,0},{0,1},{6,2},{4,3},{3,4},{1,5},{7,6},{5,7},{10,8},{8,9},{14,1... | collective-permute-start | bytes 1572872 | tf_op jit(solution)/shard_map/ppermute | solution.py:98
  580.1 18.9 %collective-permute-start.7 = (bf16[256,1024]{1,0:T(8,128)(2,1)S(1)}, bf16[256,1024]{1,0:T(8,128)(2,1)}, u32[]{:S(2)}, u32[]{:S(2)}) collective-permute-start(bf16[256,1024]{1,0:T(8,128)(2,1)S(1)} %get-tuple-element.109), channel_id=1, source_target_pairs={{0,0},{2,1},{4,2},{6,3},{1,4},{3,5},{5,6},{7,7},{8,8},{10,9},{12,1... | collective-permute-start | bytes 1572872 | tf_op jit(solution)/shard_map/ppermute | solution.py:97
  588.0 14.0 %copy-start.32 = (bf16[2,256,1024]{2,1,0:T(8,128)(2,1)S(1)}, bf16[2,256,1024]{2,1,0:T(8,128)(2,1)}, u32[]{:S(2)}) copy-start(bf16[2,256,1024]{2,1,0:T(8,128)(2,1)} %get-tuple-element.54) | copy-start | bytes 3145732
  (2 other events, 1.9 us)

commit v4 on v3

--- a/solution.py
+++ b/solution.py
@@ -157,96 +157,6 @@
             pl.semaphore_signal(barrier, inc=1, device_id=(same_place, other), device_id_type=MESH)
     pl.semaphore_wait(barrier, len(others) + len(planes) * (1 + len(crossed)))
 
-def gather_kernel(count, *refs):
-    shards, wholes = refs[:count], refs[count : 2 * count]
-    (own_sem, send_z, recv_z, send_x, recv_x, send_y, recv_y, send_d, recv_d, send_c, recv_c) = refs[2 * count :]
-    me, partner, across, down = neighbours()
-    plane = lax.axis_index("tensor")
-    diagonal = across + down - me
-    planes = [lax.rem(plane + offset, 4) for offset in (1, 2, 3)]
-    greet(plane, (partner, across, down), planes)
-    started = []
-
-    def remote(source, target, send, recv, device):
-        copy = pltpu.make_async_remote_copy(source, target, send, recv, device_id=device, device_id_type=MESH)
-        copy.start()
-        started.append(copy)
-
-    def spread(part, source, slot, block):
-        view = wholes[part].at[slot, :, lanes(block)]
-        remote(source, view, send_x.at[part, slot], recv_x.at[part, slot], (across, plane))
-        remote(source, view, send_y.at[part, slot], recv_y.at[part, slot], (down, plane))
-        remote(source, view, send_c.at[part, slot, 0], recv_c.at[part, slot, 0], (partner, plane))
-
-    def landed(part, slot, block, sem):
-        view = wholes[part].at[slot, :, lanes(block)]
-        pltpu.make_async_copy(view, view, sem).wait()
-        return view
-
-    locals_ = []
-    def stage_first(part):
-        view = wholes[part].at[plane, :, lanes(me)]
-        copy = pltpu.make_async_copy(shards[part], view, own_sem.at[part])
-        copy.start()
-        locals_.append(copy)
-        for index, other in enumerate(planes):
-            remote(shards[part], view, send_z.at[part, index], recv_z.at[part, index], (me, other))
-        spread(part, shards[part], plane, me)
-
-    def stage_z(part):
-        for index, offset in enumerate((1, 2, 3)):
-            slot = lax.rem(plane + 4 - offset, 4)
-            view = landed(part, slot, me, recv_z.at[part, index])
-            spread(part, view, slot, me)
-
-    def stage_xy(part):
-        for slot in range(4):
-            view = landed(part, slot, across, recv_x.at[part, slot])
-            remote(view, view, send_c.at[part, slot, 1], recv_c.at[part, slot, 1], (partner, plane))
-            if slot < 2:
-                remote(view, view, send_d.at[part, slot], recv_d.at[part, slot], (down, plane))
-            view = landed(part, slot, down, recv_y.at[part, slot])
-            remote(view, view, send_c.at[part, slot, 2], recv_c.at[part, slot, 2], (partner, plane))
-            if slot >= 2:
-                remote(view, view, send_d.at[part, slot], recv_d.at[part, slot], (across, plane))
-
-    def stage_diagonal(part):
-        for slot in range(4):
-            view = landed(part, slot, diagonal, recv_d.at[part, slot])
-            remote(view, view, send_c.at[part, slot, 3], recv_c.at[part, slot, 3], (partner, plane))
-
-    stages = (stage_first, stage_z, stage_xy, stage_diagonal)
-    for part in range(count):
-        stage_first(part)
-    for step in range(count + 2):
-        for stage in (3, 2, 1):
-            part = step - (stage - 1)
-            if 0 <= part < count:
-                stages[stage](part)
-    flip = lambda block: block + 1 - 2 * lax.rem(block, 2)
-    for part in range(count):
-        for slot in range(4):
-            for index, block in enumerate((me, across, down, diagonal)):
-                landed(part, slot, flip(block), recv_c.at[part, slot, index])
-    for copy in locals_:
-        copy.wait()
-    for copy in started:
-        copy.wait_send()
-
-def gather_blocks(shards, collective_id):
-    count = len(shards)
-    sem = pltpu.SemaphoreType.DMA
-    return pl.pallas_call(
-        functools.partial(gather_kernel, count),
-        out_shape=[jax.ShapeDtypeStruct((4, s.shape[0], 1024), s.dtype) for s in shards],
-        in_specs=[pl.BlockSpec(memory_space=pl.ANY)] * count,
-        out_specs=[pl.BlockSpec(memory_space=pl.ANY)] * count,
-        scratch_shapes=[sem((count,)), sem((count, 3)), sem((count, 3))] + [sem((count, 4))] * 6 + [sem((count, 4, 4))] * 2,
-        compiler_params=pltpu.CompilerParams(collective_id=collective_id, has_side_effects=True),
-        name="gather_blocks",
-    )(*shards)
-
-
 def add_into(target, source, rows, step):
     @pl.loop(0, rows // step)
     def _(index):
@@ -430,16 +340,305 @@
     return taken
 
 
+def gather_plan(shards, wholes, sems):
+    own_sem, send_up, send_down, recv_z, send_x, recv_x, send_y, recv_y, send_d, recv_d, send_c, recv_c = sems
+    me, partner, across, down = neighbours()
+    plane = lax.axis_index("tensor")
+    diagonal = across + down - me
+    flip = lambda block: block + 1 - 2 * lax.rem(block, 2)
+
+    def place(part, slot, block):
+        return wholes[part].at[slot, :, lanes(block)]
+
+    def spread(part, source, slot):
+        view = place(part, slot, me)
+        send_to(source, view, send_x.at[part, slot], recv_x.at[part, slot], (across, plane))
+        send_to(source, view, send_y.at[part, slot], recv_y.at[part, slot], (down, plane))
+        send_to(source, view, send_c.at[part, slot, 0], recv_c.at[part, slot, 0], (partner, plane))
+
+    def pass_on(part, source, slot, upward):
+        view = place(part, slot, me)
+        sem = (send_up if upward else send_down).at[part, slot]
+        send_to(source, view, sem, recv_z.at[part, slot], (me, plane + 1 if upward else plane - 1))
+
+    def stage_own(part):
+        pltpu.make_async_copy(shards[part], place(part, plane, me), own_sem.at[part]).start()
+
+        @pl.when(plane < 3)
+        def _():
+            pass_on(part, shards[part], plane, True)
+
+        @pl.when(plane > 0)
+        def _():
+            pass_on(part, shards[part], plane, False)
+
+        spread(part, shards[part], plane)
+
+    def stage_z(part):
+        for distance in (1, 2, 3):
+            for upward in (True, False):
+                slot = plane - distance if upward else plane + distance
+
+                @pl.when(slot >= 0 if upward else slot <= 3)
+                def _():
+                    view = place(part, slot, me)
+                    wait_for(view, recv_z.at[part, slot])
+
+                    @pl.when(plane < 3 if upward else plane > 0)
+                    def _():
+                        pass_on(part, view, slot, upward)
+
+                    spread(part, view, slot)
+
+    def stage_xy(part):
+        for slot in range(4):
+            view = place(part, slot, across)
+            wait_for(view, recv_x.at[part, slot])
+            if slot < 2:
+                send_to(view, view, send_d.at[part, slot], recv_d.at[part, slot], (down, plane))
+            send_to(view, view, send_c.at[part, slot, 1], recv_c.at[part, slot, 1], (partner, plane))
+            view = place(part, slot, down)
+            wait_for(view, recv_y.at[part, slot])
+            if slot >= 2:
+                send_to(view, view, send_d.at[part, slot], recv_d.at[part, slot], (across, plane))
+            send_to(view, view, send_c.at[part, slot, 2], recv_c.at[part, slot, 2], (partner, plane))
+
+    def stage_diagonal(part):
+        for slot in range(4):
+            view = place(part, slot, diagonal)
+            wait_for(view, recv_d.at[part, slot])
+            send_to(view, view, send_c.at[part, slot, 3], recv_c.at[part, slot, 3], (partner, plane))
+
+    def arrive(part):
+        wait_for(shards[part], own_sem.at[part])
+        for slot in range(4):
+            for index, block in enumerate((me, across, down, diagonal)):
+                wait_for(place(part, slot, flip(block)), recv_c.at[part, slot, index])
+
+    def finish(part):
+        for slot in range(4):
+            @pl.when(jnp.logical_and(slot <= plane, plane < 3))
+            def _():
+                wait_for(shards[part], send_up.at[part, slot])
+
+            @pl.when(jnp.logical_and(slot >= plane, plane > 0))
+            def _():
+                wait_for(shards[part], send_down.at[part, slot])
+
+            for sem in (send_x, send_y, send_d):
+                wait_for(shards[part], sem.at[part, slot])
+            for index in range(4):
+                wait_for(shards[part], send_c.at[part, slot, index])
+
+    return (stage_own, stage_z, stage_xy, stage_diagonal, arrive, finish)
+
+
+def normed_rows(rows, gain):
+    centre = rows - jnp.mean(rows, axis=1, keepdims=True)
+    inverse = lax.rsqrt(jnp.mean(centre * centre, axis=1, keepdims=True) + NORM_EPS)
+    return centre * inverse * gain
+
+
+def forward_kernel(*refs):
+    refs = list(refs)
+    shards, (inputs, cotangent, lengths, gains, cosine, sine) = take(refs, 6), take(refs, 6)
+    wholes, (rows_low, grad_rows) = take(refs, 6), take(refs, 2)
+    low_one, queries, own, other, context, log_total, bias, middle, low_two = take(refs, 9)
+    other_lengths, weight, attn_weight = take(refs, 3)
+    sems = take(refs, 12)
+    pair_send, pair_recv, length_send, length_recv, weight_sem, attn_sem = take(refs, 6)
+    move_send, move_recv, move_own = refs
+    me, partner, across, down = neighbours()
+    plane = lax.axis_index("tensor")
+    core = lax.rem(me, 2)
+    stage_own, stage_z, stage_xy, stage_diagonal, arrive, finish = gather_plan(shards, wholes, sems)
+    moves = [
+        move_plan(False, source, target, move_send.at[index], move_recv.at[index], move_own.at[index])
+        for index, (source, target) in enumerate(((inputs, rows_low), (cotangent, grad_rows)))
+    ]
+    greet(plane, (partner, across, down), [lax.rem(plane + offset, 4) for offset in (1, 2, 3)])
+    count, width = rows_low.shape
+    third = shards[0].shape[0]
+    step = 64
+
+    stage_own(0)
+    stage_own(1)
+    send_to(lengths, other_lengths, length_send, length_recv, (partner, plane))
+    stage_z(0)
+    stage_own(2)
+    stage_z(1)
+    stage_xy(0)
+    stage_own(3)
+    stage_z(2)
+    stage_xy(1)
+    stage_diagonal(0)
+    stage_own(4)
+    stage_z(3)
+    stage_xy(2)
+    stage_diagonal(1)
+    stage_own(5)
+    stage_z(4)
+    moves[0][0]()
+    stage_xy(3)
+    stage_diagonal(2)
+    stage_z(5)
+    moves[1][0]()
+    stage_diagonal(3)
+    stage_xy(4)
+    wait_for(other_lengths, length_recv)
+    mine = core == lax.rem(plane, 2)
+    both = jnp.where(mine, lengths[...], other_lengths[...])
+    length = jnp.where(plane < 2, both[0:1], both[1:2])
+    position = lax.broadcasted_iota(jnp.int32, bias.shape, 0)
+    position = lax.rem(position + core * count, 2 * count).astype(jnp.float32)
+    bias[...] = jnp.where(position < length, 0.0, MASK_VALUE)
+    moves[0][1]()
+
+    @pl.loop(0, count // step)
+    def _(index):
+        window = pl.ds(pl.multiple_of(index * step, step), step)
+        low_one[window] = low(normed_rows(rows_low[window].astype(jnp.float32), gains[0:1]))
+
+    for part in range(3):
+        arrive(part)
+
+    def load(group):
+        for part in range(3):
+            slot = lax.rem(group, 2)
+            pltpu.make_async_copy(wholes[part].at[group], weight.at[slot, part], weight_sem.at[slot, part]).start()
+
+    load(0)
+
+    @pl.loop(0, 4)
+    def _(group):
+        @pl.when(group < 3)
+        def _():
+            load(group + 1)
+
+        slot = lax.rem(group, 2)
+        for part in range(3):
+            wait_for(weight.at[slot, part], weight_sem.at[slot, part])
+            result = product_of(low_one[...], weight[slot, part], ((1,), (1,)))
+            for first in range(0, third, 128):
+                columns = pl.ds(pl.multiple_of(group * third + first, 128), 128)
+                piece = result[:, first : first + 128]
+                if part < 2:
+                    piece = turned(piece, cosine[0:count], sine[0:count])
+                if part == 0:
+                    queries[:, columns] = low(piece * SCORE_SCALE)
+                else:
+                    own[part - 1, :, columns] = low(piece)
+
+    send_to(own, other, pair_send, pair_recv, (partner, plane))
+    wait_for(other, pair_recv)
+    arrive(3)
+    attn_copy = pltpu.make_async_copy(wholes[3], attn_weight, attn_sem)
+    attn_copy.start()
+    schedule = {3: (stage_xy, 5), 6: (stage_diagonal, 4)}
+
+    @pl.loop(0, width // 128)
+    def _(index):
+        for place, (stage, part) in schedule.items():
+            @pl.when(index == place)
+            def _():
+                stage(part)
+
+        attend_pair(lanes(index), queries, own, other, bias, context, log_total.at[index])
+
+    attn_copy.wait()
+
+    @pl.loop(0, count // 128)
+    def _(index):
+        window = pl.ds(pl.multiple_of(index * 128, 128), 128)
+        rows = rows_low[window].astype(jnp.float32)
+        for group in range(4):
+            piece = context[window, third * group : third * group + third]
+            rows = rows + product_of(piece, attn_weight[group], ((1,), (0,)))
+        middle[window] = rows
+        low_two[window] = low(normed_rows(rows, gains[1:2]))
+
+    stage_diagonal(5)
+    for part in (4, 5):
+        arrive(part)
+    for part in range(6):
+        finish(part)
+    wait_for(own, pair_send)
+    wait_for(lengths, length_send)
+    moves[1][1]()
+
+
+def forward(shards, inputs, cotangent, lengths, gains, cosine, sine, collective_id):
+    sem = pltpu.SemaphoreType.DMA
+    anywhere = pl.BlockSpec(memory_space=pl.ANY)
+    local = pl.BlockSpec(memory_space=pltpu.VMEM)
+    bf16, f32 = jnp.bfloat16, jnp.float32
+    count, width = 2 * inputs.shape[1], inputs.shape[2]
+    third = shards[0].shape[0]
+    shape = jax.ShapeDtypeStruct
+    return pl.pallas_call(
+        forward_kernel,
+        out_shape=[shape((4, shard.shape[0], width), bf16) for shard in shards]
+        + [
+            shape((count, width), bf16),
+            shape((count, width), bf16),
+            shape((count, width), bf16),
+            shape((count, width), bf16),
+            shape((2, count, width), bf16),
+            shape((2, count, width), bf16),
+            shape((count, width), bf16),
+            shape((width // 128, 8, count), f32),
+            shape((2 * count, 128), f32),
+            shape((count, width), f32),
+            shape((count, width), bf16),
+        ],
+        in_specs=[anywhere] * 8 + [local] * 4,
+        out_specs=[anywhere] * 6 + [local, anywhere] + [local] * 9,
+        scratch_shapes=[
+            pltpu.VMEM(lengths.shape, f32),
+            pltpu.VMEM((2, 3, third, width), bf16),
+            pltpu.VMEM((4, third, width), bf16),
+            sem((6,)),
+        ]
+        + [sem((6, 4))] * 9
+        + [sem((6, 4, 4))] * 2
+        + [sem, sem, sem, sem, sem((2, 3)), sem]
+        + [sem((2, 2)), sem((2, 2)), sem((2,))],
+        compiler_params=pltpu.CompilerParams(
+            collective_id=collective_id, has_side_effects=True, vmem_limit_bytes=58 * 1024 * 1024
+        ),
+        name="forward",
+    )(*shards, inputs, cotangent, lengths, gains, cosine, sine)
+
+
+def attend_pair(columns, queries, own, other, bias, context, log_total):
+    query_turned = queries[:, columns].T
+    keys = jnp.concatenate([own[0, :, columns], other[0, :, columns]], axis=0)
+    value_turned = jnp.concatenate([own[1, :, columns].T, other[1, :, columns].T], axis=1)
+    parts, logs = [], []
+    for head in range(2):
+        scores = scores_of(keys, head_rows(query_turned, head), bias[...])
+        highest = jnp.max(scores, axis=0, keepdims=True)
+        weights = jnp.exp(scores - highest)
+        total = jnp.sum(weights, axis=0, keepdims=True)
+        part = product_of(value_turned[64 * head : 64 * head + 64], low(weights), ((1,), (0,)))
+        parts.append(part / total)
+        logs.append(highest + jnp.log(total))
+    context[:, columns] = low(jnp.concatenate(parts, axis=0)).T
+    log_total[...] = jnp.concatenate(logs + logs * 3, axis=0)
+
+
 def backward_kernel(*refs):
     refs = list(refs)
     grad_out, grad_in, grad_attn, rows_in = take(refs, 4)
-    low_rows, queries, own, other, bias, grad, context, log_total, cosine, sine = take(refs, 10)
-    sums, (grad_query, grad_pair), (rows_out,) = take(refs, 4), take(refs, 2), take(refs, 1)
+    far, (bias, log_total, cosine, sine) = take(refs, 6), take(refs, 4)
+    sums, (far_query, far_pair), (rows_out,) = take(refs, 4), take(refs, 2), take(refs, 1)
     weight_grads = take(refs, 3)
+    near, (grad_query, grad_pair) = take(refs, 6), take(refs, 2)
+    low_rows, queries, own, other, grad, context = near
     grad_other, arrived, staged = take(refs, 3)
     buffers = [take(refs, 7) for _ in range(6)] + [take(refs, 1)]
     sems = take(refs, 13)
-    pair_send, pair_recv, stage_sem, move_send, move_recv, move_own = refs
+    pair_send, pair_recv, stage_sem, load_sem, out_sem, move_send, move_recv, move_own = refs
     me, partner, across, down = neighbours()
     plane = lax.axis_index("tensor")
     height, third = grad_out.shape[1], grad_attn.shape[1]
@@ -451,10 +650,36 @@
     stages, finish = scatter_plan(parts, targets, buffers, sems)
     start_move, finish_move = move_plan(True, rows_in, rows_out, move_send, move_recv, move_own)
     greet(plane, (partner, across, down), [lax.rem(plane + offset, 4) for offset in (1, 2, 3)])
+    copies = [
+        pltpu.make_async_copy(source, target, load_sem.at[index])
+        for index, (source, target) in enumerate(zip(far, near))
+    ]
     stages[0](0)
-    schedule = {0: ((0, 1),), 1: ((1, 0), (0, 2)), 3: ((1, 1), (0, 3)), 6: ((2, 0),), 7: ((1, 2),)}
-
-    @pl.loop(0, queries.shape[1] // 128)
+    for copy in copies:
+        copy.start()
+    start_move()
+    schedule = {
+        0: ((1, 0), (0, 1)),
+        4: ((2, 0), (1, 1), (0, 2), (0, 3)),
+        7: ((3, 0),),
+    }
+    for copy in copies[1:]:
+        copy.wait()
+
+    def exchanged(index):
+        return (arrived.at[:, :, lanes(index)], pair_recv.at[index])
+
+    def add_pair(index):
+        wait_for(*exchanged(index))
+        columns = lanes(index)
+        for which in range(2):
+            total = grad_pair[which, :, columns].astype(jnp.float32)
+            total = total + arrived[which, :, columns].astype(jnp.float32)
+            grad_pair[which, :, columns] = low(total)
+
+    last_pair = queries.shape[1] // 128 - 1
+
+    @pl.loop(0, last_pair + 1)
     def _(index):
         for position, calls in schedule.items():
             @pl.when(index == position)
@@ -463,9 +688,16 @@
                     stages[stage](part)
 
         attend_back_pair(lanes(index), queries, own, other, bias, grad, context, log_total.at[index], cosine, sine, grad_query, grad_pair, grad_other)
-
-    send_to(grad_other, arrived, pair_send, pair_recv, (partner, plane))
-    start_move()
+        target, sem = exchanged(index)
+        send_to(grad_other.at[:, :, lanes(index)], target, pair_send.at[index], sem, (partner, plane))
+
+        @pl.when(index > 0)
+        def _():
+            add_pair(index - 1)
+
+    copies[0].wait()
+    query_copy = pltpu.make_async_copy(grad_query, far_query, out_sem.at[0])
+    query_copy.start()
 
     def weight_grad(which, values):
         target = weight_grads[which]
@@ -481,29 +713,24 @@
 
     weight_grad(0, grad_query)
     stages[0](4)
-    stages[2](1)
-    wait_for(arrived, pair_recv)
-    step = 128
-
-    @pl.loop(0, grad_pair.shape[1] // step)
-    def _(index):
-        window = pl.ds(pl.multiple_of(index * step, step), step)
-        total = grad_pair[:, window].astype(jnp.float32) + arrived[:, window].astype(jnp.float32)
-        grad_pair[:, window] = low(total)
-
+    add_pair(last_pair)
+    pair_copy = pltpu.make_async_copy(grad_pair, far_pair, out_sem.at[1])
+    pair_copy.start()
     weight_grad(1, grad_pair.at[0])
     stages[0](5)
-    stages[1](3)
     weight_grad(2, grad_pair.at[1])
     stages[0](6)
     calls = [(stage, step - (stage - 1)) for step in range(10) for stage in (4, 3, 2, 1)]
-    done = {(1, 0), (1, 1), (1, 2), (1, 3), (2, 0), (2, 1)}
+    done = {(1, 0), (2, 0), (1, 1), (3, 0)}
     for stage, part in calls:
         if 0 <= part < 7 and (stage, part) not in done:
             stages[stage](part)
     for part in range(7):
         finish(part)
-    wait_for(grad_other, pair_send)
+    for index in range(last_pair + 1):
+        wait_for(arrived.at[:, :, lanes(index)], pair_send.at[index])
+    query_copy.wait()
+    pair_copy.wait()
     finish_move()
 
 
@@ -527,21 +754,26 @@
             jax.ShapeDtypeStruct((2, count // 2, width), rows_in.dtype),
         ]
         + [jax.ShapeDtypeStruct(grad_attn.shape, bf16)] * 3,
-        in_specs=[anywhere] * 4 + [local] * 10,
-        out_specs=[local] * 6 + [anywhere] * 4,
+        in_specs=[anywhere] * 10 + [local] * 4,
+        out_specs=[local] * 4 + [anywhere] * 6,
         scratch_shapes=[
+            pltpu.VMEM(rows.shape, bf16) for rows in (low_rows, queries, own, other, grad, context)
+        ]
+        + [
+            pltpu.VMEM((count, width), bf16),
+            pltpu.VMEM((2, count, width), bf16),
             pltpu.VMEM((2, count, width), bf16),
             pltpu.VMEM((2, count, width), bf16),
             pltpu.VMEM((2, third, width), bf16),
         ]
         + buffers
         + sems
-        + [sem, sem, sem((2,)), sem((2,)), sem((2,)), sem],
+        + [sem((8,)), sem((8,)), sem((2,)), sem((6,)), sem((2,)), sem((2,)), sem((2,)), sem],
         compiler_params=pltpu.CompilerParams(
             collective_id=collective_id, has_side_effects=True, vmem_limit_bytes=60 * 1024 * 1024
         ),
         name="backward",
-    )(grad_out, grad_in, grad_attn, rows_in, low_rows, queries, own, other, bias, grad, context, log_total, cosine, sine)
+    )(grad_out, grad_in, grad_attn, rows_in, low_rows, queries, own, other, grad, context, bias, log_total, cosine, sine)
     return outs[:7]
 
 
@@ -862,13 +1094,14 @@
     )(whole)
 
 
-def gather_weights(weights):
-    tensor_count, dp_count = lax.axis_size("tensor"), lax.axis_size("dp")
+def weight_shards(weights):
     shards = [turn(weight) for weight in weights]
     third = shards[0].shape[0] // 3
-    shards = [shards[0][third * part : third * part + third] for part in range(3)] + shards[1:]
-    if (tensor_count, dp_count, shards[0].shape[1]) == (4, 8, 128):
-        return gather_blocks(shards, 1)
+    return [shards[0][third * part : third * part + third] for part in range(3)] + shards[1:]
+
+
+def gather_weights(shards):
+    tensor_count, dp_count = lax.axis_size("tensor"), lax.axis_size("dp")
     wholes = [lax.all_gather(shard, ("tensor", "dp")) for shard in shards]
     wholes = [
         whole.reshape(tensor_count, dp_count, *whole.shape[1:]).transpose(0, 2, 1, 3)
@@ -1117,38 +1350,49 @@
     weights = (qkv_weight, attn_out_weight, ffn_in_weight, ffn_out_weight)
     row_count = qkv_weight.shape[0]
 
-    rows_low = to_sequences(inputs[:, 0], lists, odd, upper)
-    query_all, key_all, value_all, attn_all, ffn_in_all, ffn_out_all = gather_weights(weights)
-    cotangent_low = to_sequences(cotangent[:, 0], lists, odd, upper)
-    rows_in = rows_low.astype(jnp.float32)
-    grad_rows = cotangent_low.astype(jnp.float32)
-    local_rows = rows_in.shape[0]
-    own_lengths = swap_partner(lengths)
-    both_lengths = jnp.where(
-        core == 0,
-        jnp.concatenate([lengths, own_lengths], 1),
-        jnp.concatenate([own_lengths, lengths], 1),
-    )
-    length = lax.dynamic_index_in_dim(both_lengths.reshape(-1), tensor_index, 0, keepdims=False)
+    width = inputs.shape[3]
+    local_rows = 2 * inputs.shape[2]
+    fits = (tensor_count, dp_count, row_count, width) == (4, 8, 128, 1024)
     positions = jnp.concatenate(
         [core * local_rows + jnp.arange(local_rows), (1 - core) * local_rows + jnp.arange(local_rows)]
     )
     cosine, sine = rotary(positions)
-    bias = jnp.where(positions < length, 0.0, MASK_VALUE).astype(jnp.float32)
-    bias = jnp.broadcast_to(bias[:, None], (positions.shape[0], 128))
-
+    shards = weight_shards(weights)
+    if fits:
+        sizes = lengths.astype(jnp.float32)
+        sizes = jnp.broadcast_to(jnp.pad(sizes, ((0, 6), (0, 0))), (8, 128))
+        outs = forward(shards, inputs[:, 0], cotangent[:, 0], sizes, norm_gains, cosine, sine, 1)
+        wholes, (rows_low, cotangent_low) = outs[:6], outs[6:8]
+        low_one, queries, own, other, context, log_total, bias, middle, low_two = outs[8:]
+    else:
+        wholes = gather_weights(shards)
+        rows_low = to_sequences(inputs[:, 0], lists, odd, upper)
+        cotangent_low = to_sequences(cotangent[:, 0], lists, odd, upper)
+    query_all, key_all, value_all, attn_all, ffn_in_all, ffn_out_all = wholes
+    attn_rows = attn_all.reshape(-1, width)
+    rows_in = rows_low.astype(jnp.float32)
+    grad_rows = cotangent_low.astype(jnp.float32)
     normed_one, inverse_one, scaled_one = layer_norm_parts(rows_in, norm_gains[0])
-    low_one = low(scaled_one)
-    width = rows_in.shape[1]
-    attn_rows = attn_all.reshape(-1, width)
-    queries, own = project(
-        low_one, query_all, key_all, value_all, cosine[:local_rows], sine[:local_rows]
-    )
-    other = swap_partner(own)
-    context, log_total = attend(queries, own, other, bias)
-    middle = rows_in + einsum("sk,kn->sn", context, attn_rows)
+    if not fits:
+        own_lengths = swap_partner(lengths)
+        both_lengths = jnp.where(
+            core == 0,
+            jnp.concatenate([lengths, own_lengths], 1),
+            jnp.concatenate([own_lengths, lengths], 1),
+        )
+        length = lax.dynamic_index_in_dim(both_lengths.reshape(-1), tensor_index, 0, keepdims=False)
+        bias = jnp.where(positions < length, 0.0, MASK_VALUE).astype(jnp.float32)
+        bias = jnp.broadcast_to(bias[:, None], (positions.shape[0], 128))
+        low_one = low(scaled_one)
+        queries, own = project(
+            low_one, query_all, key_all, value_all, cosine[:local_rows], sine[:local_rows]
+        )
+        other = swap_partner(own)
+        context, log_total = attend(queries, own, other, bias)
+        middle = rows_in + einsum("sk,kn->sn", context, attn_rows)
     normed_two, inverse_two, scaled_two = layer_norm_parts(middle, norm_gains[1])
-    low_two = low(scaled_two)
+    if not fits:
+        low_two = low(scaled_two)
     ffn_branch, grad_scaled_two, grad_ffn_in, grad_ffn_out = feed(
         low_two, cotangent_low, ffn_in_all, ffn_out_all
     )
@@ -1160,7 +1404,6 @@
     grad_branch = low(grad_middle)
     grad_context = low(einsum("sn,kn->sk", grad_branch, attn_rows))
     grad_attn_out = low(einsum("sk,sn->kn", context, grad_branch)).reshape(attn_all.shape)
-    fits = (tensor_count, dp_count, row_count, width) == (4, 8, 128, 1024)
     attention = (queries, own, other, bias, grad_context, context, log_total, cosine, sine)
     if fits:
         outs = backward(grad_ffn_out, grad_ffn_in, grad_attn_out, result, low_one, *attention, 2)

time: 613 us -> 521 us (0.85)
  Pallas kernels: 494 us -> 460 us
  waiting for transfers between devices: 21.4 us -> 0.01 us
  other arithmetic: 40.4 us -> 29 us
  local copies, waits for them, and re-layouts: 20.2 us -> 9.94 us
  starting transfers between devices: 10.9 us -> 4.41 us
    pallas_call x3 -> x1, Pallas kernels: 159 us -> 123 us  [forward(): pl.pallas_call(forward_kernel, out_shape=[shape((4, shard.shape[0], width...]
    pallas_call x1, Pallas kernels: 37.7 us -> 49.2 us  [own_matrix(): pl.pallas_call(functools.partial(owner_kernel, rows), out_shape=[jax.Shap...]
    ppermute x6 -> x0, waiting for transfers between devices: 11.4 us -> none  [the longest x2 10.5 us: to_sequences(): first = lax.ppermute(jnp.where(odd, blocks[1], blocks[0]), BOTH, lists[0])]
    select_n x5 -> x0, other arithmetic: 8.79 us -> none  [the longest x1 2.95 us: to_sequences(): jnp.where(upper, jnp.concatenate([second, first]), jnp.concatenate([first...]
    ppermute x6 -> x0, starting transfers between devices: 8.78 us -> none  [the longest x2 7.59 us: to_sequences(): first = lax.ppermute(jnp.where(odd, blocks[1], blocks[0]), BOTH, lists[0])]
    ppermute x1, waiting for transfers between devices: 7.06 us -> 0.01 us  [from_sequences(): first = lax.ppermute(jnp.where(upper, bottom, top), BOTH, back[0])]
    convert_element_type x6 -> x3, other arithmetic: 10 us -> 3.61 us  [low(): return values.astype(jnp.bfloat16)]
    pallas_call x1, Pallas kernels: 144 us -> 137 us  [backward(): pl.pallas_call(backward_kernel, out_shape=[jax.ShapeDtypeStruct((rows, 12...]
  transfers between devices with their start and end apart: 8 -> 2, of which waited for: 4 -> 0; matrix products, arithmetic and copies ran while one was open for 4% -> 3% of each run, Pallas kernels for 22% -> 32%
where the time goes in v4:
time: 521 us; the launch traced here: 516 us
  Pallas kernels  460 us (88%)
  other arithmetic  29 us (6%)
  matrix products  10.8 us (2%)
  local copies, waits for them, and re-layouts  9.94 us (2%)
    pallas_call x1, Pallas kernels, backward(): pl.pallas_call(backward_kernel, out_shape=[jax.ShapeDtypeStruct((rows, 12...  137 us
    pallas_call x1, Pallas kernels, forward(): pl.pallas_call(forward_kernel, out_shape=[shape((4, shard.shape[0], width...  123 us
    pallas_call x1, Pallas kernels, return_steps(): pl.pallas_call(functools.partial(return_kernel, rows), out_shape=[jax.Sha...  62 us
    pallas_call x1, Pallas kernels, iterate_owned(): pl.pallas_call(functools.partial(iterate_kernel, rows), out_shape=jax.Sha...  55.7 us
    pallas_call x1, Pallas kernels, own_matrix(): pl.pallas_call(functools.partial(owner_kernel, rows), out_shape=[jax.Shap...  49.2 us
    pallas_call x1, Pallas kernels, feed(): pl.pallas_call(feed_kernel, grid=(groups,), out_shape=[jax.ShapeDtypeStru...  32.6 us
    dot_general x5, matrix products, einsum(): return jnp.einsum(spec, *operands, preferred_element_type=jnp.float32)  10.8 us
  transfers between devices with their start and end apart: 2, of which 0 were waited for; matrix products, arithmetic and copies ran while one was open for 3% of the time, Pallas kernels for 32%

profile of v4, /device:TPU:9, one launch (start us, length us, event | category | flops | bytes accessed | tf_op | source)
XLA Modules:
  0.0 515.7 jit_solution(8892595846520460718)
XLA Ops:
  0.6 0.0 copy-start.18
  0.7 1.1 copy.37
  1.8 0.7 slice_bitcast_fusion
  2.5 1.6 copy.38
  4.0 0.7 convert_element_type.93
  4.7 1.9 fusion.20
  6.6 1.3 pad_maximum_fusion.refs_10_.refs_12_
  7.9 1.3 pad_maximum_fusion.1.refs_11_.refs_13_
  9.2 0.7 broadcast_in_dim.7.refs_8_
  9.8 123.4 %forward.1 = (bf16[4,256,1024]{2,1,0:T(8,128)(2,1)}, bf16[4,256,1024]{2,1,0:T(8,128)(2,1)}, bf16[4,256,1024]{2,1,0:T(8,128)(2,1)}, bf16[4,256,1024]{2,1,0:T(8,12...) custom-call(bf16[256,128]{1,0:T(8,128)(2,1)} %get-tuple-element.129., ...), custom_call_target="tpu_custom_call" | custom-call | tf_op jit(solution)/shard_map/forward/pallas_call | solution.py:578
  133.3 1.9 reduce_sum.90
  135.2 0.3 copy-done
  135.5 0.3 multiply_reduce_fusion.2
  135.8 32.6 %feed.1 = (f32[512,1024]{1,0:T(8,128)}, f32[512,1024]{1,0:T(8,128)}, bf16[4,1312,1024]{2,1,0:T(8,128)(2,1)}, bf16[4,656,1024]{2,1,0:T(8,128)(2,1)}) custom-call(bf16[512,1024]{1,0:T(8,128)(2,1)} %get-tuple-element.47.rows, bf16[512,1024]{1,0:T(8,128)(2,1)} %get-tuple-element.48.cotangent, bf16[4,1312,1024]{2,1,0:T(8,128)(2,1)} %get-tuple-element.49.in_weight, ...), custom_call_target="tpu_custom_call" | custom-call | tf_op jit(solution)/shard_map/feed/pallas_call | solution.py:1277
  168.5 4.2 multiply_reduce_fusion
  172.7 0.0 copy-start.7
  172.7 0.7 multiply_add_fusion
  173.5 0.0 copy-start.3
  173.5 0.5 copy-done.7
  173.9 2.6 convolution_convert_fusion
  176.5 0.0 copy-done.3
  176.6 2.3 convolution_convert_fusion.1.refs_8_
  178.9 0.2 convert_reduce_fusion
  179.1 0.4 fusion.11
  179.5 137.2 %backward.1 = (f32[768,128]{1,0:T(8,128)}, f32[256,128]{1,0:T(8,128)}, f32[1312,128]{1,0:T(8,128)}, f32[656,128]{1,0:T(8,128)}, bf16[512,1024]{1,0:T(8,128)(2,1)...) custom-call(bf16[4,656,1024]{2,1,0:T(8,128)(2,1)} %get-tuple-element, ...), custom_call_target="tpu_custom_call" | custom-call | tf_op jit(solution)/shard_map/backward/pallas_call | solution.py:745
  316.8 2.6 fusion.30
  319.5 1.3 fusion.14
  320.7 0.3 copy-done.23
  321.1 2.0 fusion.10
  323.0 0.8 fusion.9
  323.8 0.0 copy-start.14
  323.8 0.0 copy-start.10
  323.9 0.1 broadcast_select_fusion.1
  323.9 3.3 collective-permute-start.1
  327.2 1.1 collective-permute-start
  328.4 0.2 copy.40
  328.6 1.0 copy.42
  329.6 0.1 broadcast_multiply_fusion
  329.7 0.0 copy-start.15
  329.7 1.8 fusion.28
  331.5 0.7 fusion.23
  332.2 1.0 fusion.27
  333.2 0.8 fusion.21
  334.1 0.6 pad_maximum_fusion.2.refs_4_
  334.7 49.2 %own_matrix.1 = (bf16[5248,1024]{1,0:T(8,128)(2,1)}, f32[2,1024]{1,0:T(2,128)}) custom-call(bf16[768,128]{1,0:T(8,128)(2,1)} %get-tuple-element.118.refs_0_, bf16[256,128]{1,0:T(8,128)(2,1)} %get-tuple-element.126.refs_1_, bf16[1312,128]{1,0:T(8,128)(2,1)} %get-tuple-element.116.refs_2_, bf16[656,128]{1,0:T(8,128)(2,1)} %get-tuple-element.124.refs_3_, ...), custom_call_target="tpu_custom_call" | custom-call | tf_op jit(solution)/shard_map/own_matrix/pallas_call | solution.py:910
  383.9 55.7 %iterate_owned.1.refs_0_ = bf16[5248,128]{1,0:T(8,128)(2,1)} custom-call(bf16[5248,1024]{1,0:T(8,128)(2,1)} %get-tuple-element.75.whole), custom_call_target="tpu_custom_call" | custom-call | tf_op jit(solution)/shard_map/iterate_owned/pallas_call | solution.py:1086
  439.7 62.0 %return_steps.1 = (bf16[768,128]{1,0:T(8,128)(2,1)}, bf16[256,128]{1,0:T(8,128)(2,1)}, bf16[1312,128]{1,0:T(8,128)(2,1)}, bf16[656,128]{1,0:T(8,128)(2,1)}) custom-call(bf16[5248,128]{1,0:T(8,128)(2,1)} %iterate_owned.1.refs_0_), custom_call_target="tpu_custom_call" | custom-call | tf_op jit(solution)/shard_map/return_steps/pallas_call | solution.py:952
  501.7 1.0 convert_multiply_fusion.1
  502.6 0.0 copy-start.9
  502.7 0.9 bitcast_subtract_fusion.2
  503.6 1.0 convert_multiply_fusion
  504.6 0.0 copy-start.6
  504.6 1.7 bitcast_subtract_fusion.1
  506.4 0.6 multiply_subtract_fusion.1
  507.0 0.9 copy.41
  507.9 0.2 copy.43
  508.1 0.8 copy.46
  508.9 0.8 copy.47
  509.6 0.8 bitcast_subtract_fusion
  510.4 0.9 multiply_subtract_fusion
  511.3 0.0 collective-permute-done.1
  511.3 0.0 collective-permute-done
  511.3 3.1 fusion.12
  514.5 1.0 copy.49
  (58 shorter events, 0.2 us)
Async XLA Ops:
  0.6 7.2 %copy-start.18 = (f32[2,1024]{1,0:T(2,128)S(1)}, f32[2,1024]{1,0:T(2,128)}, u32[]{:S(2)}) copy-start(f32[2,1024]{1,0:T(2,128)} %refs_9_.1) | copy-start | bytes 24580
  133.3 2.2 copy-start
  168.5 4.2 copy-start.2
  168.5 4.2 copy-start.5
  172.7 1.2 copy-start.7
  173.5 3.1 copy-start.3
  173.9 2.6 copy-start.26
  176.6 2.3 copy-start.1
  179.5 137.3 %copy-start.25 = (bf16[4,256,1024]{2,1,0:T(8,128)(2,1)S(1)}, bf16[4,256,1024]{2,1,0:T(8,128)(2,1)}, u32[]{:S(2)}) copy-start(bf16[4,256,1024]{2,1,0:T(8,128)(2,1)} %get-tuple-element.67) | copy-start | bytes 6291460
  316.8 2.7 copy-start.24
  316.8 2.7 copy-start.27
  319.5 1.6 copy-start.23
  321.1 2.0 copy-start.4
  323.8 4.5 copy-start.14
  323.8 5.8 %copy-start.10 = (f32[128,2,656]{0,2,1:T(8,128)S(1)}, f32[128,2,656]{0,2,1:T(8,128)}, u32[]{:S(2)}) copy-start(f32[128,2,656]{0,2,1:T(8,128)} %param.24) | copy-start | bytes 2015236
  323.9 187.4 %collective-permute-start.1 = (bf16[256,1024]{1,0:T(8,128)(2,1)S(1)}, bf16[256,1024]{1,0:T(8,128)(2,1)}, u32[]{:S(2)}, u32[]{:S(2)}) collective-permute-start(bf16[256,1024]{1,0:T(8,128)(2,1)S(1)} %get-tuple-element.122), channel_id=1, source_target_pairs={{0,0},{2,1},{4,2},{6,3},{1,4},{3,5},{5,6},{7,7},{8,8},{10,9},{12,1... | collective-permute-start | bytes 1572872 | tf_op jit(solution)/shard_map/ppermute | solution.py:97
  327.2 4.3 copy-start.17
  327.2 184.1 %collective-permute-start = (bf16[256,1024]{1,0:T(8,128)(2,1)S(1)}, bf16[256,1024]{1,0:T(8,128)(2,1)}, u32[]{:S(2)}, u32[]{:S(2)}) collective-permute-start(bf16[256,1024]{1,0:T(8,128)(2,1)S(1)} %get-tuple-element.121), channel_id=1, source_target_pairs={{2,0},{0,1},{6,2},{4,3},{3,4},{1,5},{7,6},{5,7},{10,8},{8,9},{14,1... | collective-permute-start | bytes 1572872 | tf_op jit(solution)/shard_map/ppermute | solution.py:98
  328.4 3.8 copy-start.11
  329.7 3.5 copy-start.15
  329.7 3.5 copy-start.16
  383.9 118.7 %copy-start.13 = (bf16[128,256]{0,1:T(8,128)(2,1)S(1)}, bf16[128,256]{0,1:T(8,128)(2,1)}, u32[]{:S(2)}) copy-start(bf16[128,256]{0,1:T(8,128)(2,1)} %copy.38) | copy-start | bytes 196612
  439.7 64.9 %copy-start.12 = (bf16[128,656]{0,1:T(8,128)(2,1)S(1)}, bf16[128,656]{0,1:T(8,128)(2,1)}, u32[]{:S(2)}) copy-start(bf16[128,656]{0,1:T(8,128)(2,1)} %param.20) | copy-start | bytes 503812
  439.7 66.7 %copy-start.19 = (f32[2,1024]{1,0:T(2,128)S(1)}, f32[2,1024]{1,0:T(2,128)}, u32[]{:S(2)}) copy-start(f32[2,1024]{1,0:T(2,128)} %refs_9_.1) | copy-start | bytes 24580
  439.7 66.7 %copy-start.20 = (f32[2,1024]{1,0:T(2,128)S(1)}, f32[2,1024]{1,0:T(2,128)}, u32[]{:S(2)}) copy-start(f32[2,1024]{1,0:T(2,128)} %param.27) | copy-start | bytes 24580
  439.7 66.7 %copy-start.21 = (f32[2,1024]{1,0:T(2,128)S(1)}, f32[2,1024]{1,0:T(2,128)}, u32[]{:S(2)}) copy-start(f32[2,1024]{1,0:T(2,128)} %param.26) | copy-start | bytes 24580
  439.7 66.7 %copy-start.22 = (f32[2,1024]{1,0:T(2,128)S(1)}, f32[2,1024]{1,0:T(2,128)}, u32[]{:S(2)}) copy-start(f32[2,1024]{1,0:T(2,128)} %get-tuple-element.80) | copy-start | bytes 24580
  502.6 7.0 %copy-start.9 = (bf16[128,3,256]{2,0,1:T(8,128)(2,1)S(1)}, bf16[128,3,256]{2,0,1:T(8,128)(2,1)}, u32[]{:S(2)}) copy-start(bf16[128,3,256]{2,0,1:T(8,128)(2,1)} %param.17) | copy-start | bytes 589828
  504.6 5.8 %copy-start.6 = (bf16[128,2,656]{0,2,1:T(8,128)(2,1)S(1)}, bf16[128,2,656]{0,2,1:T(8,128)(2,1)}, u32[]{:S(2)}) copy-start(bf16[128,2,656]{0,2,1:T(8,128)(2,1)} %param.19) | copy-start | bytes 1007620
  510.4 4.1 copy-start.8

commit v5 on v4

--- a/solution.py
+++ b/solution.py
@@ -808,207 +808,203 @@
     grad_query[:, columns] = low(turned(query_rows, cosine[own_rows], -sine[own_rows]))
 
 
-def owner_kernel(rows, *refs):
-    count = len(rows)
-    shards, gain, whole, gain_out = refs[:count], refs[count], refs[count + 1], refs[count + 2]
-    (gain_parts, own_sem, send_z, recv_z, send_x, recv_x, send_y, recv_y, send_d, recv_d, send_c, recv_c, send_g, recv_g) = refs[count + 3 :]
+def product_of(left, right, dims):
+    return lax.dot_general(left, right, (dims, ((), ())), preferred_element_type=jnp.float32)
+
+def optimize_kernel(heights, *refs):
+    refs = list(refs)
+    count, size, tile = len(heights), 1024, 256
+    f32, bf16 = jnp.float32, jnp.bfloat16
+    sums, moments, weights = take(refs, count), take(refs, count), take(refs, count)
+    (gain_two, gains), far = take(refs, 2), take(refs, 8)
+    new_moments, new_weights = take(refs, count), take(refs, count)
+    gain_out, rows_out = take(refs, 2)
+    blocks, backs = take(refs, count), take(refs, count)
+    whole, steps, gain_parts = take(refs, 3)
+    iterate, poly, product, total = take(refs, 4)
+    iterate_low, poly_low, other_low, total_low = take(refs, 4)
+    value_rows, rows_in, rows_low = take(refs, 3)
+    load_sem, own_sem, send_z, recv_z, send_x, recv_x, send_y, recv_y, send_d, recv_d, send_c, recv_c = take(refs, 12)
+    send_g, recv_g, back_sem, send_b, recv_b, move_send, move_recv, move_own = refs
     me, partner, across, down = neighbours()
     plane = lax.axis_index("tensor")
     diagonal = across + down - me
     planes = [lax.rem(plane + offset, 4) for offset in (1, 2, 3)]
+    flip = lambda block: block + 1 - 2 * lax.rem(block, 2)
+    half = rows_low.shape[0]
+    start_move, finish_move = move_plan(True, rows_low, rows_out, move_send, move_recv, move_own)
+    near = (
+        poly_low, other_low, total_low, iterate_low.at[0:half], iterate_low.at[half : 2 * half],
+        value_rows, rows_in, poly.at[0:half],
+    )
+    loads = [
+        pltpu.make_async_copy(source, target, load_sem.at[index])
+        for index, (source, target) in enumerate(zip(far, near))
+    ]
+    for load in loads:
+        load.start()
+
+    def place(part, slot, block):
+        height = heights[part]
+        return whole.at[pl.ds(pl.multiple_of(slot * height, 16), height), lanes(block)]
+
+    def spread(part, source, slot):
+        view = place(part, slot, me)
+        send_to(source, view, send_x.at[slot], recv_x.at[slot], (across, plane))
+        send_to(source, view, send_y.at[slot], recv_y.at[slot], (down, plane))
+        send_to(source, view, send_c.at[slot, 0], recv_c.at[slot, 0], (partner, plane))
+
+    def on_plane(body):
+        for part in range(count):
+            @pl.when(plane == part)
+            def _():
+                body(part)
+
+    def off_plane(body):
+        for part in range(count):
+            @pl.when(plane != part)
+            def _():
+                body(part)
+
+    def tiles_of(part):
+        height = heights[part]
+        return [(first, min(128, height - first)) for first in range(0, height, 128)]
+
     greet(plane, (partner, across, down), planes)
-    flip = lambda block: block + 1 - 2 * lax.rem(block, 2)
-
-    def remote(source, target, send, recv, device):
-        copy = pltpu.make_async_remote_copy(source, target, send, recv, device_id=device, device_id_type=MESH)
-        copy.start()
-        return copy
-
-    def wait(view, sem):
-        pltpu.make_async_copy(view, view, sem).wait()
-
-    def place(part, slot, block):
-        height = rows[part]
-        first = pl.multiple_of(slot * height, 16)
-        return whole.at[pl.ds(first, height), lanes(block)]
-
-    for part in range(count):
+    for part in (2, 0, 3, 1):
+        for first, extent in tiles_of(part):
+            rows, columns = pl.ds(first, extent), slice(first, first + extent)
+            added = MOMENTUM * moments[part][:, columns] + sums[part][rows].T
+            new_moments[part][:, columns] = added
+            blocks[part][rows] = low(added.T)
+
         @pl.when(plane != part)
         def _():
             offset = lax.rem(plane + 3 - part, 4)
-            remote(shards[part], place(part, plane, me), send_z.at[part], recv_z.at[offset], (me, part))
-    gain_copies = [
-        remote(gain, gain_parts.at[index], send_g.at[index], recv_g.at[index], (me, other))
-        for index, other in enumerate(planes)
-    ]
-
-    def spread(part, source, slot):
-        view = place(part, slot, me)
-        remote(source, view, send_x.at[slot], recv_x.at[slot], (across, plane))
-        remote(source, view, send_y.at[slot], recv_y.at[slot], (down, plane))
-        remote(source, view, send_c.at[slot, 0], recv_c.at[slot, 0], (partner, plane))
-
-    for part in range(count):
+            send_to(blocks[part], place(part, plane, me), send_z.at[part], recv_z.at[offset], (me, part))
+
         @pl.when(plane == part)
         def _():
-            pltpu.make_async_copy(shards[part], place(part, part, me), own_sem).start()
-            spread(part, shards[part], part)
-            for distance in (1, 3, 2):
-                slot = (part + distance) % 4
-                view = place(part, slot, me)
-                wait(view, recv_z.at[(slot + 3 - part) % 4])
-                spread(part, view, slot)
-            for slot in range(4):
-                view = place(part, slot, across)
-                wait(view, recv_x.at[slot])
-                remote(view, view, send_c.at[slot, 1], recv_c.at[slot, 1], (partner, plane))
-                if slot < 2:
-                    remote(view, view, send_d.at[slot], recv_d.at[slot], (down, plane))
-                view = place(part, slot, down)
-                wait(view, recv_y.at[slot])
-                remote(view, view, send_c.at[slot, 2], recv_c.at[slot, 2], (partner, plane))
-                if slot >= 2:
-                    remote(view, view, send_d.at[slot], recv_d.at[slot], (across, plane))
-
-    total = gain[...]
-    for index in range(3):
-        gain_copies[index].wait()
-        total = total + gain_parts[index]
-    gain_out[...] = total
-    for index, other in ((3, across), (4, down), (5, partner)):
-        copy = remote(gain_out, gain_parts.at[index], send_g.at[index], recv_g.at[index], (other, plane))
-        copy.wait()
-        gain_out[...] = gain_out[...] + gain_parts[index]
-
-    for part in range(count):
-        @pl.when(plane == part)
-        def _():
-            for slot in range(4):
-                view = place(part, slot, diagonal)
-                wait(view, recv_d.at[slot])
-                remote(view, view, send_c.at[slot, 3], recv_c.at[slot, 3], (partner, plane))
-            for slot in range(4):
-                for index, block in enumerate((me, across, down, diagonal)):
-                    wait(place(part, slot, flip(block)), recv_c.at[slot, index])
-            wait(place(part, part, me), own_sem)
-            for slot in range(4):
-                view = place(part, slot, me)
-                for sem in (send_x.at[slot], send_y.at[slot], send_d.at[slot]):
-                    wait(view, sem)
-                for index in range(4):
-                    wait(view, send_c.at[slot, index])
-        @pl.when(plane != part)
-        def _():
-            wait(shards[part], send_z.at[part])
-
-def own_matrix(shards, gain, collective_id):
-    rows = [s.shape[0] for s in shards]
-    count = len(shards)
-    sem = pltpu.SemaphoreType.DMA
-    anyspec = pl.BlockSpec(memory_space=pl.ANY)
-    vm = pl.BlockSpec(memory_space=pltpu.VMEM)
-    return pl.pallas_call(
-        functools.partial(owner_kernel, rows),
-        out_shape=[jax.ShapeDtypeStruct((4 * max(rows), 1024), shards[0].dtype), jax.ShapeDtypeStruct(gain.shape, gain.dtype)],
-        in_specs=[anyspec] * count + [vm],
-        out_specs=[anyspec, vm],
-        scratch_shapes=[pltpu.VMEM((6,) + gain.shape, gain.dtype), sem, sem((count,)), sem((3,))] + [sem((4,))] * 6 + [sem((4, 4))] * 2 + [sem((6,))] * 2,
-        compiler_params=pltpu.CompilerParams(collective_id=collective_id, has_side_effects=True),
-        name="own_matrix",
-    )(*shards, gain)
-
-def return_kernel(rows, *refs):
-    count = len(rows)
-    steps, outs = refs[0], refs[1 : 1 + count]
-    own_sem, send_z, recv_z = refs[1 + count :]
-    me = lax.axis_index("dp")
-    plane = lax.axis_index("tensor")
-    planes = [lax.rem(plane + offset, 4) for offset in (1, 2, 3)]
-    greet(plane, (), planes)
-    wait = lambda view, sem: pltpu.make_async_copy(view, view, sem).wait()
-    for part in range(count):
-        @pl.when(plane == part)
-        def _():
-            for slot in range(4):
-                view = steps.at[pl.ds(slot * rows[part], rows[part]), :]
-                if slot == part:
-                    pltpu.make_async_copy(view, outs[part], own_sem).start()
-                else:
-                    pltpu.make_async_remote_copy(view, outs[part], send_z.at[slot], recv_z.at[part], device_id=(me, slot), device_id_type=MESH).start()
-    for part in range(count):
-        @pl.when(plane == part)
-        def _():
-            wait(outs[part], own_sem)
-            for slot in range(4):
-                if slot != part:
-                    wait(outs[part], send_z.at[slot])
-        @pl.when(plane != part)
-        def _():
-            wait(outs[part], recv_z.at[part])
-
-def return_steps(steps, rows, collective_id):
-    sem = pltpu.SemaphoreType.DMA
-    anyspec = pl.BlockSpec(memory_space=pl.ANY)
-    return pl.pallas_call(
-        functools.partial(return_kernel, rows),
-        out_shape=[jax.ShapeDtypeStruct((r, 128), steps.dtype) for r in rows],
-        in_specs=[anyspec],
-        out_specs=[anyspec] * len(rows),
-        scratch_shapes=[sem, sem((4,)), sem((4,))],
-        compiler_params=pltpu.CompilerParams(collective_id=collective_id, has_side_effects=True),
-        name="return_steps",
-    )(steps)
-
-def product_of(left, right, dims):
-    return lax.dot_general(left, right, (dims, ((), ())), preferred_element_type=jnp.float32)
-
-def iterate_kernel(rows, whole, steps, iterate, poly, product, total, iterate_low, poly_low, other_low, total_low):
-    size, tile = iterate.shape[0], 256
-    plane = lax.axis_index("tensor")
-    me = lax.axis_index("dp")
-    f32, bf16 = jnp.float32, jnp.bfloat16
+            pltpu.make_async_copy(blocks[part], place(part, part, me), own_sem).start()
+            spread(part, blocks[part], part)
+
+    def pass_z(part):
+        for distance in (1, 3, 2):
+            slot = (part + distance) % 4
+            view = place(part, slot, me)
+            wait_for(view, recv_z.at[(slot + 3 - part) % 4])
+            spread(part, view, slot)
+
+    on_plane(pass_z)
+
+    for load in loads:
+        load.wait()
+    gain_out[1:2] = gain_two[...]
+    gain_out[0:1] = jnp.zeros((1, size), f32)
+
+    @pl.loop(0, half // 64)
+    def _(index):
+        first = pl.multiple_of(index * 64, 64)
+        window = pl.ds(first, 64)
+        other_window = pl.ds(pl.multiple_of(first + half, 64), 64)
+        grad = product_of(iterate_low[window], poly_low[...], ((1,), (0,)))
+        grad = grad + product_of(iterate_low[other_window], other_low[...], ((1,), (0,)))
+        grad = grad + product_of(value_rows[window], total_low[...], ((1,), (0,)))
+        rows = rows_in[window].astype(f32)
+        centre = rows - jnp.mean(rows, axis=1, keepdims=True)
+        inverse = lax.rsqrt(jnp.mean(centre * centre, axis=1, keepdims=True) + NORM_EPS)
+        normed = centre * inverse
+        scaled = grad * gains[0:1]
+        mean_grad = jnp.mean(scaled, axis=1, keepdims=True)
+        mean_cross = jnp.mean(scaled * normed, axis=1, keepdims=True)
+        back = inverse * (scaled - mean_grad - normed * mean_cross)
+        rows_low[window] = low(poly[window] + back)
+        gain_out[0:1] += jnp.sum(grad * normed, axis=0, keepdims=True)
+
+    start_move()
+    for index, other in enumerate(planes):
+        send_to(gain_out, gain_parts.at[index], send_g.at[index], recv_g.at[index], (me, other))
+
+    def pass_xy(part):
+        for slot in range(4):
+            view = place(part, slot, across)
+            wait_for(view, recv_x.at[slot])
+            if slot < 2:
+                send_to(view, view, send_d.at[slot], recv_d.at[slot], (down, plane))
+            send_to(view, view, send_c.at[slot, 1], recv_c.at[slot, 1], (partner, plane))
+            view = place(part, slot, down)
+            wait_for(view, recv_y.at[slot])
+            if slot >= 2:
+                send_to(view, view, send_d.at[slot], recv_d.at[slot], (across, plane))
+            send_to(view, view, send_c.at[slot, 2], recv_c.at[slot, 2], (partner, plane))
+
+    on_plane(pass_xy)
+
+    def pass_diagonal(part):
+        for slot in range(4):
+            view = place(part, slot, diagonal)
+            wait_for(view, recv_d.at[slot])
+            send_to(view, view, send_c.at[slot, 3], recv_c.at[slot, 3], (partner, plane))
+        for slot in range(4):
+            for index, block in enumerate((me, across, down, diagonal)):
+                wait_for(place(part, slot, flip(block)), recv_c.at[slot, index])
+        wait_for(blocks[part], own_sem)
+
+    on_plane(pass_diagonal)
+
     windows = [pl.ds(first, tile) for first in range(0, size, tile)]
     zero = jnp.zeros((1, 1), f32)
+    blank = jnp.zeros((1, size), f32)
     corner = lax.broadcasted_iota(jnp.int32, (tile, tile), 0) == lax.broadcasted_iota(jnp.int32, (tile, tile), 1)
 
+    def gram(part):
+        rows = slice(0, 4 * heights[part])
+        for group in range(2):
+            edge = group * size // 2
+
+            @pl.loop(0, 2)
+            def _(index):
+                window = pl.ds(pl.multiple_of(edge + index * tile, tile), tile)
+                iterate[window, edge:] = product_of(whole[rows, window], whole[rows, edge:], ((0,), (0,)))
+
+    on_plane(gram)
+
+    def upper(window):
+        return slice(window.start, size)
+
     def store(window, result, shift, full, low_copy):
-        fixed = [
-            result[:, columns.start : columns.start + tile]
-            - (jnp.where(corner, shift, 0.0) if columns.start == window.start else 0.0)
-            for columns in windows
-        ]
-        result = jnp.concatenate(fixed, axis=1)
-        full[window] = result
-        low_copy[window] = result.astype(bf16)
+        corner_block = result[:, :tile] - jnp.where(corner, shift, 0.0)
+        result = jnp.concatenate([corner_block, result[:, tile:]], axis=1) if result.shape[1] > tile else corner_block
+        full[window, upper(window)] = result
+        result_low = low(result)
+        low_copy[window, upper(window)] = result_low
+        for first in range(tile, result.shape[1], tile):
+            low_copy[pl.ds(window.start + first, tile), window] = result_low[:, first : first + tile].T
         return result
 
-    def fold(values):
-        return jnp.sum(values, axis=0, keepdims=True)
+    def fold(left, right, window):
+        sums_of = jnp.sum(left * right, axis=0, keepdims=True)
+        weighted = jnp.concatenate([sums_of[:, :tile], 2.0 * sums_of[:, tile:]], axis=1) if sums_of.shape[1] > tile else sums_of
+        return jnp.concatenate([blank[:, : window.start], weighted], axis=1) if window.start else weighted
 
     def finish(row):
         return jnp.sum(row, axis=1, keepdims=True) / size
 
-    for part, height in enumerate(rows):
-        @pl.when(plane == part)
-        def _():
-            @pl.loop(0, size // tile)
-            def _(index):
-                window = pl.ds(pl.multiple_of(index * tile, tile), tile)
-                block = whole[0 : 4 * height, window]
-                iterate[window] = product_of(block, whole[0 : 4 * height, :], ((0,), (0,)))
+    def multiply(left, right, window):
+        return product_of(left[window], right[:, upper(window)], ((1,), (0,)))
+
     trace = zero
     for window in windows:
         block = jnp.where(corner, iterate[window, window], 0.0)
-        trace = trace + jnp.sum(fold(block), axis=1, keepdims=True)
+        trace = trace + jnp.sum(jnp.sum(block, axis=0, keepdims=True), axis=1, keepdims=True)
     factor = 1.0 / (jnp.sqrt(trace) + NORM_FLOOR)
     squared = factor * factor
     mean = trace * squared / size
-    row = jnp.zeros((1, size), f32)
+    row = blank
     for window in windows:
-        rest = store(window, iterate[window] * squared, mean, iterate, iterate_low)
-        row = row + fold(rest * rest)
+        rest = store(window, iterate[window, upper(window)] * squared, mean, iterate, iterate_low)
+        row = row + fold(rest, rest, window)
     square = finish(row)
-    blank = jnp.zeros((1, size), f32)
 
     def polynomial(mean, square, with_total):
         linear = QUINTIC_THREE + 2.0 * QUINTIC_FIVE * mean
@@ -1016,46 +1012,44 @@
         poly_mean = QUINTIC_ONE + QUINTIC_THREE * mean + QUINTIC_FIVE * (mean * mean) + shift
         row, total_row = blank, blank
         for window in windows:
-            mine = iterate[window]
-            rest = product_of(iterate_low[window], iterate_low[...], ((1,), (0,)))
-            rest = linear * mine + QUINTIC_FIVE * rest
+            mine = iterate[window, upper(window)]
+            rest = linear * mine + QUINTIC_FIVE * multiply(iterate_low, iterate_low, window)
             rest = store(window, rest, shift, poly, poly_low)
-            row = row + fold(rest * mine)
+            row = row + fold(rest, mine, window)
             if with_total:
-                total_row = total_row + fold(rest * total[window])
+                total_row = total_row + fold(rest, total[window, upper(window)], window)
         return (poly_mean, finish(row), finish(total_row))
 
     def grow_total(poly_mean, total_mean, cross):
         for window in windows:
-            result = poly_mean * total[window] + total_mean * poly[window]
-            result = result + product_of(poly_low[window], total_low[...], ((1,), (0,)))
+            result = poly_mean * total[window, upper(window)] + total_mean * poly[window, upper(window)]
+            result = result + multiply(poly_low, total_low, window)
             store(window, result, cross, total, other_low)
-        for window in windows:
-            total_low[window] = other_low[window]
+        total_low[...] = other_low[...]
         return poly_mean * total_mean + cross
 
     def advance(poly_mean, mean, cross):
         row = blank
         for window in windows:
-            rest = poly[window]
-            result = poly_mean * iterate[window] + mean * rest
-            result = result + product_of(poly_low[window], iterate_low[...], ((1,), (0,)))
+            rest = poly[window, upper(window)]
+            result = poly_mean * iterate[window, upper(window)] + mean * rest
+            result = result + multiply(poly_low, iterate_low, window)
             result = store(window, result, cross, product, other_low)
-            row = row + fold(result * rest)
+            row = row + fold(result, rest, window)
         product_mean = poly_mean * mean + cross
         cross = finish(row)
         row = blank
         for window in windows:
-            result = poly_mean * product[window] + product_mean * poly[window]
-            result = result + product_of(poly_low[window], other_low[...], ((1,), (0,)))
+            result = poly_mean * product[window, upper(window)] + product_mean * poly[window, upper(window)]
+            result = result + multiply(poly_low, other_low, window)
             result = store(window, result, cross, iterate, iterate_low)
-            row = row + fold(result * result)
+            row = row + fold(result, result, window)
         return (poly_mean * product_mean + cross, finish(row))
 
     total_mean, cross, _ = polynomial(mean, square, False)
     for window in windows:
-        total[window] = poly[window]
-        total_low[window] = poly_low[window]
+        total[window, upper(window)] = poly[window, upper(window)]
+    total_low[...] = poly_low[...]
     mean, square = advance(total_mean, mean, cross)
 
     def sweep(_, carry):
@@ -1068,30 +1062,95 @@
     poly_mean, _, cross_total = polynomial(mean, square, True)
     total_mean = grow_total(poly_mean, total_mean, cross_total)
 
-    mine = pl.ds(pl.multiple_of(me * 128, 128), 128)
+    mine = lanes(me)
     columns = total_low[:, mine]
-    for part, height in enumerate(rows):
-        @pl.when(plane == part)
-        def _():
-            @pl.loop(0, 4)
-            def _(slot):
-                window = pl.ds(pl.multiple_of(slot * height, 16), height)
-                result = product_of(whole[window, :], columns, ((1,), (0,)))
-                result = result + total_mean * whole[window, mine].astype(f32)
-                steps[window, :] = (factor * result).astype(bf16)
-
-def iterate_owned(whole, rows):
-    size = whole.shape[1]
+
+    def step_home(part):
+        height = heights[part]
+
+        @pl.loop(0, 4)
+        def _(turn_of):
+            slot = lax.rem(part + 1 + turn_of, 4)
+            window = pl.ds(pl.multiple_of(slot * height, 16), height)
+            result = product_of(whole[window, :], columns, ((1,), (0,)))
+            result = result + total_mean * whole[window, mine].astype(f32)
+            steps[window, :] = low(factor * result)
+
+            @pl.when(turn_of == 3)
+            def _():
+                pltpu.make_async_copy(steps.at[window, :], backs[part], back_sem).start()
+
+            @pl.when(turn_of < 3)
+            def _():
+                send_to(steps.at[window, :], backs[part], send_b.at[turn_of], recv_b.at[part], (me, slot))
+
+    on_plane(step_home)
+
+    for index in range(3):
+        wait_for(gain_out, send_g.at[index])
+        wait_for(gain_parts.at[index], recv_g.at[index])
+    gain_out[...] = gain_out[...] + gain_parts[0] + gain_parts[1] + gain_parts[2]
+    for index, other in ((3, across), (4, down), (5, partner)):
+        send_to(gain_out, gain_parts.at[index], send_g.at[index], recv_g.at[index], (other, plane))
+        wait_for(gain_out, send_g.at[index])
+        wait_for(gain_parts.at[index], recv_g.at[index])
+        gain_out[...] = gain_out[...] + gain_parts[index]
+
+    on_plane(lambda part: wait_for(backs[part], back_sem))
+    off_plane(lambda part: wait_for(backs[part], recv_b.at[part]))
+    for part in range(count):
+        rate = MUON_RATE * 0.2 * math.sqrt(4 * heights[part])
+        for first, extent in tiles_of(part):
+            rows, columns_of = pl.ds(first, extent), slice(first, first + extent)
+            step = backs[part][rows].astype(f32).T
+            kept = weights[part][:, columns_of].astype(f32) * (1.0 - MUON_RATE * DECAY_RATE)
+            new_weights[part][:, columns_of] = kept - rate * step
+
+    def last_waits(part):
+        for slot in range(4):
+            for sem in (send_x.at[slot], send_y.at[slot], send_d.at[slot]):
+                wait_for(blocks[part], sem)
+            for index in range(4):
+                wait_for(blocks[part], send_c.at[slot, index])
+        for index in range(3):
+            wait_for(blocks[part], send_b.at[index])
+
+    on_plane(last_waits)
+    off_plane(lambda part: wait_for(blocks[part], send_z.at[part]))
+    finish_move()
+
+
+def optimize(sums, moments, weights, gain_two, gains, far, collective_id):
+    heights = [part.shape[0] for part in sums]
+    count, size = len(heights), gains.shape[1]
     f32, bf16 = jnp.float32, jnp.bfloat16
-    return pl.pallas_call(
-        functools.partial(iterate_kernel, rows),
-        out_shape=jax.ShapeDtypeStruct((whole.shape[0], 128), bf16),
-        in_specs=[pl.BlockSpec(memory_space=pltpu.VMEM)],
-        out_specs=pl.BlockSpec(memory_space=pltpu.VMEM),
-        scratch_shapes=[pltpu.VMEM((size, size), f32)] * 4 + [pltpu.VMEM((size, size), bf16)] * 4,
-        compiler_params=pltpu.CompilerParams(vmem_limit_bytes=58 * 1024 * 1024),
-        name="iterate_owned",
-    )(whole)
+    sem = pltpu.SemaphoreType.DMA
+    anywhere = pl.BlockSpec(memory_space=pl.ANY)
+    local = pl.BlockSpec(memory_space=pltpu.VMEM)
+    half = far[6].shape[0]
+    outs = pl.pallas_call(
+        functools.partial(optimize_kernel, heights),
+        out_shape=[jax.ShapeDtypeStruct((128, height), f32) for height in heights] * 2
+        + [jax.ShapeDtypeStruct(gains.shape, f32), jax.ShapeDtypeStruct((2, half // 2, size), bf16)],
+        in_specs=[local] * (3 * count + 2) + [anywhere] * 8,
+        out_specs=[local] * (2 * count + 1) + [anywhere],
+        scratch_shapes=[pltpu.VMEM((height, 128), bf16) for height in heights] * 2
+        + [pltpu.VMEM((4 * max(heights), size), bf16), pltpu.VMEM((4 * max(heights), 128), bf16)]
+        + [pltpu.VMEM((6,) + gains.shape, f32)]
+        + [pltpu.VMEM((size, size), f32)] * 4
+        + [pltpu.VMEM((size, size), bf16)] * 4
+        + [pltpu.VMEM((half, size), bf16)] * 3
+        + [sem((8,)), sem, sem((count,)), sem((3,))]
+        + [sem((4,))] * 6
+        + [sem((4, 4))] * 2
+        + [sem((6,))] * 2
+        + [sem, sem((3,)), sem((count,)), sem((2,)), sem((2,)), sem],
+        compiler_params=pltpu.CompilerParams(
+            collective_id=collective_id, has_side_effects=True, vmem_limit_bytes=60 * 1024 * 1024
+        ),
+        name="optimize",
+    )(*sums, *moments, *weights, gain_two, gains, *far)
+    return (outs[:count], outs[count : 2 * count], outs[2 * count], outs[2 * count + 1])
 
 
 def weight_shards(weights):
@@ -1300,12 +1359,8 @@
 
 
 def orthogonal_steps(blocks, gain_part):
-    tensor_count, dp_count = lax.axis_size("tensor"), lax.axis_size("dp")
+    tensor_count = lax.axis_size("tensor")
     heights = [block.shape[0] for block in blocks]
-    if (tensor_count, dp_count, blocks[0].shape[1]) == (4, 8, 128):
-        whole, gain_grad = own_matrix(blocks, gain_part, 3)
-        steps = iterate_owned(whole, heights)
-        return (return_steps(steps, heights, 4), gain_grad)
     row_count = blocks[0].shape[1]
     first_row = lax.axis_index("dp") * row_count
     gain_grad = lax.psum(gain_part, BOTH)
@@ -1411,38 +1466,49 @@
     else:
         grad_query, grad_own, grad_other = attend_back(*attention)
         grad_pair = low(grad_own + swap_partner(grad_other).astype(jnp.float32))
+    moments = (qkv_moment, attn_out_moment, ffn_in_moment, ffn_out_moment)
     grad_parts = (grad_query, grad_pair[0], grad_pair[1])
-    grad_scaled_one = sum(
-        einsum("sk,kn->sn", part, weight.reshape(-1, width))
-        for part, weight in zip(grad_parts, (query_all, key_all, value_all))
-    )
-    grad_from_one, gain_one = layer_norm_back(
-        grad_scaled_one, normed_one, inverse_one, norm_gains[0]
-    )
-    input_low = low(grad_middle + grad_from_one)
-    if not fits:
+    weight_parts = [part.reshape(-1, width) for part in (query_all, key_all, value_all)]
+    if fits:
+        far = (*weight_parts, *grad_parts, rows_low, grad_middle)
+        new_moments, new_weights, gain_grad, input_grad = optimize(
+            sums,
+            [moment.reshape(row_count, -1) for moment in moments],
+            [weight.reshape(row_count, -1) for weight in weights],
+            gain_two[None],
+            norm_gains,
+            far,
+            3,
+        )
+        new_moments = [part.reshape(like.shape) for part, like in zip(new_moments, moments)]
+        new_weights = [part.reshape(like.shape) for part, like in zip(new_weights, moments)]
+    else:
+        grad_scaled_one = sum(
+            einsum("sk,kn->sn", part, weight) for part, weight in zip(grad_parts, weight_parts)
+        )
+        grad_from_one, gain_one = layer_norm_back(
+            grad_scaled_one, normed_one, inverse_one, norm_gains[0]
+        )
         grads = [low(einsum("sk,sn->kn", part, low_one)) for part in grad_parts]
         grads = [grad.reshape(query_all.shape) for grad in grads]
         sums = reduce_grads(grads + [grad_attn_out, grad_ffn_in, grad_ffn_out])
+        sums = [jnp.concatenate(sums[:3])] + list(sums[3:])
         outputs = from_sequences(result, lists, odd, upper)
-        sums = [jnp.concatenate(sums[:3])] + list(sums[3:])
-    input_grad = from_sequences(input_low, lists, odd, upper)
+        input_grad = from_sequences(low(grad_middle + grad_from_one), lists, odd, upper)
+        turned_sums = [turn_back(part, moment) for part, moment in zip(sums, moments)]
+        new_moments = [MOMENTUM * moment + part for moment, part in zip(moments, turned_sums)]
+        steps, gain_grad = orthogonal_steps(
+            [low(turn(moment)) for moment in new_moments], jnp.stack([gain_one, gain_two])
+        )
+        new_weights = [
+            weight.astype(jnp.float32) * (1.0 - MUON_RATE * DECAY_RATE)
+            - MUON_RATE
+            * 0.2
+            * math.sqrt(step.shape[0] * tensor_count)
+            * turn_back(step, weight).astype(jnp.float32)
+            for weight, step in zip(weights, steps)
+        ]
     outputs, input_grad = outputs[:, None], input_grad[:, None].astype(jnp.float32)
-
-    moments = (qkv_moment, attn_out_moment, ffn_in_moment, ffn_out_moment)
-    gain_part = jnp.stack([gain_one, gain_two])
-    turned = [turn(moment) for moment in moments]
-    turned = [MOMENTUM * moment + part for moment, part in zip(turned, sums)]
-    new_moments = [turn_back(part, moment) for part, moment in zip(turned, moments)]
-    steps, gain_grad = orthogonal_steps([low(part) for part in turned], gain_part)
-    new_weights = [
-        weight.astype(jnp.float32) * (1.0 - MUON_RATE * DECAY_RATE)
-        - MUON_RATE
-        * 0.2
-        * math.sqrt(step.shape[0] * tensor_count)
-        * turn_back(step, weight).astype(jnp.float32)
-        for weight, step in zip(weights, steps)
-    ]
     gain_first_new = BETA_ONE * gain_first + (1.0 - BETA_ONE) * gain_grad
     gain_second_new = BETA_TWO * gain_second + (1.0 - BETA_TWO) * gain_grad * gain_grad
     first_hat = gain_first_new / (1.0 - BETA_ONE**STEP)

time: 521 us -> 467 us (0.90)
  Pallas kernels: 460 us -> 419 us
  other arithmetic: 29 us -> 14 us
  local copies, waits for them, and re-layouts: 9.94 us -> 22.5 us
  matrix products: 10.8 us -> 4.89 us
    pallas_call x3 -> x1, Pallas kernels: 167 us -> 126 us  [optimize(): pl.pallas_call(functools.partial(optimize_kernel, heights), out_shape=[ja...]
    convert_element_type x4 -> x0, other arithmetic: 6.75 us -> none  [the longest x3 3.61 us: low(): return values.astype(jnp.bfloat16)]
    dot_general x5 -> x2, matrix products: 10.8 us -> 4.89 us  [einsum(): return jnp.einsum(spec, *operands, preferred_element_type=jnp.float32)]
  transfers between devices with their start and end apart: 2 -> 0, of which waited for: 0 -> 0; matrix products, arithmetic and copies ran while one was open for 3% -> 0% of each run, Pallas kernels for 32% -> 0%
where the time goes in v5:
time: 467 us; the launch traced here: 462 us
  Pallas kernels  419 us (90%)
  local copies, waits for them, and re-layouts  22.5 us (5%)
  other arithmetic  14 us (3%)
  matrix products  4.89 us (1%)
    pallas_call x1, Pallas kernels, backward(): pl.pallas_call(backward_kernel, out_shape=[jax.ShapeDtypeStruct((rows, 12...  137 us
    pallas_call x1, Pallas kernels, optimize(): pl.pallas_call(functools.partial(optimize_kernel, heights), out_shape=[ja...  126 us
    pallas_call x1, Pallas kernels, forward(): pl.pallas_call(forward_kernel, out_shape=[shape((4, shard.shape[0], width...  123 us
    pallas_call x1, Pallas kernels, feed(): pl.pallas_call(feed_kernel, grid=(groups,), out_shape=[jax.ShapeDtypeStru...  33 us
    unnamed x62, local copies, waits for them, and re-layouts  12.3 us

profile of v5, /device:TPU:9, one launch (start us, length us, event | category | flops | bytes accessed | tf_op | source)
XLA Modules:
  0.0 461.7 jit_solution(10952383504680080901)
XLA Ops:
  0.6 1.1 copy.63
  1.7 0.7 slice_bitcast_fusion.2
  2.4 1.6 copy.64
  4.0 0.7 convert_element_type.40
  4.7 0.7 broadcast_in_dim.9.refs_8_
  5.3 1.9 fusion.2
  7.3 1.3 pad_maximum_fusion.refs_10_.refs_12_
  8.5 1.3 pad_maximum_fusion.1.refs_11_.refs_13_
  9.8 122.8 %forward.1 = (bf16[4,256,1024]{2,1,0:T(8,128)(2,1)}, bf16[4,256,1024]{2,1,0:T(8,128)(2,1)}, bf16[4,256,1024]{2,1,0:T(8,128)(2,1)}, bf16[4,256,1024]{2,1,0:T(8,12...) custom-call(bf16[256,128]{1,0:T(8,128)(2,1)} %get-tuple-element.139., ...), custom_call_target="tpu_custom_call" | custom-call | tf_op jit(solution)/shard_map/forward/pallas_call | solution.py:578
  132.6 0.0 copy-start
  132.6 33.0 %feed.1 = (f32[512,1024]{1,0:T(8,128)}, f32[512,1024]{1,0:T(8,128)}, bf16[4,1312,1024]{2,1,0:T(8,128)(2,1)}, bf16[4,656,1024]{2,1,0:T(8,128)(2,1)}) custom-call(bf16[512,1024]{1,0:T(8,128)(2,1)} %get-tuple-element.51.rows, bf16[512,1024]{1,0:T(8,128)(2,1)} %get-tuple-element.52.cotangent, bf16[4,1312,1024]{2,1,0:T(8,128)(2,1)} %get-tuple-element.53.in_weight, ...), custom_call_target="tpu_custom_call" | custom-call | tf_op jit(solution)/shard_map/feed/pallas_call | solution.py:1336
  165.7 0.0 copy-done
  165.7 0.0 copy-start.19
  165.7 0.2 reduce_sum.45
  165.9 0.3 multiply_reduce_fusion.2
  166.2 0.1 copy-done.19
  166.4 1.1 copy-done.2
  167.4 4.1 multiply_reduce_fusion
  171.5 0.0 copy-done.3
  171.6 0.7 multiply_add_fusion.refs_21_
  172.3 0.5 copy-done.6
  172.8 2.6 convolution_convert_fusion
  175.4 0.0 copy-done.1
  175.4 0.0 copy-done.24
  175.4 2.3 convolution_convert_fusion.1.refs_8_
  177.7 137.4 %backward.1 = (f32[768,128]{1,0:T(8,128)}, f32[256,128]{1,0:T(8,128)}, f32[1312,128]{1,0:T(8,128)}, f32[656,128]{1,0:T(8,128)}, bf16[512,1024]{1,0:T(8,128)(2,1)...) custom-call(bf16[4,656,1024]{2,1,0:T(8,128)(2,1)} %get-tuple-element, ...), custom_call_target="tpu_custom_call" | custom-call | tf_op jit(solution)/shard_map/backward/pallas_call | solution.py:745
  315.1 0.0 copy-start.16
  315.1 0.0 copy-start.5
  315.1 0.0 copy-done.11
  315.1 0.2 copy.66
  315.3 0.0 copy-start.10
  315.3 0.0 copy-start.4
  315.3 0.9 copy.68.refs_4_
  316.2 2.2 copy.69.refs_6_
  318.4 0.0 copy-done.16
  318.4 0.9 copy.70.refs_7_
  319.4 0.8 copy.71.refs_8_
  320.2 0.0 copy-done.5
  320.2 0.9 copy.72.refs_10_
  321.1 0.0 copy-done.10
  321.1 0.8 copy.73.refs_11_
  321.9 0.0 copy-done.4
  321.9 1.5 slice_bitcast_fusion
  323.4 125.8 %optimize.1 = (f32[128,768]{1,0:T(8,128)}, f32[128,256]{1,0:T(8,128)}, f32[128,1312]{1,0:T(8,128)}, f32[128,656]{1,0:T(8,128)}, f32[128,768]{1,0:T(8,128)}, /*in...) custom-call(f32[768,128]{1,0:T(8,128)} %get-tuple-element.69.refs_0_, ...), custom_call_target="tpu_custom_call" | custom-call | tf_op jit(solution)/shard_map/optimize/pallas_call | solution.py:1131
  449.2 0.0 copy-start.15
  449.3 0.0 copy-start.14
  449.3 2.9 bitcast_convert_fusion
  452.1 0.2 copy.74
  452.3 0.9 copy.80
  453.2 0.0 copy-done.14
  453.2 0.2 copy.75
  453.4 0.9 copy.81
  454.3 1.1 copy.76
  455.4 1.1 copy.77
  456.5 0.9 copy.82
  457.4 0.0 copy-done.12
  457.4 0.9 copy.83
  458.3 0.0 copy-done.21
  458.3 0.0 copy-done.23
  458.3 0.6 multiply_subtract_fusion
  459.0 1.0 copy.87
  459.9 0.0 copy-done.18
  459.9 0.7 copy.88
  460.6 0.7 copy.89
  (34 shorter events, 0.1 us)
Async XLA Ops:
  132.6 33.1 %copy-start = (f32[512,1024]{1,0:T(8,128)S(1)}, f32[512,1024]{1,0:T(8,128)}, u32[]{:S(2)}) copy-start(f32[512,1024]{1,0:T(8,128)} %get-tuple-element.58) | copy-start | bytes 6291460
  165.7 0.7 copy-start.19
  165.9 1.6 copy-start.2
  167.4 4.1 copy-start.3
  171.6 1.2 copy-start.6
  172.8 2.6 copy-start.1
  172.8 2.6 copy-start.24
  177.7 137.4 %copy-start.11 = (f32[128,3,256]{2,0,1:T(8,128)S(1)}, f32[128,3,256]{2,0,1:T(8,128)}, u32[]{:S(2)}) copy-start(f32[128,3,256]{2,0,1:T(8,128)} %param.22) | copy-start | bytes 1179652
  315.1 3.4 copy-start.16
  315.1 5.1 %copy-start.5 = (bf16[128,2,656]{0,2,1:T(8,128)(2,1)S(1)}, bf16[128,2,656]{0,2,1:T(8,128)(2,1)}, u32[]{:S(2)}) copy-start(bf16[128,2,656]{0,2,1:T(8,128)(2,1)} %param.19) | copy-start | bytes 1007620
  315.3 5.8 %copy-start.10 = (bf16[128,656]{0,1:T(8,128)(2,1)S(1)}, bf16[128,656]{0,1:T(8,128)(2,1)}, u32[]{:S(2)}) copy-start(bf16[128,656]{0,1:T(8,128)(2,1)} %param.20) | copy-start | bytes 503812
  315.3 6.6 %copy-start.4 = (bf16[2,512,1024]{2,1,0:T(8,128)(2,1)S(1)}, bf16[2,512,1024]{2,1,0:T(8,128)(2,1)}, u32[]{:S(2)}) copy-start(bf16[2,512,1024]{2,1,0:T(8,128)(2,1)} %get-tuple-element.77) | copy-start | bytes 6291460
  449.2 2.9 copy-start.15
  449.3 4.0 copy-start.14
  452.1 2.2 copy-start.9
  452.1 3.3 copy-start.8
  453.2 3.3 copy-start.13
  453.4 4.0 copy-start.12
  454.3 4.0 copy-start.20
  454.3 4.0 copy-start.21
  454.3 4.0 copy-start.22
  454.3 4.0 copy-start.23
  454.3 4.6 %copy-start.7 = (bf16[2,256,1024]{2,1,0:T(8,128)(2,1)S(1)}, bf16[2,256,1024]{2,1,0:T(8,128)(2,1)}, u32[]{:S(2)}) copy-start(bf16[2,256,1024]{2,1,0:T(8,128)(2,1)} %get-tuple-element.68) | copy-start | bytes 3145732
  456.5 3.4 copy-start.18
  456.5 4.1 copy-start.17

commit v6 on v5

--- a/solution.py
+++ b/solution.py
@@ -135,7 +135,7 @@
 
 
 def step_of(rows):
-    return next(step for step in (128, 64, 32, 16) if rows % step == 0)
+    return next(step for step in (128, 64, 48, 32, 16) if rows % step == 0)
 
 
 def lanes(block):
@@ -627,44 +627,311 @@
     log_total[...] = jnp.concatenate(logs + logs * 3, axis=0)
 
 
+def add_rows(target, source, extent):
+    step = step_of(extent)
+
+    @pl.loop(0, extent // step)
+    def _(index):
+        window = pl.ds(pl.multiple_of(index * step, step), step)
+        target[window] = low(target[window].astype(jnp.float32) + source[window].astype(jnp.float32))
+
+
+def slot_of(part):
+    return (4 - part) % 4
+
+
+def slot_plan(grads, sums, buffers, sems):
+    held, from_x, from_y, from_yx, from_xy = buffers[:5]
+    from_z, staging = buffers[5][0], buffers[6][0]
+    (load_sem, send_c, recv_c, send_x, recv_x, send_y, recv_y, send_yx, recv_yx, send_xy, recv_xy, send_z, recv_z) = sems
+    me, partner, across, down = neighbours()
+    plane = lax.axis_index("tensor")
+    flip = lambda block: block + 1 - 2 * lax.rem(block, 2)
+    blocks = (me, across, down, across + down - me)
+    order = (3, 1, 2, 0)
+    rows, early = grads.shape[1], from_x[0].shape[1]
+    late = rows - early
+    one, two = pl.ds(0, early), pl.ds(early, late)
+
+    def stage_core(part):
+        for index in order:
+            send_to(grads.at[slot_of(part), :, lanes(flip(blocks[index]))], held[part].at[index], send_c.at[part, index], recv_c.at[part, index], (partner, plane))
+
+    def stage_first(part):
+        for index in order:
+            pltpu.make_async_copy(grads.at[slot_of(part), :, lanes(blocks[index])], staging.at[index], load_sem.at[part, index]).start()
+        for index in order:
+            wait_for(staging.at[index], load_sem.at[part, index])
+            wait_for(held[part].at[index], recv_c.at[part, index])
+            add_rows(held[part].at[index], staging.at[index], rows)
+            if index % 2 == 1:
+                send_to(held[part].at[index, one], from_x[part].at[index // 2], send_x.at[part, index // 2], recv_x.at[part, index // 2], (across, plane))
+            if index // 2 == 1:
+                send_to(held[part].at[index, two], from_y[part].at[index % 2], send_y.at[part, index % 2], recv_y.at[part, index % 2], (down, plane))
+
+    def stage_second(part):
+        for side in (1, 0):
+            wait_for(from_x[part].at[side], recv_x.at[part, side])
+            add_rows(held[part].at[2 * side, one], from_x[part].at[side], early)
+            if side == 1:
+                send_to(held[part].at[2, one], from_yx[part], send_yx.at[part], recv_yx.at[part], (down, plane))
+            wait_for(from_y[part].at[side], recv_y.at[part, side])
+            add_rows(held[part].at[side, two], from_y[part].at[side], late)
+            if side == 1:
+                send_to(held[part].at[1, two], from_xy[part], send_xy.at[part], recv_xy.at[part], (across, plane))
+
+    def stage_third(part):
+        wait_for(from_yx[part], recv_yx.at[part])
+        add_rows(held[part].at[0, one], from_yx[part], early)
+        wait_for(from_xy[part], recv_xy.at[part])
+        add_rows(held[part].at[0, two], from_xy[part], late)
+
+        @pl.when(plane != slot_of(part))
+        def _():
+            offset = lax.rem(plane + 3 - slot_of(part), 4)
+            send_to(held[part].at[0], from_z.at[offset], send_z.at[part], recv_z.at[offset], (me, slot_of(part)))
+
+    def stage_last(part):
+        @pl.when(plane == slot_of(part))
+        def _():
+            for offset in range(3):
+                wait_for(from_z.at[offset], recv_z.at[offset])
+            for target, first, extent in sums:
+                step = step_of(extent)
+
+                @pl.loop(0, extent // step)
+                def _(index):
+                    offset = pl.multiple_of(index * step, step)
+                    window = pl.ds(pl.multiple_of(first + offset, 16), step)
+                    total = held[part][0, window].astype(jnp.float32)
+                    for other in range(3):
+                        total = total + from_z[other, window].astype(jnp.float32)
+                    target[pl.ds(offset, step)] = total
+
+    def finish(part):
+        for index in range(4):
+            wait_for(held[part].at[index], send_c.at[part, index])
+        for side in range(2):
+            wait_for(from_x[part].at[side], send_x.at[part, side])
+            wait_for(from_y[part].at[side], send_y.at[part, side])
+        wait_for(from_yx[part], send_yx.at[part])
+        wait_for(from_xy[part], send_xy.at[part])
+
+        @pl.when(plane != slot_of(part))
+        def _():
+            wait_for(from_z.at[0], send_z.at[part])
+
+    return ((stage_core, stage_first, stage_second, stage_third, stage_last), finish)
+
+
+def slot_scratch(rows, early):
+    sem = pltpu.SemaphoreType.DMA
+    late = rows - early
+    shapes = [(4, rows)] * 4 + [(2, early)] * 4 + [(2, late)] * 4 + [(early,)] * 4 + [(late,)] * 4
+    shapes += [(3, rows), (4, rows)]
+    buffers = [pltpu.VMEM(shape + (128,), jnp.bfloat16) for shape in shapes]
+    sems = [sem((4, 4))] * 3 + [sem((4, 2))] * 4 + [sem((4,))] * 4 + [sem((4,)), sem((3,))]
+    return (buffers, sems)
+
+
 def backward_kernel(*refs):
     refs = list(refs)
-    grad_out, grad_in, grad_attn, rows_in = take(refs, 4)
-    far, (bias, log_total, cosine, sine) = take(refs, 6), take(refs, 4)
-    sums, (far_query, far_pair), (rows_out,) = take(refs, 4), take(refs, 2), take(refs, 1)
-    weight_grads = take(refs, 3)
-    near, (grad_query, grad_pair) = take(refs, 6), take(refs, 2)
-    low_rows, queries, own, other, grad, context = near
-    grad_other, arrived, staged = take(refs, 3)
-    buffers = [take(refs, 7) for _ in range(6)] + [take(refs, 1)]
+    f32, bf16 = jnp.float32, jnp.bfloat16
+    in_weight, out_weight, attn_weight, far_two, far_cot, far_middle = take(refs, 6)
+    far_query, far_own, far_other, far_context, far_one = take(refs, 5)
+    bias, log_total, cosine, sine, gains = take(refs, 5)
+    sums, (far_grad_query, far_pair, rows_out, far_grad_middle, gain_two) = take(refs, 4), take(refs, 5)
+    grad_feed, weight_grads = take(refs, 1)[0], take(refs, 4)
+    branch, cotangent, low_rows, queries, own, other, grad, context = take(refs, 8)
+    grad_query, grad_pair, grad_other, arrived, staged = take(refs, 5)
+    result, grad_rows, middle = take(refs, 3)
+    slot_buffers = [take(refs, 4) for _ in range(5)] + [take(refs, 1), take(refs, 1)]
+    slot_sems = take(refs, 13)
+    buffers = [take(refs, 4) for _ in range(6)] + [take(refs, 1)]
     sems = take(refs, 13)
-    pair_send, pair_recv, stage_sem, load_sem, out_sem, move_send, move_recv, move_own = refs
+    pair_send, pair_recv, stage_sem, load_sem, out_sem, weight_sem, feed_sem, middle_sem = take(refs, 8)
+    move_send, move_recv, move_own = refs
     me, partner, across, down = neighbours()
     plane = lax.axis_index("tensor")
-    height, third = grad_out.shape[1], grad_attn.shape[1]
-    parts = [(grad_out, 0, height), (grad_in, 0, height), (grad_in, height, height)]
-    parts += [(grad_attn, 0, third)] + [(ref, 0, third) for ref in weight_grads]
+    height, third = out_weight.shape[1], attn_weight.shape[1]
+    count, width = cotangent.shape
     sum_qkv, sum_attn, sum_in, sum_out = sums
-    targets = [(sum_out, 0), (sum_in, 0), (sum_in, height), (sum_attn, 0)]
-    targets += [(sum_qkv, third * index) for index in range(3)]
+    feed_sums = [(sum_in, 0, 2 * height), (sum_out, 2 * height, height)]
+    feed_stages, feed_finish = slot_plan(grad_feed, feed_sums, slot_buffers, slot_sems)
+    parts = [(ref, 0, third) for ref in weight_grads]
+    targets = [(sum_attn, 0)] + [(sum_qkv, third * index) for index in range(3)]
     stages, finish = scatter_plan(parts, targets, buffers, sems)
-    start_move, finish_move = move_plan(True, rows_in, rows_out, move_send, move_recv, move_own)
+    start_move, finish_move = move_plan(True, cotangent, rows_out, move_send, move_recv, move_own)
+
+    def call(stage, part):
+        if part < 4:
+            feed_stages[stage](part)
+        else:
+            stages[stage](part - 4)
+
+    pieces = ((0, 336), (336, height - 336))
+    weight_slots = (
+        (own.at[0], own.at[1], grad_pair.at[0]),
+        (other.at[0], other.at[1], grad_pair.at[1]),
+    )
+    grad_slots = ((grad_other.at[0], grad_other.at[1], grad_query), (queries, context, grad))
+
+    def weight_copies(group, piece):
+        first, extent = pieces[piece]
+        sources = ((in_weight, first), (in_weight, height + first), (out_weight, first))
+        return [
+            pltpu.make_async_copy(source.at[lax.rem(4 - group, 4), pl.ds(offset, extent)], target.at[pl.ds(0, extent)], weight_sem.at[piece, index])
+            for index, ((source, offset), target) in enumerate(zip(sources, weight_slots[piece]))
+        ]
+
+    def grad_copies(group, piece):
+        first, extent = pieces[piece]
+        return [
+            pltpu.make_async_copy(source.at[pl.ds(0, extent)], grad_feed.at[lax.rem(4 - group, 4), pl.ds(index * height + first, extent)], feed_sem.at[piece, index])
+            for index, source in enumerate(grad_slots[piece])
+        ]
+
+    def start_all(copies):
+        for copy in copies:
+            copy.start()
+
+    def wait_all(copies):
+        for copy in copies:
+            copy.wait()
+
+    first_loads = [
+        pltpu.make_async_copy(far_two, branch, load_sem.at[0]),
+        pltpu.make_async_copy(far_cot, cotangent, load_sem.at[1]),
+    ]
+    start_all(first_loads)
+    start_all(weight_copies(0, 0))
+    start_all(weight_copies(0, 1))
     greet(plane, (partner, across, down), [lax.rem(plane + offset, 4) for offset in (1, 2, 3)])
-    copies = [
+    result[...] = jnp.zeros_like(result)
+    grad_rows[...] = jnp.zeros_like(grad_rows)
+    wait_all(first_loads)
+    feed_calls = {(1, 1): ((1, 0),), (2, 1): ((1, 1),), (3, 0): ((2, 0),), (3, 1): ((1, 2),)}
+
+    @pl.loop(0, 4)
+    def _(group):
+        @pl.when(group > 0)
+        def _():
+            for piece in range(2):
+                wait_all(grad_copies(group - 1, piece))
+            for part in range(3):
+                @pl.when(group == part + 1)
+                def _():
+                    call(0, part)
+
+        for piece, (_, extent) in enumerate(pieces):
+            for (when, place), calls in feed_calls.items():
+                if place == piece:
+                    @pl.when(group == when)
+                    def _():
+                        for stage, part in calls:
+                            call(stage, part)
+
+            window = pl.ds(0, extent)
+            wait_all(weight_copies(group, piece))
+            gate_weight, up_weight, down_weight = (ref[window] for ref in weight_slots[piece])
+            gate = product_of(gate_weight, branch[...], ((1,), (1,)))
+            up = product_of(up_weight, branch[...], ((1,), (1,)))
+            grad_hidden = product_of(down_weight, cotangent[...], ((1,), (1,)))
+            below = 0.5 + 0.5 * lax.erf(gate * math.sqrt(0.5))
+            active = gate * below
+            hidden = low(active * up)
+            slope = below + gate * jnp.exp(-0.5 * gate * gate) * (1.0 / math.sqrt(2.0 * math.pi))
+            grad_gate = low(grad_hidden * up * slope)
+            grad_up = low(grad_hidden * active)
+            grad_slots[piece][2][window] = low(product_of(hidden, cotangent[...], ((1,), (0,))))
+            grad_slots[piece][0][window] = low(product_of(grad_gate, branch[...], ((1,), (0,))))
+            grad_slots[piece][1][window] = low(product_of(grad_up, branch[...], ((1,), (0,))))
+            start_all(grad_copies(group, piece))
+            result[...] += product_of(hidden, down_weight, ((0,), (0,)))
+            grad_rows[...] += product_of(grad_gate, gate_weight, ((0,), (0,)))
+            grad_rows[...] += product_of(grad_up, up_weight, ((0,), (0,)))
+
+            @pl.when(group < 3)
+            def _():
+                start_all(weight_copies(group + 1, piece))
+
+    step = 64
+
+    def middle_copy(index):
+        window = pl.ds(pl.multiple_of(index * step, step), step)
+        slot = lax.rem(index, 2)
+        return pltpu.make_async_copy(far_middle.at[window], middle.at[slot], middle_sem.at[slot])
+
+    middle_copy(0).start()
+    for piece in range(2):
+        wait_all(grad_copies(3, piece))
+    call(0, 3)
+    near = (queries, own, other, context, low_rows)
+    loads = [
         pltpu.make_async_copy(source, target, load_sem.at[index])
-        for index, (source, target) in enumerate(zip(far, near))
+        for index, (source, target) in enumerate(zip((far_query, far_own, far_other, far_context, far_one), near))
     ]
-    stages[0](0)
-    for copy in copies:
-        copy.start()
+    start_all(loads)
+    attn_loads = [
+        pltpu.make_async_copy(
+            attn_weight.at[group], grad_other.at[group // 2, pl.ds(group % 2 * third, third)], weight_sem.at[group // 2, group % 2]
+        )
+        for group in range(4)
+    ]
+    start_all(attn_loads)
+    gain_two[...] = jnp.zeros_like(gain_two)
+
+    @pl.loop(0, count // step)
+    def _(index):
+        @pl.when(index < count // step - 1)
+        def _():
+            middle_copy(index + 1).start()
+
+        middle_copy(index).wait()
+        window = pl.ds(pl.multiple_of(index * step, step), step)
+        rows = middle[lax.rem(index, 2)]
+        centre = rows - jnp.mean(rows, axis=1, keepdims=True)
+        inverse = lax.rsqrt(jnp.mean(centre * centre, axis=1, keepdims=True) + NORM_EPS)
+        normed = centre * inverse
+        scaled = grad_rows[window] * gains[1:2]
+        mean_grad = jnp.mean(scaled, axis=1, keepdims=True)
+        mean_cross = jnp.mean(scaled * normed, axis=1, keepdims=True)
+        gain_two[...] += jnp.sum(grad_rows[window] * normed, axis=0, keepdims=True)
+        total = cotangent[window].astype(f32) + inverse * (scaled - mean_grad - normed * mean_cross)
+        grad_rows[window] = total
+        branch[window] = low(total)
+        cotangent[window] = low(rows + result[window])
+
+    call(3, 0)
+    call(2, 1)
     start_move()
-    schedule = {
-        0: ((1, 0), (0, 1)),
-        4: ((2, 0), (1, 1), (0, 2), (0, 3)),
-        7: ((3, 0),),
-    }
-    for copy in copies[1:]:
-        copy.wait()
+    middle_out = pltpu.make_async_copy(grad_rows, far_grad_middle, out_sem.at[2])
+    middle_out.start()
+    wait_all(attn_loads)
+
+    @pl.loop(0, count // 128)
+    def _(index):
+        window = pl.ds(pl.multiple_of(index * 128, 128), 128)
+        for part in range(2):
+            columns = slice(part * count, part * count + count)
+            grad[window, columns] = low(product_of(branch[window], grad_other[part], ((1,), (1,))))
+
+    wait_all(loads)
+
+    def weight_grad(which, values, rows):
+        target = weight_grads[which]
+        for group in range(4):
+            slot = staged.at[group % 2]
+            if group >= 2:
+                wait_for(slot, stage_sem.at[group % 2])
+            block = values[:, third * group : third * group + third]
+            slot[...] = low(product_of(block, rows[...], ((0,), (0,))))
+            pltpu.make_async_copy(slot, target.at[group], stage_sem.at[group % 2]).start()
+        for group in range(2):
+            wait_for(staged.at[group], stage_sem.at[group])
+
+    weight_grad(0, context, branch)
+    call(0, 4)
 
     def exchanged(index):
         return (arrived.at[:, :, lanes(index)], pair_recv.at[index])
@@ -673,11 +940,12 @@
         wait_for(*exchanged(index))
         columns = lanes(index)
         for which in range(2):
-            total = grad_pair[which, :, columns].astype(jnp.float32)
-            total = total + arrived[which, :, columns].astype(jnp.float32)
+            total = grad_pair[which, :, columns].astype(f32)
+            total = total + arrived[which, :, columns].astype(f32)
             grad_pair[which, :, columns] = low(total)
 
-    last_pair = queries.shape[1] // 128 - 1
+    last_pair = width // 128 - 1
+    schedule = {0: ((1, 3),), 2: ((3, 1), (2, 2)), 5: ((3, 2), (1, 4)), 7: ((2, 3),)}
 
     @pl.loop(0, last_pair + 1)
     def _(index):
@@ -685,7 +953,7 @@
             @pl.when(index == position)
             def _():
                 for stage, part in calls:
-                    stages[stage](part)
+                    call(stage, part)
 
         attend_back_pair(lanes(index), queries, own, other, bias, grad, context, log_total.at[index], cosine, sine, grad_query, grad_pair, grad_other)
         target, sem = exchanged(index)
@@ -695,86 +963,81 @@
         def _():
             add_pair(index - 1)
 
-    copies[0].wait()
-    query_copy = pltpu.make_async_copy(grad_query, far_query, out_sem.at[0])
+    query_copy = pltpu.make_async_copy(grad_query, far_grad_query, out_sem.at[0])
     query_copy.start()
-
-    def weight_grad(which, values):
-        target = weight_grads[which]
-        for group in range(4):
-            slot = staged.at[group % 2]
-            if group >= 2:
-                wait_for(slot, stage_sem.at[group % 2])
-            block = values[:, third * group : third * group + third]
-            slot[...] = low(product_of(block, low_rows[...], ((0,), (0,))))
-            pltpu.make_async_copy(slot, target.at[group], stage_sem.at[group % 2]).start()
-        for group in range(2):
-            wait_for(staged.at[group], stage_sem.at[group])
-
-    weight_grad(0, grad_query)
-    stages[0](4)
+    weight_grad(1, grad_query, low_rows)
+    call(0, 5)
     add_pair(last_pair)
     pair_copy = pltpu.make_async_copy(grad_pair, far_pair, out_sem.at[1])
     pair_copy.start()
-    weight_grad(1, grad_pair.at[0])
-    stages[0](5)
-    weight_grad(2, grad_pair.at[1])
-    stages[0](6)
-    calls = [(stage, step - (stage - 1)) for step in range(10) for stage in (4, 3, 2, 1)]
-    done = {(1, 0), (2, 0), (1, 1), (3, 0)}
-    for stage, part in calls:
-        if 0 <= part < 7 and (stage, part) not in done:
-            stages[stage](part)
-    for part in range(7):
+    weight_grad(2, grad_pair.at[0], low_rows)
+    call(0, 6)
+    weight_grad(3, grad_pair.at[1], low_rows)
+    call(0, 7)
+    done = {(1, 4), (3, 2), (2, 3), (1, 0), (2, 0), (1, 1), (3, 0), (2, 1), (1, 2), (3, 1), (2, 2), (1, 3)}
+    for turn_of in range(10):
+        for stage in (3, 2, 1):
+            part = turn_of - (stage - 1)
+            if 0 <= part < 8 and (stage, part) not in done:
+                call(stage, part)
+    for part in range(8):
+        call(4, part)
+    for part in range(4):
+        feed_finish(part)
         finish(part)
     for index in range(last_pair + 1):
         wait_for(arrived.at[:, :, lanes(index)], pair_send.at[index])
     query_copy.wait()
     pair_copy.wait()
+    middle_out.wait()
     finish_move()
 
 
-def backward(grad_out, grad_in, grad_attn, rows_in, low_rows, queries, own, other, bias, grad, context, log_total, cosine, sine, collective_id):
-    height, third = grad_out.shape[1], grad_attn.shape[1]
+def backward(wholes, low_two, cotangent, middle, queries, own, other, context, low_one, bias, log_total, cosine, sine, gains, collective_id):
+    attn_all, in_all, out_all = wholes
+    height, third = out_all.shape[1], attn_all.shape[1]
     count, width = queries.shape
-    buffers, sems = scatter_scratch([height] * 3 + [third] * 4)
+    early = 3 * height // 32 * 16 + 16
+    slot_buffers, slot_sems = slot_scratch(3 * height, early)
+    buffers, sems = scatter_scratch([third] * 4)
     sem = pltpu.SemaphoreType.DMA
     anywhere = pl.BlockSpec(memory_space=pl.ANY)
     local = pl.BlockSpec(memory_space=pltpu.VMEM)
-    bf16 = jnp.bfloat16
+    bf16, f32 = jnp.bfloat16, jnp.float32
+    shape, vmem = jax.ShapeDtypeStruct, pltpu.VMEM
     outs = pl.pallas_call(
         backward_kernel,
-        out_shape=[
-            jax.ShapeDtypeStruct((rows, 128), jnp.float32)
-            for rows in (3 * third, third, 2 * height, height)
+        out_shape=[shape((rows, 128), f32) for rows in (3 * third, third, 2 * height, height)]
+        + [
+            shape((count, width), bf16),
+            shape((2, count, width), bf16),
+            shape((2, count // 2, width), bf16),
+            shape((count, width), f32),
+            shape((1, width), f32),
+            shape((4, 3 * height, width), bf16),
         ]
-        + [
-            jax.ShapeDtypeStruct((count, width), bf16),
-            jax.ShapeDtypeStruct((2, count, width), bf16),
-            jax.ShapeDtypeStruct((2, count // 2, width), rows_in.dtype),
-        ]
-        + [jax.ShapeDtypeStruct(grad_attn.shape, bf16)] * 3,
-        in_specs=[anywhere] * 10 + [local] * 4,
-        out_specs=[local] * 4 + [anywhere] * 6,
-        scratch_shapes=[
-            pltpu.VMEM(rows.shape, bf16) for rows in (low_rows, queries, own, other, grad, context)
-        ]
-        + [
-            pltpu.VMEM((count, width), bf16),
-            pltpu.VMEM((2, count, width), bf16),
-            pltpu.VMEM((2, count, width), bf16),
-            pltpu.VMEM((2, count, width), bf16),
-            pltpu.VMEM((2, third, width), bf16),
-        ]
+        + [shape(attn_all.shape, bf16)] * 4,
+        in_specs=[anywhere] * 11 + [local] * 5,
+        out_specs=[local] * 4 + [anywhere] * 4 + [local] + [anywhere] * 5,
+        scratch_shapes=[vmem((count, width), bf16)] * 4
+        + [vmem((2, count, width), bf16)] * 2
+        + [vmem((count, width), bf16)] * 3
+        + [vmem((2, count, width), bf16)] * 3
+        + [vmem((2, third, width), bf16)]
+        + [vmem((count, width), f32)] * 2
+        + [vmem((2, 64, width), f32)]
+        + slot_buffers
+        + slot_sems
         + buffers
         + sems
-        + [sem((8,)), sem((8,)), sem((2,)), sem((6,)), sem((2,)), sem((2,)), sem((2,)), sem],
+        + [sem((8,)), sem((8,)), sem((2,)), sem((5,)), sem((3,)), sem((2, 3)), sem((2, 3)), sem((2,))]
+        + [sem((2,)), sem((2,)), sem],
         compiler_params=pltpu.CompilerParams(
-            collective_id=collective_id, has_side_effects=True, vmem_limit_bytes=60 * 1024 * 1024
+            collective_id=collective_id, has_side_effects=True, vmem_limit_bytes=62 * 1024 * 1024
         ),
         name="backward",
-    )(grad_out, grad_in, grad_attn, rows_in, low_rows, queries, own, other, grad, context, bias, log_total, cosine, sine)
-    return outs[:7]
+    )(in_all, out_all, attn_all, low_two, cotangent, middle, queries, own, other, context, low_one, bias, log_total, cosine, sine, gains)
+    return outs[:9]
 
 
 def attend_back_pair(columns, queries, own, other, bias, grad, context, log_total, cosine, sine, grad_query, grad_own, grad_other):
@@ -1448,23 +1711,40 @@
     normed_two, inverse_two, scaled_two = layer_norm_parts(middle, norm_gains[1])
     if not fits:
         low_two = low(scaled_two)
-    ffn_branch, grad_scaled_two, grad_ffn_in, grad_ffn_out = feed(
-        low_two, cotangent_low, ffn_in_all, ffn_out_all
-    )
-    result = low(middle + ffn_branch)
-    grad_from_two, gain_two = layer_norm_back(
-        grad_scaled_two, normed_two, inverse_two, norm_gains[1]
-    )
-    grad_middle = grad_rows + grad_from_two
-    grad_branch = low(grad_middle)
-    grad_context = low(einsum("sn,kn->sk", grad_branch, attn_rows))
-    grad_attn_out = low(einsum("sk,sn->kn", context, grad_branch)).reshape(attn_all.shape)
-    attention = (queries, own, other, bias, grad_context, context, log_total, cosine, sine)
     if fits:
-        outs = backward(grad_ffn_out, grad_ffn_in, grad_attn_out, result, low_one, *attention, 2)
-        sums, (grad_query, grad_pair, outputs) = outs[:4], outs[4:]
+        outs = backward(
+            (attn_all, ffn_in_all, ffn_out_all),
+            low_two,
+            cotangent_low,
+            middle,
+            queries,
+            own,
+            other,
+            context,
+            low_one,
+            bias,
+            log_total,
+            cosine,
+            sine,
+            norm_gains,
+            2,
+        )
+        sums, (grad_query, grad_pair, outputs, grad_middle, gain_two) = outs[:4], outs[4:]
     else:
-        grad_query, grad_own, grad_other = attend_back(*attention)
+        ffn_branch, grad_scaled_two, grad_ffn_in, grad_ffn_out = feed(
+            low_two, cotangent_low, ffn_in_all, ffn_out_all
+        )
+        result = low(middle + ffn_branch)
+        grad_from_two, gain_two = layer_norm_back(
+            grad_scaled_two, normed_two, inverse_two, norm_gains[1]
+        )
+        grad_middle = grad_rows + grad_from_two
+        grad_branch = low(grad_middle)
+        grad_context = low(einsum("sn,kn->sk", grad_branch, attn_rows))
+        grad_attn_out = low(einsum("sk,sn->kn", context, grad_branch)).reshape(attn_all.shape)
+        grad_query, grad_own, grad_other = attend_back(
+            queries, own, other, bias, grad_context, context, log_total, cosine, sine
+        )
         grad_pair = low(grad_own + swap_partner(grad_other).astype(jnp.float32))
     moments = (qkv_moment, attn_out_moment, ffn_in_moment, ffn_out_moment)
     grad_parts = (grad_query, grad_pair[0], grad_pair[1])
@@ -1475,7 +1755,7 @@
             sums,
             [moment.reshape(row_count, -1) for moment in moments],
             [weight.reshape(row_count, -1) for weight in weights],
-            gain_two[None],
+            gain_two,
             norm_gains,
             far,
             3,

time: 467 us -> 442 us (0.946)
  Pallas kernels: 419 us -> 405 us
  other arithmetic: 14 us -> 7.96 us
  matrix products: 4.89 us -> 0 us
    pallas_call x1, Pallas kernels: 126 us -> 117 us  [optimize(): pl.pallas_call(functools.partial(optimize_kernel, heights), out_shape=[ja...]
    pallas_call x2 -> x1, Pallas kernels: 170 us -> 165 us  [backward(): pl.pallas_call(backward_kernel, out_shape=[shape((rows, 128), f32) for ro...]
    dot_general x2 -> x0, matrix products: 4.89 us -> none  [einsum(): return jnp.einsum(spec, *operands, preferred_element_type=jnp.float32)]
    unnamed x62 -> x54, local copies, waits for them, and re-layouts: 12.3 us -> 8.78 us
where the time goes in v6:
time: 442 us; the launch traced here: 434 us
  Pallas kernels  405 us (92%)
  local copies, waits for them, and re-layouts  19.5 us (4%)
  other arithmetic  7.96 us (2%)
    pallas_call x1, Pallas kernels, backward(): pl.pallas_call(backward_kernel, out_shape=[shape((rows, 128), f32) for ro...  165 us
    pallas_call x1, Pallas kernels, forward(): pl.pallas_call(forward_kernel, out_shape=[shape((4, shard.shape[0], width...  123 us
    pallas_call x1, Pallas kernels, optimize(): pl.pallas_call(functools.partial(optimize_kernel, heights), out_shape=[ja...  117 us

profile of v6, /device:TPU:9, one launch (start us, length us, event | category | flops | bytes accessed | tf_op | source)
XLA Modules:
  0.0 433.6 jit_solution(11022926062593922589)
XLA Ops:
  0.7 0.0 copy-start.13
  0.7 1.9 fusion
  2.6 0.0 copy-start.12
  2.6 0.0 copy-start.20
  2.6 1.3 pad_maximum_fusion.1.refs_11_.refs_14_
  3.9 1.3 pad_maximum_fusion.refs_10_.refs_13_
  5.2 0.0 copy-done.13
  5.2 0.2 copy.63
  5.3 0.7 slice_bitcast_fusion.2
  6.0 0.0 copy-done.12
  6.0 0.7 copy.64
  6.8 0.0 copy-done.20
  6.8 0.7 broadcast_in_dim.14.refs_8_
  7.4 122.9 %forward.1 = (bf16[4,256,1024]{2,1,0:T(8,128)(2,1)}, bf16[4,256,1024]{2,1,0:T(8,128)(2,1)}, bf16[4,256,1024]{2,1,0:T(8,128)(2,1)}, bf16[4,256,1024]{2,1,0:T(8,12...) custom-call(bf16[256,128]{1,0:T(8,128)(2,1)} %get-tuple-element.131., ...), custom_call_target="tpu_custom_call" | custom-call | tf_op jit(solution)/shard_map/forward/pallas_call | solution.py:578
  130.3 164.9 %backward.1 = (f32[768,128]{1,0:T(8,128)}, f32[256,128]{1,0:T(8,128)}, f32[1312,128]{1,0:T(8,128)}, f32[656,128]{1,0:T(8,128)}, bf16[512,1024]{1,0:T(8,128)(2,1)...) custom-call(bf16[4,1312,1024]{2,1,0:T(8,128)(2,1)} %get-tuple-elemen, ...), custom_call_target="tpu_custom_call" | custom-call | tf_op jit(solution)/shard_map/backward/pallas_call | solution.py:1008
  295.3 0.0 copy-start.6
  295.3 0.0 copy-start.4
  295.3 3.1 slice_bitcast_fusion
  298.4 0.0 copy-start.11
  298.4 0.0 copy-start
  298.4 0.8 copy.71.refs_8_
  299.2 0.0 copy-done.6
  299.3 0.2 copy.66
  299.4 0.9 copy.68.refs_4_
  300.3 0.0 copy-done.4
  300.3 1.1 copy.69.refs_6_
  301.5 0.0 copy-done.11
  301.5 0.9 copy.70.refs_7_
  302.4 0.0 copy-done
  302.4 0.9 copy.72.refs_10_
  303.3 0.0 copy-done.5
  303.3 0.8 copy.73.refs_11_
  304.1 117.1 %optimize.1 = (f32[128,768]{1,0:T(8,128)}, f32[128,256]{1,0:T(8,128)}, f32[128,1312]{1,0:T(8,128)}, f32[128,656]{1,0:T(8,128)}, f32[128,768]{1,0:T(8,128)}, /*in...) custom-call(f32[768,128]{1,0:T(8,128)} %get-tuple-element.63.refs_0_, ...), custom_call_target="tpu_custom_call" | custom-call | tf_op jit(solution)/shard_map/optimize/pallas_call | solution.py:1394
  421.2 0.0 copy-start.10
  421.2 0.0 copy-start.9
  421.2 2.9 bitcast_convert_fusion
  424.1 0.0 copy-done.10
  424.1 0.2 copy.74
  424.3 0.9 copy.80
  425.2 0.0 copy-done.9
  425.2 0.2 copy.75
  425.4 0.0 copy-start.7
  425.4 0.9 copy.81
  426.3 0.0 copy-done.3
  426.3 0.0 copy-start.19
  426.3 0.0 copy-start.1
  426.3 1.1 copy.76
  427.4 0.0 copy-done.2
  427.4 1.1 copy.77
  428.5 0.0 copy-done.8
  428.5 0.9 copy.82
  429.4 0.0 copy-done.7
  429.4 0.9 copy.83
  430.3 0.0 copy-done.14
  430.3 0.0 copy-done.17
  430.3 0.0 copy-done.18
  430.3 0.0 copy-done.19
  430.3 0.6 multiply_subtract_fusion
  431.0 0.0 copy-done.1
  431.0 1.0 copy.87
  431.9 0.0 copy-done.16
  431.9 0.7 copy.88
  432.6 0.0 copy-done.15
  432.6 0.7 copy.89
  (14 shorter events, 0.0 us)
Async XLA Ops:
  0.7 4.5 %copy-start.13 = (bf16[128,3,256]{2,0,1:T(8,128)(2,1)S(1)}, bf16[128,3,256]{2,0,1:T(8,128)(2,1)}, u32[]{:S(2)}) copy-start(bf16[128,3,256]{2,0,1:T(8,128)(2,1)} %param.17) | copy-start | bytes 589828
  2.6 3.4 copy-start.12
  2.6 4.1 copy-start.20
  295.3 4.0 copy-start.6
  295.3 5.0 %copy-start.4 = (f32[128,2,656]{0,2,1:T(8,128)S(1)}, f32[128,2,656]{0,2,1:T(8,128)}, u32[]{:S(2)}) copy-start(f32[128,2,656]{0,2,1:T(8,128)} %param.24) | copy-start | bytes 2015236
  298.4 3.1 copy-start.11
  298.4 4.0 copy-start
  299.2 4.1 copy-start.5
  421.2 2.9 copy-start.10
  421.2 4.0 copy-start.9
  424.1 2.2 copy-start.3
  424.1 3.3 copy-start.2
  425.2 3.3 copy-start.8
  425.4 4.0 copy-start.7
  426.3 4.0 copy-start.14
  426.3 4.0 copy-start.17
  426.3 4.0 copy-start.18
  426.3 4.0 copy-start.19
  426.3 4.6 %copy-start.1 = (bf16[2,256,1024]{2,1,0:T(8,128)(2,1)S(1)}, bf16[2,256,1024]{2,1,0:T(8,128)(2,1)}, u32[]{:S(2)}) copy-start(bf16[2,256,1024]{2,1,0:T(8,128)(2,1)} %get-tuple-element.62) | copy-start | bytes 3145732
  428.5 3.4 copy-start.16
  428.5 4.1 copy-start.15

commit v7 on v6

--- a/solution.py
+++ b/solution.py
@@ -3,6 +3,7 @@
 
 import jax
 import jax.numpy as jnp
+import numpy as np
 from jax import lax
 from jax.experimental import pallas as pl
 from jax.experimental.pallas import tpu as pltpu
@@ -441,9 +442,10 @@
 
 def forward_kernel(*refs):
     refs = list(refs)
-    shards, (inputs, cotangent, lengths, gains, cosine, sine) = take(refs, 6), take(refs, 6)
+    shards, (inputs, cotangent, lengths, gains, frequency) = take(refs, 6), take(refs, 5)
     wholes, (rows_low, grad_rows) = take(refs, 6), take(refs, 2)
     low_one, queries, own, other, context, log_total, bias, middle, low_two = take(refs, 9)
+    cosine, sine = take(refs, 2)
     other_lengths, weight, attn_weight = take(refs, 3)
     sems = take(refs, 12)
     pair_send, pair_recv, length_send, length_recv, weight_sem, attn_sem = take(refs, 6)
@@ -492,6 +494,17 @@
     position = lax.broadcasted_iota(jnp.int32, bias.shape, 0)
     position = lax.rem(position + core * count, 2 * count).astype(jnp.float32)
     bias[...] = jnp.where(position < length, 0.0, MASK_VALUE)
+
+    @pl.loop(0, bias.shape[0] // 128)
+    def _(index):
+        first = pl.multiple_of(index * 128, 128)
+        place = lax.broadcasted_iota(jnp.int32, (128, 128), 0) + first + core * count
+        angles = lax.rem(place, 2 * count).astype(jnp.float32) * frequency[0:1]
+        half_lane = lax.rem(lane_of((128, 128)), HEAD_DIM) < HEAD_DIM // 2
+        cosine[pl.ds(first, 128)] = jnp.cos(angles)
+        turned_sine = jnp.sin(angles)
+        sine[pl.ds(first, 128)] = jnp.where(half_lane, -turned_sine, turned_sine)
+
     moves[0][1]()
 
     @pl.loop(0, count // step)
@@ -567,7 +580,7 @@
     moves[1][1]()
 
 
-def forward(shards, inputs, cotangent, lengths, gains, cosine, sine, collective_id):
+def forward(shards, inputs, cotangent, lengths, gains, frequency, collective_id):
     sem = pltpu.SemaphoreType.DMA
     anywhere = pl.BlockSpec(memory_space=pl.ANY)
     local = pl.BlockSpec(memory_space=pltpu.VMEM)
@@ -590,9 +603,11 @@
             shape((2 * count, 128), f32),
             shape((count, width), f32),
             shape((count, width), bf16),
+            shape((2 * count, 128), f32),
+            shape((2 * count, 128), f32),
         ],
-        in_specs=[anywhere] * 8 + [local] * 4,
-        out_specs=[anywhere] * 6 + [local, anywhere] + [local] * 9,
+        in_specs=[anywhere] * 8 + [local] * 3,
+        out_specs=[anywhere] * 6 + [local, anywhere] + [local] * 11,
         scratch_shapes=[
             pltpu.VMEM(lengths.shape, f32),
             pltpu.VMEM((2, 3, third, width), bf16),
@@ -607,7 +622,7 @@
             collective_id=collective_id, has_side_effects=True, vmem_limit_bytes=58 * 1024 * 1024
         ),
         name="forward",
-    )(*shards, inputs, cotangent, lengths, gains, cosine, sine)
+    )(*shards, inputs, cotangent, lengths, gains, frequency)
 
 
 def attend_pair(columns, queries, own, other, bias, context, log_total):
@@ -1074,15 +1089,27 @@
 def product_of(left, right, dims):
     return lax.dot_general(left, right, (dims, ((), ())), preferred_element_type=jnp.float32)
 
+def tiles_of(like):
+    if len(like.shape) == 2 and like.shape[1] == 128:
+        return [(pl.ds(0, like.shape[0]), (slice(None), slice(None)), True)]
+    width = like.shape[-1]
+    tiles = []
+    for part in range(like.shape[0] if len(like.shape) == 3 else 1):
+        for first in range(0, width, 128):
+            columns = slice(first, first + 128)
+            place = (part, slice(None), columns) if len(like.shape) == 3 else (slice(None), columns)
+            tiles.append((pl.ds(part * width + first, 128), place, False))
+    return tiles
+
+
 def optimize_kernel(heights, *refs):
     refs = list(refs)
     count, size, tile = len(heights), 1024, 256
     f32, bf16 = jnp.float32, jnp.bfloat16
-    sums, moments, weights = take(refs, count), take(refs, count), take(refs, count)
-    (gain_two, gains), far = take(refs, 2), take(refs, 8)
-    new_moments, new_weights = take(refs, count), take(refs, count)
-    gain_out, rows_out = take(refs, 2)
-    blocks, backs = take(refs, count), take(refs, count)
+    sums, moments = take(refs, count), take(refs, count)
+    (gain_two, gains), far = take(refs, 2), take(refs, 7)
+    far = far[:4] + [far[4].at[0], far[4].at[1]] + far[5:]
+    backs, (gain_out, rows_out), blocks = take(refs, count), take(refs, 2), take(refs, count)
     whole, steps, gain_parts = take(refs, 3)
     iterate, poly, product, total = take(refs, 4)
     iterate_low, poly_low, other_low, total_low = take(refs, 4)
@@ -1129,17 +1156,12 @@
             def _():
                 body(part)
 
-    def tiles_of(part):
-        height = heights[part]
-        return [(first, min(128, height - first)) for first in range(0, height, 128)]
-
     greet(plane, (partner, across, down), planes)
     for part in (2, 0, 3, 1):
-        for first, extent in tiles_of(part):
-            rows, columns = pl.ds(first, extent), slice(first, first + extent)
-            added = MOMENTUM * moments[part][:, columns] + sums[part][rows].T
-            new_moments[part][:, columns] = added
-            blocks[part][rows] = low(added.T)
+        for rows, place_of, is_turned in tiles_of(moments[part]):
+            moment = moments[part][place_of]
+            moment = moment if is_turned else moment.T
+            blocks[part][rows] = low(MOMENTUM * moment + sums[part][rows])
 
         @pl.when(plane != part)
         def _():
@@ -1361,14 +1383,6 @@
 
     on_plane(lambda part: wait_for(backs[part], back_sem))
     off_plane(lambda part: wait_for(backs[part], recv_b.at[part]))
-    for part in range(count):
-        rate = MUON_RATE * 0.2 * math.sqrt(4 * heights[part])
-        for first, extent in tiles_of(part):
-            rows, columns_of = pl.ds(first, extent), slice(first, first + extent)
-            step = backs[part][rows].astype(f32).T
-            kept = weights[part][:, columns_of].astype(f32) * (1.0 - MUON_RATE * DECAY_RATE)
-            new_weights[part][:, columns_of] = kept - rate * step
-
     def last_waits(part):
         for slot in range(4):
             for sem in (send_x.at[slot], send_y.at[slot], send_d.at[slot]):
@@ -1383,21 +1397,21 @@
     finish_move()
 
 
-def optimize(sums, moments, weights, gain_two, gains, far, collective_id):
+def optimize(sums, moments, gain_two, gains, far, collective_id):
     heights = [part.shape[0] for part in sums]
     count, size = len(heights), gains.shape[1]
     f32, bf16 = jnp.float32, jnp.bfloat16
     sem = pltpu.SemaphoreType.DMA
     anywhere = pl.BlockSpec(memory_space=pl.ANY)
     local = pl.BlockSpec(memory_space=pltpu.VMEM)
-    half = far[6].shape[0]
+    half = far[5].shape[0]
     outs = pl.pallas_call(
         functools.partial(optimize_kernel, heights),
-        out_shape=[jax.ShapeDtypeStruct((128, height), f32) for height in heights] * 2
+        out_shape=[jax.ShapeDtypeStruct((height, 128), bf16) for height in heights]
         + [jax.ShapeDtypeStruct(gains.shape, f32), jax.ShapeDtypeStruct((2, half // 2, size), bf16)],
-        in_specs=[local] * (3 * count + 2) + [anywhere] * 8,
-        out_specs=[local] * (2 * count + 1) + [anywhere],
-        scratch_shapes=[pltpu.VMEM((height, 128), bf16) for height in heights] * 2
+        in_specs=[local] * (2 * count + 2) + [anywhere] * 7,
+        out_specs=[local] * (count + 1) + [anywhere],
+        scratch_shapes=[pltpu.VMEM((height, 128), bf16) for height in heights]
         + [pltpu.VMEM((4 * max(heights), size), bf16), pltpu.VMEM((4 * max(heights), 128), bf16)]
         + [pltpu.VMEM((6,) + gains.shape, f32)]
         + [pltpu.VMEM((size, size), f32)] * 4
@@ -1412,8 +1426,37 @@
             collective_id=collective_id, has_side_effects=True, vmem_limit_bytes=60 * 1024 * 1024
         ),
         name="optimize",
-    )(*sums, *moments, *weights, gain_two, gains, *far)
-    return (outs[:count], outs[count : 2 * count], outs[2 * count], outs[2 * count + 1])
+    )(*sums, *moments, gain_two, gains, *far)
+    return (outs[:count], outs[count], outs[count + 1])
+
+
+def settle_kernel(*refs):
+    refs = list(refs)
+    sums, steps, moments, weights = (take(refs, 4) for _ in range(4))
+    new_moments, new_weights = take(refs, 4), take(refs, 4)
+    for part in range(4):
+        rate = MUON_RATE * 0.2 * math.sqrt(4 * sums[part].shape[0])
+        for rows, place, is_turned in tiles_of(moments[part]):
+            gradient, step = sums[part][rows], steps[part][rows].astype(jnp.float32)
+            if not is_turned:
+                gradient, step = gradient.T, step.T
+            kept = weights[part][place].astype(jnp.float32) * (1.0 - MUON_RATE * DECAY_RATE)
+            new_moments[part][place] = MOMENTUM * moments[part][place] + gradient
+            new_weights[part][place] = kept - rate * step
+
+
+def settle(sums, steps, moments, weights):
+    local = pl.BlockSpec(memory_space=pltpu.VMEM)
+    shapes = [jax.ShapeDtypeStruct(moment.shape, jnp.float32) for moment in moments]
+    outs = pl.pallas_call(
+        settle_kernel,
+        out_shape=shapes * 2,
+        in_specs=[local] * 16,
+        out_specs=[local] * 8,
+        compiler_params=pltpu.CompilerParams(vmem_limit_bytes=48 * 1024 * 1024),
+        name="settle",
+    )(*sums, *steps, *moments, *weights)
+    return (outs[:4], outs[4:])
 
 
 def weight_shards(weights):
@@ -1641,6 +1684,18 @@
     return ([returned[index, :, :height].T for index, height in enumerate(heights)], gain_grad)
 
 
+def view_of(block):
+    if block.shape[-1] % 128:
+        return turn(block)
+    return block.transpose(1, 0, 2) if block.ndim == 3 else block
+
+
+def unview(view, like):
+    if like.shape[-1] % 128:
+        return turn_back(view, like)
+    return view.transpose(1, 0, 2) if like.ndim == 3 else view
+
+
 def on_device(
     inputs,
     cotangent,
@@ -1674,15 +1729,19 @@
     positions = jnp.concatenate(
         [core * local_rows + jnp.arange(local_rows), (1 - core) * local_rows + jnp.arange(local_rows)]
     )
-    cosine, sine = rotary(positions)
     shards = weight_shards(weights)
     if fits:
         sizes = lengths.astype(jnp.float32)
         sizes = jnp.broadcast_to(jnp.pad(sizes, ((0, 6), (0, 0))), (8, 128))
-        outs = forward(shards, inputs[:, 0], cotangent[:, 0], sizes, norm_gains, cosine, sine, 1)
+        exponents = np.arange(HEAD_DIM // 2, dtype=np.float32) / np.float32(HEAD_DIM // 2)
+        frequency = np.power(np.float32(ROPE_BASE), -exponents).astype(np.float32)
+        frequency = jnp.asarray(np.tile(frequency, (8, 4)))
+        outs = forward(shards, inputs[:, 0], cotangent[:, 0], sizes, norm_gains, frequency, 1)
         wholes, (rows_low, cotangent_low) = outs[:6], outs[6:8]
-        low_one, queries, own, other, context, log_total, bias, middle, low_two = outs[8:]
+        low_one, queries, own, other, context, log_total, bias, middle, low_two = outs[8:17]
+        cosine, sine = outs[17:]
     else:
+        cosine, sine = rotary(positions)
         wholes = gather_weights(shards)
         rows_low = to_sequences(inputs[:, 0], lists, odd, upper)
         cotangent_low = to_sequences(cotangent[:, 0], lists, odd, upper)
@@ -1750,18 +1809,13 @@
     grad_parts = (grad_query, grad_pair[0], grad_pair[1])
     weight_parts = [part.reshape(-1, width) for part in (query_all, key_all, value_all)]
     if fits:
-        far = (*weight_parts, *grad_parts, rows_low, grad_middle)
-        new_moments, new_weights, gain_grad, input_grad = optimize(
-            sums,
-            [moment.reshape(row_count, -1) for moment in moments],
-            [weight.reshape(row_count, -1) for weight in weights],
-            gain_two,
-            norm_gains,
-            far,
-            3,
+        far = (*weight_parts, grad_query, grad_pair, rows_low, grad_middle)
+        viewed = [view_of(moment) for moment in moments]
+        steps, gain_grad, input_grad = optimize(sums, viewed, gain_two, norm_gains, far, 3)
+        outs = settle(sums, steps, viewed, [view_of(weight) for weight in weights])
+        new_moments, new_weights = (
+            [unview(part, like) for part, like in zip(parts, moments)] for parts in outs
         )
-        new_moments = [part.reshape(like.shape) for part, like in zip(new_moments, moments)]
-        new_weights = [part.reshape(like.shape) for part, like in zip(new_weights, moments)]
     else:
         grad_scaled_one = sum(
             einsum("sk,kn->sn", part, weight) for part, weight in zip(grad_parts, weight_parts)

time: 442 us -> 429 us (0.971)
  local copies, waits for them, and re-layouts: 19.5 us -> 8.72 us
where the time goes in v7:
time: 429 us; the launch traced here: 422 us
  Pallas kernels  407 us (95%)
  local copies, waits for them, and re-layouts  8.72 us (2%)
  other arithmetic  4.93 us (1%)
    pallas_call x1, Pallas kernels, backward(): pl.pallas_call(backward_kernel, out_shape=[shape((rows, 128), f32) for ro...  165 us
    pallas_call x1, Pallas kernels, forward(): pl.pallas_call(forward_kernel, out_shape=[shape((4, shard.shape[0], width...  125 us
    pallas_call x1, Pallas kernels, optimize(): pl.pallas_call(functools.partial(optimize_kernel, heights), out_shape=[ja...  116 us

profile of v7, /device:TPU:9, one launch (start us, length us, event | category | flops | bytes accessed | tf_op | source)
XLA Modules:
  0.0 421.9 jit_solution(1860849134442945342)
XLA Ops:
  0.6 0.7 convert_element_type.11
  1.3 0.7 broadcast_in_dim.12.refs_8_
  2.0 1.6 copy.29
  3.5 1.1 copy.28
  4.6 0.7 slice_bitcast_fusion
  5.3 124.9 %forward.1 = (bf16[4,256,1024]{2,1,0:T(8,128)(2,1)}, bf16[4,256,1024]{2,1,0:T(8,128)(2,1)}, bf16[4,256,1024]{2,1,0:T(8,128)(2,1)}, bf16[4,256,1024]{2,1,0:T(8,12...) custom-call(bf16[256,128]{1,0:T(8,128)(2,1)} %get-tuple-element.115., ...), custom_call_target="tpu_custom_call" | custom-call | tf_op jit(solution)/shard_map/forward/pallas_call | solution.py:591
  130.2 164.8 %backward.1 = (f32[768,128]{1,0:T(8,128)}, f32[256,128]{1,0:T(8,128)}, f32[1312,128]{1,0:T(8,128)}, f32[656,128]{1,0:T(8,128)}, bf16[512,1024]{1,0:T(8,128)(2,1)...) custom-call(bf16[4,1312,1024]{2,1,0:T(8,128)(2,1)} %get-tuple-elemen, ...), custom_call_target="tpu_custom_call" | custom-call | tf_op jit(solution)/shard_map/backward/pallas_call | solution.py:1023
  295.0 0.0 copy-start.17
  295.0 0.0 copy-start.18
  295.0 0.0 copy-start.19
  295.0 0.0 copy-start.7
  295.0 0.0 copy-start.8
  295.0 0.0 copy-start.9
  295.0 0.0 copy-start.10
  295.1 115.6 %optimize.1 = (bf16[768,128]{1,0:T(8,128)(2,1)}, bf16[256,128]{1,0:T(8,128)(2,1)}, bf16[1312,128]{1,0:T(8,128)(2,1)}, bf16[656,128]{1,0:T(8,128)(2,1)}, f32[2,10...) custom-call(f32[768,128]{1,0:T(8,128)} %get-tuple-element.71.refs_0_, f32[256,128]{1,0:T(8,128)} %get-tuple-element.72.refs_1_, ...), custom_call_target="tpu_custom_call" | custom-call | tf_op jit(solution)/shard_map/optimize/pallas_call | solution.py:1408
  410.7 0.0 copy-start
  410.7 0.0 copy-start.1
  410.7 0.0 copy-start.2
  410.7 0.0 copy-start.3
  410.8 0.0 copy-start.4
  410.8 0.0 copy-start.5
  410.8 0.0 copy-start.6
  410.8 0.0 copy-start.12
  410.8 0.0 copy-done.17
  410.8 0.0 copy-done.18
  410.8 0.0 copy-done.19
  410.8 1.5 multiply_subtract_fusion
  412.3 2.8 bitcast_convert_fusion
  415.1 0.0 copy-done.7
  415.1 0.0 copy-done.8
  415.1 0.0 copy-done.9
  415.1 0.0 copy-done.10
  415.1 0.0 copy-done
  415.1 0.0 copy-done.1
  415.1 0.0 copy-done.2
  415.1 0.0 copy-done.3
  415.2 0.0 copy-done.4
  415.2 0.0 copy-done.5
  415.2 0.0 copy-done.6
  415.2 0.0 copy-done.12
  415.2 0.0 copy-start.11
  415.2 1.0 copy-done.11
  416.2 0.0 copy-start.13
  416.2 0.9 copy-done.13
  417.1 0.0 copy-start.14
  417.1 0.9 copy-done.14
  418.0 0.0 copy-start.15
  418.0 0.8 copy-done.15
  418.9 0.0 copy-start.16
  418.9 1.9 settle.1
  420.7 0.0 copy-done.16
  420.8 1.0 copy.33
  (1 shorter events, 0.0 us)
Async XLA Ops:
  295.0 115.8 %copy-start.17 = (f32[2,1024]{1,0:T(2,128)S(1)}, f32[2,1024]{1,0:T(2,128)}, u32[]{:S(2)}) copy-start(f32[2,1024]{1,0:T(2,128)} %refs_9_.4) | copy-start | bytes 24580
  295.0 115.8 %copy-start.18 = (f32[2,1024]{1,0:T(2,128)S(1)}, f32[2,1024]{1,0:T(2,128)}, u32[]{:S(2)}) copy-start(f32[2,1024]{1,0:T(2,128)} %param.28) | copy-start | bytes 24580
  295.0 115.8 %copy-start.19 = (f32[2,1024]{1,0:T(2,128)S(1)}, f32[2,1024]{1,0:T(2,128)}, u32[]{:S(2)}) copy-start(f32[2,1024]{1,0:T(2,128)} %param.27) | copy-start | bytes 24580
  295.0 120.1 %copy-start.7 = (bf16[128,3,256]{2,0,1:T(8,128)(2,1)S(1)}, bf16[128,3,256]{2,0,1:T(8,128)(2,1)}, u32[]{:S(2)}) copy-start(bf16[128,3,256]{2,0,1:T(8,128)(2,1)} %param.18) | copy-start | bytes 589828
  295.0 120.1 %copy-start.8 = (bf16[128,656]{0,1:T(8,128)(2,1)S(1)}, bf16[128,656]{0,1:T(8,128)(2,1)}, u32[]{:S(2)}) copy-start(bf16[128,656]{0,1:T(8,128)(2,1)} %param.21) | copy-start | bytes 503812
  295.0 120.1 %copy-start.9 = (f32[128,256]{1,0:T(8,128)S(1)}, f32[128,256]{1,0:T(8,128)}, u32[]{:S(2)}) copy-start(f32[128,256]{1,0:T(8,128)} %refs_9_.5) | copy-start | bytes 393220
  295.0 120.1 %copy-start.10 = (f32[256,128]{1,0:T(8,128)S(1)}, f32[256,128]{1,0:T(8,128)}, u32[]{:S(2)}) copy-start(f32[256,128]{1,0:T(8,128)} %get-tuple-element.72.refs_1_) | copy-start | bytes 393220
  410.7 4.4 %copy-start = (f32[128,2,656]{0,2,1:T(8,128)S(1)}, f32[128,2,656]{0,2,1:T(8,128)}, u32[]{:S(2)}) copy-start(f32[128,2,656]{0,2,1:T(8,128)} %param.25) | copy-start | bytes 2015236
  410.7 4.4 %copy-start.1 = (f32[1312,128]{1,0:T(8,128)S(1)}, f32[1312,128]{1,0:T(8,128)}, u32[]{:S(2)}) copy-start(f32[1312,128]{1,0:T(8,128)} %get-tuple-element.73.refs_2_) | copy-start | bytes 2015236
  410.7 4.4 %copy-start.2 = (f32[128,3,256]{2,0,1:T(8,128)S(1)}, f32[128,3,256]{2,0,1:T(8,128)}, u32[]{:S(2)}) copy-start(f32[128,3,256]{2,0,1:T(8,128)} %param.23) | copy-start | bytes 1179652
  410.7 4.4 %copy-start.3 = (f32[768,128]{1,0:T(8,128)S(1)}, f32[768,128]{1,0:T(8,128)}, u32[]{:S(2)}) copy-start(f32[768,128]{1,0:T(8,128)} %get-tuple-element.71.refs_0_) | copy-start | bytes 1179652
  410.8 4.4 %copy-start.4 = (bf16[128,2,656]{0,2,1:T(8,128)(2,1)S(1)}, bf16[128,2,656]{0,2,1:T(8,128)(2,1)}, u32[]{:S(2)}) copy-start(bf16[128,2,656]{0,2,1:T(8,128)(2,1)} %param.20) | copy-start | bytes 1007620
  410.8 4.4 %copy-start.5 = (f32[128,656]{0,1:T(8,128)S(1)}, f32[128,656]{0,1:T(8,128)}, u32[]{:S(2)}) copy-start(f32[128,656]{0,1:T(8,128)} %param.26) | copy-start | bytes 1007620
  410.8 4.4 %copy-start.6 = (f32[656,128]{1,0:T(8,128)S(1)}, f32[656,128]{1,0:T(8,128)}, u32[]{:S(2)}) copy-start(f32[656,128]{1,0:T(8,128)} %get-tuple-element.74.refs_3_) | copy-start | bytes 1007620
  410.8 4.4 %copy-start.12 = (bf16[128,256]{1,0:T(8,128)(2,1)S(1)}, bf16[128,256]{1,0:T(8,128)(2,1)}, u32[]{:S(2)}) copy-start(bf16[128,256]{1,0:T(8,128)(2,1)} %refs_13_.1) | copy-start | bytes 196612
  415.2 1.0 copy-start.11
  416.2 0.9 copy-start.13
  417.1 0.9 copy-start.14
  418.0 0.8 copy-start.15
  418.9 1.9 copy-start.16

commit v8 on v7

--- a/solution.py
+++ b/solution.py
@@ -443,13 +443,19 @@
 def forward_kernel(*refs):
     refs = list(refs)
     shards, (inputs, cotangent, lengths, gains, frequency) = take(refs, 6), take(refs, 5)
-    wholes, (rows_low, grad_rows) = take(refs, 6), take(refs, 2)
-    low_one, queries, own, other, context, log_total, bias, middle, low_two = take(refs, 9)
-    cosine, sine = take(refs, 2)
+    wholes, (far_rows, grad_rows) = take(refs, 6), take(refs, 2)
+    far = [far_rows] + take(refs, 4)
+    context, log_total, bias, middle, low_two, cosine, sine = take(refs, 7)
+    near = take(refs, 5)
+    rows_low, low_one, queries, own, other = near
     other_lengths, weight, attn_weight = take(refs, 3)
     sems = take(refs, 12)
-    pair_send, pair_recv, length_send, length_recv, weight_sem, attn_sem = take(refs, 6)
+    pair_send, pair_recv, length_send, length_recv, weight_sem, attn_sem, out_sem = take(refs, 7)
     move_send, move_recv, move_own = refs
+    outward = [
+        pltpu.make_async_copy(source, target, out_sem.at[index])
+        for index, (source, target) in enumerate(zip(near, far))
+    ]
     me, partner, across, down = neighbours()
     plane = lax.axis_index("tensor")
     core = lax.rem(me, 2)
@@ -512,6 +518,8 @@
         window = pl.ds(pl.multiple_of(index * step, step), step)
         low_one[window] = low(normed_rows(rows_low[window].astype(jnp.float32), gains[0:1]))
 
+    outward[0].start()
+    outward[1].start()
     for part in range(3):
         arrive(part)
 
@@ -543,7 +551,10 @@
                     own[part - 1, :, columns] = low(piece)
 
     send_to(own, other, pair_send, pair_recv, (partner, plane))
+    outward[2].start()
+    outward[3].start()
     wait_for(other, pair_recv)
+    outward[4].start()
     arrive(3)
     attn_copy = pltpu.make_async_copy(wholes[3], attn_weight, attn_sem)
     attn_copy.start()
@@ -575,6 +586,8 @@
         arrive(part)
     for part in range(6):
         finish(part)
+    for copy in outward:
+        copy.wait()
     wait_for(own, pair_send)
     wait_for(lengths, length_send)
     moves[1][1]()
@@ -607,8 +620,13 @@
             shape((2 * count, 128), f32),
         ],
         in_specs=[anywhere] * 8 + [local] * 3,
-        out_specs=[anywhere] * 6 + [local, anywhere] + [local] * 11,
+        out_specs=[anywhere] * 12 + [local] * 7,
         scratch_shapes=[
+            pltpu.VMEM((count, width), bf16),
+            pltpu.VMEM((count, width), bf16),
+            pltpu.VMEM((count, width), bf16),
+            pltpu.VMEM((2, count, width), bf16),
+            pltpu.VMEM((2, count, width), bf16),
             pltpu.VMEM(lengths.shape, f32),
             pltpu.VMEM((2, 3, third, width), bf16),
             pltpu.VMEM((4, third, width), bf16),
@@ -616,7 +634,7 @@
         ]
         + [sem((6, 4))] * 9
         + [sem((6, 4, 4))] * 2
-        + [sem, sem, sem, sem, sem((2, 3)), sem]
+        + [sem, sem, sem, sem, sem((2, 3)), sem, sem((5,))]
         + [sem((2, 2)), sem((2, 2)), sem((2,))],
         compiler_params=pltpu.CompilerParams(
             collective_id=collective_id, has_side_effects=True, vmem_limit_bytes=58 * 1024 * 1024
@@ -982,6 +1000,7 @@
     query_copy.start()
     weight_grad(1, grad_query, low_rows)
     call(0, 5)
+    call(3, 3)
     add_pair(last_pair)
     pair_copy = pltpu.make_async_copy(grad_pair, far_pair, out_sem.at[1])
     pair_copy.start()
@@ -989,7 +1008,7 @@
     call(0, 6)
     weight_grad(3, grad_pair.at[1], low_rows)
     call(0, 7)
-    done = {(1, 4), (3, 2), (2, 3), (1, 0), (2, 0), (1, 1), (3, 0), (2, 1), (1, 2), (3, 1), (2, 2), (1, 3)}
+    done = {(3, 3), (1, 4), (3, 2), (2, 3), (1, 0), (2, 0), (1, 1), (3, 0), (2, 1), (1, 2), (3, 1), (2, 2), (1, 3)}
     for turn_of in range(10):
         for stage in (3, 2, 1):
             part = turn_of - (stage - 1)

time: 429 us -> 422 us (0.984)
  Pallas kernels: 407 us -> 400 us
    pallas_call x1, Pallas kernels: 165 us -> 158 us  [backward(): pl.pallas_call(backward_kernel, out_shape=[shape((rows, 128), f32) for ro...]
where the time goes in v8:
time: 422 us; the launch traced here: 415 us
  Pallas kernels  400 us (95%)
  local copies, waits for them, and re-layouts  8.72 us (2%)
  other arithmetic  4.93 us (1%)
    pallas_call x1, Pallas kernels, backward(): pl.pallas_call(backward_kernel, out_shape=[shape((rows, 128), f32) for ro...  158 us
    pallas_call x1, Pallas kernels, forward(): pl.pallas_call(forward_kernel, out_shape=[shape((4, shard.shape[0], width...  123 us
    pallas_call x1, Pallas kernels, optimize(): pl.pallas_call(functools.partial(optimize_kernel, heights), out_shape=[ja...  117 us

profile of v8, /device:TPU:9, one launch (start us, length us, event | category | flops | bytes accessed | tf_op | source)
XLA Modules:
  0.0 414.7 jit_solution(296842123098717893)
XLA Ops:
  0.6 0.7 convert_element_type.11
  1.3 0.7 broadcast_in_dim.12.refs_8_
  2.0 1.6 copy.29
  3.5 1.1 copy.28
  4.6 0.7 slice_bitcast_fusion
  5.3 123.0 %forward.1 = (bf16[4,256,1024]{2,1,0:T(8,128)(2,1)}, bf16[4,256,1024]{2,1,0:T(8,128)(2,1)}, bf16[4,256,1024]{2,1,0:T(8,128)(2,1)}, bf16[4,256,1024]{2,1,0:T(8,12...) custom-call(bf16[256,128]{1,0:T(8,128)(2,1)} %get-tuple-element.115., ...), custom_call_target="tpu_custom_call" | custom-call | tf_op jit(solution)/shard_map/forward/pallas_call | solution.py:604
  128.4 158.2 %backward.1 = (f32[768,128]{1,0:T(8,128)}, f32[256,128]{1,0:T(8,128)}, f32[1312,128]{1,0:T(8,128)}, f32[656,128]{1,0:T(8,128)}, bf16[512,1024]{1,0:T(8,128)(2,1)...) custom-call(bf16[4,1312,1024]{2,1,0:T(8,128)(2,1)} %get-tuple-elemen, ...), custom_call_target="tpu_custom_call" | custom-call | tf_op jit(solution)/shard_map/backward/pallas_call | solution.py:1042
  286.6 0.0 copy-start.17
  286.6 0.0 copy-start.18
  286.6 0.0 copy-start.19
  286.6 0.0 copy-start.7
  286.6 0.0 copy-start.8
  286.6 0.0 copy-start.9
  286.6 0.0 copy-start.10
  286.6 116.9 %optimize.1 = (bf16[768,128]{1,0:T(8,128)(2,1)}, bf16[256,128]{1,0:T(8,128)(2,1)}, bf16[1312,128]{1,0:T(8,128)(2,1)}, bf16[656,128]{1,0:T(8,128)(2,1)}, f32[2,10...) custom-call(f32[768,128]{1,0:T(8,128)} %get-tuple-element.71.refs_0_, f32[256,128]{1,0:T(8,128)} %get-tuple-element.72.refs_1_, ...), custom_call_target="tpu_custom_call" | custom-call | tf_op jit(solution)/shard_map/optimize/pallas_call | solution.py:1427
  403.5 0.0 copy-start
  403.5 0.0 copy-start.1
  403.6 0.0 copy-start.2
  403.6 0.0 copy-start.3
  403.6 0.0 copy-start.4
  403.6 0.0 copy-start.5
  403.6 0.0 copy-start.6
  403.6 0.0 copy-start.12
  403.6 0.0 copy-done.17
  403.6 0.0 copy-done.18
  403.6 0.0 copy-done.19
  403.7 1.5 multiply_subtract_fusion
  405.1 2.8 bitcast_convert_fusion
  407.9 0.0 copy-done.7
  407.9 0.0 copy-done.8
  407.9 0.0 copy-done.9
  407.9 0.0 copy-done.10
  407.9 0.0 copy-done
  408.0 0.0 copy-done.1
  408.0 0.0 copy-done.2
  408.0 0.0 copy-done.3
  408.0 0.0 copy-done.4
  408.0 0.0 copy-done.5
  408.0 0.0 copy-done.6
  408.0 0.0 copy-done.12
  408.0 0.0 copy-start.11
  408.0 1.0 copy-done.11
  409.0 0.0 copy-start.13
  409.0 0.9 copy-done.13
  409.9 0.0 copy-start.14
  409.9 0.9 copy-done.14
  410.8 0.0 copy-start.15
  410.8 0.8 copy-done.15
  411.7 0.0 copy-start.16
  411.7 1.9 settle.1
  413.6 0.0 copy-done.16
  413.6 1.0 copy.33
  (1 shorter events, 0.0 us)
Async XLA Ops:
  286.6 117.1 %copy-start.17 = (f32[2,1024]{1,0:T(2,128)S(1)}, f32[2,1024]{1,0:T(2,128)}, u32[]{:S(2)}) copy-start(f32[2,1024]{1,0:T(2,128)} %refs_9_.4) | copy-start | bytes 24580
  286.6 117.1 %copy-start.18 = (f32[2,1024]{1,0:T(2,128)S(1)}, f32[2,1024]{1,0:T(2,128)}, u32[]{:S(2)}) copy-start(f32[2,1024]{1,0:T(2,128)} %param.28) | copy-start | bytes 24580
  286.6 117.1 %copy-start.19 = (f32[2,1024]{1,0:T(2,128)S(1)}, f32[2,1024]{1,0:T(2,128)}, u32[]{:S(2)}) copy-start(f32[2,1024]{1,0:T(2,128)} %param.27) | copy-start | bytes 24580
  286.6 121.3 %copy-start.7 = (bf16[128,3,256]{2,0,1:T(8,128)(2,1)S(1)}, bf16[128,3,256]{2,0,1:T(8,128)(2,1)}, u32[]{:S(2)}) copy-start(bf16[128,3,256]{2,0,1:T(8,128)(2,1)} %param.18) | copy-start | bytes 589828
  286.6 121.3 %copy-start.8 = (bf16[128,656]{0,1:T(8,128)(2,1)S(1)}, bf16[128,656]{0,1:T(8,128)(2,1)}, u32[]{:S(2)}) copy-start(bf16[128,656]{0,1:T(8,128)(2,1)} %param.21) | copy-start | bytes 503812
  286.6 121.3 %copy-start.9 = (f32[128,256]{1,0:T(8,128)S(1)}, f32[128,256]{1,0:T(8,128)}, u32[]{:S(2)}) copy-start(f32[128,256]{1,0:T(8,128)} %refs_9_.5) | copy-start | bytes 393220
  286.6 121.3 %copy-start.10 = (f32[256,128]{1,0:T(8,128)S(1)}, f32[256,128]{1,0:T(8,128)}, u32[]{:S(2)}) copy-start(f32[256,128]{1,0:T(8,128)} %get-tuple-element.72.refs_1_) | copy-start | bytes 393220
  403.5 4.4 %copy-start = (f32[128,2,656]{0,2,1:T(8,128)S(1)}, f32[128,2,656]{0,2,1:T(8,128)}, u32[]{:S(2)}) copy-start(f32[128,2,656]{0,2,1:T(8,128)} %param.25) | copy-start | bytes 2015236
  403.5 4.4 %copy-start.1 = (f32[1312,128]{1,0:T(8,128)S(1)}, f32[1312,128]{1,0:T(8,128)}, u32[]{:S(2)}) copy-start(f32[1312,128]{1,0:T(8,128)} %get-tuple-element.73.refs_2_) | copy-start | bytes 2015236
  403.6 4.4 %copy-start.2 = (f32[128,3,256]{2,0,1:T(8,128)S(1)}, f32[128,3,256]{2,0,1:T(8,128)}, u32[]{:S(2)}) copy-start(f32[128,3,256]{2,0,1:T(8,128)} %param.23) | copy-start | bytes 1179652
  403.6 4.4 %copy-start.3 = (f32[768,128]{1,0:T(8,128)S(1)}, f32[768,128]{1,0:T(8,128)}, u32[]{:S(2)}) copy-start(f32[768,128]{1,0:T(8,128)} %get-tuple-element.71.refs_0_) | copy-start | bytes 1179652
  403.6 4.4 %copy-start.4 = (bf16[128,2,656]{0,2,1:T(8,128)(2,1)S(1)}, bf16[128,2,656]{0,2,1:T(8,128)(2,1)}, u32[]{:S(2)}) copy-start(bf16[128,2,656]{0,2,1:T(8,128)(2,1)} %param.20) | copy-start | bytes 1007620
  403.6 4.4 %copy-start.5 = (f32[128,656]{0,1:T(8,128)S(1)}, f32[128,656]{0,1:T(8,128)}, u32[]{:S(2)}) copy-start(f32[128,656]{0,1:T(8,128)} %param.26) | copy-start | bytes 1007620
  403.6 4.4 %copy-start.6 = (f32[656,128]{1,0:T(8,128)S(1)}, f32[656,128]{1,0:T(8,128)}, u32[]{:S(2)}) copy-start(f32[656,128]{1,0:T(8,128)} %get-tuple-element.74.refs_3_) | copy-start | bytes 1007620
  403.6 4.4 %copy-start.12 = (bf16[128,256]{1,0:T(8,128)(2,1)S(1)}, bf16[128,256]{1,0:T(8,128)(2,1)}, u32[]{:S(2)}) copy-start(bf16[128,256]{1,0:T(8,128)(2,1)} %refs_13_.1) | copy-start | bytes 196612
  408.0 1.0 copy-start.11
  409.0 0.9 copy-start.13
  409.9 0.9 copy-start.14
  410.8 0.8 copy-start.15
  411.7 1.9 copy-start.16

commit v9 on v8

--- a/solution.py
+++ b/solution.py
@@ -156,7 +156,11 @@
     for other in planes:
         for same_place in [me] + crossed:
             pl.semaphore_signal(barrier, inc=1, device_id=(same_place, other), device_id_type=MESH)
-    pl.semaphore_wait(barrier, len(others) + len(planes) * (1 + len(crossed)))
+    return len(others) + len(planes) * (1 + len(crossed))
+
+
+def greeted(total):
+    pl.semaphore_wait(pltpu.get_barrier_semaphore(), total)
 
 def add_into(target, source, rows, step):
     @pl.loop(0, rows // step)
@@ -464,7 +468,7 @@
         move_plan(False, source, target, move_send.at[index], move_recv.at[index], move_own.at[index])
         for index, (source, target) in enumerate(((inputs, rows_low), (cotangent, grad_rows)))
     ]
-    greet(plane, (partner, across, down), [lax.rem(plane + offset, 4) for offset in (1, 2, 3)])
+    greeted(greet(plane, (partner, across, down), [lax.rem(plane + offset, 4) for offset in (1, 2, 3)]))
     count, width = rows_low.shape
     third = shards[0].shape[0]
     step = 64
@@ -836,13 +840,14 @@
         pltpu.make_async_copy(far_two, branch, load_sem.at[0]),
         pltpu.make_async_copy(far_cot, cotangent, load_sem.at[1]),
     ]
+    expected = greet(plane, (partner, across, down), [lax.rem(plane + offset, 4) for offset in (1, 2, 3)])
     start_all(first_loads)
     start_all(weight_copies(0, 0))
     start_all(weight_copies(0, 1))
-    greet(plane, (partner, across, down), [lax.rem(plane + offset, 4) for offset in (1, 2, 3)])
     result[...] = jnp.zeros_like(result)
     grad_rows[...] = jnp.zeros_like(grad_rows)
     wait_all(first_loads)
+    greeted(expected)
     feed_calls = {(1, 1): ((1, 0),), (2, 1): ((1, 1),), (3, 0): ((2, 0),), (3, 1): ((1, 2),)}
 
     @pl.loop(0, 4)
@@ -1150,6 +1155,7 @@
         pltpu.make_async_copy(source, target, load_sem.at[index])
         for index, (source, target) in enumerate(zip(far, near))
     ]
+    expected = greet(plane, (partner, across, down), planes)
     for load in loads:
         load.start()
 
@@ -1175,12 +1181,13 @@
             def _():
                 body(part)
 
-    greet(plane, (partner, across, down), planes)
     for part in (2, 0, 3, 1):
         for rows, place_of, is_turned in tiles_of(moments[part]):
             moment = moments[part][place_of]
             moment = moment if is_turned else moment.T
             blocks[part][rows] = low(MOMENTUM * moment + sums[part][rows])
+        if part == 2:
+            greeted(expected)
 
         @pl.when(plane != part)
         def _():

time: 422 us -> 422 us (level)
  no operation moved by 1% of the time
where the time goes in v9:
time: 422 us; the launch traced here: 414 us
  Pallas kernels  400 us (95%)
  local copies, waits for them, and re-layouts  8.72 us (2%)
  other arithmetic  4.93 us (1%)
    pallas_call x1, Pallas kernels, backward(): pl.pallas_call(backward_kernel, out_shape=[shape((rows, 128), f32) for ro...  158 us
    pallas_call x1, Pallas kernels, forward(): pl.pallas_call(forward_kernel, out_shape=[shape((4, shard.shape[0], width...  123 us
    pallas_call x1, Pallas kernels, optimize(): pl.pallas_call(functools.partial(optimize_kernel, heights), out_shape=[ja...  117 us

profile of v9, /device:TPU:9, one launch (start us, length us, event | category | flops | bytes accessed | tf_op | source)
XLA Modules:
  0.0 414.4 jit_solution(15676320154610480294)
XLA Ops:
  0.6 0.7 convert_element_type.11
  1.3 0.7 broadcast_in_dim.12.refs_8_
  2.0 1.6 copy.29
  3.5 1.1 copy.28
  4.6 0.7 slice_bitcast_fusion
  5.3 123.0 %forward.1 = (bf16[4,256,1024]{2,1,0:T(8,128)(2,1)}, bf16[4,256,1024]{2,1,0:T(8,128)(2,1)}, bf16[4,256,1024]{2,1,0:T(8,128)(2,1)}, bf16[4,256,1024]{2,1,0:T(8,12...) custom-call(bf16[256,128]{1,0:T(8,128)(2,1)} %get-tuple-element.115., ...), custom_call_target="tpu_custom_call" | custom-call | tf_op jit(solution)/shard_map/forward/pallas_call | solution.py:608
  128.4 158.0 %backward.1 = (f32[768,128]{1,0:T(8,128)}, f32[256,128]{1,0:T(8,128)}, f32[1312,128]{1,0:T(8,128)}, f32[656,128]{1,0:T(8,128)}, bf16[512,1024]{1,0:T(8,128)(2,1)...) custom-call(bf16[4,1312,1024]{2,1,0:T(8,128)(2,1)} %get-tuple-elemen, ...), custom_call_target="tpu_custom_call" | custom-call | tf_op jit(solution)/shard_map/backward/pallas_call | solution.py:1047
  286.4 0.0 copy-start.17
  286.4 0.0 copy-start.18
  286.4 0.0 copy-start.19
  286.4 0.0 copy-start.7
  286.5 0.0 copy-start.8
  286.5 0.0 copy-start.9
  286.5 0.0 copy-start.10
  286.5 116.7 %optimize.1 = (bf16[768,128]{1,0:T(8,128)(2,1)}, bf16[256,128]{1,0:T(8,128)(2,1)}, bf16[1312,128]{1,0:T(8,128)(2,1)}, bf16[656,128]{1,0:T(8,128)(2,1)}, f32[2,10...) custom-call(f32[768,128]{1,0:T(8,128)} %get-tuple-element.71.refs_0_, f32[256,128]{1,0:T(8,128)} %get-tuple-element.72.refs_1_, ...), custom_call_target="tpu_custom_call" | custom-call | tf_op jit(solution)/shard_map/optimize/pallas_call | solution.py:1434
  403.2 0.0 copy-start
  403.2 0.0 copy-start.1
  403.2 0.0 copy-start.2
  403.2 0.0 copy-start.3
  403.2 0.0 copy-start.4
  403.2 0.0 copy-start.5
  403.2 0.0 copy-start.6
  403.3 0.0 copy-start.12
  403.3 0.0 copy-done.17
  403.3 0.0 copy-done.18
  403.3 0.0 copy-done.19
  403.3 1.5 multiply_subtract_fusion
  404.8 2.8 bitcast_convert_fusion
  407.6 0.0 copy-done.7
  407.6 0.0 copy-done.8
  407.6 0.0 copy-done.9
  407.6 0.0 copy-done.10
  407.6 0.0 copy-done
  407.6 0.0 copy-done.1
  407.6 0.0 copy-done.2
  407.6 0.0 copy-done.3
  407.6 0.0 copy-done.4
  407.6 0.0 copy-done.5
  407.6 0.0 copy-done.6
  407.7 0.0 copy-done.12
  407.7 0.0 copy-start.11
  407.7 1.0 copy-done.11
  408.6 0.0 copy-start.13
  408.6 0.9 copy-done.13
  409.6 0.0 copy-start.14
  409.6 0.9 copy-done.14
  410.5 0.0 copy-start.15
  410.5 0.8 copy-done.15
  411.3 0.0 copy-start.16
  411.3 1.9 settle.1
  413.2 0.0 copy-done.16
  413.2 1.0 copy.33
  (1 shorter events, 0.0 us)
Async XLA Ops:
  286.4 116.9 %copy-start.17 = (f32[2,1024]{1,0:T(2,128)S(1)}, f32[2,1024]{1,0:T(2,128)}, u32[]{:S(2)}) copy-start(f32[2,1024]{1,0:T(2,128)} %refs_9_.4) | copy-start | bytes 24580
  286.4 116.9 %copy-start.18 = (f32[2,1024]{1,0:T(2,128)S(1)}, f32[2,1024]{1,0:T(2,128)}, u32[]{:S(2)}) copy-start(f32[2,1024]{1,0:T(2,128)} %param.28) | copy-start | bytes 24580
  286.4 116.9 %copy-start.19 = (f32[2,1024]{1,0:T(2,128)S(1)}, f32[2,1024]{1,0:T(2,128)}, u32[]{:S(2)}) copy-start(f32[2,1024]{1,0:T(2,128)} %param.27) | copy-start | bytes 24580
  286.4 121.1 %copy-start.7 = (bf16[128,3,256]{2,0,1:T(8,128)(2,1)S(1)}, bf16[128,3,256]{2,0,1:T(8,128)(2,1)}, u32[]{:S(2)}) copy-start(bf16[128,3,256]{2,0,1:T(8,128)(2,1)} %param.18) | copy-start | bytes 589828
  286.5 121.1 %copy-start.8 = (bf16[128,656]{0,1:T(8,128)(2,1)S(1)}, bf16[128,656]{0,1:T(8,128)(2,1)}, u32[]{:S(2)}) copy-start(bf16[128,656]{0,1:T(8,128)(2,1)} %param.21) | copy-start | bytes 503812
  286.5 121.1 %copy-start.9 = (f32[128,256]{1,0:T(8,128)S(1)}, f32[128,256]{1,0:T(8,128)}, u32[]{:S(2)}) copy-start(f32[128,256]{1,0:T(8,128)} %refs_9_.5) | copy-start | bytes 393220
  286.5 121.1 %copy-start.10 = (f32[256,128]{1,0:T(8,128)S(1)}, f32[256,128]{1,0:T(8,128)}, u32[]{:S(2)}) copy-start(f32[256,128]{1,0:T(8,128)} %get-tuple-element.72.refs_1_) | copy-start | bytes 393220
  403.2 4.4 %copy-start = (f32[128,2,656]{0,2,1:T(8,128)S(1)}, f32[128,2,656]{0,2,1:T(8,128)}, u32[]{:S(2)}) copy-start(f32[128,2,656]{0,2,1:T(8,128)} %param.25) | copy-start | bytes 2015236
  403.2 4.4 %copy-start.1 = (f32[1312,128]{1,0:T(8,128)S(1)}, f32[1312,128]{1,0:T(8,128)}, u32[]{:S(2)}) copy-start(f32[1312,128]{1,0:T(8,128)} %get-tuple-element.73.refs_2_) | copy-start | bytes 2015236
  403.2 4.4 %copy-start.2 = (f32[128,3,256]{2,0,1:T(8,128)S(1)}, f32[128,3,256]{2,0,1:T(8,128)}, u32[]{:S(2)}) copy-start(f32[128,3,256]{2,0,1:T(8,128)} %param.23) | copy-start | bytes 1179652
  403.2 4.4 %copy-start.3 = (f32[768,128]{1,0:T(8,128)S(1)}, f32[768,128]{1,0:T(8,128)}, u32[]{:S(2)}) copy-start(f32[768,128]{1,0:T(8,128)} %get-tuple-element.71.refs_0_) | copy-start | bytes 1179652
  403.2 4.4 %copy-start.4 = (bf16[128,2,656]{0,2,1:T(8,128)(2,1)S(1)}, bf16[128,2,656]{0,2,1:T(8,128)(2,1)}, u32[]{:S(2)}) copy-start(bf16[128,2,656]{0,2,1:T(8,128)(2,1)} %param.20) | copy-start | bytes 1007620
  403.2 4.4 %copy-start.5 = (f32[128,656]{0,1:T(8,128)S(1)}, f32[128,656]{0,1:T(8,128)}, u32[]{:S(2)}) copy-start(f32[128,656]{0,1:T(8,128)} %param.26) | copy-start | bytes 1007620
  403.2 4.4 %copy-start.6 = (f32[656,128]{1,0:T(8,128)S(1)}, f32[656,128]{1,0:T(8,128)}, u32[]{:S(2)}) copy-start(f32[656,128]{1,0:T(8,128)} %get-tuple-element.74.refs_3_) | copy-start | bytes 1007620
  403.3 4.4 %copy-start.12 = (bf16[128,256]{1,0:T(8,128)(2,1)S(1)}, bf16[128,256]{1,0:T(8,128)(2,1)}, u32[]{:S(2)}) copy-start(bf16[128,256]{1,0:T(8,128)(2,1)} %refs_13_.1) | copy-start | bytes 196612
  407.7 1.0 copy-start.11
  408.6 0.9 copy-start.13
  409.6 0.9 copy-start.14
  410.5 0.8 copy-start.15
  411.3 1.9 copy-start.16
